TPU v7x, 32 devices: a whole 2x2x4 slice. The times are simulated.
32 devices in a mesh: row: 4 (over y, core), col: 4 (over z), bin: 2 (over x).
Axes of the slice: x: 2, y: 2, z: 4, core: 2. Of those that a mesh axis runs over, the one named last changes fastest.
Arguments:
- records: bfloat16 [4096, 6656], P('row', 'col'), may hold values from -400 to 400
- offsets: int32 [4], P('col'), may hold values from 0 to 164, as said below
- live_flags: int32 [4096], P('row'), may hold values 0 or 1
Outputs:
- cross_spectra: bfloat16 [32, 2, 4096, 4096], P('bin', None, 'row', 'col')
Inputs may be any that keep to these rules, and one draw needn't show every extreme that they name: `offsets`: some window has delay 0 and some has delay 164.
All inputs are finite; a program needn't handle non-finite values. No bound on the sum of `live_flags` on one device may be relied on, other than what follows from the above.
Results may differ from a plain program's by a relative error of at most 0.007.
Values sent between devices are 32-bit elements; how exact they have to be, the bound alone decides.
No kernel may reach another device: no remote copies, remote signals or barrier semaphores. Data moves between devices by JAX's collectives and lax.ppermute only.
A program may use at most 192 MiB of HBM per device.

v0:
```python
import math

import jax
import jax.numpy as jnp
from jax import lax
from jax.sharding import PartitionSpec as P

L = 1500
NB = 32
BSTEP = 6


epsilon = 1e-05


def broadcast(block, axis, holder):
    block = jnp.where(lax.axis_index(axis) == holder, block, jnp.zeros_like(block))
    return lax.psum(block, axis)


def make_table(first_bin, bin_count, length, stride):
    bin_ids = (first_bin + lax.iota(jnp.int32, bin_count) + 1) * stride
    sample_ids = lax.iota(jnp.int32, length)
    angles = (bin_ids[:, None] * sample_ids[None, :] % length).astype(jnp.float32) * (
        2.0 * math.pi / length
    )
    tapering = 0.5 - 0.5 * jnp.cos(sample_ids.astype(jnp.float32) * (2.0 * math.pi / length))
    return jnp.stack([jnp.cos(angles) * tapering, -jnp.sin(angles) * tapering]).astype(jnp.bfloat16)


def spectra_of(records, offsets, dft_table):
    bin_count = dft_table.shape[1]
    length = dft_table.shape[2]
    flat_table = dft_table.reshape(2 * bin_count, length)
    segment = lax.dynamic_slice_in_dim(records, 0 + offsets[0], length, 1)
    product = lax.dot_general(
        flat_table, segment, (((1,), (1,)), ((), ())), preferred_element_type=jnp.float32
    )
    spectra_list = [product.reshape(2, bin_count, records.shape[0])]
    return jnp.stack(spectra_list)


def combine_block(right_block):
    turned = jnp.stack([-right_block[:, 1], right_block[:, 0]], axis=1)
    return jnp.stack([right_block, turned], axis=2)


def stack_terms(left_block, paired):
    return jnp.einsum(
        "wpfc,wpqfd->fqcd",
        left_block,
        paired,
        precision=lax.Precision.HIGHEST,
        preferred_element_type=jnp.float32,
    )


def per_device(records, offsets, live_flags):
    per_half = NB // lax.axis_size("bin")
    bin_index = lax.axis_index("bin")
    spectra = spectra_of(records, offsets, make_table(bin_index * per_half, per_half, L, BSTEP))
    energy = lax.psum(jnp.sum(spectra * spectra, axis=(1, 2)), "bin") / (2 * NB)
    scaling = live_flags.astype(jnp.float32) / jnp.sqrt(energy + epsilon)
    whitened = spectra * scaling[:, None, None, :]
    windows = whitened.shape[0] * lax.axis_size("col")
    own_block = lax.all_gather(whitened, "col", axis=0, tiled=True)
    mirror_rows = broadcast(own_block, "row", lax.axis_index("col"))
    stacked = stack_terms(own_block, combine_block(mirror_rows))
    return (stacked / windows).astype(jnp.bfloat16)


def solution(mesh):
    in_specs = (P("row", "col"), P("col"), P("row"))
    out_specs = P("bin", None, "row", "col")
    return jax.shard_map(
        per_device, mesh=mesh, in_specs=in_specs, out_specs=out_specs, check_vma=False
    )
```

profile of v0, /device:TPU:0, one launch (start us, length us, event | category | flops | bytes accessed | tf_op | source)
XLA Modules:
  0.0 275.5 jit_solution(7527861671928079049)
XLA Ops:
  6.5 0.0 copy-start
  6.5 0.0 all-reduce.2.cloned.1.call-start
  6.5 0.1 multiply_subtract_fusion
  7.4 0.9 convert_element_type.40
  8.3 0.5 multiply_convert_fusion.1
  8.8 0.7 pad_maximum_fusion
  9.4 0.0 copy-done
  9.4 2.2 multiply_reduce_fusion
  11.6 5.8 %psum.14 = f32[1,1024]{1,0:T(1,128)S(1)} all-reduce(f32[1,1024]{1,0:T(1,128)S(1)} %bitcast.33), channel_id=1, replica_groups=mesh['row'=4,'col'=4,'bin'=2] {'bin'}, use_global_device_ids=true, to_apply=%region_1.2 | all-reduce | flops 1024 | bytes 8192 | tf_op jit(solution)/shard_map/psum | solution.py:62
  17.5 16.5 %all_gather.3 = f32[4,2,16,1024]{3,2,1,0:T(8,128)} all-gather(f32[1,2,16,1024]{3,2,1,0:T(8,128)S(1)} %broadcast_multiply_fusion), channel_id=1, replica_groups=mesh['row'=4,'col'=4,'bin'=2] {'col'}, dimensions={0}, use_global_device_ids=true | all-gather | bytes 655360 | tf_op jit(solution)/shard_map/all_gather | solution.py:66
  34.0 2.2 copy_select_fusion
  36.3 0.0 all-reduce.2.cloned.1.call-update
  36.3 35.0 %all-reduce.2.cloned.1.call-done = f32[4,2,16,1024]{3,0,1,2:T(4,128)} async-done(((f32[4,2,16,1024]{3,0,1,2:T(4,128)}), f32[4,2,16,1024]{3,0,1,2:T(4,128)}) %all-reduce.2.cloned.1.call-update) | async-done | bytes 524304 | tf_op jit(solution)/shard_map/psum | solution.py:18
  71.3 1.1 slice_negate_fusion
  72.4 0.1 maximum_bitcast_fusion
  72.5 1.3 fusion.19
  73.8 112.2 %fusion.1 = bf16[16,2,1024,1024]{2,3,1,0:T(8,128)(2,1)} fusion(f32[4,2,16,1024,1]{3,2,1,0,4:T(8,128)} %bitcast.28, f32[4,2,2,16,1024]{4,0,1,2,3:T(4,128)S(1)} %fusion.19), kind=kOutput, calls=%fused_computation.2 | convolution fusion | flops 3288334336 | bytes 68681728 | tf_op jit(solution)/shard_map/wpfc,wpqfd->fqcd/dot_general | solution.py:49
  186.1 82.6 %copy.10 = bf16[16,2,1024,1024]{3,2,1,0:T(8,128)(2,1)} copy(bf16[16,2,1024,1024]{2,3,1,0:T(8,128)(2,1)} %fusion.1) | data formatting | bytes 134217728 | tf_op jit(solution)/shard_map/convert_element_type | solution.py:69
  (3 shorter events, 0.0 us)
Async XLA Ops:
  6.5 2.9 %copy-start = (bf16[1024,1664]{1,0:T(8,128)(2,1)S(1)}, bf16[1024,1664]{1,0:T(8,128)(2,1)}, u32[]{:S(2)}) copy-start(bf16[1024,1664]{1,0:T(8,128)(2,1)} %param.3) | copy-start | bytes 10223620
  6.5 64.7 %all-reduce.2.cloned.1.call-start = ((), (), s32[]{:S(2)}) async-start(), calls=%async_computation | async-start | bytes 1048576 | tf_op jit(solution)/shard_map/psum | solution.py:18
Sparse Core Ops, SparseCore 0:
  36.4 34.8 all-reduce.1
where the time goes:
time: 278 us; the launch traced here: 275 us
  matrix products  114 us (41%)
  local copies, waits for them, and re-layouts  82.6 us (30%)
  waiting for transfers between devices  35 us (13%)
  blocking collectives  22.4 us (8%)
  between operations  14.2 us (5%)
  other arithmetic  6.87 us (2%)
    dot_general x1, matrix products, stack_terms(): jnp.einsum('wpfc,wpqfd->fqcd', left_block, paired, precision=lax.Precisio...  112 us
    convert_element_type x1, local copies, waits for them, and re-layouts, per_device(): return (stacked / windows).astype(jnp.bfloat16)  82.6 us
    psum x1, waiting for transfers between devices, broadcast(): return lax.psum(block, axis)  35 us
    all_gather x1, blocking collectives, per_device(): own_block = lax.all_gather(whitened, 'col', axis=0, tiled=True)  16.5 us
    psum x1, blocking collectives, per_device(): energy = lax.psum(jnp.sum(spectra * spectra, axis=(1, 2)), 'bin') / (2 * NB)  5.85 us
  transfers between devices with their start and end apart: 1, of which 1 were waited for; matrix products, arithmetic and copies ran while one was open for 0% of the time, Pallas kernels for 0%

commit v1 on v0

v1 whole, which is shorter than its diff:
```python
import functools
import math

import jax
import jax.numpy as jnp
import numpy as np
from jax import lax
from jax.experimental import pallas as pl
from jax.experimental.pallas import tpu as pltpu
from jax.sharding import PartitionSpec as P

L = 1500
NB = 32
BSTEP = 6
EPSILON = 1e-05
GROUP = 4


def padded_table(width):
    k = (np.arange(NB) + 1) * BSTEP
    n = np.arange(L)
    angle = (k[:, None] * n[None, :] % L) * (2.0 * math.pi / L)
    taper = 0.5 - 0.5 * np.cos(n * (2.0 * math.pi / L))
    parts = np.stack([np.cos(angle) * taper, -np.sin(angle) * taper], axis=1)
    table = np.zeros((2 * NB, width), np.float32)
    table[:, :L] = parts.reshape(2 * NB, L)
    return jnp.asarray(table.astype(jnp.bfloat16))


def whiten_kernel(sizes, place_ref, table_ref, records_ref, live_ref, *refs):
    outs, (shifted, product) = refs[: len(sizes)], refs[len(sizes):]
    samples = records_ref.shape[1]

    @pl.when(pl.program_id(0) == 0)
    def _():
        turned = pltpu.roll(table_ref[...].astype(jnp.float32), place_ref[0], 1)
        shifted[...] = turned[:, :samples].astype(jnp.bfloat16)

    spectra = lax.dot_general(
        shifted[...], records_ref[...], (((1,), (1,)), ((), ())),
        preferred_element_type=jnp.float32,
    )
    product[...] = spectra
    energy = jnp.sum(spectra * spectra, axis=0, keepdims=True) / (2 * NB)
    scaling = live_ref[...].astype(jnp.float32) / jnp.sqrt(energy + EPSILON)
    held = 2 * sum(sizes)
    start = pl.multiple_of(place_ref[1] * held, 8)
    for size, out in zip(sizes, outs):
        out[...] = product[pl.ds(start, 2 * size), :] * scaling
        start = pl.multiple_of(start + 2 * size, 8)


def whiten(records, offset, bin_index, live, sizes):
    channels, samples = records.shape
    block = min(256, channels)
    width = -(-(samples + 128) // 128) * 128
    place = jnp.stack([offset, bin_index])
    return pl.pallas_call(
        functools.partial(whiten_kernel, sizes),
        grid_spec=pltpu.PrefetchScalarGridSpec(
            num_scalar_prefetch=1,
            grid=(channels // block,),
            in_specs=[
                pl.BlockSpec((2 * NB, width), lambda i, s: (0, 0)),
                pl.BlockSpec((block, samples), lambda i, s: (i, 0)),
                pl.BlockSpec((1, block), lambda i, s: (0, i)),
            ],
            out_specs=[pl.BlockSpec((2 * size, block), lambda i, s: (0, i)) for size in sizes],
            scratch_shapes=[
                pltpu.VMEM((2 * NB, samples), jnp.bfloat16),
                pltpu.VMEM((2 * NB, block), jnp.float32),
            ],
        ),
        out_shape=[jax.ShapeDtypeStruct((2 * size, channels), jnp.float32) for size in sizes],
        compiler_params=pltpu.CompilerParams(vmem_limit_bytes=32 * 2**20),
        cost_estimate=pl.CostEstimate(
            flops=4 * NB * samples * channels, bytes_accessed=2 * samples * channels, transcendentals=0
        ),
        name="whiten",
    )(place, padded_table(width), records, live.reshape(1, channels))


def split(values):
    high = values.astype(jnp.bfloat16).astype(jnp.float32)
    return high, values - high


def cross_kernel(windows, size, slots_ref, *refs):
    own, mirror = refs[:windows], refs[windows : 2 * windows]
    out_ref, held, left, right = refs[-4:]
    bin_id = pl.program_id(0)
    rows = 2 * GROUP
    terms = windows * rows
    groups = size // GROUP

    def gather(parts, first):
        for i, part in enumerate(parts):
            slot = slots_ref[first + i]
            for g in range(groups):
                at = pl.multiple_of(g * terms + slot * rows, 8)
                held[pl.ds(at, rows), :] = part[g * rows : (g + 1) * rows, :]

    @pl.when(bin_id == 0)
    def _():
        gather(own, 0)
        for g in range(groups):
            high, low = split(held[g * terms : (g + 1) * terms, :] * (1.0 / windows))
            stacked = jnp.concatenate([high, high, low], axis=0)
            left[g] = stacked.T.astype(jnp.bfloat16)
        gather(mirror, windows)
        for g in range(groups):
            values = held[g * terms : (g + 1) * terms, :]
            part = lax.broadcasted_iota(jnp.int32, values.shape, 0) % 2
            turned = jnp.where(
                part == 0, -pltpu.roll(values, terms - 1, 0), pltpu.roll(values, 1, 0)
            )
            for q, block in enumerate((values, turned)):
                high, low = split(block)
                stacked = jnp.concatenate([high, low, high], axis=0)
                right[g, q] = stacked.astype(jnp.bfloat16)

    group, inner = bin_id // GROUP, bin_id % GROUP
    lane = lax.broadcasted_iota(jnp.int32, (1, 3 * terms), 1)
    mask = jnp.where(lane % rows // 2 == inner, 1.0, 0.0).astype(jnp.bfloat16)
    picked = left[group] * mask
    columns = out_ref.shape[3]
    tile = min(512, columns)
    for q in range(2):
        for first in range(0, columns, tile):
            out_ref[0, q, :, first : first + tile] = jnp.dot(
                picked, right[group, q, :, first : first + tile], preferred_element_type=jnp.float32
            ).astype(jnp.bfloat16)


def cross(own, mirror, slots, so_far, first, size, bins):
    windows = len(own)
    channels = own[0].shape[1]
    terms = windows * 2 * GROUP
    groups = size // GROUP
    whole = pl.BlockSpec((2 * size, channels), lambda f, s: (0, 0))
    previous = [] if so_far is None else [so_far]
    return pl.pallas_call(
        functools.partial(cross_kernel, windows, size),
        grid_spec=pltpu.PrefetchScalarGridSpec(
            num_scalar_prefetch=1,
            grid=(size,),
            in_specs=[whole] * (2 * windows) + [pl.BlockSpec(memory_space=pl.ANY)] * len(previous),
            out_specs=pl.BlockSpec((1, 2, channels, channels), lambda f, s: (f + first, 0, 0, 0)),
            scratch_shapes=[
                pltpu.VMEM((groups * terms, channels), jnp.float32),
                pltpu.VMEM((groups, channels, 3 * terms), jnp.bfloat16),
                pltpu.VMEM((groups, 2, 3 * terms, channels), jnp.bfloat16),
            ],
        ),
        out_shape=jax.ShapeDtypeStruct((bins, 2, channels, channels), jnp.bfloat16),
        input_output_aliases={2 * windows + 1: 0} if previous else {},
        compiler_params=pltpu.CompilerParams(vmem_limit_bytes=48 * 2**20),
        cost_estimate=pl.CostEstimate(
            flops=2 * size * 2 * channels * channels * 256,
            bytes_accessed=4 * size * channels * channels,
            transcendentals=0,
        ),
        name="cross",
    )(slots, *own, *mirror, *previous)


def per_device(records, offsets, live_flags):
    row, col = lax.axis_index("row"), lax.axis_index("col")
    n = lax.axis_size("col")
    bins = NB // lax.axis_size("bin")
    sizes = (GROUP, bins - GROUP)
    spectra = whiten(records, offsets[0], lax.axis_index("bin"), live_flags, sizes)
    steps = jnp.arange(n, dtype=jnp.int32)
    slots = jnp.concatenate([(col - steps) % n, (row - steps) % n])
    moved = []
    for block in spectra:
        own = [block] + [
            lax.ppermute(block, "col", [(c, (c + s) % n) for c in range(n)]) for s in range(1, n)
        ]
        mirror = [
            lax.ppermute(
                block, ("row", "col"),
                [(r * n + w, (w + s) % n * n + r) for r in range(n) for w in range(n)],
            )
            for s in range(n)
        ]
        moved.append((own, mirror))
    out, first = None, 0
    for (own, mirror), size in zip(moved, sizes):
        out = cross(own, mirror, slots, out, first, size, bins)
        first += size
    return out


def solution(mesh):
    in_specs = (P("row", "col"), P("col"), P("row"))
    out_specs = P("bin", None, "row", "col")
    return jax.shard_map(
        per_device, mesh=mesh, in_specs=in_specs, out_specs=out_specs, check_vma=False
    )
```

time: 278 us -> 74.2 us (0.27)
  matrix products: 114 us -> 0 us
  local copies, waits for them, and re-layouts: 82.6 us -> 3.59 us
  starting transfers between devices: 0.01 us -> 35.6 us
  waiting for transfers between devices: 35 us -> 0.7 us
  Pallas kernels: 0 us -> 33.2 us
  blocking collectives: 22.4 us -> 0 us
  between operations: 14.2 us -> 0.73 us
  other arithmetic: 6.87 us -> 0.16 us
    dot_general x2 -> x0, matrix products: 114 us -> none  [the longest x1 112 us: stack_terms(): jnp.einsum('wpfc,wpqfd->fqcd', left_block, paired, precision=lax.Precisio...]
    convert_element_type x1 -> x0, local copies, waits for them, and re-layouts: 82.6 us -> none  [per_device(): return (stacked / windows).astype(jnp.bfloat16)]
    ppermute x0 -> x14, starting transfers between devices: none -> 35.6 us  [the longest x6 24.7 us: per_device(): lax.ppermute(block, 'col', [(c, (c + s) % n) for c in range(n)])]
    psum x1 -> x0, waiting for transfers between devices: 35 us -> none  [broadcast(): return lax.psum(block, axis)]
    pallas_call x0 -> x3, Pallas kernels: none -> 33.2 us  [the longest x2 30.7 us: cross(): pl.pallas_call(functools.partial(cross_kernel, windows, size), grid_spec=...]
    all_gather x1 -> x0, blocking collectives: 16.5 us -> none  [per_device(): own_block = lax.all_gather(whitened, 'col', axis=0, tiled=True)]
    psum x1 -> x0, blocking collectives: 5.85 us -> none  [per_device(): energy = lax.psum(jnp.sum(spectra * spectra, axis=(1, 2)), 'bin') / (2 * NB)]
    unnamed x2 -> x6, local copies, waits for them, and re-layouts: 0.01 us -> 3.59 us
  transfers between devices with their start and end apart: 1 -> 14, of which waited for: 1 -> 2; matrix products, arithmetic and copies ran while one was open for 0% -> 0% of each run, Pallas kernels for 0% -> 12%
where the time goes in v1:
time: 74.2 us; the launch traced here: 74 us
  starting transfers between devices  35.6 us (48%)
  Pallas kernels  33.2 us (45%)
  local copies, waits for them, and re-layouts  3.59 us (5%)
    pallas_call x2, Pallas kernels, cross(): pl.pallas_call(functools.partial(cross_kernel, windows, size), grid_spec=...  30.7 us
    ppermute x6, starting transfers between devices, per_device(): lax.ppermute(block, 'col', [(c, (c + s) % n) for c in range(n)])  24.7 us
    ppermute x8, starting transfers between devices, per_device(): lax.ppermute(block, ('row', 'col'), [(r * n + w, (w + s) % n * n + r) for...  10.9 us
    unnamed x6, local copies, waits for them, and re-layouts  3.59 us
    pallas_call x1, Pallas kernels, whiten(): pl.pallas_call(functools.partial(whiten_kernel, sizes), grid_spec=pltpu.P...  2.51 us
  transfers between devices with their start and end apart: 14, of which 2 were waited for; matrix products, arithmetic and copies ran while one was open for 0% of the time, Pallas kernels for 12%

profile of v1, /device:TPU:0, one launch (start us, length us, event | category | flops | bytes accessed | tf_op | source)
XLA Modules:
  0.0 74.0 jit_solution(3857288342390859831)
XLA Ops:
  0.7 0.1 pad_add_fusion.1.place_ref
  0.7 2.0 %copy-done = bf16[1024,1664]{1,0:T(8,128)(2,1)S(1)} copy-done((bf16[1024,1664]{1,0:T(8,128)(2,1)S(1)}, bf16[1024,1664]{1,0:T(8,128)(2,1)}, u32[]{:S(2)}) %copy-start) | copy-done | bytes 3407896
  2.7 0.9 %copy-done.1 = bf16[64,1792]{1,0:T(8,128)(2,1)S(1)} copy-done((bf16[64,1792]{1,0:T(8,128)(2,1)S(1)}, bf16[64,1792]{1,0:T(8,128)(2,1)}, u32[]{:S(2)}) %copy-start.1) | copy-done | bytes 229400
  3.6 0.7 copy-done.2
  4.3 2.5 %whiten.1 = (f32[8,1024]{1,0:T(8,128)S(1)}, f32[24,1024]{1,0:T(8,128)S(1)}) custom-call(s32[2]{0:T(128)S(1)} %pad_add_fusion.1.place_ref, bf16[64,1792]{1,0:T(8,128)(2,1)S(1)} %copy-done.1, bf16[1024,1664]{1,0:T(8,128)(2,1)S(1)} %copy-done, s32[1,1024]{1,0:T(1,128)S(1)} %bitcast.2), custom_call_target="tpu_custom_call" | custom-call | flops 218103808 | bytes 3407872 | tf_op jit(solution)/shard_map/whiten/pallas_call | solution.py:58
  6.8 2.5 %collective-permute-start.13 = (f32[8,1024]{1,0:T(8,128)S(1)}, f32[8,1024]{1,0:T(8,128)S(1)}, u32[]{:S(2)}, u32[]{:S(2)}) collective-permute-start(f32[8,1024]{1,0:T(8,128)S(1)} %get-tuple-element.8.refs_0_), channel_id=1, source_target_pairs={{0,24},{2,0},{4,8},{6,16},{8,26},{10,2},{12,10},{14,18},{16,28},{1... | collective-permute-start | bytes 98312 | tf_op jit(solution)/shard_map/ppermute | solution.py:181
  9.3 2.6 %collective-permute-start.12 = (f32[8,1024]{1,0:T(8,128)S(1)}, f32[8,1024]{1,0:T(8,128)S(1)}, u32[]{:S(2)}, u32[]{:S(2)}) collective-permute-start(f32[8,1024]{1,0:T(8,128)S(1)} %get-tuple-element.8.refs_0_), channel_id=1, source_target_pairs={{0,16},{2,24},{4,0},{6,8},{8,18},{10,26},{12,2},{14,10},{16,20},{1... | collective-permute-start | bytes 98312 | tf_op jit(solution)/shard_map/ppermute | solution.py:181
  11.9 0.6 collective-permute-start.11
  12.5 0.7 collective-permute-start.10
  13.2 6.2 %collective-permute-start.9 = (f32[8,1024]{1,0:T(8,128)S(1)}, f32[8,1024]{1,0:T(8,128)S(1)}, u32[]{:S(2)}, u32[]{:S(2)}) collective-permute-start(f32[8,1024]{1,0:T(8,128)S(1)} %get-tuple-element.8.refs_0_), channel_id=1, source_target_pairs={{0,6},{2,0},{4,2},{6,4},{1,7},{3,1},{5,3},{7,5},{8,14},{10,8},{12,... | collective-permute-start | bytes 98312 | tf_op jit(solution)/shard_map/ppermute | solution.py:178
  19.4 0.1 collective-permute-start.8
  19.5 0.6 collective-permute-start.7
  20.1 0.9 %collective-permute-start.6 = (f32[24,1024]{1,0:T(8,128)S(1)}, f32[24,1024]{1,0:T(8,128)S(1)}, u32[]{:S(2)}, u32[]{:S(2)}) collective-permute-start(f32[24,1024]{1,0:T(8,128)S(1)} %get-tuple-element.7.refs_0_), channel_id=1, source_target_pairs={{0,24},{2,0},{4,8},{6,16},{8,26},{10,2},{12,10},{14,18},{16,28},{1... | collective-permute-start | bytes 294920 | tf_op jit(solution)/shard_map/ppermute | solution.py:181
  20.9 2.1 %collective-permute-start.5 = (f32[24,1024]{1,0:T(8,128)S(1)}, f32[24,1024]{1,0:T(8,128)S(1)}, u32[]{:S(2)}, u32[]{:S(2)}) collective-permute-start(f32[24,1024]{1,0:T(8,128)S(1)} %get-tuple-element.7.refs_0_), channel_id=1, source_target_pairs={{0,16},{2,24},{4,0},{6,8},{8,18},{10,26},{12,2},{14,10},{16,20},{1... | collective-permute-start | bytes 294920 | tf_op jit(solution)/shard_map/ppermute | solution.py:181
  23.1 0.1 pad_add_fusion.slots_ref
  23.1 1.0 %collective-permute-start.4 = (f32[24,1024]{1,0:T(8,128)S(1)}, f32[24,1024]{1,0:T(8,128)S(1)}, u32[]{:S(2)}, u32[]{:S(2)}) collective-permute-start(f32[24,1024]{1,0:T(8,128)S(1)} %get-tuple-element.7.refs_0_), channel_id=1, source_target_pairs={{0,8},{2,16},{4,24},{6,0},{8,10},{10,18},{12,26},{14,2},{16,12},{1... | collective-permute-start | bytes 294920 | tf_op jit(solution)/shard_map/ppermute | solution.py:181
  24.1 0.4 collective-permute-done.8.refs_2_
  24.6 0.7 collective-permute-start.3
  25.2 0.2 collective-permute-done.7.refs_1_
  25.4 6.2 %collective-permute-start.2 = (f32[24,1024]{1,0:T(8,128)S(1)}, f32[24,1024]{1,0:T(8,128)S(1)}, u32[]{:S(2)}, u32[]{:S(2)}) collective-permute-start(f32[24,1024]{1,0:T(8,128)S(1)} %get-tuple-element.7.refs_0_), channel_id=1, source_target_pairs={{0,6},{2,0},{4,2},{6,4},{1,7},{3,1},{5,3},{7,5},{8,14},{10,8},{12,... | collective-permute-start | bytes 294920 | tf_op jit(solution)/shard_map/ppermute | solution.py:178
  31.6 9.9 %collective-permute-start.1 = (f32[24,1024]{1,0:T(8,128)S(1)}, f32[24,1024]{1,0:T(8,128)S(1)}, u32[]{:S(2)}, u32[]{:S(2)}) collective-permute-start(f32[24,1024]{1,0:T(8,128)S(1)} %get-tuple-element.7.refs_0_), channel_id=1, source_target_pairs={{0,4},{2,6},{4,0},{6,2},{1,5},{3,7},{5,1},{7,3},{8,12},{10,14},{12... | collective-permute-start | bytes 294920 | tf_op jit(solution)/shard_map/ppermute | solution.py:178
  41.5 1.8 %collective-permute-start = (f32[24,1024]{1,0:T(8,128)S(1)}, f32[24,1024]{1,0:T(8,128)S(1)}, u32[]{:S(2)}, u32[]{:S(2)}) collective-permute-start(f32[24,1024]{1,0:T(8,128)S(1)} %get-tuple-element.7.refs_0_), channel_id=1, source_target_pairs={{0,2},{2,4},{4,6},{6,0},{1,3},{3,5},{5,7},{7,1},{8,10},{10,12},{12... | collective-permute-start | bytes 294920 | tf_op jit(solution)/shard_map/ppermute | solution.py:178
  43.3 8.7 %cross.2.refs_8_ = bf16[16,2,1024,1024]{3,2,1,0:T(8,128)(2,1)} custom-call(s32[8]{0:T(128)S(1)} %pad_add_fusion.slots_ref, f32[8,1024]{1,0:T(8,128)S(1)} %get-tuple-element.8.refs_0_, f32[8,1024]{1,0:T(8,128)S(1)} %collective-permute-done.7.refs_1_, f32[8,1024]{1,0:T(8,128)S(1)} %collective-permute-done.8.refs_2_, ...), custom_call_target="tpu_custom_call" | custom-call | flops 4294967296 | bytes 16777216 | tf_op jit(solution)/shard_map/cross/pallas_call | solution.py:142
  52.0 22.0 %cross.3 = bf16[16,2,1024,1024]{3,2,1,0:T(8,128)(2,1)} custom-call(s32[8]{0:T(128)S(1)} %pad_add_fusion.slots_ref, f32[24,1024]{1,0:T(8,128)S(1)} %get-tuple-element.7.refs_0_, f32[24,1024]{1,0:T(8,128)S(1)} %collective-permute-done.refs_1_, f32[24,1024]{1,0:T(8,128)S(1)} %collective-permute-done.1.refs_2_, ...), custom_call_target="tpu_custom_call", output_to_operand_aliasing={{}: (9, {})} | custom-call | flops 12884901888 | bytes 50331648 | tf_op jit(solution)/shard_map/cross/pallas_call | solution.py:142
  (16 shorter events, 0.0 us)
Async XLA Ops:
  0.7 2.0 %copy-start = (bf16[1024,1664]{1,0:T(8,128)(2,1)S(1)}, bf16[1024,1664]{1,0:T(8,128)(2,1)}, u32[]{:S(2)}) copy-start(bf16[1024,1664]{1,0:T(8,128)(2,1)} %records_ref.1) | copy-start | bytes 10223620
  2.7 0.9 %copy-start.1 = (bf16[64,1792]{1,0:T(8,128)(2,1)S(1)}, bf16[64,1792]{1,0:T(8,128)(2,1)}, u32[]{:S(2)}) copy-start(bf16[64,1792]{1,0:T(8,128)(2,1)} %constant.33.clone.table_ref) | copy-start | bytes 688132
  3.6 0.7 copy-start.2
  6.8 12.5 %collective-permute-start.13 = (f32[8,1024]{1,0:T(8,128)S(1)}, f32[8,1024]{1,0:T(8,128)S(1)}, u32[]{:S(2)}, u32[]{:S(2)}) collective-permute-start(f32[8,1024]{1,0:T(8,128)S(1)} %get-tuple-element.8.refs_0_), channel_id=1, source_target_pairs={{0,24},{2,0},{4,8},{6,16},{8,26},{10,2},{12,10},{14,18},{16,28},{1... | collective-permute-start | bytes 98312 | tf_op jit(solution)/shard_map/ppermute | solution.py:181
  9.3 10.2 %collective-permute-start.12 = (f32[8,1024]{1,0:T(8,128)S(1)}, f32[8,1024]{1,0:T(8,128)S(1)}, u32[]{:S(2)}, u32[]{:S(2)}) collective-permute-start(f32[8,1024]{1,0:T(8,128)S(1)} %get-tuple-element.8.refs_0_), channel_id=1, source_target_pairs={{0,16},{2,24},{4,0},{6,8},{8,18},{10,26},{12,2},{14,10},{16,20},{1... | collective-permute-start | bytes 98312 | tf_op jit(solution)/shard_map/ppermute | solution.py:181
  11.9 8.2 %collective-permute-start.11 = (f32[8,1024]{1,0:T(8,128)S(1)}, f32[8,1024]{1,0:T(8,128)S(1)}, u32[]{:S(2)}, u32[]{:S(2)}) collective-permute-start(f32[8,1024]{1,0:T(8,128)S(1)} %get-tuple-element.8.refs_0_), channel_id=1, source_target_pairs={{0,8},{2,16},{4,24},{6,0},{8,10},{10,18},{12,26},{14,2},{16,12},{1... | collective-permute-start | bytes 98312 | tf_op jit(solution)/shard_map/ppermute | solution.py:181
  12.5 8.4 %collective-permute-start.10 = (f32[8,1024]{1,0:T(8,128)S(1)}, f32[8,1024]{1,0:T(8,128)S(1)}, u32[]{:S(2)}, u32[]{:S(2)}) collective-permute-start(f32[8,1024]{1,0:T(8,128)S(1)} %get-tuple-element.8.refs_0_), channel_id=1, source_target_pairs={{0,0},{2,8},{4,16},{6,24},{8,2},{10,10},{12,18},{14,26},{16,4},{18... | collective-permute-start | bytes 98312 | tf_op jit(solution)/shard_map/ppermute | solution.py:181
  13.2 10.0 %collective-permute-start.9 = (f32[8,1024]{1,0:T(8,128)S(1)}, f32[8,1024]{1,0:T(8,128)S(1)}, u32[]{:S(2)}, u32[]{:S(2)}) collective-permute-start(f32[8,1024]{1,0:T(8,128)S(1)} %get-tuple-element.8.refs_0_), channel_id=1, source_target_pairs={{0,6},{2,0},{4,2},{6,4},{1,7},{3,1},{5,3},{7,5},{8,14},{10,8},{12,... | collective-permute-start | bytes 98312 | tf_op jit(solution)/shard_map/ppermute | solution.py:178
  19.4 5.2 %collective-permute-start.8 = (f32[8,1024]{1,0:T(8,128)S(1)}, f32[8,1024]{1,0:T(8,128)S(1)}, u32[]{:S(2)}, u32[]{:S(2)}) collective-permute-start(f32[8,1024]{1,0:T(8,128)S(1)} %get-tuple-element.8.refs_0_), channel_id=1, source_target_pairs={{0,4},{2,6},{4,0},{6,2},{1,5},{3,7},{5,1},{7,3},{8,12},{10,14},{12... | collective-permute-start | bytes 98312 | tf_op jit(solution)/shard_map/ppermute | solution.py:178
  19.5 6.0 %collective-permute-start.7 = (f32[8,1024]{1,0:T(8,128)S(1)}, f32[8,1024]{1,0:T(8,128)S(1)}, u32[]{:S(2)}, u32[]{:S(2)}) collective-permute-start(f32[8,1024]{1,0:T(8,128)S(1)} %get-tuple-element.8.refs_0_), channel_id=1, source_target_pairs={{0,2},{2,4},{4,6},{6,0},{1,3},{3,5},{5,7},{7,1},{8,10},{10,12},{12... | collective-permute-start | bytes 98312 | tf_op jit(solution)/shard_map/ppermute | solution.py:178
  20.1 11.6 %collective-permute-start.6 = (f32[24,1024]{1,0:T(8,128)S(1)}, f32[24,1024]{1,0:T(8,128)S(1)}, u32[]{:S(2)}, u32[]{:S(2)}) collective-permute-start(f32[24,1024]{1,0:T(8,128)S(1)} %get-tuple-element.7.refs_0_), channel_id=1, source_target_pairs={{0,24},{2,0},{4,8},{6,16},{8,26},{10,2},{12,10},{14,18},{16,28},{1... | collective-permute-start | bytes 294920 | tf_op jit(solution)/shard_map/ppermute | solution.py:181
  20.9 20.6 %collective-permute-start.5 = (f32[24,1024]{1,0:T(8,128)S(1)}, f32[24,1024]{1,0:T(8,128)S(1)}, u32[]{:S(2)}, u32[]{:S(2)}) collective-permute-start(f32[24,1024]{1,0:T(8,128)S(1)} %get-tuple-element.7.refs_0_), channel_id=1, source_target_pairs={{0,16},{2,24},{4,0},{6,8},{8,18},{10,26},{12,2},{14,10},{16,20},{1... | collective-permute-start | bytes 294920 | tf_op jit(solution)/shard_map/ppermute | solution.py:181
  23.1 28.8 %collective-permute-start.4 = (f32[24,1024]{1,0:T(8,128)S(1)}, f32[24,1024]{1,0:T(8,128)S(1)}, u32[]{:S(2)}, u32[]{:S(2)}) collective-permute-start(f32[24,1024]{1,0:T(8,128)S(1)} %get-tuple-element.7.refs_0_), channel_id=1, source_target_pairs={{0,8},{2,16},{4,24},{6,0},{8,10},{10,18},{12,26},{14,2},{16,12},{1... | collective-permute-start | bytes 294920 | tf_op jit(solution)/shard_map/ppermute | solution.py:181
  24.6 27.4 %collective-permute-start.3 = (f32[24,1024]{1,0:T(8,128)S(1)}, f32[24,1024]{1,0:T(8,128)S(1)}, u32[]{:S(2)}, u32[]{:S(2)}) collective-permute-start(f32[24,1024]{1,0:T(8,128)S(1)} %get-tuple-element.7.refs_0_), channel_id=1, source_target_pairs={{0,0},{2,8},{4,16},{6,24},{8,2},{10,10},{12,18},{14,26},{16,4},{18... | collective-permute-start | bytes 294920 | tf_op jit(solution)/shard_map/ppermute | solution.py:181
  25.4 26.5 %collective-permute-start.2 = (f32[24,1024]{1,0:T(8,128)S(1)}, f32[24,1024]{1,0:T(8,128)S(1)}, u32[]{:S(2)}, u32[]{:S(2)}) collective-permute-start(f32[24,1024]{1,0:T(8,128)S(1)} %get-tuple-element.7.refs_0_), channel_id=1, source_target_pairs={{0,6},{2,0},{4,2},{6,4},{1,7},{3,1},{5,3},{7,5},{8,14},{10,8},{12,... | collective-permute-start | bytes 294920 | tf_op jit(solution)/shard_map/ppermute | solution.py:178
  31.6 20.3 %collective-permute-start.1 = (f32[24,1024]{1,0:T(8,128)S(1)}, f32[24,1024]{1,0:T(8,128)S(1)}, u32[]{:S(2)}, u32[]{:S(2)}) collective-permute-start(f32[24,1024]{1,0:T(8,128)S(1)} %get-tuple-element.7.refs_0_), channel_id=1, source_target_pairs={{0,4},{2,6},{4,0},{6,2},{1,5},{3,7},{5,1},{7,3},{8,12},{10,14},{12... | collective-permute-start | bytes 294920 | tf_op jit(solution)/shard_map/ppermute | solution.py:178
  41.5 10.5 %collective-permute-start = (f32[24,1024]{1,0:T(8,128)S(1)}, f32[24,1024]{1,0:T(8,128)S(1)}, u32[]{:S(2)}, u32[]{:S(2)}) collective-permute-start(f32[24,1024]{1,0:T(8,128)S(1)} %get-tuple-element.7.refs_0_), channel_id=1, source_target_pairs={{0,2},{2,4},{4,6},{6,0},{1,3},{3,5},{5,7},{7,1},{8,10},{10,12},{12... | collective-permute-start | bytes 294920 | tf_op jit(solution)/shard_map/ppermute | solution.py:178

commit v2 on v1

v2 whole, which is shorter than its diff:
```python
import functools
import math

import jax
import jax.numpy as jnp
import numpy as np
from jax import lax
from jax.experimental import pallas as pl
from jax.experimental.pallas import tpu as pltpu
from jax.sharding import PartitionSpec as P

L = 1500
NB = 32
BSTEP = 6
EPSILON = 1e-05
GROUP = 4


def padded_table(width):
    k = (np.arange(NB) + 1) * BSTEP
    n = np.arange(L)
    angle = (k[:, None] * n[None, :] % L) * (2.0 * math.pi / L)
    taper = 0.5 - 0.5 * np.cos(n * (2.0 * math.pi / L))
    parts = np.stack([np.cos(angle) * taper, -np.sin(angle) * taper], axis=1)
    table = np.zeros((2 * NB, width), np.float32)
    table[:, :L] = parts.reshape(2 * NB, L)
    return jnp.asarray(table.astype(jnp.bfloat16).astype(np.float32))


def whiten_kernel(sizes, place_ref, table_ref, records_ref, live_ref, *refs):
    outs, (shifted, product) = refs[: len(sizes)], refs[len(sizes):]
    samples = records_ref.shape[1]

    @pl.when(pl.program_id(0) == 0)
    def _():
        turned = pltpu.roll(table_ref[...], place_ref[0], 1)
        shifted[...] = turned[:, :samples].astype(jnp.bfloat16)

    spectra = lax.dot_general(
        shifted[...], records_ref[...], (((1,), (1,)), ((), ())),
        preferred_element_type=jnp.float32,
    )
    product[...] = spectra
    energy = jnp.sum(spectra * spectra, axis=0, keepdims=True) / (2 * NB)
    scaling = live_ref[...].astype(jnp.float32) / jnp.sqrt(energy + EPSILON)
    held = 2 * sum(sizes)
    start = pl.multiple_of(place_ref[1] * held, 8)
    for size, out in zip(sizes, outs):
        out[...] = product[pl.ds(start, 2 * size), :] * scaling
        start = pl.multiple_of(start + 2 * size, 8)


def whiten(records, offset, bin_index, live, sizes):
    channels, samples = records.shape
    block = min(256, channels)
    width = -(-(samples + 128) // 128) * 128
    place = jnp.stack([offset, bin_index])
    return pl.pallas_call(
        functools.partial(whiten_kernel, sizes),
        grid_spec=pltpu.PrefetchScalarGridSpec(
            num_scalar_prefetch=1,
            grid=(channels // block,),
            in_specs=[
                pl.BlockSpec((2 * NB, width), lambda i, s: (0, 0)),
                pl.BlockSpec((block, samples), lambda i, s: (i, 0)),
                pl.BlockSpec((1, block), lambda i, s: (0, i)),
            ],
            out_specs=[pl.BlockSpec((2 * size, block), lambda i, s: (0, i)) for size in sizes],
            scratch_shapes=[
                pltpu.VMEM((2 * NB, samples), jnp.bfloat16),
                pltpu.VMEM((2 * NB, block), jnp.float32),
            ],
        ),
        out_shape=[jax.ShapeDtypeStruct((2 * size, channels), jnp.float32) for size in sizes],
        compiler_params=pltpu.CompilerParams(vmem_limit_bytes=60 * 2**20),
        cost_estimate=pl.CostEstimate(
            flops=4 * NB * samples * channels, bytes_accessed=2 * samples * channels, transcendentals=0
        ),
        name="whiten",
    )(place, padded_table(width), records, live.reshape(1, channels))


def split(values):
    high = values.astype(jnp.bfloat16).astype(jnp.float32)
    return high, values - high


def stack_group(ref, group):
    rows = 2 * GROUP
    parts = [ref[w, group * rows : (group + 1) * rows, :] for w in range(ref.shape[0])]
    return jnp.concatenate(parts, axis=0)


def cross_kernel(size, wide, own, mirror, *refs):
    out_ref, left, right = refs[-3:]
    bin_id = pl.program_id(0)
    windows = own.shape[0]
    rows = 2 * GROUP
    terms = windows * rows

    @pl.when(bin_id == 0)
    def _():
        for g in range(size // GROUP):
            high, low = split(stack_group(own, g) * (1.0 / windows))
            left[g] = jnp.concatenate([high, high, low], axis=0).T.astype(jnp.bfloat16)
            values = stack_group(mirror, g)
            part = lax.broadcasted_iota(jnp.int32, values.shape, 0) % 2
            turned = jnp.where(
                part == 0, -pltpu.roll(values, terms - 1, 0), pltpu.roll(values, 1, 0)
            )
            for q, block in enumerate((values, turned)):
                high, low = split(block)
                right[g, q] = jnp.concatenate([high, low, high], axis=0).astype(jnp.bfloat16)

    group, inner = bin_id // GROUP, bin_id % GROUP
    lane = lax.broadcasted_iota(jnp.int32, (1, 3 * terms), 1)
    mask = jnp.where(lane % rows // 2 == inner, 1.0, 0.0).astype(jnp.bfloat16)
    channels = out_ref.shape[3]
    tile = min(256, channels)
    for q in range(2):
        for first in range(0, channels, tile):
            if wide:
                out_ref[0, q, first : first + tile, :] = jnp.dot(
                    left[group, first : first + tile, :] * mask, right[group, q],
                    preferred_element_type=jnp.float32,
                ).astype(jnp.bfloat16)
            else:
                out_ref[0, q, :, first : first + tile] = jnp.dot(
                    left[group] * mask, right[group, q, :, first : first + tile],
                    preferred_element_type=jnp.float32,
                ).astype(jnp.bfloat16)


def cross(own, mirror, so_far, first, size, bins, wide):
    windows, _, channels = own.shape
    terms = windows * 2 * GROUP
    groups = size // GROUP
    whole = pl.BlockSpec(own.shape, lambda f: (0, 0, 0))
    previous = [] if so_far is None else [so_far]
    return pl.pallas_call(
        functools.partial(cross_kernel, size, wide),
        grid=(size,),
        in_specs=[whole] * 2 + [pl.BlockSpec(memory_space=pl.ANY)] * len(previous),
        out_specs=pl.BlockSpec((1, 2, channels, channels), lambda f: (f + first, 0, 0, 0)),
        scratch_shapes=[
            pltpu.VMEM((groups, channels, 3 * terms), jnp.bfloat16),
            pltpu.VMEM((groups, 2, 3 * terms, channels), jnp.bfloat16),
        ],
        out_shape=jax.ShapeDtypeStruct((bins, 2, channels, channels), jnp.bfloat16),
        input_output_aliases={2: 0} if previous else {},
        compiler_params=pltpu.CompilerParams(vmem_limit_bytes=48 * 2**20),
        cost_estimate=pl.CostEstimate(
            flops=2 * size * 2 * channels * channels * 256,
            bytes_accessed=4 * size * channels * channels,
            transcendentals=0,
        ),
        name="cross",
    )(own, mirror, *previous)


def per_device(records, offsets, live_flags):
    n = lax.axis_size("col")
    bins = NB // lax.axis_size("bin")
    sizes = (GROUP, bins - GROUP)
    spectra = whiten(records, offsets[0], lax.axis_index("bin"), live_flags, sizes)
    swap = [(r * n + w, w * n + r) for r in range(n) for w in range(n)]
    moved = []
    for block in spectra:
        if moved:
            block, _ = lax.optimization_barrier((block, moved[-1][0]))
        other = lax.ppermute(block, ("row", "col"), swap)
        own, mirror = (
            lax.all_to_all(jnp.broadcast_to(x[None], (n, *x.shape)), axis, 0, 0)
            for x, axis in ((block, "col"), (other, "row"))
        )
        moved.append((own, mirror))
    out, first = None, 0
    for (own, mirror), size in zip(moved, sizes):
        out = cross(own, mirror, out, first, size, bins, first > 0)
        first += size
    return out


def solution(mesh):
    in_specs = (P("row", "col"), P("col"), P("row"))
    out_specs = P("bin", None, "row", "col")
    return jax.shard_map(
        per_device, mesh=mesh, in_specs=in_specs, out_specs=out_specs, check_vma=False
    )
```

time: 74.2 us -> 86.2 us (1.16)
  starting transfers between devices: 35.6 us -> 18.1 us
  blocking collectives: 0 us -> 16.1 us
  waiting for transfers between devices: 0.7 us -> 11.2 us
  Pallas kernels: 33.2 us -> 35 us
    ppermute x14 -> x2, starting transfers between devices: 35.6 us -> 2.94 us  [per_device(): other = lax.ppermute(block, ('row', 'col'), swap)]
    all_to_all x0 -> x1, blocking collectives: none -> 16.1 us  [per_device(): lax.all_to_all(jnp.broadcast_to(x[None], (n, *x.shape)), axis, 0, 0)]
    all_to_all x0 -> x3, starting transfers between devices: none -> 15.2 us  [per_device(): lax.all_to_all(jnp.broadcast_to(x[None], (n, *x.shape)), axis, 0, 0)]
    all_to_all x0 -> x3, waiting for transfers between devices: none -> 11.2 us  [per_device(): lax.all_to_all(jnp.broadcast_to(x[None], (n, *x.shape)), axis, 0, 0)]
    broadcast_in_dim x0 -> x4, local copies, waits for them, and re-layouts: none -> 3.78 us  [per_device(): jnp.broadcast_to(x[None], (n, *x.shape))]
    unnamed x6 -> x0, local copies, waits for them, and re-layouts: 3.59 us -> none
    pallas_call x1, Pallas kernels: 2.51 us -> 5.48 us  [whiten(): pl.pallas_call(functools.partial(whiten_kernel, sizes), grid_spec=pltpu.P...]
    pallas_call x2, Pallas kernels: 30.7 us -> 29.5 us  [cross(): pl.pallas_call(functools.partial(cross_kernel, size, wide), grid=(size,),...]
  transfers between devices with their start and end apart: 14 -> 5, of which waited for: 2 -> 3; matrix products, arithmetic and copies ran while one was open for 0% -> 0% of each run, Pallas kernels for 12% -> 9%
where the time goes in v2:
time: 86.2 us; the launch traced here: 85.5 us
  Pallas kernels  35 us (41%)
  starting transfers between devices  18.1 us (21%)
  blocking collectives  16.1 us (19%)
  waiting for transfers between devices  11.2 us (13%)
  local copies, waits for them, and re-layouts  3.78 us (4%)
    pallas_call x2, Pallas kernels, cross(): pl.pallas_call(functools.partial(cross_kernel, size, wide), grid=(size,),...  29.5 us
    all_to_all x1, blocking collectives, per_device(): lax.all_to_all(jnp.broadcast_to(x[None], (n, *x.shape)), axis, 0, 0)  16.1 us
    all_to_all x3, starting transfers between devices, per_device(): lax.all_to_all(jnp.broadcast_to(x[None], (n, *x.shape)), axis, 0, 0)  15.2 us
    all_to_all x3, waiting for transfers between devices, per_device(): lax.all_to_all(jnp.broadcast_to(x[None], (n, *x.shape)), axis, 0, 0)  11.2 us
    pallas_call x1, Pallas kernels, whiten(): pl.pallas_call(functools.partial(whiten_kernel, sizes), grid_spec=pltpu.P...  5.48 us
    broadcast_in_dim x4, local copies, waits for them, and re-layouts, per_device(): jnp.broadcast_to(x[None], (n, *x.shape))  3.78 us
    ppermute x2, starting transfers between devices, per_device(): other = lax.ppermute(block, ('row', 'col'), swap)  2.94 us
  transfers between devices with their start and end apart: 5, of which 3 were waited for; matrix products, arithmetic and copies ran while one was open for 0% of the time, Pallas kernels for 9%

profile of v2, /device:TPU:0, one launch (start us, length us, event | category | flops | bytes accessed | tf_op | source)
XLA Modules:
  0.0 85.5 jit_solution(5439867764448077932)
XLA Ops:
  0.7 0.6 pad_add_fusion.place_ref
  1.3 5.5 %whiten.1 = (f32[8,1024]{1,0:T(8,128)}, f32[24,1024]{1,0:T(8,128)}) custom-call(s32[2]{0:T(128)} %pad_add_fusion.place_ref, f32[64,1792]{1,0:T(8,128)} %constant.6.clone.table_ref, bf16[1024,1664]{1,0:T(8,128)(2,1)} %records_ref.1, s32[1,1024]{1,0:T(1,128)} %bitcast.2), custom_call_target="tpu_custom_call" | custom-call | flops 218103808 | bytes 3407872 | tf_op jit(solution)/shard_map/whiten/pallas_call | solution.py:58
  6.7 1.4 %broadcast_in_dim.8 = f32[4,8,1024]{2,1,0:T(8,128)} broadcast(f32[8,1024]{1,0:T(8,128)} %get-tuple-element.9), dimensions={1,2} | broadcast | bytes 163840 | tf_op jit(solution)/shard_map/broadcast_in_dim | solution.py:173
  8.2 6.3 %all-to-all-start = ((f32[4,8,1024]{2,1,0:T(8,128)}), f32[4,8,1024]{2,1,0:T(8,128)S(1)}, u32[]{:S(2)}, u32[]{:S(2)}) async-start(f32[4,8,1024]{2,1,0:T(8,128)} %broadcast_in_dim.8), calls=%async_computation | async-start | bytes 262144 | tf_op jit(solution)/shard_map/all_to_all | solution.py:173
  14.5 1.4 %collective-permute-start.1 = (f32[8,1024]{1,0:T(8,128)}, f32[8,1024]{1,0:T(8,128)S(1)}, u32[]{:S(2)}, u32[]{:S(2)}) collective-permute-start(f32[8,1024]{1,0:T(8,128)} %get-tuple-element.9), channel_id=1, source_target_pairs={{0,0},{2,8},{4,16},{6,24},{8,2},{10,10},{12,18},{14,26},{16,4},{18... | collective-permute-start | bytes 98312 | tf_op jit(solution)/shard_map/ppermute | solution.py:171
  15.9 0.0 collective-permute-done.1
  15.9 4.7 %all-to-all-done.own = f32[4,8,1024]{2,1,0:T(8,128)S(1)} async-done(((f32[4,8,1024]{2,1,0:T(8,128)}), f32[4,8,1024]{2,1,0:T(8,128)S(1)}, u32[]{:S(2)}, u32[]{:S(2)}) %all-to-all-start) | async-done | bytes 131104 | tf_op jit(solution)/shard_map/all_to_all | solution.py:173
  20.6 0.7 broadcast_in_dim.11
  21.3 5.3 %all-to-all-start.3 = ((f32[4,8,1024]{2,1,0:T(8,128)}), f32[4,8,1024]{2,1,0:T(8,128)S(1)}, u32[]{:S(2)}, u32[]{:S(2)}) async-start(f32[4,8,1024]{2,1,0:T(8,128)} %broadcast_in_dim.11), calls=%async_computation.3 | async-start | bytes 262144 | tf_op jit(solution)/shard_map/all_to_all | solution.py:173
  26.6 1.5 %collective-permute-start = (f32[24,1024]{1,0:T(8,128)}, f32[24,1024]{1,0:T(8,128)S(1)}, u32[]{:S(2)}, u32[]{:S(2)}) collective-permute-start(f32[24,1024]{1,0:T(8,128)} %get-tuple-element.10), channel_id=1, source_target_pairs={{0,0},{2,8},{4,16},{6,24},{8,2},{10,10},{12,18},{14,26},{16,4},{18... | collective-permute-start | bytes 294920 | tf_op jit(solution)/shard_map/ppermute | solution.py:171
  28.1 3.1 %all-to-all-done.3.mirror = f32[4,8,1024]{2,1,0:T(8,128)S(1)} async-done(((f32[4,8,1024]{2,1,0:T(8,128)}), f32[4,8,1024]{2,1,0:T(8,128)S(1)}, u32[]{:S(2)}, u32[]{:S(2)}) %all-to-all-start.3) | async-done | bytes 131104 | tf_op jit(solution)/shard_map/all_to_all | solution.py:173
  31.2 0.0 collective-permute-done
  31.2 16.1 %all_to_all.20.mirror = f32[4,24,1024]{2,1,0:T(8,128)S(1)} all-to-all(f32[4,24,1024]{2,1,0:T(8,128)S(1)} %broadcast_in_dim.10), channel_id=1, replica_groups=mesh['row'=4,'col'=4,'bin'=2] {'row'}, dimensions={0} | all-to-all | bytes 786432 | tf_op jit(solution)/shard_map/all_to_all | solution.py:173
  47.4 1.7 %broadcast_in_dim.9 = f32[4,24,1024]{2,1,0:T(8,128)} broadcast(f32[24,1024]{1,0:T(8,128)} %get-tuple-element.10), dimensions={1,2} | broadcast | bytes 491520 | tf_op jit(solution)/shard_map/broadcast_in_dim | solution.py:173
  49.0 3.6 %all-to-all-start.1 = ((f32[4,24,1024]{2,1,0:T(8,128)}), f32[4,24,1024]{2,1,0:T(8,128)S(1)}, u32[]{:S(2)}, u32[]{:S(2)}) async-start(f32[4,24,1024]{2,1,0:T(8,128)} %broadcast_in_dim.9), calls=%async_computation.1 | async-start | bytes 786432 | tf_op jit(solution)/shard_map/all_to_all | solution.py:173
  52.6 8.1 %cross.2.refs_0_ = bf16[16,2,1024,1024]{3,2,1,0:T(8,128)(2,1)} custom-call(f32[4,8,1024]{2,1,0:T(8,128)S(1)} %all-to-all-done.own, f32[4,8,1024]{2,1,0:T(8,128)S(1)} %all-to-all-done.3.mirror), custom_call_target="tpu_custom_call" | custom-call | flops 4294967296 | bytes 16777216 | tf_op jit(solution)/shard_map/cross/pallas_call | solution.py:140
  60.7 3.4 %all-to-all-done.1.own = f32[4,24,1024]{2,1,0:T(8,128)S(1)} async-done(((f32[4,24,1024]{2,1,0:T(8,128)}), f32[4,24,1024]{2,1,0:T(8,128)S(1)}, u32[]{:S(2)}, u32[]{:S(2)}) %all-to-all-start.1) | async-done | bytes 393248 | tf_op jit(solution)/shard_map/all_to_all | solution.py:173
  64.1 21.4 %cross.3 = bf16[16,2,1024,1024]{3,2,1,0:T(8,128)(2,1)} custom-call(f32[4,24,1024]{2,1,0:T(8,128)S(1)} %all-to-all-done.1.own, f32[4,24,1024]{2,1,0:T(8,128)S(1)} %all_to_all.20.mirror, bf16[16,2,1024,1024]{3,2,1,0:T(8,128)(2,1)} %cross.2.refs_0_), custom_call_target="tpu_custom_call", output_to_operand_aliasing={{}: (2, {})} | custom-call | flops 12884901888 | bytes 50331648 | tf_op jit(solution)/shard_map/cross/pallas_call | solution.py:140
  (1 shorter events, 0.0 us)
Async XLA Ops:
  8.2 12.4 %all-to-all-start = ((f32[4,8,1024]{2,1,0:T(8,128)}), f32[4,8,1024]{2,1,0:T(8,128)S(1)}, u32[]{:S(2)}, u32[]{:S(2)}) async-start(f32[4,8,1024]{2,1,0:T(8,128)} %broadcast_in_dim.8), calls=%async_computation | async-start | bytes 262144 | tf_op jit(solution)/shard_map/all_to_all | solution.py:173
  14.5 1.4 %collective-permute-start.1 = (f32[8,1024]{1,0:T(8,128)}, f32[8,1024]{1,0:T(8,128)S(1)}, u32[]{:S(2)}, u32[]{:S(2)}) collective-permute-start(f32[8,1024]{1,0:T(8,128)} %get-tuple-element.9), channel_id=1, source_target_pairs={{0,0},{2,8},{4,16},{6,24},{8,2},{10,10},{12,18},{14,26},{16,4},{18... | collective-permute-start | bytes 98312 | tf_op jit(solution)/shard_map/ppermute | solution.py:171
  21.3 9.9 %all-to-all-start.3 = ((f32[4,8,1024]{2,1,0:T(8,128)}), f32[4,8,1024]{2,1,0:T(8,128)S(1)}, u32[]{:S(2)}, u32[]{:S(2)}) async-start(f32[4,8,1024]{2,1,0:T(8,128)} %broadcast_in_dim.11), calls=%async_computation.3 | async-start | bytes 262144 | tf_op jit(solution)/shard_map/all_to_all | solution.py:173
  26.6 4.6 %collective-permute-start = (f32[24,1024]{1,0:T(8,128)}, f32[24,1024]{1,0:T(8,128)S(1)}, u32[]{:S(2)}, u32[]{:S(2)}) collective-permute-start(f32[24,1024]{1,0:T(8,128)} %get-tuple-element.10), channel_id=1, source_target_pairs={{0,0},{2,8},{4,16},{6,24},{8,2},{10,10},{12,18},{14,26},{16,4},{18... | collective-permute-start | bytes 294920 | tf_op jit(solution)/shard_map/ppermute | solution.py:171
  49.0 15.0 %all-to-all-start.1 = ((f32[4,24,1024]{2,1,0:T(8,128)}), f32[4,24,1024]{2,1,0:T(8,128)S(1)}, u32[]{:S(2)}, u32[]{:S(2)}) async-start(f32[4,24,1024]{2,1,0:T(8,128)} %broadcast_in_dim.9), calls=%async_computation.1 | async-start | bytes 786432 | tf_op jit(solution)/shard_map/all_to_all | solution.py:173

commit v3 on v2

v3 whole, which is shorter than its diff:
```python
import functools
import math

import jax
import jax.numpy as jnp
import numpy as np
from jax import lax
from jax.experimental import pallas as pl
from jax.experimental.pallas import tpu as pltpu
from jax.sharding import PartitionSpec as P

L = 1500
NB = 32
BSTEP = 6
EPSILON = 1e-05
GROUP = 4


def padded_table(width):
    k = (np.arange(NB) + 1) * BSTEP
    n = np.arange(L)
    angle = (k[:, None] * n[None, :] % L) * (2.0 * math.pi / L)
    taper = 0.5 - 0.5 * np.cos(n * (2.0 * math.pi / L))
    parts = np.stack([np.cos(angle) * taper, -np.sin(angle) * taper], axis=1)
    table = np.zeros((2 * NB, width), np.float32)
    table[:, :L] = parts.reshape(2 * NB, L)
    return jnp.asarray(table.astype(jnp.bfloat16).astype(np.float32))


def whiten_kernel(
    place_ref, table_hbm, records_hbm, live_hbm, out_ref, table, records, live, shifted, product, sems
):
    pieces, block, samples = records.shape
    copies = [
        pltpu.make_async_copy(table_hbm, table, sems.at[0]),
        pltpu.make_async_copy(live_hbm, live, sems.at[1]),
    ]
    for i in range(pieces):
        source = records_hbm.at[pl.ds(i * block, block)]
        copies.append(pltpu.make_async_copy(source, records.at[i], sems.at[2 + i]))
    for copy in copies:
        copy.start()
    copies[0].wait()
    turned = pltpu.roll(table[...], place_ref[0], 1)
    shifted[...] = turned[:, :samples].astype(jnp.bfloat16)
    copies[1].wait()
    held = out_ref.shape[0]
    start = pl.multiple_of(place_ref[1] * held, 8)
    for i in range(pieces):
        copies[2 + i].wait()
        spectra = lax.dot_general(
            shifted[...], records[i], (((1,), (1,)), ((), ())),
            preferred_element_type=jnp.float32,
        )
        product[...] = spectra
        energy = jnp.sum(spectra * spectra, axis=0, keepdims=True) / (2 * NB)
        columns = slice(i * block, (i + 1) * block)
        scaling = live[:, columns].astype(jnp.float32) / jnp.sqrt(energy + EPSILON)
        out_ref[:, columns] = product[pl.ds(start, held), :] * scaling


def whiten(records, offset, bin_index, live, bins):
    channels, samples = records.shape
    block = min(256, channels)
    pieces = channels // block
    width = -(-(samples + 128) // 128) * 128
    place = jnp.stack([offset, bin_index])
    return pl.pallas_call(
        whiten_kernel,
        in_specs=[pl.BlockSpec(memory_space=pltpu.SMEM)] + [pl.BlockSpec(memory_space=pl.ANY)] * 3,
        out_specs=pl.BlockSpec(memory_space=pltpu.VMEM),
        scratch_shapes=[
            pltpu.VMEM((2 * NB, width), jnp.float32),
            pltpu.VMEM((pieces, block, samples), jnp.bfloat16),
            pltpu.VMEM((1, channels), jnp.int32),
            pltpu.VMEM((2 * NB, samples), jnp.bfloat16),
            pltpu.VMEM((2 * NB, block), jnp.float32),
            pltpu.SemaphoreType.DMA((2 + pieces,)),
        ],
        out_shape=jax.ShapeDtypeStruct((2 * bins, channels), jnp.float32),
        compiler_params=pltpu.CompilerParams(vmem_limit_bytes=61 * 2**20),
        cost_estimate=pl.CostEstimate(
            flops=4 * NB * samples * channels, bytes_accessed=2 * samples * channels, transcendentals=0
        ),
        name="whiten",
    )(place, padded_table(width), records, live.reshape(1, channels))


def split(values):
    high = values.astype(jnp.bfloat16).astype(jnp.float32)
    return high, values - high


def cross_kernel(size, first, turn_ref, own_low, own_high, mirror_low, mirror_high, *refs):
    out_hbm, held, left, right, done, sems = refs[-6:]
    step = pl.program_id(0)
    half = own_low.shape[0]
    windows = 2 * half
    rows = 2 * GROUP
    terms = windows * rows
    channels = out_hbm.shape[3]
    tile = min(256, channels)
    tiles = channels // tile

    def gather(low, high, turn, group):
        for w in range(windows):
            part = (low if w < half else high)[w % half, group * rows : (group + 1) * rows, :]
            held[pl.ds(pl.multiple_of((w ^ turn) * rows, 8), rows), :] = part

    def copy(f, slot, q, t):
        piece = pl.ds(t * tile, tile)
        return pltpu.make_async_copy(
            done.at[slot, q, piece], out_hbm.at[first + f, q, piece], sems.at[slot, q * tiles + t]
        )

    @pl.when(step == 0)
    def _():
        for g in range(size // GROUP):
            gather(own_low, own_high, 0, g)
            high, low = split(held[...] * (1.0 / windows))
            left[g] = jnp.concatenate([high, high, low], axis=0).T.astype(jnp.bfloat16)
            gather(mirror_low, mirror_high, turn_ref[0], g)
            values = held[...]
            part = lax.broadcasted_iota(jnp.int32, values.shape, 0) % 2
            turned = jnp.where(
                part == 0, -pltpu.roll(values, terms - 1, 0), pltpu.roll(values, 1, 0)
            )
            for q, block in enumerate((values, turned)):
                high, low = split(block)
                right[g, q] = jnp.concatenate([high, low, high], axis=0).astype(jnp.bfloat16)

    group, inner = step // GROUP, step % GROUP
    slot = step % 2
    lane = lax.broadcasted_iota(jnp.int32, (1, 3 * terms), 1)
    mask = jnp.where(lane % rows // 2 == inner, 1.0, 0.0).astype(jnp.bfloat16)
    for q in range(2):
        for t in range(tiles):
            @pl.when(step >= 2)
            def _():
                copy(step - 2, slot, q, t).wait()

            done[slot, q, t * tile : (t + 1) * tile, :] = jnp.dot(
                left[group, t * tile : (t + 1) * tile, :] * mask, right[group, q],
                preferred_element_type=jnp.float32,
            ).astype(jnp.bfloat16)
            copy(step, slot, q, t).start()

    @pl.when(step == size - 1)
    def _():
        for f in (size - 2, size - 1):
            for q in range(2):
                for t in range(tiles):
                    copy(f, f % 2, q, t).wait()


def cross(turn, own, mirror, so_far, first, size, bins):
    windows = 2 * own[0].shape[0]
    channels = own[0].shape[2]
    terms = windows * 2 * GROUP
    groups = size // GROUP
    tiles = channels // min(256, channels)
    previous = [] if so_far is None else [so_far]
    return pl.pallas_call(
        functools.partial(cross_kernel, size, first),
        grid_spec=pltpu.PrefetchScalarGridSpec(
            num_scalar_prefetch=1,
            grid=(size,),
            in_specs=[pl.BlockSpec(x.shape, lambda f, s: (0, 0, 0)) for x in (*own, *mirror)]
            + [pl.BlockSpec(memory_space=pl.ANY)] * len(previous),
            out_specs=pl.BlockSpec(memory_space=pl.ANY),
            scratch_shapes=[
                pltpu.VMEM((terms, channels), jnp.float32),
                pltpu.VMEM((groups, channels, 3 * terms), jnp.bfloat16),
                pltpu.VMEM((groups, 2, 3 * terms, channels), jnp.bfloat16),
                pltpu.VMEM((2, 2, channels, channels), jnp.bfloat16),
                pltpu.SemaphoreType.DMA((2, 2 * tiles)),
            ],
        ),
        out_shape=jax.ShapeDtypeStruct((bins, 2, channels, channels), jnp.bfloat16),
        input_output_aliases={5: 0} if previous else {},
        compiler_params=pltpu.CompilerParams(vmem_limit_bytes=48 * 2**20),
        cost_estimate=pl.CostEstimate(
            flops=2 * size * 2 * channels * channels * 256,
            bytes_accessed=4 * size * channels * channels,
            transcendentals=0,
        ),
        name="cross",
    )(turn, *own, *mirror, *previous)


def exchange(block, axis, distance):
    n = lax.axis_size(axis)
    return lax.ppermute(block, axis, [(i, i ^ distance) for i in range(n)])


def double(block, axis):
    held, distance = block[None], 1
    while distance < lax.axis_size(axis) // 2:
        held = jnp.concatenate([held, exchange(held, axis, distance)])
        distance *= 2
    return held


def per_device(records, offsets, live_flags):
    row, col = lax.axis_index("row"), lax.axis_index("col")
    n = lax.axis_size("col")
    bins = NB // lax.axis_size("bin")
    sizes = (GROUP, bins - GROUP)
    whitened = whiten(records, offsets[0], lax.axis_index("bin"), live_flags, bins)
    turn = (row ^ col).reshape(1)
    other = lax.ppermute(
        whitened, ("row", "col"), [(r * n + w, w * n + r) for r in range(n) for w in range(n)]
    )
    own, mirror = double(whitened, "col"), double(other, "row")
    parts, first = [], 0
    for size in sizes:
        rows = slice(2 * first, 2 * (first + size))
        halves = (own[:, rows], mirror[:, rows])
        parts.append([(x, exchange(x, axis, n // 2)) for x, axis in zip(halves, ("col", "row"))])
        first += size
    out, first = None, 0
    for size, (own_pair, mirror_pair) in zip(sizes, parts):
        out = cross(turn, own_pair, mirror_pair, out, first, size, bins)
        first += size
    return out


def solution(mesh):
    in_specs = (P("row", "col"), P("col"), P("row"))
    out_specs = P("bin", None, "row", "col")
    return jax.shard_map(
        per_device, mesh=mesh, in_specs=in_specs, out_specs=out_specs, check_vma=False
    )
```

time: 86.2 us -> 68.2 us (0.79)
  blocking collectives: 16.1 us -> 0 us
  Pallas kernels: 35 us -> 43.7 us
  starting transfers between devices: 18.1 us -> 13.9 us
  waiting for transfers between devices: 11.2 us -> 7.26 us
  local copies, waits for them, and re-layouts: 3.78 us -> 0 us
  other arithmetic: 0.61 us -> 2.35 us
    all_to_all x1 -> x0, blocking collectives: 16.1 us -> none  [per_device(): lax.all_to_all(jnp.broadcast_to(x[None], (n, *x.shape)), axis, 0, 0)]
    all_to_all x3 -> x0, starting transfers between devices: 15.2 us -> none  [per_device(): lax.all_to_all(jnp.broadcast_to(x[None], (n, *x.shape)), axis, 0, 0)]
    all_to_all x3 -> x0, waiting for transfers between devices: 11.2 us -> none  [per_device(): lax.all_to_all(jnp.broadcast_to(x[None], (n, *x.shape)), axis, 0, 0)]
    ppermute x2 -> x7, starting transfers between devices: 2.94 us -> 13.9 us  [the longest x6 12.3 us: exchange(): return lax.ppermute(block, axis, [(i, i ^ distance) for i in range(n)])]
    pallas_call x3, Pallas kernels: 35 us -> 43.7 us  [the longest x2 38.6 us: cross(): pl.pallas_call(functools.partial(cross_kernel, size, first), grid_spec=pl...]
    ppermute x2 -> x7, waiting for transfers between devices: 0.01 us -> 7.26 us  [the longest x6 7.26 us: exchange(): return lax.ppermute(block, axis, [(i, i ^ distance) for i in range(n)])]
    broadcast_in_dim x4 -> x0, local copies, waits for them, and re-layouts: 3.78 us -> none  [per_device(): jnp.broadcast_to(x[None], (n, *x.shape))]
    concatenate x0 -> x4, other arithmetic: none -> 1.69 us  [double(): held = jnp.concatenate([held, exchange(held, axis, distance)])]
  transfers between devices with their start and end apart: 5 -> 7, of which waited for: 3 -> 2; matrix products, arithmetic and copies ran while one was open for 0% -> 2% of each run, Pallas kernels for 9% -> 15%
where the time goes in v3:
time: 68.2 us; the launch traced here: 67.9 us
  Pallas kernels  43.7 us (64%)
  starting transfers between devices  13.9 us (20%)
  waiting for transfers between devices  7.26 us (11%)
  other arithmetic  2.35 us (3%)
  between operations  0.7 us (1%)
    pallas_call x2, Pallas kernels, cross(): pl.pallas_call(functools.partial(cross_kernel, size, first), grid_spec=pl...  38.6 us
    ppermute x6, starting transfers between devices, exchange(): return lax.ppermute(block, axis, [(i, i ^ distance) for i in range(n)])  12.3 us
    ppermute x6, waiting for transfers between devices, exchange(): return lax.ppermute(block, axis, [(i, i ^ distance) for i in range(n)])  7.26 us
    pallas_call x1, Pallas kernels, whiten(): pl.pallas_call(whiten_kernel, in_specs=[pl.BlockSpec(memory_space=pltpu.S...  5.11 us
    concatenate x4, other arithmetic, double(): held = jnp.concatenate([held, exchange(held, axis, distance)])  1.69 us
    ppermute x1, starting transfers between devices, per_device(): lax.ppermute(whitened, ('row', 'col'), [(r * n + w, w * n + r) for r in r...  1.56 us
  transfers between devices with their start and end apart: 7, of which 2 were waited for; matrix products, arithmetic and copies ran while one was open for 2% of the time, Pallas kernels for 15%

profile of v3, /device:TPU:0, one launch (start us, length us, event | category | flops | bytes accessed | tf_op | source)
XLA Modules:
  0.0 67.9 jit_solution(15699272690410510819)
XLA Ops:
  0.7 0.7 pad_add_fusion.place_ref
  1.3 5.1 %whiten.1 = f32[32,1024]{1,0:T(8,128)} custom-call(s32[2]{0:T(128)} %pad_add_fusion.place_ref, f32[64,1792]{1,0:T(8,128)} %constant.13.clone.table_hbm, bf16[1024,1664]{1,0:T(8,128)(2,1)} %records_hbm.1, s32[1,1024]{1,0:T(1,128)} %bitcast.11), custom_call_target="tpu_custom_call" | custom-call | flops 218103808 | bytes 3407872 | tf_op jit(solution)/shard_map/whiten/pallas_call | solution.py:68
  6.4 1.6 %collective-permute-start.2 = (f32[32,1024]{1,0:T(8,128)}, f32[32,1024]{1,0:T(8,128)S(1)}, u32[]{:S(2)}, u32[]{:S(2)}) collective-permute-start(f32[32,1024]{1,0:T(8,128)} %whiten.1), channel_id=1, source_target_pairs={{0,0},{2,8},{4,16},{6,24},{8,2},{10,10},{12,18},{14,26},{16,4},{18... | collective-permute-start | bytes 393224 | tf_op jit(solution)/shard_map/ppermute | solution.py:211
  8.0 3.5 %collective-permute-start = (f32[1,32,1024]{2,1,0:T(8,128)}, f32[1,32,1024]{2,1,0:T(8,128)S(1)}, u32[]{:S(2)}, u32[]{:S(2)}) collective-permute-start(f32[1,32,1024]{2,1,0:T(8,128)} %bitcast.5), channel_id=1, source_target_pairs={{0,2},{2,0},{4,6},{6,4},{1,3},{3,1},{5,7},{7,5},{8,10},{10,8},{12,... | collective-permute-start | bytes 393224 | tf_op jit(solution)/shard_map/ppermute | solution.py:193
  11.5 0.0 collective-permute-done.2
  11.5 3.0 %collective-permute-start.3 = (f32[1,32,1024]{2,1,0:T(8,128)S(1)}, f32[1,32,1024]{2,1,0:T(8,128)S(1)}, u32[]{:S(2)}, u32[]{:S(2)}) collective-permute-start(f32[1,32,1024]{2,1,0:T(8,128)S(1)} %bitcast.8), channel_id=1, source_target_pairs={{0,8},{8,0},{16,24},{24,16},{1,9},{9,1},{17,25},{25,17},{2,10},{10... | collective-permute-start | bytes 393224 | tf_op jit(solution)/shard_map/ppermute | solution.py:193
  14.5 4.9 %collective-permute-done = f32[1,32,1024]{2,1,0:T(8,128)S(1)} collective-permute-done((f32[1,32,1024]{2,1,0:T(8,128)}, f32[1,32,1024]{2,1,0:T(8,128)S(1)}, u32[]{:S(2)}, u32[]{:S(2)}) %collective-permute-start) | collective-permute-done | bytes 131104 | tf_op jit(solution)/shard_map/ppermute | solution.py:193
  19.3 0.8 %pad_maximum_fusion.1.own_low = f32[2,8,1024]{2,1,0:T(8,128)S(1)} fusion(f32[1,32,1024]{2,1,0:T(8,128)S(1)} %collective-permute-done, f32[1,32,1024]{2,1,0:T(8,128)} %bitcast.6), kind=kLoop, calls=%fused_computation.7 | loop fusion | flops 16384 | bytes 327680 | tf_op jit(solution)/shard_map/concatenate | solution.py:199
  20.1 2.2 %collective-permute-start.5 = (f32[2,8,1024]{2,1,0:T(8,128)S(1)}, f32[2,8,1024]{2,1,0:T(8,128)S(1)}, u32[]{:S(2)}, u32[]{:S(2)}) collective-permute-start(f32[2,8,1024]{2,1,0:T(8,128)S(1)} %pad_maximum_fusion.1.own_low), channel_id=1, source_target_pairs={{0,4},{2,6},{4,0},{6,2},{1,5},{3,7},{5,1},{7,3},{8,12},{10,14},{12... | collective-permute-start | bytes 196616 | tf_op jit(solution)/shard_map/ppermute | solution.py:193
  22.3 0.9 %fusion.1.own_low = f32[2,24,1024]{2,1,0:T(8,128)S(1)} fusion(f32[1,32,1024]{2,1,0:T(8,128)} %bitcast.7, f32[1,32,1024]{2,1,0:T(8,128)S(1)} %collective-permute-done), kind=kLoop, calls=%fused_computation.5 | loop fusion | flops 49152 | bytes 458752 | tf_op jit(solution)/shard_map/concatenate | solution.py:199
  23.2 0.8 %collective-permute-start.1 = (f32[2,24,1024]{2,1,0:T(8,128)S(1)}, f32[2,24,1024]{2,1,0:T(8,128)S(1)}, u32[]{:S(2)}, u32[]{:S(2)}) collective-permute-start(f32[2,24,1024]{2,1,0:T(8,128)S(1)} %fusion.1.own_low), channel_id=1, source_target_pairs={{0,4},{2,6},{4,0},{6,2},{1,5},{3,7},{5,1},{7,3},{8,12},{10,14},{12... | collective-permute-start | bytes 589832 | tf_op jit(solution)/shard_map/ppermute | solution.py:193
  24.0 0.0 collective-permute-done.3
  24.0 2.8 %collective-permute-start.6 = (f32[2,8,1024]{2,1,0:T(8,128)S(1)}, f32[2,8,1024]{2,1,0:T(8,128)S(1)}, u32[]{:S(2)}, u32[]{:S(2)}) collective-permute-start(f32[2,8,1024]{2,1,0:T(8,128)S(1)} %pad_maximum_fusion.mirror_low), channel_id=1, source_target_pairs={{0,16},{8,24},{16,0},{24,8},{1,17},{9,25},{17,1},{25,9},{2,18},{10... | collective-permute-start | bytes 196616 | tf_op jit(solution)/shard_map/ppermute | solution.py:193
  26.8 0.1 collective-permute-start.4
  26.9 0.0 collective-permute-done.5.own_high
  26.9 2.4 %collective-permute-done.6.mirror_high = f32[2,8,1024]{2,1,0:T(8,128)S(1)} collective-permute-done((f32[2,8,1024]{2,1,0:T(8,128)S(1)}, f32[2,8,1024]{2,1,0:T(8,128)S(1)}, u32[]{:S(2)}, u32[]{:S(2)}) %collective-permute-start.6) | collective-permute-done | bytes 65568 | tf_op jit(solution)/shard_map/ppermute | solution.py:193
  29.3 10.1 %cross.2.refs_0_ = bf16[16,2,1024,1024]{3,2,1,0:T(8,128)(2,1)} custom-call(s32[1]{0:T(128)} %bitcast.turn_ref, f32[2,8,1024]{2,1,0:T(8,128)S(1)} %pad_maximum_fusion.1.own_low, f32[2,8,1024]{2,1,0:T(8,128)S(1)} %collective-permute-done.5.own_high, f32[2,8,1024]{2,1,0:T(8,128)S(1)} %pad_maximum_fusion.mirror_low, ...), custom_call_target="tpu_custom_call" | custom-call | flops 4294967296 | bytes 16777216 | tf_op jit(solution)/shard_map/cross/pallas_call | solution.py:163
  39.4 0.0 collective-permute-done.1.own_high
  39.4 0.0 collective-permute-done.4.mirror_high
  39.4 28.5 %cross.3 = bf16[16,2,1024,1024]{3,2,1,0:T(8,128)(2,1)} custom-call(s32[1]{0:T(128)} %bitcast.turn_ref, f32[2,24,1024]{2,1,0:T(8,128)S(1)} %fusion.1.own_low, f32[2,24,1024]{2,1,0:T(8,128)S(1)} %collective-permute-done.1.own_high, f32[2,24,1024]{2,1,0:T(8,128)S(1)} %fusion.mirror_low, ...), custom_call_target="tpu_custom_call", output_to_operand_aliasing={{}: (5, {})} | custom-call | flops 12884901888 | bytes 50331648 | tf_op jit(solution)/shard_map/cross/pallas_call | solution.py:163
  (2 shorter events, 0.0 us)
Async XLA Ops:
  6.4 5.0 %collective-permute-start.2 = (f32[32,1024]{1,0:T(8,128)}, f32[32,1024]{1,0:T(8,128)S(1)}, u32[]{:S(2)}, u32[]{:S(2)}) collective-permute-start(f32[32,1024]{1,0:T(8,128)} %whiten.1), channel_id=1, source_target_pairs={{0,0},{2,8},{4,16},{6,24},{8,2},{10,10},{12,18},{14,26},{16,4},{18... | collective-permute-start | bytes 393224 | tf_op jit(solution)/shard_map/ppermute | solution.py:211
  8.0 11.3 %collective-permute-start = (f32[1,32,1024]{2,1,0:T(8,128)}, f32[1,32,1024]{2,1,0:T(8,128)S(1)}, u32[]{:S(2)}, u32[]{:S(2)}) collective-permute-start(f32[1,32,1024]{2,1,0:T(8,128)} %bitcast.5), channel_id=1, source_target_pairs={{0,2},{2,0},{4,6},{6,4},{1,3},{3,1},{5,7},{7,5},{8,10},{10,8},{12,... | collective-permute-start | bytes 393224 | tf_op jit(solution)/shard_map/ppermute | solution.py:193
  11.5 12.6 %collective-permute-start.3 = (f32[1,32,1024]{2,1,0:T(8,128)S(1)}, f32[1,32,1024]{2,1,0:T(8,128)S(1)}, u32[]{:S(2)}, u32[]{:S(2)}) collective-permute-start(f32[1,32,1024]{2,1,0:T(8,128)S(1)} %bitcast.8), channel_id=1, source_target_pairs={{0,8},{8,0},{16,24},{24,16},{1,9},{9,1},{17,25},{25,17},{2,10},{10... | collective-permute-start | bytes 393224 | tf_op jit(solution)/shard_map/ppermute | solution.py:193
  20.1 6.8 %collective-permute-start.5 = (f32[2,8,1024]{2,1,0:T(8,128)S(1)}, f32[2,8,1024]{2,1,0:T(8,128)S(1)}, u32[]{:S(2)}, u32[]{:S(2)}) collective-permute-start(f32[2,8,1024]{2,1,0:T(8,128)S(1)} %pad_maximum_fusion.1.own_low), channel_id=1, source_target_pairs={{0,4},{2,6},{4,0},{6,2},{1,5},{3,7},{5,1},{7,3},{8,12},{10,14},{12... | collective-permute-start | bytes 196616 | tf_op jit(solution)/shard_map/ppermute | solution.py:193
  23.2 16.2 %collective-permute-start.1 = (f32[2,24,1024]{2,1,0:T(8,128)S(1)}, f32[2,24,1024]{2,1,0:T(8,128)S(1)}, u32[]{:S(2)}, u32[]{:S(2)}) collective-permute-start(f32[2,24,1024]{2,1,0:T(8,128)S(1)} %fusion.1.own_low), channel_id=1, source_target_pairs={{0,4},{2,6},{4,0},{6,2},{1,5},{3,7},{5,1},{7,3},{8,12},{10,14},{12... | collective-permute-start | bytes 589832 | tf_op jit(solution)/shard_map/ppermute | solution.py:193
  24.0 5.2 %collective-permute-start.6 = (f32[2,8,1024]{2,1,0:T(8,128)S(1)}, f32[2,8,1024]{2,1,0:T(8,128)S(1)}, u32[]{:S(2)}, u32[]{:S(2)}) collective-permute-start(f32[2,8,1024]{2,1,0:T(8,128)S(1)} %pad_maximum_fusion.mirror_low), channel_id=1, source_target_pairs={{0,16},{8,24},{16,0},{24,8},{1,17},{9,25},{17,1},{25,9},{2,18},{10... | collective-permute-start | bytes 196616 | tf_op jit(solution)/shard_map/ppermute | solution.py:193
  26.8 12.6 %collective-permute-start.4 = (f32[2,24,1024]{2,1,0:T(8,128)S(1)}, f32[2,24,1024]{2,1,0:T(8,128)S(1)}, u32[]{:S(2)}, u32[]{:S(2)}) collective-permute-start(f32[2,24,1024]{2,1,0:T(8,128)S(1)} %fusion.mirror_low), channel_id=1, source_target_pairs={{0,16},{8,24},{16,0},{24,8},{1,17},{9,25},{17,1},{25,9},{2,18},{10... | collective-permute-start | bytes 589832 | tf_op jit(solution)/shard_map/ppermute | solution.py:193

commit v4 on v3

--- a/solution.py
+++ b/solution.py
@@ -28,7 +28,7 @@
 
 
 def whiten_kernel(
-    place_ref, table_hbm, records_hbm, live_hbm, out_ref, table, records, live, shifted, product, sems
+    offset_ref, table_hbm, records_hbm, live_hbm, out_ref, table, records, live, shifted, product, sems
 ):
     pieces, block, samples = records.shape
     copies = [
@@ -41,30 +41,29 @@
     for copy in copies:
         copy.start()
     copies[0].wait()
-    turned = pltpu.roll(table[...], place_ref[0], 1)
+    turned = pltpu.roll(table[...], offset_ref[0], 1)
     shifted[...] = turned[:, :samples].astype(jnp.bfloat16)
     copies[1].wait()
     held = out_ref.shape[0]
-    start = pl.multiple_of(place_ref[1] * held, 8)
+    start = pl.multiple_of(lax.axis_index("bin") * held, 8)
     for i in range(pieces):
         copies[2 + i].wait()
         spectra = lax.dot_general(
-            shifted[...], records[i], (((1,), (1,)), ((), ())),
+            records[i], shifted[...], (((1,), (1,)), ((), ())),
             preferred_element_type=jnp.float32,
-        )
-        product[...] = spectra
+        ).T
+        product[i] = spectra
         energy = jnp.sum(spectra * spectra, axis=0, keepdims=True) / (2 * NB)
         columns = slice(i * block, (i + 1) * block)
         scaling = live[:, columns].astype(jnp.float32) / jnp.sqrt(energy + EPSILON)
-        out_ref[:, columns] = product[pl.ds(start, held), :] * scaling
-
-
-def whiten(records, offset, bin_index, live, bins):
+        out_ref[:, columns] = product[i, pl.ds(start, held), :] * scaling
+
+
+def whiten(records, offsets, live, bins):
     channels, samples = records.shape
     block = min(256, channels)
     pieces = channels // block
     width = -(-(samples + 128) // 128) * 128
-    place = jnp.stack([offset, bin_index])
     return pl.pallas_call(
         whiten_kernel,
         in_specs=[pl.BlockSpec(memory_space=pltpu.SMEM)] + [pl.BlockSpec(memory_space=pl.ANY)] * 3,
@@ -74,7 +73,7 @@
             pltpu.VMEM((pieces, block, samples), jnp.bfloat16),
             pltpu.VMEM((1, channels), jnp.int32),
             pltpu.VMEM((2 * NB, samples), jnp.bfloat16),
-            pltpu.VMEM((2 * NB, block), jnp.float32),
+            pltpu.VMEM((pieces, 2 * NB, block), jnp.float32),
             pltpu.SemaphoreType.DMA((2 + pieces,)),
         ],
         out_shape=jax.ShapeDtypeStruct((2 * bins, channels), jnp.float32),
@@ -83,7 +82,7 @@
             flops=4 * NB * samples * channels, bytes_accessed=2 * samples * channels, transcendentals=0
         ),
         name="whiten",
-    )(place, padded_table(width), records, live.reshape(1, channels))
+    )(offsets, padded_table(width), records, live.reshape(1, channels))
 
 
 def split(values):
@@ -91,7 +90,7 @@
     return high, values - high
 
 
-def cross_kernel(size, first, turn_ref, own_low, own_high, mirror_low, mirror_high, *refs):
+def cross_kernel(size, first, wide, turn_ref, own_low, own_high, mirror_low, mirror_high, *refs):
     out_hbm, held, left, right, done, sems = refs[-6:]
     step = pl.program_id(0)
     half = own_low.shape[0]
@@ -133,24 +132,31 @@
     slot = step % 2
     lane = lax.broadcasted_iota(jnp.int32, (1, 3 * terms), 1)
     mask = jnp.where(lane % rows // 2 == inner, 1.0, 0.0).astype(jnp.bfloat16)
-    for q in range(2):
-        for t in range(tiles):
-            @pl.when(step >= 2)
-            def _():
-                copy(step - 2, slot, q, t).wait()
-
+    pieces = [(q, t) for q in range(2) for t in range(tiles)]
+
+    @pl.when(step >= 2)
+    def _():
+        for q, t in pieces:
+            copy(step - 2, slot, q, t).wait()
+
+    picked = left[group] * mask
+    for q, t in pieces:
+        if wide:
             done[slot, q, t * tile : (t + 1) * tile, :] = jnp.dot(
-                left[group, t * tile : (t + 1) * tile, :] * mask, right[group, q],
-                preferred_element_type=jnp.float32,
+                picked[t * tile : (t + 1) * tile], right[group, q], preferred_element_type=jnp.float32
             ).astype(jnp.bfloat16)
-            copy(step, slot, q, t).start()
+        else:
+            done[slot, q, :, t * tile : (t + 1) * tile] = jnp.dot(
+                picked, right[group, q, :, t * tile : (t + 1) * tile], preferred_element_type=jnp.float32
+            ).astype(jnp.bfloat16)
+    for q, t in pieces:
+        copy(step, slot, q, t).start()
 
     @pl.when(step == size - 1)
     def _():
         for f in (size - 2, size - 1):
-            for q in range(2):
-                for t in range(tiles):
-                    copy(f, f % 2, q, t).wait()
+            for q, t in pieces:
+                copy(f, f % 2, q, t).wait()
 
 
 def cross(turn, own, mirror, so_far, first, size, bins):
@@ -161,7 +167,7 @@
     tiles = channels // min(256, channels)
     previous = [] if so_far is None else [so_far]
     return pl.pallas_call(
-        functools.partial(cross_kernel, size, first),
+        functools.partial(cross_kernel, size, first, first > 0),
         grid_spec=pltpu.PrefetchScalarGridSpec(
             num_scalar_prefetch=1,
             grid=(size,),
@@ -206,7 +212,7 @@
     n = lax.axis_size("col")
     bins = NB // lax.axis_size("bin")
     sizes = (GROUP, bins - GROUP)
-    whitened = whiten(records, offsets[0], lax.axis_index("bin"), live_flags, bins)
+    whitened = whiten(records, offsets, live_flags, bins)
     turn = (row ^ col).reshape(1)
     other = lax.ppermute(
         whitened, ("row", "col"), [(r * n + w, w * n + r) for r in range(n) for w in range(n)]

time: 68.2 us -> 57.1 us (0.84)
  Pallas kernels: 43.7 us -> 33.4 us
    pallas_call x2, Pallas kernels: 38.6 us -> 28.8 us  [cross(): pl.pallas_call(functools.partial(cross_kernel, size, first, first > 0), g...]
  transfers between devices with their start and end apart: 7 -> 7, of which waited for: 2 -> 2; matrix products, arithmetic and copies ran while one was open for 2% -> 3% of each run, Pallas kernels for 15% -> 14%
where the time goes in v4:
time: 57.1 us; the launch traced here: 56.9 us
  Pallas kernels  33.4 us (58%)
  starting transfers between devices  13.9 us (24%)
  waiting for transfers between devices  7.26 us (13%)
  other arithmetic  1.69 us (3%)
  between operations  0.7 us (1%)
    pallas_call x2, Pallas kernels, cross(): pl.pallas_call(functools.partial(cross_kernel, size, first, first > 0), g...  28.8 us
    ppermute x6, starting transfers between devices, exchange(): return lax.ppermute(block, axis, [(i, i ^ distance) for i in range(n)])  12.3 us
    ppermute x6, waiting for transfers between devices, exchange(): return lax.ppermute(block, axis, [(i, i ^ distance) for i in range(n)])  7.26 us
    pallas_call x1, Pallas kernels, whiten(): pl.pallas_call(whiten_kernel, in_specs=[pl.BlockSpec(memory_space=pltpu.S...  4.51 us
    concatenate x4, other arithmetic, double(): held = jnp.concatenate([held, exchange(held, axis, distance)])  1.69 us
    ppermute x1, starting transfers between devices, per_device(): lax.ppermute(whitened, ('row', 'col'), [(r * n + w, w * n + r) for r in r...  1.56 us
  transfers between devices with their start and end apart: 7, of which 2 were waited for; matrix products, arithmetic and copies ran while one was open for 3% of the time, Pallas kernels for 14%

profile of v4, /device:TPU:0, one launch (start us, length us, event | category | flops | bytes accessed | tf_op | source)
XLA Modules:
  0.0 56.9 jit_solution(10321062747540703712)
XLA Ops:
  0.7 4.5 %whiten.1 = f32[32,1024]{1,0:T(8,128)} custom-call(s32[1]{0:T(128)S(6)} %copy.7.offset_ref, f32[64,1792]{1,0:T(8,128)} %constant.11.clone.table_hbm, bf16[1024,1664]{1,0:T(8,128)(2,1)} %records_hbm.1, s32[1,1024]{1,0:T(1,128)} %bitcast.10), custom_call_target="tpu_custom_call" | custom-call | flops 218103808 | bytes 3407872 | tf_op jit(solution)/shard_map/whiten/pallas_call | solution.py:67
  5.2 1.6 %collective-permute-start.2 = (f32[32,1024]{1,0:T(8,128)}, f32[32,1024]{1,0:T(8,128)S(1)}, u32[]{:S(2)}, u32[]{:S(2)}) collective-permute-start(f32[32,1024]{1,0:T(8,128)} %whiten.1), channel_id=1, source_target_pairs={{0,0},{2,8},{4,16},{6,24},{8,2},{10,10},{12,18},{14,26},{16,4},{18... | collective-permute-start | bytes 393224 | tf_op jit(solution)/shard_map/ppermute | solution.py:217
  6.7 3.5 %collective-permute-start = (f32[1,32,1024]{2,1,0:T(8,128)}, f32[1,32,1024]{2,1,0:T(8,128)S(1)}, u32[]{:S(2)}, u32[]{:S(2)}) collective-permute-start(f32[1,32,1024]{2,1,0:T(8,128)} %bitcast.4), channel_id=1, source_target_pairs={{0,2},{2,0},{4,6},{6,4},{1,3},{3,1},{5,7},{7,5},{8,10},{10,8},{12,... | collective-permute-start | bytes 393224 | tf_op jit(solution)/shard_map/ppermute | solution.py:199
  10.2 0.0 collective-permute-done.2
  10.2 3.0 %collective-permute-start.3 = (f32[1,32,1024]{2,1,0:T(8,128)S(1)}, f32[1,32,1024]{2,1,0:T(8,128)S(1)}, u32[]{:S(2)}, u32[]{:S(2)}) collective-permute-start(f32[1,32,1024]{2,1,0:T(8,128)S(1)} %bitcast.7), channel_id=1, source_target_pairs={{0,8},{8,0},{16,24},{24,16},{1,9},{9,1},{17,25},{25,17},{2,10},{10... | collective-permute-start | bytes 393224 | tf_op jit(solution)/shard_map/ppermute | solution.py:199
  13.2 4.9 %collective-permute-done = f32[1,32,1024]{2,1,0:T(8,128)S(1)} collective-permute-done((f32[1,32,1024]{2,1,0:T(8,128)}, f32[1,32,1024]{2,1,0:T(8,128)S(1)}, u32[]{:S(2)}, u32[]{:S(2)}) %collective-permute-start) | collective-permute-done | bytes 131104 | tf_op jit(solution)/shard_map/ppermute | solution.py:199
  18.1 0.8 %pad_maximum_fusion.1.own_low = f32[2,8,1024]{2,1,0:T(8,128)S(1)} fusion(f32[1,32,1024]{2,1,0:T(8,128)S(1)} %collective-permute-done, f32[1,32,1024]{2,1,0:T(8,128)} %bitcast.5), kind=kLoop, calls=%fused_computation.7 | loop fusion | flops 16384 | bytes 327680 | tf_op jit(solution)/shard_map/concatenate | solution.py:205
  18.8 2.2 %collective-permute-start.5 = (f32[2,8,1024]{2,1,0:T(8,128)S(1)}, f32[2,8,1024]{2,1,0:T(8,128)S(1)}, u32[]{:S(2)}, u32[]{:S(2)}) collective-permute-start(f32[2,8,1024]{2,1,0:T(8,128)S(1)} %pad_maximum_fusion.1.own_low), channel_id=1, source_target_pairs={{0,4},{2,6},{4,0},{6,2},{1,5},{3,7},{5,1},{7,3},{8,12},{10,14},{12... | collective-permute-start | bytes 196616 | tf_op jit(solution)/shard_map/ppermute | solution.py:199
  21.1 0.9 %fusion.1.own_low = f32[2,24,1024]{2,1,0:T(8,128)S(1)} fusion(f32[1,32,1024]{2,1,0:T(8,128)} %bitcast.6, f32[1,32,1024]{2,1,0:T(8,128)S(1)} %collective-permute-done), kind=kLoop, calls=%fused_computation.5 | loop fusion | flops 49152 | bytes 458752 | tf_op jit(solution)/shard_map/concatenate | solution.py:205
  22.0 0.8 %collective-permute-start.1 = (f32[2,24,1024]{2,1,0:T(8,128)S(1)}, f32[2,24,1024]{2,1,0:T(8,128)S(1)}, u32[]{:S(2)}, u32[]{:S(2)}) collective-permute-start(f32[2,24,1024]{2,1,0:T(8,128)S(1)} %fusion.1.own_low), channel_id=1, source_target_pairs={{0,4},{2,6},{4,0},{6,2},{1,5},{3,7},{5,1},{7,3},{8,12},{10,14},{12... | collective-permute-start | bytes 589832 | tf_op jit(solution)/shard_map/ppermute | solution.py:199
  22.7 0.0 collective-permute-done.3
  22.8 2.8 %collective-permute-start.6 = (f32[2,8,1024]{2,1,0:T(8,128)S(1)}, f32[2,8,1024]{2,1,0:T(8,128)S(1)}, u32[]{:S(2)}, u32[]{:S(2)}) collective-permute-start(f32[2,8,1024]{2,1,0:T(8,128)S(1)} %pad_maximum_fusion.mirror_low), channel_id=1, source_target_pairs={{0,16},{8,24},{16,0},{24,8},{1,17},{9,25},{17,1},{25,9},{2,18},{10... | collective-permute-start | bytes 196616 | tf_op jit(solution)/shard_map/ppermute | solution.py:199
  25.5 0.1 collective-permute-start.4
  25.6 0.0 collective-permute-done.5.own_high
  25.6 2.4 %collective-permute-done.6.mirror_high = f32[2,8,1024]{2,1,0:T(8,128)S(1)} collective-permute-done((f32[2,8,1024]{2,1,0:T(8,128)S(1)}, f32[2,8,1024]{2,1,0:T(8,128)S(1)}, u32[]{:S(2)}, u32[]{:S(2)}) %collective-permute-start.6) | collective-permute-done | bytes 65568 | tf_op jit(solution)/shard_map/ppermute | solution.py:199
  28.0 8.0 %cross.2.refs_0_ = bf16[16,2,1024,1024]{3,2,1,0:T(8,128)(2,1)} custom-call(s32[1]{0:T(128)} %bitcast.turn_ref, f32[2,8,1024]{2,1,0:T(8,128)S(1)} %pad_maximum_fusion.1.own_low, f32[2,8,1024]{2,1,0:T(8,128)S(1)} %collective-permute-done.5.own_high, f32[2,8,1024]{2,1,0:T(8,128)S(1)} %pad_maximum_fusion.mirror_low, ...), custom_call_target="tpu_custom_call" | custom-call | flops 4294967296 | bytes 16777216 | tf_op jit(solution)/shard_map/cross/pallas_call | solution.py:169
  36.0 0.0 collective-permute-done.1.own_high
  36.0 0.0 collective-permute-done.4.mirror_high
  36.0 20.8 %cross.3 = bf16[16,2,1024,1024]{3,2,1,0:T(8,128)(2,1)} custom-call(s32[1]{0:T(128)} %bitcast.turn_ref, f32[2,24,1024]{2,1,0:T(8,128)S(1)} %fusion.1.own_low, f32[2,24,1024]{2,1,0:T(8,128)S(1)} %collective-permute-done.1.own_high, f32[2,24,1024]{2,1,0:T(8,128)S(1)} %fusion.mirror_low, ...), custom_call_target="tpu_custom_call", output_to_operand_aliasing={{}: (5, {})} | custom-call | flops 12884901888 | bytes 50331648 | tf_op jit(solution)/shard_map/cross/pallas_call | solution.py:169
  (2 shorter events, 0.0 us)
Async XLA Ops:
  5.2 5.0 %collective-permute-start.2 = (f32[32,1024]{1,0:T(8,128)}, f32[32,1024]{1,0:T(8,128)S(1)}, u32[]{:S(2)}, u32[]{:S(2)}) collective-permute-start(f32[32,1024]{1,0:T(8,128)} %whiten.1), channel_id=1, source_target_pairs={{0,0},{2,8},{4,16},{6,24},{8,2},{10,10},{12,18},{14,26},{16,4},{18... | collective-permute-start | bytes 393224 | tf_op jit(solution)/shard_map/ppermute | solution.py:217
  6.7 11.3 %collective-permute-start = (f32[1,32,1024]{2,1,0:T(8,128)}, f32[1,32,1024]{2,1,0:T(8,128)S(1)}, u32[]{:S(2)}, u32[]{:S(2)}) collective-permute-start(f32[1,32,1024]{2,1,0:T(8,128)} %bitcast.4), channel_id=1, source_target_pairs={{0,2},{2,0},{4,6},{6,4},{1,3},{3,1},{5,7},{7,5},{8,10},{10,8},{12,... | collective-permute-start | bytes 393224 | tf_op jit(solution)/shard_map/ppermute | solution.py:199
  10.2 12.6 %collective-permute-start.3 = (f32[1,32,1024]{2,1,0:T(8,128)S(1)}, f32[1,32,1024]{2,1,0:T(8,128)S(1)}, u32[]{:S(2)}, u32[]{:S(2)}) collective-permute-start(f32[1,32,1024]{2,1,0:T(8,128)S(1)} %bitcast.7), channel_id=1, source_target_pairs={{0,8},{8,0},{16,24},{24,16},{1,9},{9,1},{17,25},{25,17},{2,10},{10... | collective-permute-start | bytes 393224 | tf_op jit(solution)/shard_map/ppermute | solution.py:199
  18.8 6.8 %collective-permute-start.5 = (f32[2,8,1024]{2,1,0:T(8,128)S(1)}, f32[2,8,1024]{2,1,0:T(8,128)S(1)}, u32[]{:S(2)}, u32[]{:S(2)}) collective-permute-start(f32[2,8,1024]{2,1,0:T(8,128)S(1)} %pad_maximum_fusion.1.own_low), channel_id=1, source_target_pairs={{0,4},{2,6},{4,0},{6,2},{1,5},{3,7},{5,1},{7,3},{8,12},{10,14},{12... | collective-permute-start | bytes 196616 | tf_op jit(solution)/shard_map/ppermute | solution.py:199
  22.0 14.0 %collective-permute-start.1 = (f32[2,24,1024]{2,1,0:T(8,128)S(1)}, f32[2,24,1024]{2,1,0:T(8,128)S(1)}, u32[]{:S(2)}, u32[]{:S(2)}) collective-permute-start(f32[2,24,1024]{2,1,0:T(8,128)S(1)} %fusion.1.own_low), channel_id=1, source_target_pairs={{0,4},{2,6},{4,0},{6,2},{1,5},{3,7},{5,1},{7,3},{8,12},{10,14},{12... | collective-permute-start | bytes 589832 | tf_op jit(solution)/shard_map/ppermute | solution.py:199
  22.8 5.2 %collective-permute-start.6 = (f32[2,8,1024]{2,1,0:T(8,128)S(1)}, f32[2,8,1024]{2,1,0:T(8,128)S(1)}, u32[]{:S(2)}, u32[]{:S(2)}) collective-permute-start(f32[2,8,1024]{2,1,0:T(8,128)S(1)} %pad_maximum_fusion.mirror_low), channel_id=1, source_target_pairs={{0,16},{8,24},{16,0},{24,8},{1,17},{9,25},{17,1},{25,9},{2,18},{10... | collective-permute-start | bytes 196616 | tf_op jit(solution)/shard_map/ppermute | solution.py:199
  25.5 10.5 %collective-permute-start.4 = (f32[2,24,1024]{2,1,0:T(8,128)S(1)}, f32[2,24,1024]{2,1,0:T(8,128)S(1)}, u32[]{:S(2)}, u32[]{:S(2)}) collective-permute-start(f32[2,24,1024]{2,1,0:T(8,128)S(1)} %fusion.mirror_low), channel_id=1, source_target_pairs={{0,16},{8,24},{16,0},{24,8},{1,17},{9,25},{17,1},{25,9},{2,18},{10... | collective-permute-start | bytes 589832 | tf_op jit(solution)/shard_map/ppermute | solution.py:199

commit v5 on v4

v5 whole, which is shorter than its diff:
```python
import functools
import math

import jax
import jax.numpy as jnp
import numpy as np
from jax import lax
from jax.experimental import pallas as pl
from jax.experimental.pallas import tpu as pltpu
from jax.sharding import PartitionSpec as P

L = 1500
NB = 32
BSTEP = 6
EPSILON = 1e-05
GROUP = 4
CHUNK = 128
SLOTS = 8


def padded_table(width):
    k = (np.arange(NB) + 1) * BSTEP
    n = np.arange(L)
    angle = (k[:, None] * n[None, :] % L) * (2.0 * math.pi / L)
    taper = 0.5 - 0.5 * np.cos(n * (2.0 * math.pi / L))
    parts = np.stack([np.cos(angle) * taper, -np.sin(angle) * taper], axis=1)
    table = np.zeros((2 * NB, width), np.float32)
    table[:, :L] = parts.reshape(2 * NB, L)
    return jnp.asarray(table.astype(jnp.bfloat16).astype(np.float32))


def whiten_kernel(
    offset_ref, table_hbm, records_hbm, live_hbm, *refs
):
    outs, (table, records, live, shifted, product, sems) = refs[:-6], refs[-6:]
    pieces, block, samples = records.shape
    copies = [
        pltpu.make_async_copy(table_hbm, table, sems.at[0]),
        pltpu.make_async_copy(live_hbm, live, sems.at[1]),
    ]
    for i in range(pieces):
        source = records_hbm.at[pl.ds(i * block, block)]
        copies.append(pltpu.make_async_copy(source, records.at[i], sems.at[2 + i]))
    for copy in copies:
        copy.start()
    copies[0].wait()
    turned = pltpu.roll(table[...], offset_ref[0], 1)
    shifted[...] = turned[:, :samples].astype(jnp.bfloat16)
    copies[1].wait()
    held = sum(out.shape[0] for out in outs)
    start = pl.multiple_of(lax.axis_index("bin") * held, 8)
    for i in range(pieces):
        copies[2 + i].wait()
        spectra = lax.dot_general(
            records[i], shifted[...], (((1,), (1,)), ((), ())),
            preferred_element_type=jnp.float32,
        ).T
        product[i] = spectra
        energy = jnp.sum(spectra * spectra, axis=0, keepdims=True) / (2 * NB)
        columns = slice(i * block, (i + 1) * block)
        scaling = live[:, columns].astype(jnp.float32) / jnp.sqrt(energy + EPSILON)
        at = start
        for out in outs:
            out[:, columns] = product[i, pl.ds(at, out.shape[0]), :] * scaling
            at = pl.multiple_of(at + out.shape[0], 8)


def whiten(records, offsets, live, sizes):
    channels, samples = records.shape
    block = min(256, channels)
    pieces = channels // block
    width = -(-(samples + 128) // 128) * 128
    return pl.pallas_call(
        whiten_kernel,
        in_specs=[pl.BlockSpec(memory_space=pltpu.SMEM)] + [pl.BlockSpec(memory_space=pl.ANY)] * 3,
        out_specs=[pl.BlockSpec(memory_space=pltpu.VMEM)] * len(sizes),
        scratch_shapes=[
            pltpu.VMEM((2 * NB, width), jnp.float32),
            pltpu.VMEM((pieces, block, samples), jnp.bfloat16),
            pltpu.VMEM((1, channels), jnp.int32),
            pltpu.VMEM((2 * NB, samples), jnp.bfloat16),
            pltpu.VMEM((pieces, 2 * NB, block), jnp.float32),
            pltpu.SemaphoreType.DMA((2 + pieces,)),
        ],
        out_shape=[jax.ShapeDtypeStruct((2 * size, channels), jnp.float32) for size in sizes],
        compiler_params=pltpu.CompilerParams(vmem_limit_bytes=32 * 2**20),
        cost_estimate=pl.CostEstimate(
            flops=4 * NB * samples * channels, bytes_accessed=2 * samples * channels, transcendentals=0
        ),
        name="whiten",
    )(offsets, *(
        pltpu.with_memory_space_constraint(x, pltpu.HBM)
        for x in (padded_table(width), records, live.reshape(1, channels))
    ))


def split(values):
    high = values.astype(jnp.bfloat16).astype(jnp.float32)
    return high, values - high


def cross_kernel(size, first, turn_ref, own_low, own_high, mirror_low, mirror_high, *refs):
    out_hbm, held, left, right, picked, done, sems = refs[-7:]
    step = pl.program_id(0)
    half = own_low.shape[0]
    windows = 2 * half
    rows = 2 * GROUP
    terms = windows * rows
    depth, channels = right.shape[1:]
    width = left.shape[1]
    tile = min(256, channels)
    pieces = [(q, t) for q in range(2) for t in range(channels // tile)]
    slot, inner = step % 2, step % GROUP

    def gather(low, high, turn):
        at = pl.multiple_of(step * 2, rows)
        for w in range(windows):
            part = (low if w < half else high)[w % half, pl.ds(at, rows), :]
            held[pl.ds(pl.multiple_of((w ^ turn) * rows, 8), rows), :] = part
        return held[...]

    def copy(f, slot, q, t):
        piece = pl.ds(t * tile, tile)
        return pltpu.make_async_copy(
            done.at[slot, q, piece], out_hbm.at[first + f, q, piece], sems.at[slot, q * (channels // tile) + t]
        )

    @pl.when(step == 0)
    def _():
        picked[...] = jnp.zeros_like(picked)
        right[...] = jnp.zeros_like(right)

    @pl.when(inner == 0)
    def _():
        high, low = split(gather(own_low, own_high, 0) * (1.0 / windows))
        blank = [jnp.zeros((width - 3 * terms, channels), jnp.float32)] if width > 3 * terms else []
        left[...] = jnp.concatenate([high, high, low, *blank], axis=0).T.astype(jnp.bfloat16)
        values = gather(mirror_low, mirror_high, turn_ref[0])
        part = lax.broadcasted_iota(jnp.int32, values.shape, 0) % 2
        turned = jnp.where(part == 0, -pltpu.roll(values, terms - 1, 0), pltpu.roll(values, 1, 0))
        for q, block in enumerate((values, turned)):
            high, low = split(block)
            right[q, : 3 * terms] = jnp.concatenate([high, low, high], axis=0).astype(jnp.bfloat16)

    @pl.when(step >= 2)
    def _():
        for q, t in pieces:
            copy(step - 2, slot, q, t).wait()

    lane = lax.broadcasted_iota(jnp.int32, (1, width), 1)
    mask = jnp.where(lane % rows // 2 == inner, 1.0, 0.0).astype(jnp.bfloat16)
    picked[:, :width] = left[...] * mask

    def multiply(*accs):
        def stage(number):
            n, k = stages[number]
            for q in range(2):
                held_block = right[q, k * 256 : (k + 1) * 256, n * 256 : (n + 1) * 256]
                pltpu.matmul_push_rhs(held_block, number % 2, q)

        def retire(n, j, place):
            for q in range(2):
                done[slot, q, j * CHUNK : (j + 1) * CHUNK, n * 256 : (n + 1) * 256] = pltpu.matmul_pop(
                    accs[q * SLOTS + place]
                ).astype(jnp.bfloat16)

        chunks, deep = channels // CHUNK, depth // 256
        stages = [(n, k) for n in range(channels // 256) for k in range(deep)]
        waiting = []
        stage(0)
        for number, (n, k) in enumerate(stages):
            for j in range(chunks):
                place = (n * chunks + j) % SLOTS
                if k == 0 and len(waiting) > SLOTS // 2:
                    retire(*waiting.pop(0))
                for q in range(2):
                    pltpu.matmul_acc_lhs(
                        accs[q * SLOTS + place],
                        picked[j * CHUNK : (j + 1) * CHUNK, k * 256 : (k + 1) * 256],
                        load_staged_rhs=number % 2 if j == 0 else None,
                    )
                if j == 0 and number + 1 < len(stages):
                    stage(number + 1)
                if k == deep - 1:
                    waiting.append((n, j, place))
        for entry in waiting:
            retire(*entry)

    pl.run_scoped(
        multiply, *(pltpu.ACC(q)((CHUNK, 256), jnp.float32) for q in range(2) for _ in range(SLOTS))
    )
    for q, t in pieces:
        copy(step, slot, q, t).start()

    @pl.when(step == size - 1)
    def _():
        for f in (size - 2, size - 1):
            for q, t in pieces:
                copy(f, f % 2, q, t).wait()


def cross(turn, own, mirror, so_far, first, size, bins):
    windows = 2 * own[0].shape[0]
    channels = own[0].shape[2]
    terms = windows * 2 * GROUP
    width = -(-3 * terms // 128) * 128
    depth = -(-3 * terms // 256) * 256
    tiles = channels // min(256, channels)
    previous = [] if so_far is None else [so_far]
    return pl.pallas_call(
        functools.partial(cross_kernel, size, first),
        grid_spec=pltpu.PrefetchScalarGridSpec(
            num_scalar_prefetch=1,
            grid=(size,),
            in_specs=[pl.BlockSpec(x.shape, lambda f, s: (0, 0, 0)) for x in (*own, *mirror)]
            + [pl.BlockSpec(memory_space=pl.ANY)] * len(previous),
            out_specs=pl.BlockSpec(memory_space=pl.ANY),
            scratch_shapes=[
                pltpu.VMEM((terms, channels), jnp.float32),
                pltpu.VMEM((channels, width), jnp.bfloat16),
                pltpu.VMEM((2, depth, channels), jnp.bfloat16),
                pltpu.VMEM((channels, depth), jnp.bfloat16),
                pltpu.VMEM((2, 2, channels, channels), jnp.bfloat16),
                pltpu.SemaphoreType.DMA((2, 2 * tiles)),
            ],
        ),
        out_shape=jax.ShapeDtypeStruct((bins, 2, channels, channels), jnp.bfloat16),
        input_output_aliases={5: 0} if previous else {},
        compiler_params=pltpu.CompilerParams(vmem_limit_bytes=48 * 2**20),
        cost_estimate=pl.CostEstimate(
            flops=2 * size * 2 * channels * channels * 256,
            bytes_accessed=4 * size * channels * channels,
            transcendentals=0,
        ),
        name="cross",
    )(turn, *own, *mirror, *previous)


def exchange(block, axis, distance):
    n = lax.axis_size(axis)
    return lax.ppermute(block, axis, [(i, i ^ distance) for i in range(n)])


def double(block, axis):
    held, distance = block[None], 1
    while distance < lax.axis_size(axis) // 2:
        held = jnp.concatenate([held, exchange(held, axis, distance)])
        distance *= 2
    return held


def per_device(records, offsets, live_flags):
    row, col = lax.axis_index("row"), lax.axis_index("col")
    n = lax.axis_size("col")
    bins = NB // lax.axis_size("bin")
    sizes = (GROUP, bins - GROUP)
    turn = (row ^ col).reshape(1)
    swap = [(r * n + w, w * n + r) for r in range(n) for w in range(n)]
    parts = []
    for block in whiten(records, offsets, live_flags, sizes):
        other = lax.ppermute(block, ("row", "col"), swap)
        pairs = []
        for x, axis in ((block, "col"), (other, "row")):
            near = double(x, axis)
            pairs.append((near, exchange(near, axis, n // 2)))
        parts.append(pairs)
    out, first = None, 0
    for size, (own, mirror) in zip(sizes, parts):
        out = cross(turn, own, mirror, out, first, size, bins)
        first += size
    return out


def solution(mesh):
    in_specs = (P("row", "col"), P("col"), P("row"))
    out_specs = P("bin", None, "row", "col")
    return jax.shard_map(
        per_device, mesh=mesh, in_specs=in_specs, out_specs=out_specs, check_vma=False
    )
```

time: 57.1 us -> 54.2 us (0.949)
  waiting for transfers between devices: 7.26 us -> 0.18 us
  starting transfers between devices: 13.9 us -> 20.2 us
  other arithmetic: 1.69 us -> 0.05 us
    ppermute x6 -> x8, waiting for transfers between devices: 7.26 us -> 0.18 us  [exchange(): return lax.ppermute(block, axis, [(i, i ^ distance) for i in range(n)])]
    ppermute x6 -> x8, starting transfers between devices: 12.3 us -> 18.9 us  [exchange(): return lax.ppermute(block, axis, [(i, i ^ distance) for i in range(n)])]
    concatenate x4, other arithmetic: 1.69 us -> 0.05 us  [double(): held = jnp.concatenate([held, exchange(held, axis, distance)])]
    pallas_call x1, Pallas kernels: 4.51 us -> 3.86 us  [whiten(): pl.pallas_call(whiten_kernel, in_specs=[pl.BlockSpec(memory_space=pltpu.S...]
    ppermute x1 -> x2, starting transfers between devices: 1.56 us -> 1.32 us  [per_device(): other = lax.ppermute(block, ('row', 'col'), swap)]
  transfers between devices with their start and end apart: 7 -> 10, of which waited for: 2 -> 1; matrix products, arithmetic and copies ran while one was open for 3% -> 0% of each run, Pallas kernels for 14% -> 15%
where the time goes in v5:
time: 54.2 us; the launch traced here: 54 us
  Pallas kernels  32.9 us (61%)
  starting transfers between devices  20.2 us (37%)
  between operations  0.72 us (1%)
    pallas_call x2, Pallas kernels, cross(): pl.pallas_call(functools.partial(cross_kernel, size, first), grid_spec=pl...  29 us
    ppermute x8, starting transfers between devices, exchange(): return lax.ppermute(block, axis, [(i, i ^ distance) for i in range(n)])  18.9 us
    pallas_call x1, Pallas kernels, whiten(): pl.pallas_call(whiten_kernel, in_specs=[pl.BlockSpec(memory_space=pltpu.S...  3.86 us
    ppermute x2, starting transfers between devices, per_device(): other = lax.ppermute(block, ('row', 'col'), swap)  1.32 us
  transfers between devices with their start and end apart: 10, of which 1 were waited for; matrix products, arithmetic and copies ran while one was open for 0% of the time, Pallas kernels for 15%

profile of v5, /device:TPU:0, one launch (start us, length us, event | category | flops | bytes accessed | tf_op | source)
XLA Modules:
  0.0 54.0 jit_solution(3019770663332060438)
XLA Ops:
  0.7 3.9 %whiten.1 = (f32[8,1024]{1,0:T(8,128)S(1)}, f32[24,1024]{1,0:T(8,128)S(1)}) custom-call(s32[1]{0:T(128)S(6)} %copy.7.offset_ref, f32[64,1792]{1,0:T(8,128)} %constant.11.clone.table_hbm, bf16[1024,1664]{1,0:T(8,128)(2,1)} %records_hbm.1, s32[1,1024]{1,0:T(1,128)} %bitcast.14), custom_call_target="tpu_custom_call" | custom-call | flops 218103808 | bytes 3407872 | tf_op jit(solution)/shard_map/whiten/pallas_call | solution.py:73
  4.5 0.7 %collective-permute-start.7 = (f32[8,1024]{1,0:T(8,128)S(1)}, f32[8,1024]{1,0:T(8,128)S(1)}, u32[]{:S(2)}, u32[]{:S(2)}) collective-permute-start(f32[8,1024]{1,0:T(8,128)S(1)} %get-tuple-element.8), channel_id=1, source_target_pairs={{0,0},{2,8},{4,16},{6,24},{8,2},{10,10},{12,18},{14,26},{16,4},{18... | collective-permute-start | bytes 98312 | tf_op jit(solution)/shard_map/ppermute | solution.py:261
  5.2 4.3 %collective-permute-start.5 = (f32[1,8,1024]{2,1,0:T(8,128)S(1)}, f32[1,8,1024]{2,1,0:T(8,128)S(1)}, u32[]{:S(2)}, u32[]{:S(2)}) collective-permute-start(f32[1,8,1024]{2,1,0:T(8,128)S(1)} %bitcast.8), channel_id=1, source_target_pairs={{0,2},{2,0},{4,6},{6,4},{1,3},{3,1},{5,7},{7,5},{8,10},{10,8},{12,... | collective-permute-start | bytes 98312 | tf_op jit(solution)/shard_map/ppermute | solution.py:241
  9.5 0.7 %collective-permute-start.2 = (f32[24,1024]{1,0:T(8,128)S(1)}, f32[24,1024]{1,0:T(8,128)S(1)}, u32[]{:S(2)}, u32[]{:S(2)}) collective-permute-start(f32[24,1024]{1,0:T(8,128)S(1)} %get-tuple-element.7), channel_id=1, source_target_pairs={{0,0},{2,8},{4,16},{6,24},{8,2},{10,10},{12,18},{14,26},{16,4},{18... | collective-permute-start | bytes 294920 | tf_op jit(solution)/shard_map/ppermute | solution.py:261
  10.2 3.1 %collective-permute-start = (f32[1,24,1024]{2,1,0:T(8,128)S(1)}, f32[1,24,1024]{2,1,0:T(8,128)S(1)}, u32[]{:S(2)}, u32[]{:S(2)}) collective-permute-start(f32[1,24,1024]{2,1,0:T(8,128)S(1)} %bitcast.6), channel_id=1, source_target_pairs={{0,2},{2,0},{4,6},{6,4},{1,3},{3,1},{5,7},{7,5},{8,10},{10,8},{12,... | collective-permute-start | bytes 294920 | tf_op jit(solution)/shard_map/ppermute | solution.py:241
  13.3 0.0 collective-permute-done.7
  13.3 0.0 collective-permute-start.8
  13.3 0.0 collective-permute-done.5
  13.3 5.4 %collective-permute-start.6 = (f32[2,8,1024]{2,1,0:T(8,128)S(1)}, f32[2,8,1024]{2,1,0:T(8,128)S(1)}, u32[]{:S(2)}, u32[]{:S(2)}) collective-permute-start(f32[2,8,1024]{2,1,0:T(8,128)S(1)} %pad_maximum_fusion.2.own_low), channel_id=1, source_target_pairs={{0,4},{2,6},{4,0},{6,2},{1,5},{3,7},{5,1},{7,3},{8,12},{10,14},{12... | collective-permute-start | bytes 196616 | tf_op jit(solution)/shard_map/ppermute | solution.py:241
  18.7 0.0 collective-permute-done.8
  18.7 0.1 collective-permute-start.9
  18.8 0.0 collective-permute-done.2
  18.8 0.2 collective-permute-start.3
  19.1 0.0 collective-permute-done
  19.1 5.3 %collective-permute-start.1 = (f32[2,24,1024]{2,1,0:T(8,128)S(1)}, f32[2,24,1024]{2,1,0:T(8,128)S(1)}, u32[]{:S(2)}, u32[]{:S(2)}) collective-permute-start(f32[2,24,1024]{2,1,0:T(8,128)S(1)} %pad_maximum_fusion.own_low), channel_id=1, source_target_pairs={{0,4},{2,6},{4,0},{6,2},{1,5},{3,7},{5,1},{7,3},{8,12},{10,14},{12... | collective-permute-start | bytes 589832 | tf_op jit(solution)/shard_map/ppermute | solution.py:241
  24.3 0.0 collective-permute-done.3
  24.4 0.5 collective-permute-start.4
  24.9 0.0 collective-permute-done.6.own_high
  24.9 0.0 collective-permute-done.9.mirror_high
  24.9 8.2 %cross.2.refs_0_ = bf16[16,2,1024,1024]{3,2,1,0:T(8,128)(2,1)} custom-call(s32[1]{0:T(128)} %bitcast.turn_ref, f32[2,8,1024]{2,1,0:T(8,128)S(1)} %pad_maximum_fusion.2.own_low, f32[2,8,1024]{2,1,0:T(8,128)S(1)} %collective-permute-done.6.own_high, f32[2,8,1024]{2,1,0:T(8,128)S(1)} %pad_maximum_fusion.3.mirror_low, ...), custom_call_target="tpu_custom_call" | custom-call | flops 4294967296 | bytes 16777216 | tf_op jit(solution)/shard_map/cross/pallas_call | solution.py:210
  33.1 0.2 collective-permute-done.1.own_high
  33.2 0.0 collective-permute-done.4.mirror_high
  33.2 20.8 %cross.3 = bf16[16,2,1024,1024]{3,2,1,0:T(8,128)(2,1)} custom-call(s32[1]{0:T(128)} %bitcast.turn_ref, f32[2,24,1024]{2,1,0:T(8,128)S(1)} %pad_maximum_fusion.own_low, f32[2,24,1024]{2,1,0:T(8,128)S(1)} %collective-permute-done.1.own_high, f32[2,24,1024]{2,1,0:T(8,128)S(1)} %pad_maximum_fusion.1.mirror_low, ...), custom_call_target="tpu_custom_call", output_to_operand_aliasing={{}: (5, {})} | custom-call | flops 12884901888 | bytes 50331648 | tf_op jit(solution)/shard_map/cross/pallas_call | solution.py:210
  (4 shorter events, 0.0 us)
Async XLA Ops:
  4.5 8.7 %collective-permute-start.7 = (f32[8,1024]{1,0:T(8,128)S(1)}, f32[8,1024]{1,0:T(8,128)S(1)}, u32[]{:S(2)}, u32[]{:S(2)}) collective-permute-start(f32[8,1024]{1,0:T(8,128)S(1)} %get-tuple-element.8), channel_id=1, source_target_pairs={{0,0},{2,8},{4,16},{6,24},{8,2},{10,10},{12,18},{14,26},{16,4},{18... | collective-permute-start | bytes 98312 | tf_op jit(solution)/shard_map/ppermute | solution.py:261
  5.2 8.1 %collective-permute-start.5 = (f32[1,8,1024]{2,1,0:T(8,128)S(1)}, f32[1,8,1024]{2,1,0:T(8,128)S(1)}, u32[]{:S(2)}, u32[]{:S(2)}) collective-permute-start(f32[1,8,1024]{2,1,0:T(8,128)S(1)} %bitcast.8), channel_id=1, source_target_pairs={{0,2},{2,0},{4,6},{6,4},{1,3},{3,1},{5,7},{7,5},{8,10},{10,8},{12,... | collective-permute-start | bytes 98312 | tf_op jit(solution)/shard_map/ppermute | solution.py:241
  9.5 9.3 %collective-permute-start.2 = (f32[24,1024]{1,0:T(8,128)S(1)}, f32[24,1024]{1,0:T(8,128)S(1)}, u32[]{:S(2)}, u32[]{:S(2)}) collective-permute-start(f32[24,1024]{1,0:T(8,128)S(1)} %get-tuple-element.7), channel_id=1, source_target_pairs={{0,0},{2,8},{4,16},{6,24},{8,2},{10,10},{12,18},{14,26},{16,4},{18... | collective-permute-start | bytes 294920 | tf_op jit(solution)/shard_map/ppermute | solution.py:261
  10.2 8.9 %collective-permute-start = (f32[1,24,1024]{2,1,0:T(8,128)S(1)}, f32[1,24,1024]{2,1,0:T(8,128)S(1)}, u32[]{:S(2)}, u32[]{:S(2)}) collective-permute-start(f32[1,24,1024]{2,1,0:T(8,128)S(1)} %bitcast.6), channel_id=1, source_target_pairs={{0,2},{2,0},{4,6},{6,4},{1,3},{3,1},{5,7},{7,5},{8,10},{10,8},{12,... | collective-permute-start | bytes 294920 | tf_op jit(solution)/shard_map/ppermute | solution.py:241
  13.3 5.5 %collective-permute-start.8 = (f32[1,8,1024]{2,1,0:T(8,128)S(1)}, f32[1,8,1024]{2,1,0:T(8,128)S(1)}, u32[]{:S(2)}, u32[]{:S(2)}) collective-permute-start(f32[1,8,1024]{2,1,0:T(8,128)S(1)} %bitcast.12), channel_id=1, source_target_pairs={{0,8},{8,0},{16,24},{24,16},{1,9},{9,1},{17,25},{25,17},{2,10},{10... | collective-permute-start | bytes 98312 | tf_op jit(solution)/shard_map/ppermute | solution.py:241
  13.3 11.6 %collective-permute-start.6 = (f32[2,8,1024]{2,1,0:T(8,128)S(1)}, f32[2,8,1024]{2,1,0:T(8,128)S(1)}, u32[]{:S(2)}, u32[]{:S(2)}) collective-permute-start(f32[2,8,1024]{2,1,0:T(8,128)S(1)} %pad_maximum_fusion.2.own_low), channel_id=1, source_target_pairs={{0,4},{2,6},{4,0},{6,2},{1,5},{3,7},{5,1},{7,3},{8,12},{10,14},{12... | collective-permute-start | bytes 196616 | tf_op jit(solution)/shard_map/ppermute | solution.py:241
  18.7 6.1 %collective-permute-start.9 = (f32[2,8,1024]{2,1,0:T(8,128)S(1)}, f32[2,8,1024]{2,1,0:T(8,128)S(1)}, u32[]{:S(2)}, u32[]{:S(2)}) collective-permute-start(f32[2,8,1024]{2,1,0:T(8,128)S(1)} %pad_maximum_fusion.3.mirror_low), channel_id=1, source_target_pairs={{0,16},{8,24},{16,0},{24,8},{1,17},{9,25},{17,1},{25,9},{2,18},{10... | collective-permute-start | bytes 196616 | tf_op jit(solution)/shard_map/ppermute | solution.py:241
  18.8 5.5 %collective-permute-start.3 = (f32[1,24,1024]{2,1,0:T(8,128)S(1)}, f32[1,24,1024]{2,1,0:T(8,128)S(1)}, u32[]{:S(2)}, u32[]{:S(2)}) collective-permute-start(f32[1,24,1024]{2,1,0:T(8,128)S(1)} %bitcast.10), channel_id=1, source_target_pairs={{0,8},{8,0},{16,24},{24,16},{1,9},{9,1},{17,25},{25,17},{2,10},{10... | collective-permute-start | bytes 294920 | tf_op jit(solution)/shard_map/ppermute | solution.py:241
  19.1 14.1 %collective-permute-start.1 = (f32[2,24,1024]{2,1,0:T(8,128)S(1)}, f32[2,24,1024]{2,1,0:T(8,128)S(1)}, u32[]{:S(2)}, u32[]{:S(2)}) collective-permute-start(f32[2,24,1024]{2,1,0:T(8,128)S(1)} %pad_maximum_fusion.own_low), channel_id=1, source_target_pairs={{0,4},{2,6},{4,0},{6,2},{1,5},{3,7},{5,1},{7,3},{8,12},{10,14},{12... | collective-permute-start | bytes 589832 | tf_op jit(solution)/shard_map/ppermute | solution.py:241
  24.4 8.9 %collective-permute-start.4 = (f32[2,24,1024]{2,1,0:T(8,128)S(1)}, f32[2,24,1024]{2,1,0:T(8,128)S(1)}, u32[]{:S(2)}, u32[]{:S(2)}) collective-permute-start(f32[2,24,1024]{2,1,0:T(8,128)S(1)} %pad_maximum_fusion.1.mirror_low), channel_id=1, source_target_pairs={{0,16},{8,24},{16,0},{24,8},{1,17},{9,25},{17,1},{25,9},{2,18},{10... | collective-permute-start | bytes 589832 | tf_op jit(solution)/shard_map/ppermute | solution.py:241

commit v6 on v5

--- a/solution.py
+++ b/solution.py
@@ -13,25 +13,25 @@
 NB = 32
 BSTEP = 6
 EPSILON = 1e-05
+PAD = 168
 GROUP = 4
 CHUNK = 128
+BUFFERS = 4
 SLOTS = 8
 
 
-def padded_table(width):
+def padded_table(samples):
     k = (np.arange(NB) + 1) * BSTEP
     n = np.arange(L)
     angle = (k[:, None] * n[None, :] % L) * (2.0 * math.pi / L)
     taper = 0.5 - 0.5 * np.cos(n * (2.0 * math.pi / L))
     parts = np.stack([np.cos(angle) * taper, -np.sin(angle) * taper], axis=1)
-    table = np.zeros((2 * NB, width), np.float32)
-    table[:, :L] = parts.reshape(2 * NB, L)
+    table = np.zeros((PAD + samples, 2 * NB), np.float32)
+    table[PAD : PAD + L] = parts.reshape(2 * NB, L).T
     return jnp.asarray(table.astype(jnp.bfloat16).astype(np.float32))
 
 
-def whiten_kernel(
-    offset_ref, table_hbm, records_hbm, live_hbm, *refs
-):
+def whiten_kernel(sizes, offset_ref, table_hbm, records_hbm, live_hbm, *refs):
     outs, (table, records, live, shifted, product, sems) = refs[:-6], refs[-6:]
     pieces, block, samples = records.shape
     copies = [
@@ -44,45 +44,41 @@
     for copy in copies:
         copy.start()
     copies[0].wait()
-    turned = pltpu.roll(table[...], offset_ref[0], 1)
-    shifted[...] = turned[:, :samples].astype(jnp.bfloat16)
+    shifted[...] = table[pl.ds(PAD - offset_ref[0], samples), :].astype(jnp.bfloat16)
     copies[1].wait()
-    held = sum(out.shape[0] for out in outs)
-    start = pl.multiple_of(lax.axis_index("bin") * held, 8)
+    start = pl.multiple_of(lax.axis_index("bin") * (2 * sum(sizes)), 8)
     for i in range(pieces):
         copies[2 + i].wait()
-        spectra = lax.dot_general(
-            records[i], shifted[...], (((1,), (1,)), ((), ())),
-            preferred_element_type=jnp.float32,
-        ).T
+        spectra = jnp.dot(records[i], shifted[...], preferred_element_type=jnp.float32).T
         product[i] = spectra
         energy = jnp.sum(spectra * spectra, axis=0, keepdims=True) / (2 * NB)
         columns = slice(i * block, (i + 1) * block)
         scaling = live[:, columns].astype(jnp.float32) / jnp.sqrt(energy + EPSILON)
-        at = start
-        for out in outs:
-            out[:, columns] = product[i, pl.ds(at, out.shape[0]), :] * scaling
-            at = pl.multiple_of(at + out.shape[0], 8)
+        at = 0
+        for size, out in zip(sizes, outs):
+            rows = pl.ds(pl.multiple_of(start + at, 8), 2 * size)
+            out[:, columns] = product[i, rows, :] * scaling
+            at += 2 * size
 
 
 def whiten(records, offsets, live, sizes):
     channels, samples = records.shape
     block = min(256, channels)
     pieces = channels // block
-    width = -(-(samples + 128) // 128) * 128
+    rows = [2 * size for size in sizes]
     return pl.pallas_call(
-        whiten_kernel,
+        functools.partial(whiten_kernel, sizes),
         in_specs=[pl.BlockSpec(memory_space=pltpu.SMEM)] + [pl.BlockSpec(memory_space=pl.ANY)] * 3,
-        out_specs=[pl.BlockSpec(memory_space=pltpu.VMEM)] * len(sizes),
+        out_specs=[pl.BlockSpec(memory_space=pltpu.VMEM)] * len(rows),
         scratch_shapes=[
-            pltpu.VMEM((2 * NB, width), jnp.float32),
+            pltpu.VMEM((PAD + samples, 2 * NB), jnp.float32),
             pltpu.VMEM((pieces, block, samples), jnp.bfloat16),
             pltpu.VMEM((1, channels), jnp.int32),
-            pltpu.VMEM((2 * NB, samples), jnp.bfloat16),
+            pltpu.VMEM((samples, 2 * NB), jnp.bfloat16),
             pltpu.VMEM((pieces, 2 * NB, block), jnp.float32),
             pltpu.SemaphoreType.DMA((2 + pieces,)),
         ],
-        out_shape=[jax.ShapeDtypeStruct((2 * size, channels), jnp.float32) for size in sizes],
+        out_shape=[jax.ShapeDtypeStruct((count, channels), jnp.float32) for count in rows],
         compiler_params=pltpu.CompilerParams(vmem_limit_bytes=32 * 2**20),
         cost_estimate=pl.CostEstimate(
             flops=4 * NB * samples * channels, bytes_accessed=2 * samples * channels, transcendentals=0
@@ -90,7 +86,7 @@
         name="whiten",
     )(offsets, *(
         pltpu.with_memory_space_constraint(x, pltpu.HBM)
-        for x in (padded_table(width), records, live.reshape(1, channels))
+        for x in (padded_table(samples), records, live.reshape(1, channels))
     ))
 
 
@@ -108,21 +104,25 @@
     terms = windows * rows
     depth, channels = right.shape[1:]
     width = left.shape[1]
-    tile = min(256, channels)
-    pieces = [(q, t) for q in range(2) for t in range(channels // tile)]
-    slot, inner = step % 2, step % GROUP
+    height = done.shape[2]
+    tile = min(256, height)
+    pieces = [(q, t) for q in range(2) for t in range(height // tile)]
+    slot, inner = step % BUFFERS, step // 2 % GROUP
+    top = pl.multiple_of(step % 2 * height, height)
 
     def gather(low, high, turn):
-        at = pl.multiple_of(step * 2, rows)
+        at = pl.multiple_of(step, rows)
         for w in range(windows):
             part = (low if w < half else high)[w % half, pl.ds(at, rows), :]
             held[pl.ds(pl.multiple_of((w ^ turn) * rows, 8), rows), :] = part
         return held[...]
 
-    def copy(f, slot, q, t):
-        piece = pl.ds(t * tile, tile)
+    def copy(at_step, slot, q, t):
+        target = pl.ds(pl.multiple_of(at_step % 2 * height + t * tile, tile), tile)
         return pltpu.make_async_copy(
-            done.at[slot, q, piece], out_hbm.at[first + f, q, piece], sems.at[slot, q * (channels // tile) + t]
+            done.at[slot, q, pl.ds(t * tile, tile)],
+            out_hbm.at[first + at_step // 2, q, target],
+            sems.at[slot, q * (height // tile) + t],
         )
 
     @pl.when(step == 0)
@@ -130,7 +130,7 @@
         picked[...] = jnp.zeros_like(picked)
         right[...] = jnp.zeros_like(right)
 
-    @pl.when(inner == 0)
+    @pl.when(step % (2 * GROUP) == 0)
     def _():
         high, low = split(gather(own_low, own_high, 0) * (1.0 / windows))
         blank = [jnp.zeros((width - 3 * terms, channels), jnp.float32)] if width > 3 * terms else []
@@ -142,14 +142,14 @@
             high, low = split(block)
             right[q, : 3 * terms] = jnp.concatenate([high, low, high], axis=0).astype(jnp.bfloat16)
 
-    @pl.when(step >= 2)
+    @pl.when(step >= BUFFERS)
     def _():
         for q, t in pieces:
-            copy(step - 2, slot, q, t).wait()
+            copy(step - BUFFERS, slot, q, t).wait()
 
     lane = lax.broadcasted_iota(jnp.int32, (1, width), 1)
     mask = jnp.where(lane % rows // 2 == inner, 1.0, 0.0).astype(jnp.bfloat16)
-    picked[:, :width] = left[...] * mask
+    picked[:, :width] = left[pl.ds(top, height), :] * mask
 
     def multiply(*accs):
         def stage(number):
@@ -164,7 +164,7 @@
                     accs[q * SLOTS + place]
                 ).astype(jnp.bfloat16)
 
-        chunks, deep = channels // CHUNK, depth // 256
+        chunks, deep = height // CHUNK, depth // 256
         stages = [(n, k) for n in range(channels // 256) for k in range(deep)]
         waiting = []
         stage(0)
@@ -190,13 +190,13 @@
         multiply, *(pltpu.ACC(q)((CHUNK, 256), jnp.float32) for q in range(2) for _ in range(SLOTS))
     )
     for q, t in pieces:
-        copy(step, slot, q, t).start()
-
-    @pl.when(step == size - 1)
-    def _():
-        for f in (size - 2, size - 1):
+        copy(step, slot, q, t).start(priority=t % 2)
+
+    @pl.when(step == 2 * size - 1)
+    def _():
+        for last in range(2 * size - BUFFERS, 2 * size):
             for q, t in pieces:
-                copy(f, f % 2, q, t).wait()
+                copy(last, last % BUFFERS, q, t).wait()
 
 
 def cross(turn, own, mirror, so_far, first, size, bins):
@@ -205,13 +205,13 @@
     terms = windows * 2 * GROUP
     width = -(-3 * terms // 128) * 128
     depth = -(-3 * terms // 256) * 256
-    tiles = channels // min(256, channels)
+    height = channels // 2
     previous = [] if so_far is None else [so_far]
     return pl.pallas_call(
         functools.partial(cross_kernel, size, first),
         grid_spec=pltpu.PrefetchScalarGridSpec(
             num_scalar_prefetch=1,
-            grid=(size,),
+            grid=(2 * size,),
             in_specs=[pl.BlockSpec(x.shape, lambda f, s: (0, 0, 0)) for x in (*own, *mirror)]
             + [pl.BlockSpec(memory_space=pl.ANY)] * len(previous),
             out_specs=pl.BlockSpec(memory_space=pl.ANY),
@@ -219,9 +219,9 @@
                 pltpu.VMEM((terms, channels), jnp.float32),
                 pltpu.VMEM((channels, width), jnp.bfloat16),
                 pltpu.VMEM((2, depth, channels), jnp.bfloat16),
-                pltpu.VMEM((channels, depth), jnp.bfloat16),
-                pltpu.VMEM((2, 2, channels, channels), jnp.bfloat16),
-                pltpu.SemaphoreType.DMA((2, 2 * tiles)),
+                pltpu.VMEM((height, depth), jnp.bfloat16),
+                pltpu.VMEM((BUFFERS, 2, height, channels), jnp.bfloat16),
+                pltpu.SemaphoreType.DMA((BUFFERS, 2 * (height // min(256, height)))),
             ],
         ),
         out_shape=jax.ShapeDtypeStruct((bins, 2, channels, channels), jnp.bfloat16),
@@ -241,8 +241,8 @@
     return lax.ppermute(block, axis, [(i, i ^ distance) for i in range(n)])
 
 
-def double(block, axis):
-    held, distance = block[None], 1
+def double(held, axis):
+    distance = 1
     while distance < lax.axis_size(axis) // 2:
         held = jnp.concatenate([held, exchange(held, axis, distance)])
         distance *= 2
@@ -255,13 +255,13 @@
     bins = NB // lax.axis_size("bin")
     sizes = (GROUP, bins - GROUP)
     turn = (row ^ col).reshape(1)
-    swap = [(r * n + w, w * n + r) for r in range(n) for w in range(n)]
+    swap = [(r * n + w, w * n + r) for r in range(n) for w in range(n) if r != w]
     parts = []
     for block in whiten(records, offsets, live_flags, sizes):
-        other = lax.ppermute(block, ("row", "col"), swap)
+        other = jnp.where(row == col, block, lax.ppermute(block, ("row", "col"), swap))
         pairs = []
         for x, axis in ((block, "col"), (other, "row")):
-            near = double(x, axis)
+            near = double(x[None], axis)
             pairs.append((near, exchange(near, axis, n // 2)))
         parts.append(pairs)
     out, first = None, 0

time: 54.2 us -> 53.6 us (0.989)
  Pallas kernels: 32.9 us -> 31.8 us
    pallas_call x2, Pallas kernels: 29 us -> 28.4 us  [cross(): pl.pallas_call(functools.partial(cross_kernel, size, first), grid_spec=pl...]
where the time goes in v6:
time: 53.6 us; the launch traced here: 53.4 us
  Pallas kernels  31.8 us (59%)
  starting transfers between devices  20.3 us (38%)
  between operations  0.75 us (1%)
    pallas_call x2, Pallas kernels, cross(): pl.pallas_call(functools.partial(cross_kernel, size, first), grid_spec=pl...  28.4 us
    ppermute x8, starting transfers between devices, exchange(): return lax.ppermute(block, axis, [(i, i ^ distance) for i in range(n)])  19 us
    pallas_call x1, Pallas kernels, whiten(): pl.pallas_call(functools.partial(whiten_kernel, sizes), in_specs=[pl.Bloc...  3.46 us
    ppermute x2, starting transfers between devices, per_device(): lax.ppermute(block, ('row', 'col'), swap)  1.32 us
  transfers between devices with their start and end apart: 10, of which 1 were waited for; matrix products, arithmetic and copies ran while one was open for 0% of the time, Pallas kernels for 15%

profile of v6, /device:TPU:0, one launch (start us, length us, event | category | flops | bytes accessed | tf_op | source)
XLA Modules:
  0.0 53.4 jit_solution(16260668402551617336)
XLA Ops:
  0.7 3.5 %whiten.1 = (f32[8,1024]{1,0:T(8,128)S(1)}, f32[24,1024]{1,0:T(8,128)S(1)}) custom-call(s32[1]{0:T(128)S(6)} %copy.7.offset_ref, f32[1832,64]{1,0:T(8,128)} %constant.11.clone.table_hbm, bf16[1024,1664]{1,0:T(8,128)(2,1)} %records_hbm.1, s32[1,1024]{1,0:T(1,128)} %bitcast.12), custom_call_target="tpu_custom_call" | custom-call | flops 218103808 | bytes 3407872 | tf_op jit(solution)/shard_map/whiten/pallas_call | solution.py:69
  4.1 0.7 %collective-permute-start.7 = (f32[8,1024]{1,0:T(8,128)S(1)}, f32[8,1024]{1,0:T(8,128)S(1)}, u32[]{:S(2)}, u32[]{:S(2)}) collective-permute-start(f32[8,1024]{1,0:T(8,128)S(1)} %get-tuple-element.8), channel_id=1, source_target_pairs={{2,8},{4,16},{6,24},{8,2},{12,18},{14,26},{16,4},{18,12},{22,28},{... | collective-permute-start | bytes 98312 | tf_op jit(solution)/shard_map/ppermute | solution.py:261
  4.8 4.3 %collective-permute-start.5 = (f32[1,8,1024]{2,1,0:T(8,128)S(1)}, f32[1,8,1024]{2,1,0:T(8,128)S(1)}, u32[]{:S(2)}, u32[]{:S(2)}) collective-permute-start(f32[1,8,1024]{2,1,0:T(8,128)S(1)} %bitcast.10), channel_id=1, source_target_pairs={{0,2},{2,0},{4,6},{6,4},{1,3},{3,1},{5,7},{7,5},{8,10},{10,8},{12,... | collective-permute-start | bytes 98312 | tf_op jit(solution)/shard_map/ppermute | solution.py:241
  9.1 0.7 %collective-permute-start.2 = (f32[24,1024]{1,0:T(8,128)S(1)}, f32[24,1024]{1,0:T(8,128)S(1)}, u32[]{:S(2)}, u32[]{:S(2)}) collective-permute-start(f32[24,1024]{1,0:T(8,128)S(1)} %get-tuple-element.7), channel_id=1, source_target_pairs={{2,8},{4,16},{6,24},{8,2},{12,18},{14,26},{16,4},{18,12},{22,28},{... | collective-permute-start | bytes 294920 | tf_op jit(solution)/shard_map/ppermute | solution.py:261
  9.8 3.1 %collective-permute-start = (f32[1,24,1024]{2,1,0:T(8,128)S(1)}, f32[1,24,1024]{2,1,0:T(8,128)S(1)}, u32[]{:S(2)}, u32[]{:S(2)}) collective-permute-start(f32[1,24,1024]{2,1,0:T(8,128)S(1)} %bitcast.8), channel_id=1, source_target_pairs={{0,2},{2,0},{4,6},{6,4},{1,3},{3,1},{5,7},{7,5},{8,10},{10,8},{12,... | collective-permute-start | bytes 294920 | tf_op jit(solution)/shard_map/ppermute | solution.py:241
  12.9 0.0 collective-permute-done.7
  12.9 0.1 collective-permute-start.8
  13.0 0.0 collective-permute-done.5
  13.0 5.4 %collective-permute-start.6 = (f32[2,8,1024]{2,1,0:T(8,128)S(1)}, f32[2,8,1024]{2,1,0:T(8,128)S(1)}, u32[]{:S(2)}, u32[]{:S(2)}) collective-permute-start(f32[2,8,1024]{2,1,0:T(8,128)S(1)} %pad_maximum_fusion.2.own_low), channel_id=1, source_target_pairs={{0,4},{2,6},{4,0},{6,2},{1,5},{3,7},{5,1},{7,3},{8,12},{10,14},{12... | collective-permute-start | bytes 196616 | tf_op jit(solution)/shard_map/ppermute | solution.py:241
  18.4 0.0 collective-permute-done.8
  18.4 0.1 collective-permute-start.9
  18.5 0.0 collective-permute-done.2
  18.5 0.2 collective-permute-start.3
  18.8 0.0 collective-permute-done
  18.8 5.2 %collective-permute-start.1 = (f32[2,24,1024]{2,1,0:T(8,128)S(1)}, f32[2,24,1024]{2,1,0:T(8,128)S(1)}, u32[]{:S(2)}, u32[]{:S(2)}) collective-permute-start(f32[2,24,1024]{2,1,0:T(8,128)S(1)} %pad_maximum_fusion.own_low), channel_id=1, source_target_pairs={{0,4},{2,6},{4,0},{6,2},{1,5},{3,7},{5,1},{7,3},{8,12},{10,14},{12... | collective-permute-start | bytes 589832 | tf_op jit(solution)/shard_map/ppermute | solution.py:241
  23.9 0.0 collective-permute-done.3
  24.0 0.6 %collective-permute-start.4 = (f32[2,24,1024]{2,1,0:T(8,128)S(1)}, f32[2,24,1024]{2,1,0:T(8,128)S(1)}, u32[]{:S(2)}, u32[]{:S(2)}) collective-permute-start(f32[2,24,1024]{2,1,0:T(8,128)S(1)} %pad_maximum_fusion.1.mirror_low), channel_id=1, source_target_pairs={{0,16},{8,24},{16,0},{24,8},{1,17},{9,25},{17,1},{25,9},{2,18},{10... | collective-permute-start | bytes 589832 | tf_op jit(solution)/shard_map/ppermute | solution.py:241
  24.6 0.0 collective-permute-done.6.own_high
  24.6 0.0 collective-permute-done.9.mirror_high
  24.6 7.8 %cross.2.refs_0_ = bf16[16,2,1024,1024]{3,2,1,0:T(8,128)(2,1)} custom-call(s32[1]{0:T(128)} %bitcast.turn_ref, f32[2,8,1024]{2,1,0:T(8,128)S(1)} %pad_maximum_fusion.2.own_low, f32[2,8,1024]{2,1,0:T(8,128)S(1)} %collective-permute-done.6.own_high, f32[2,8,1024]{2,1,0:T(8,128)S(1)} %pad_maximum_fusion.3.mirror_low, ...), custom_call_target="tpu_custom_call" | custom-call | flops 4294967296 | bytes 16777216 | tf_op jit(solution)/shard_map/cross/pallas_call | solution.py:210
  32.4 0.4 collective-permute-done.1.own_high
  32.8 0.0 collective-permute-done.4.mirror_high
  32.8 20.6 %cross.3 = bf16[16,2,1024,1024]{3,2,1,0:T(8,128)(2,1)} custom-call(s32[1]{0:T(128)} %bitcast.turn_ref, f32[2,24,1024]{2,1,0:T(8,128)S(1)} %pad_maximum_fusion.own_low, f32[2,24,1024]{2,1,0:T(8,128)S(1)} %collective-permute-done.1.own_high, f32[2,24,1024]{2,1,0:T(8,128)S(1)} %pad_maximum_fusion.1.mirror_low, ...), custom_call_target="tpu_custom_call", output_to_operand_aliasing={{}: (5, {})} | custom-call | flops 12884901888 | bytes 50331648 | tf_op jit(solution)/shard_map/cross/pallas_call | solution.py:210
  (6 shorter events, 0.1 us)
Async XLA Ops:
  4.1 8.8 %collective-permute-start.7 = (f32[8,1024]{1,0:T(8,128)S(1)}, f32[8,1024]{1,0:T(8,128)S(1)}, u32[]{:S(2)}, u32[]{:S(2)}) collective-permute-start(f32[8,1024]{1,0:T(8,128)S(1)} %get-tuple-element.8), channel_id=1, source_target_pairs={{2,8},{4,16},{6,24},{8,2},{12,18},{14,26},{16,4},{18,12},{22,28},{... | collective-permute-start | bytes 98312 | tf_op jit(solution)/shard_map/ppermute | solution.py:261
  4.8 8.2 %collective-permute-start.5 = (f32[1,8,1024]{2,1,0:T(8,128)S(1)}, f32[1,8,1024]{2,1,0:T(8,128)S(1)}, u32[]{:S(2)}, u32[]{:S(2)}) collective-permute-start(f32[1,8,1024]{2,1,0:T(8,128)S(1)} %bitcast.10), channel_id=1, source_target_pairs={{0,2},{2,0},{4,6},{6,4},{1,3},{3,1},{5,7},{7,5},{8,10},{10,8},{12,... | collective-permute-start | bytes 98312 | tf_op jit(solution)/shard_map/ppermute | solution.py:241
  9.1 9.4 %collective-permute-start.2 = (f32[24,1024]{1,0:T(8,128)S(1)}, f32[24,1024]{1,0:T(8,128)S(1)}, u32[]{:S(2)}, u32[]{:S(2)}) collective-permute-start(f32[24,1024]{1,0:T(8,128)S(1)} %get-tuple-element.7), channel_id=1, source_target_pairs={{2,8},{4,16},{6,24},{8,2},{12,18},{14,26},{16,4},{18,12},{22,28},{... | collective-permute-start | bytes 294920 | tf_op jit(solution)/shard_map/ppermute | solution.py:261
  9.8 9.0 %collective-permute-start = (f32[1,24,1024]{2,1,0:T(8,128)S(1)}, f32[1,24,1024]{2,1,0:T(8,128)S(1)}, u32[]{:S(2)}, u32[]{:S(2)}) collective-permute-start(f32[1,24,1024]{2,1,0:T(8,128)S(1)} %bitcast.8), channel_id=1, source_target_pairs={{0,2},{2,0},{4,6},{6,4},{1,3},{3,1},{5,7},{7,5},{8,10},{10,8},{12,... | collective-permute-start | bytes 294920 | tf_op jit(solution)/shard_map/ppermute | solution.py:241
  12.9 5.5 %collective-permute-start.8 = (f32[1,8,1024]{2,1,0:T(8,128)S(1)}, f32[1,8,1024]{2,1,0:T(8,128)S(1)}, u32[]{:S(2)}, u32[]{:S(2)}) collective-permute-start(f32[1,8,1024]{2,1,0:T(8,128)S(1)} %select_bitcast_fusion.1), channel_id=1, source_target_pairs={{0,8},{8,0},{16,24},{24,16},{1,9},{9,1},{17,25},{25,17},{2,10},{10... | collective-permute-start | bytes 98312 | tf_op jit(solution)/shard_map/ppermute | solution.py:241
  13.0 11.6 %collective-permute-start.6 = (f32[2,8,1024]{2,1,0:T(8,128)S(1)}, f32[2,8,1024]{2,1,0:T(8,128)S(1)}, u32[]{:S(2)}, u32[]{:S(2)}) collective-permute-start(f32[2,8,1024]{2,1,0:T(8,128)S(1)} %pad_maximum_fusion.2.own_low), channel_id=1, source_target_pairs={{0,4},{2,6},{4,0},{6,2},{1,5},{3,7},{5,1},{7,3},{8,12},{10,14},{12... | collective-permute-start | bytes 196616 | tf_op jit(solution)/shard_map/ppermute | solution.py:241
  18.4 6.1 %collective-permute-start.9 = (f32[2,8,1024]{2,1,0:T(8,128)S(1)}, f32[2,8,1024]{2,1,0:T(8,128)S(1)}, u32[]{:S(2)}, u32[]{:S(2)}) collective-permute-start(f32[2,8,1024]{2,1,0:T(8,128)S(1)} %pad_maximum_fusion.3.mirror_low), channel_id=1, source_target_pairs={{0,16},{8,24},{16,0},{24,8},{1,17},{9,25},{17,1},{25,9},{2,18},{10... | collective-permute-start | bytes 196616 | tf_op jit(solution)/shard_map/ppermute | solution.py:241
  18.5 5.4 %collective-permute-start.3 = (f32[1,24,1024]{2,1,0:T(8,128)S(1)}, f32[1,24,1024]{2,1,0:T(8,128)S(1)}, u32[]{:S(2)}, u32[]{:S(2)}) collective-permute-start(f32[1,24,1024]{2,1,0:T(8,128)S(1)} %select_bitcast_fusion), channel_id=1, source_target_pairs={{0,8},{8,0},{16,24},{24,16},{1,9},{9,1},{17,25},{25,17},{2,10},{10... | collective-permute-start | bytes 294920 | tf_op jit(solution)/shard_map/ppermute | solution.py:241
  18.8 14.0 %collective-permute-start.1 = (f32[2,24,1024]{2,1,0:T(8,128)S(1)}, f32[2,24,1024]{2,1,0:T(8,128)S(1)}, u32[]{:S(2)}, u32[]{:S(2)}) collective-permute-start(f32[2,24,1024]{2,1,0:T(8,128)S(1)} %pad_maximum_fusion.own_low), channel_id=1, source_target_pairs={{0,4},{2,6},{4,0},{6,2},{1,5},{3,7},{5,1},{7,3},{8,12},{10,14},{12... | collective-permute-start | bytes 589832 | tf_op jit(solution)/shard_map/ppermute | solution.py:241
  24.0 8.9 %collective-permute-start.4 = (f32[2,24,1024]{2,1,0:T(8,128)S(1)}, f32[2,24,1024]{2,1,0:T(8,128)S(1)}, u32[]{:S(2)}, u32[]{:S(2)}) collective-permute-start(f32[2,24,1024]{2,1,0:T(8,128)S(1)} %pad_maximum_fusion.1.mirror_low), channel_id=1, source_target_pairs={{0,16},{8,24},{16,0},{24,8},{1,17},{9,25},{17,1},{25,9},{2,18},{10... | collective-permute-start | bytes 589832 | tf_op jit(solution)/shard_map/ppermute | solution.py:241

commit v7 on v6

--- a/solution.py
+++ b/solution.py
@@ -254,11 +254,12 @@
     n = lax.axis_size("col")
     bins = NB // lax.axis_size("bin")
     sizes = (GROUP, bins - GROUP)
-    turn = (row ^ col).reshape(1)
-    swap = [(r * n + w, w * n + r) for r in range(n) for w in range(n) if r != w]
+    across = n // 2
+    turn = (row ^ col ^ across).reshape(1)
+    swap = [(r * n + w, (w ^ across) * n + r) for r in range(n) for w in range(n)]
     parts = []
     for block in whiten(records, offsets, live_flags, sizes):
-        other = jnp.where(row == col, block, lax.ppermute(block, ("row", "col"), swap))
+        other = lax.ppermute(block, ("row", "col"), swap)
         pairs = []
         for x, axis in ((block, "col"), (other, "row")):
             near = double(x[None], axis)

time: 53.6 us -> 50.5 us (0.942)
  starting transfers between devices: 20.3 us -> 11.1 us
  waiting for transfers between devices: 0.47 us -> 6.68 us
    ppermute x8, starting transfers between devices: 19 us -> 6.41 us  [exchange(): return lax.ppermute(block, axis, [(i, i ^ distance) for i in range(n)])]
    ppermute x8, waiting for transfers between devices: 0.46 us -> 5.47 us  [exchange(): return lax.ppermute(block, axis, [(i, i ^ distance) for i in range(n)])]
    ppermute x2, starting transfers between devices: 1.32 us -> 4.71 us  [per_device(): other = lax.ppermute(block, ('row', 'col'), swap)]
    ppermute x2, waiting for transfers between devices: 0.01 us -> 1.2 us  [per_device(): other = lax.ppermute(block, ('row', 'col'), swap)]
  transfers between devices with their start and end apart: 10 -> 10, of which waited for: 1 -> 4; matrix products, arithmetic and copies ran while one was open for 0% -> 0% of each run, Pallas kernels for 15% -> 15%
where the time goes in v7:
time: 50.5 us; the launch traced here: 50.4 us
  Pallas kernels  31.8 us (63%)
  starting transfers between devices  11.1 us (22%)
  waiting for transfers between devices  6.68 us (13%)
  between operations  0.7 us (1%)
    pallas_call x2, Pallas kernels, cross(): pl.pallas_call(functools.partial(cross_kernel, size, first), grid_spec=pl...  28.4 us
    ppermute x8, starting transfers between devices, exchange(): return lax.ppermute(block, axis, [(i, i ^ distance) for i in range(n)])  6.41 us
    ppermute x8, waiting for transfers between devices, exchange(): return lax.ppermute(block, axis, [(i, i ^ distance) for i in range(n)])  5.47 us
    ppermute x2, starting transfers between devices, per_device(): other = lax.ppermute(block, ('row', 'col'), swap)  4.71 us
    pallas_call x1, Pallas kernels, whiten(): pl.pallas_call(functools.partial(whiten_kernel, sizes), in_specs=[pl.Bloc...  3.46 us
    ppermute x2, waiting for transfers between devices, per_device(): other = lax.ppermute(block, ('row', 'col'), swap)  1.2 us
  transfers between devices with their start and end apart: 10, of which 4 were waited for; matrix products, arithmetic and copies ran while one was open for 0% of the time, Pallas kernels for 15%

profile of v7, /device:TPU:0, one launch (start us, length us, event | category | flops | bytes accessed | tf_op | source)
XLA Modules:
  0.0 50.4 jit_solution(9062054351305269320)
XLA Ops:
  0.7 3.5 %whiten.1 = (f32[8,1024]{1,0:T(8,128)S(1)}, f32[24,1024]{1,0:T(8,128)S(1)}) custom-call(s32[1]{0:T(128)S(6)} %copy.7.offset_ref, f32[1832,64]{1,0:T(8,128)} %constant.13.clone.table_hbm, bf16[1024,1664]{1,0:T(8,128)(2,1)} %records_hbm.1, s32[1,1024]{1,0:T(1,128)} %bitcast.14), custom_call_target="tpu_custom_call" | custom-call | flops 218103808 | bytes 3407872 | tf_op jit(solution)/shard_map/whiten/pallas_call | solution.py:69
  4.1 3.0 %collective-permute-start.7 = (f32[8,1024]{1,0:T(8,128)S(1)}, f32[8,1024]{1,0:T(8,128)S(1)}, u32[]{:S(2)}, u32[]{:S(2)}) collective-permute-start(f32[8,1024]{1,0:T(8,128)S(1)} %get-tuple-element.8), channel_id=1, source_target_pairs={{0,16},{2,24},{4,0},{6,8},{8,18},{10,26},{12,2},{14,10},{16,20},{1... | collective-permute-start | bytes 98312 | tf_op jit(solution)/shard_map/ppermute | solution.py:262
  7.1 0.9 %collective-permute-start.5 = (f32[1,8,1024]{2,1,0:T(8,128)S(1)}, f32[1,8,1024]{2,1,0:T(8,128)S(1)}, u32[]{:S(2)}, u32[]{:S(2)}) collective-permute-start(f32[1,8,1024]{2,1,0:T(8,128)S(1)} %bitcast.8), channel_id=1, source_target_pairs={{0,2},{2,0},{4,6},{6,4},{1,3},{3,1},{5,7},{7,5},{8,10},{10,8},{12,... | collective-permute-start | bytes 98312 | tf_op jit(solution)/shard_map/ppermute | solution.py:241
  8.0 1.7 %collective-permute-start.2 = (f32[24,1024]{1,0:T(8,128)S(1)}, f32[24,1024]{1,0:T(8,128)S(1)}, u32[]{:S(2)}, u32[]{:S(2)}) collective-permute-start(f32[24,1024]{1,0:T(8,128)S(1)} %get-tuple-element.7), channel_id=1, source_target_pairs={{0,16},{2,24},{4,0},{6,8},{8,18},{10,26},{12,2},{14,10},{16,20},{1... | collective-permute-start | bytes 294920 | tf_op jit(solution)/shard_map/ppermute | solution.py:262
  9.7 2.2 %collective-permute-start = (f32[1,24,1024]{2,1,0:T(8,128)S(1)}, f32[1,24,1024]{2,1,0:T(8,128)S(1)}, u32[]{:S(2)}, u32[]{:S(2)}) collective-permute-start(f32[1,24,1024]{2,1,0:T(8,128)S(1)} %bitcast.6), channel_id=1, source_target_pairs={{0,2},{2,0},{4,6},{6,4},{1,3},{3,1},{5,7},{7,5},{8,10},{10,8},{12,... | collective-permute-start | bytes 294920 | tf_op jit(solution)/shard_map/ppermute | solution.py:241
  11.9 0.0 collective-permute-done.7
  11.9 0.1 collective-permute-start.8
  12.1 0.0 collective-permute-done.5
  12.1 0.4 collective-permute-start.6
  12.5 0.6 %collective-permute-done.8 = f32[1,8,1024]{2,1,0:T(8,128)S(1)} collective-permute-done((f32[1,8,1024]{2,1,0:T(8,128)S(1)}, f32[1,8,1024]{2,1,0:T(8,128)S(1)}, u32[]{:S(2)}, u32[]{:S(2)}) %collective-permute-start.8) | collective-permute-done | bytes 32800 | tf_op jit(solution)/shard_map/ppermute | solution.py:241
  13.2 1.6 %collective-permute-start.9 = (f32[2,8,1024]{2,1,0:T(8,128)S(1)}, f32[2,8,1024]{2,1,0:T(8,128)S(1)}, u32[]{:S(2)}, u32[]{:S(2)}) collective-permute-start(f32[2,8,1024]{2,1,0:T(8,128)S(1)} %pad_maximum_fusion.3.mirror_low), channel_id=1, source_target_pairs={{0,16},{8,24},{16,0},{24,8},{1,17},{9,25},{17,1},{25,9},{2,18},{10... | collective-permute-start | bytes 196616 | tf_op jit(solution)/shard_map/ppermute | solution.py:241
  14.7 1.2 %collective-permute-done.2 = f32[24,1024]{1,0:T(8,128)S(1)} collective-permute-done((f32[24,1024]{1,0:T(8,128)S(1)}, f32[24,1024]{1,0:T(8,128)S(1)}, u32[]{:S(2)}, u32[]{:S(2)}) %collective-permute-start.2) | collective-permute-done | bytes 98336 | tf_op jit(solution)/shard_map/ppermute | solution.py:262
  15.9 0.0 collective-permute-start.3
  15.9 3.8 %collective-permute-done = f32[1,24,1024]{2,1,0:T(8,128)S(1)} collective-permute-done((f32[1,24,1024]{2,1,0:T(8,128)S(1)}, f32[1,24,1024]{2,1,0:T(8,128)S(1)}, u32[]{:S(2)}, u32[]{:S(2)}) %collective-permute-start) | collective-permute-done | bytes 98336 | tf_op jit(solution)/shard_map/ppermute | solution.py:241
  19.7 0.1 collective-permute-start.1
  19.8 0.0 collective-permute-done.3
  19.8 1.1 %collective-permute-start.4 = (f32[2,24,1024]{2,1,0:T(8,128)S(1)}, f32[2,24,1024]{2,1,0:T(8,128)S(1)}, u32[]{:S(2)}, u32[]{:S(2)}) collective-permute-start(f32[2,24,1024]{2,1,0:T(8,128)S(1)} %pad_maximum_fusion.1.mirror_low), channel_id=1, source_target_pairs={{0,16},{8,24},{16,0},{24,8},{1,17},{9,25},{17,1},{25,9},{2,18},{10... | collective-permute-start | bytes 589832 | tf_op jit(solution)/shard_map/ppermute | solution.py:241
  20.9 0.0 collective-permute-done.6.own_high
  20.9 0.0 collective-permute-done.9.mirror_high
  20.9 7.8 %cross.2.refs_0_ = bf16[16,2,1024,1024]{3,2,1,0:T(8,128)(2,1)} custom-call(s32[1]{0:T(128)} %bitcast.turn_ref, f32[2,8,1024]{2,1,0:T(8,128)S(1)} %pad_maximum_fusion.2.own_low, f32[2,8,1024]{2,1,0:T(8,128)S(1)} %collective-permute-done.6.own_high, f32[2,8,1024]{2,1,0:T(8,128)S(1)} %pad_maximum_fusion.3.mirror_low, ...), custom_call_target="tpu_custom_call" | custom-call | flops 4294967296 | bytes 16777216 | tf_op jit(solution)/shard_map/cross/pallas_call | solution.py:210
  28.7 1.1 %collective-permute-done.1.own_high = f32[2,24,1024]{2,1,0:T(8,128)S(1)} collective-permute-done((f32[2,24,1024]{2,1,0:T(8,128)S(1)}, f32[2,24,1024]{2,1,0:T(8,128)S(1)}, u32[]{:S(2)}, u32[]{:S(2)}) %collective-permute-start.1) | collective-permute-done | bytes 196640 | tf_op jit(solution)/shard_map/ppermute | solution.py:241
  29.8 0.0 collective-permute-done.4.mirror_high
  29.8 20.6 %cross.3 = bf16[16,2,1024,1024]{3,2,1,0:T(8,128)(2,1)} custom-call(s32[1]{0:T(128)} %bitcast.turn_ref, f32[2,24,1024]{2,1,0:T(8,128)S(1)} %pad_maximum_fusion.own_low, f32[2,24,1024]{2,1,0:T(8,128)S(1)} %collective-permute-done.1.own_high, f32[2,24,1024]{2,1,0:T(8,128)S(1)} %pad_maximum_fusion.1.mirror_low, ...), custom_call_target="tpu_custom_call", output_to_operand_aliasing={{}: (5, {})} | custom-call | flops 12884901888 | bytes 50331648 | tf_op jit(solution)/shard_map/cross/pallas_call | solution.py:210
  (4 shorter events, 0.0 us)
Async XLA Ops:
  4.1 7.8 %collective-permute-start.7 = (f32[8,1024]{1,0:T(8,128)S(1)}, f32[8,1024]{1,0:T(8,128)S(1)}, u32[]{:S(2)}, u32[]{:S(2)}) collective-permute-start(f32[8,1024]{1,0:T(8,128)S(1)} %get-tuple-element.8), channel_id=1, source_target_pairs={{0,16},{2,24},{4,0},{6,8},{8,18},{10,26},{12,2},{14,10},{16,20},{1... | collective-permute-start | bytes 98312 | tf_op jit(solution)/shard_map/ppermute | solution.py:262
  7.1 4.9 %collective-permute-start.5 = (f32[1,8,1024]{2,1,0:T(8,128)S(1)}, f32[1,8,1024]{2,1,0:T(8,128)S(1)}, u32[]{:S(2)}, u32[]{:S(2)}) collective-permute-start(f32[1,8,1024]{2,1,0:T(8,128)S(1)} %bitcast.8), channel_id=1, source_target_pairs={{0,2},{2,0},{4,6},{6,4},{1,3},{3,1},{5,7},{7,5},{8,10},{10,8},{12,... | collective-permute-start | bytes 98312 | tf_op jit(solution)/shard_map/ppermute | solution.py:241
  8.0 7.9 %collective-permute-start.2 = (f32[24,1024]{1,0:T(8,128)S(1)}, f32[24,1024]{1,0:T(8,128)S(1)}, u32[]{:S(2)}, u32[]{:S(2)}) collective-permute-start(f32[24,1024]{1,0:T(8,128)S(1)} %get-tuple-element.7), channel_id=1, source_target_pairs={{0,16},{2,24},{4,0},{6,8},{8,18},{10,26},{12,2},{14,10},{16,20},{1... | collective-permute-start | bytes 294920 | tf_op jit(solution)/shard_map/ppermute | solution.py:262
  9.7 9.9 %collective-permute-start = (f32[1,24,1024]{2,1,0:T(8,128)S(1)}, f32[1,24,1024]{2,1,0:T(8,128)S(1)}, u32[]{:S(2)}, u32[]{:S(2)}) collective-permute-start(f32[1,24,1024]{2,1,0:T(8,128)S(1)} %bitcast.6), channel_id=1, source_target_pairs={{0,2},{2,0},{4,6},{6,4},{1,3},{3,1},{5,7},{7,5},{8,10},{10,8},{12,... | collective-permute-start | bytes 294920 | tf_op jit(solution)/shard_map/ppermute | solution.py:241
  11.9 1.2 %collective-permute-start.8 = (f32[1,8,1024]{2,1,0:T(8,128)S(1)}, f32[1,8,1024]{2,1,0:T(8,128)S(1)}, u32[]{:S(2)}, u32[]{:S(2)}) collective-permute-start(f32[1,8,1024]{2,1,0:T(8,128)S(1)} %bitcast.12), channel_id=1, source_target_pairs={{0,8},{8,0},{16,24},{24,16},{1,9},{9,1},{17,25},{25,17},{2,10},{10... | collective-permute-start | bytes 98312 | tf_op jit(solution)/shard_map/ppermute | solution.py:241
  12.1 8.8 %collective-permute-start.6 = (f32[2,8,1024]{2,1,0:T(8,128)S(1)}, f32[2,8,1024]{2,1,0:T(8,128)S(1)}, u32[]{:S(2)}, u32[]{:S(2)}) collective-permute-start(f32[2,8,1024]{2,1,0:T(8,128)S(1)} %pad_maximum_fusion.2.own_low), channel_id=1, source_target_pairs={{0,4},{2,6},{4,0},{6,2},{1,5},{3,7},{5,1},{7,3},{8,12},{10,14},{12... | collective-permute-start | bytes 196616 | tf_op jit(solution)/shard_map/ppermute | solution.py:241
  13.2 7.8 %collective-permute-start.9 = (f32[2,8,1024]{2,1,0:T(8,128)S(1)}, f32[2,8,1024]{2,1,0:T(8,128)S(1)}, u32[]{:S(2)}, u32[]{:S(2)}) collective-permute-start(f32[2,8,1024]{2,1,0:T(8,128)S(1)} %pad_maximum_fusion.3.mirror_low), channel_id=1, source_target_pairs={{0,16},{8,24},{16,0},{24,8},{1,17},{9,25},{17,1},{25,9},{2,18},{10... | collective-permute-start | bytes 196616 | tf_op jit(solution)/shard_map/ppermute | solution.py:241
  15.9 3.9 %collective-permute-start.3 = (f32[1,24,1024]{2,1,0:T(8,128)S(1)}, f32[1,24,1024]{2,1,0:T(8,128)S(1)}, u32[]{:S(2)}, u32[]{:S(2)}) collective-permute-start(f32[1,24,1024]{2,1,0:T(8,128)S(1)} %bitcast.10), channel_id=1, source_target_pairs={{0,8},{8,0},{16,24},{24,16},{1,9},{9,1},{17,25},{25,17},{2,10},{10... | collective-permute-start | bytes 294920 | tf_op jit(solution)/shard_map/ppermute | solution.py:241
  19.7 10.1 %collective-permute-start.1 = (f32[2,24,1024]{2,1,0:T(8,128)S(1)}, f32[2,24,1024]{2,1,0:T(8,128)S(1)}, u32[]{:S(2)}, u32[]{:S(2)}) collective-permute-start(f32[2,24,1024]{2,1,0:T(8,128)S(1)} %pad_maximum_fusion.own_low), channel_id=1, source_target_pairs={{0,4},{2,6},{4,0},{6,2},{1,5},{3,7},{5,1},{7,3},{8,12},{10,14},{12... | collective-permute-start | bytes 589832 | tf_op jit(solution)/shard_map/ppermute | solution.py:241
  19.8 10.0 %collective-permute-start.4 = (f32[2,24,1024]{2,1,0:T(8,128)S(1)}, f32[2,24,1024]{2,1,0:T(8,128)S(1)}, u32[]{:S(2)}, u32[]{:S(2)}) collective-permute-start(f32[2,24,1024]{2,1,0:T(8,128)S(1)} %pad_maximum_fusion.1.mirror_low), channel_id=1, source_target_pairs={{0,16},{8,24},{16,0},{24,8},{1,17},{9,25},{17,1},{25,9},{2,18},{10... | collective-permute-start | bytes 589832 | tf_op jit(solution)/shard_map/ppermute | solution.py:241

commit v8 on v7

--- a/solution.py
+++ b/solution.py
@@ -15,8 +15,8 @@
 EPSILON = 1e-05
 PAD = 168
 GROUP = 4
-CHUNK = 128
-BUFFERS = 4
+SPLIT = 4
+BUFFERS = 8
 SLOTS = 8
 
 
@@ -107,21 +107,22 @@
     height = done.shape[2]
     tile = min(256, height)
     pieces = [(q, t) for q in range(2) for t in range(height // tile)]
-    slot, inner = step % BUFFERS, step // 2 % GROUP
-    top = pl.multiple_of(step % 2 * height, height)
+    slot, inner = step % BUFFERS, step // SPLIT % GROUP
+    top = pl.multiple_of(step % SPLIT * height, height)
+    chunk = min(128, height)
 
     def gather(low, high, turn):
-        at = pl.multiple_of(step, rows)
+        at = pl.multiple_of(step // SPLIT * 2, rows)
         for w in range(windows):
             part = (low if w < half else high)[w % half, pl.ds(at, rows), :]
             held[pl.ds(pl.multiple_of((w ^ turn) * rows, 8), rows), :] = part
         return held[...]
 
     def copy(at_step, slot, q, t):
-        target = pl.ds(pl.multiple_of(at_step % 2 * height + t * tile, tile), tile)
+        target = pl.ds(pl.multiple_of(at_step % SPLIT * height + t * tile, tile), tile)
         return pltpu.make_async_copy(
             done.at[slot, q, pl.ds(t * tile, tile)],
-            out_hbm.at[first + at_step // 2, q, target],
+            out_hbm.at[first + at_step // SPLIT, q, target],
             sems.at[slot, q * (height // tile) + t],
         )
 
@@ -130,7 +131,7 @@
         picked[...] = jnp.zeros_like(picked)
         right[...] = jnp.zeros_like(right)
 
-    @pl.when(step % (2 * GROUP) == 0)
+    @pl.when(step % (SPLIT * GROUP) == 0)
     def _():
         high, low = split(gather(own_low, own_high, 0) * (1.0 / windows))
         blank = [jnp.zeros((width - 3 * terms, channels), jnp.float32)] if width > 3 * terms else []
@@ -160,11 +161,11 @@
 
         def retire(n, j, place):
             for q in range(2):
-                done[slot, q, j * CHUNK : (j + 1) * CHUNK, n * 256 : (n + 1) * 256] = pltpu.matmul_pop(
+                done[slot, q, j * chunk : (j + 1) * chunk, n * 256 : (n + 1) * 256] = pltpu.matmul_pop(
                     accs[q * SLOTS + place]
                 ).astype(jnp.bfloat16)
 
-        chunks, deep = height // CHUNK, depth // 256
+        chunks, deep = height // chunk, depth // 256
         stages = [(n, k) for n in range(channels // 256) for k in range(deep)]
         waiting = []
         stage(0)
@@ -176,7 +177,7 @@
                 for q in range(2):
                     pltpu.matmul_acc_lhs(
                         accs[q * SLOTS + place],
-                        picked[j * CHUNK : (j + 1) * CHUNK, k * 256 : (k + 1) * 256],
+                        picked[j * chunk : (j + 1) * chunk, k * 256 : (k + 1) * 256],
                         load_staged_rhs=number % 2 if j == 0 else None,
                     )
                 if j == 0 and number + 1 < len(stages):
@@ -187,14 +188,14 @@
             retire(*entry)
 
     pl.run_scoped(
-        multiply, *(pltpu.ACC(q)((CHUNK, 256), jnp.float32) for q in range(2) for _ in range(SLOTS))
+        multiply, *(pltpu.ACC(q)((chunk, 256), jnp.float32) for q in range(2) for _ in range(SLOTS))
     )
     for q, t in pieces:
-        copy(step, slot, q, t).start(priority=t % 2)
-
-    @pl.when(step == 2 * size - 1)
-    def _():
-        for last in range(2 * size - BUFFERS, 2 * size):
+        copy(step, slot, q, t).start(priority=q)
+
+    @pl.when(step == SPLIT * size - 1)
+    def _():
+        for last in range(SPLIT * size - BUFFERS, SPLIT * size):
             for q, t in pieces:
                 copy(last, last % BUFFERS, q, t).wait()
 
@@ -205,13 +206,13 @@
     terms = windows * 2 * GROUP
     width = -(-3 * terms // 128) * 128
     depth = -(-3 * terms // 256) * 256
-    height = channels // 2
+    height = channels // SPLIT
     previous = [] if so_far is None else [so_far]
     return pl.pallas_call(
         functools.partial(cross_kernel, size, first),
         grid_spec=pltpu.PrefetchScalarGridSpec(
             num_scalar_prefetch=1,
-            grid=(2 * size,),
+            grid=(SPLIT * size,),
             in_specs=[pl.BlockSpec(x.shape, lambda f, s: (0, 0, 0)) for x in (*own, *mirror)]
             + [pl.BlockSpec(memory_space=pl.ANY)] * len(previous),
             out_specs=pl.BlockSpec(memory_space=pl.ANY),
@@ -257,17 +258,19 @@
     across = n // 2
     turn = (row ^ col ^ across).reshape(1)
     swap = [(r * n + w, (w ^ across) * n + r) for r in range(n) for w in range(n)]
-    parts = []
-    for block in whiten(records, offsets, live_flags, sizes):
-        other = lax.ppermute(block, ("row", "col"), swap)
-        pairs = []
-        for x, axis in ((block, "col"), (other, "row")):
-            near = double(x[None], axis)
-            pairs.append((near, exchange(near, axis, n // 2)))
-        parts.append(pairs)
+    blocks = whiten(records, offsets, live_flags, sizes)
+    others = [lax.ppermute(blocks[0], ("row", "col"), swap)]
+    for block in blocks[1:]:
+        block, others[-1] = lax.optimization_barrier((block, others[-1]))
+        others.append(lax.ppermute(block, ("row", "col"), swap))
+    own = [double(block[None], "col") for block in blocks]
+    own_far = [exchange(near, "col", n // 2) for near in own]
+    mirror = [double(other[None], "row") for other in others]
+    mirror_far = [exchange(near, "row", n // 2) for near in mirror]
+    parts = zip(zip(own, own_far), zip(mirror, mirror_far))
     out, first = None, 0
-    for size, (own, mirror) in zip(sizes, parts):
-        out = cross(turn, own, mirror, out, first, size, bins)
+    for size, pairs in zip(sizes, parts):
+        out = cross(turn, *pairs, out, first, size, bins)
         first += size
     return out
 

time: 50.5 us -> 60.6 us (1.20)
  Pallas kernels: 31.8 us -> 38.2 us
  starting transfers between devices: 11.1 us -> 13 us
  waiting for transfers between devices: 6.68 us -> 8.46 us
    pallas_call x2, Pallas kernels: 28.4 us -> 34.8 us  [cross(): pl.pallas_call(functools.partial(cross_kernel, size, first), grid_spec=pl...]
    ppermute x2, waiting for transfers between devices: 1.2 us -> 6.89 us  [the longest x1 5.38 us: per_device(): others.append(lax.ppermute(block, ('row', 'col'), swap))]
    ppermute x8, waiting for transfers between devices: 5.47 us -> 1.57 us  [exchange(): return lax.ppermute(block, axis, [(i, i ^ distance) for i in range(n)])]
    ppermute x8, starting transfers between devices: 6.41 us -> 8.07 us  [exchange(): return lax.ppermute(block, axis, [(i, i ^ distance) for i in range(n)])]
where the time goes in v8:
time: 60.6 us; the launch traced here: 60.4 us
  Pallas kernels  38.2 us (63%)
  starting transfers between devices  13 us (21%)
  waiting for transfers between devices  8.46 us (14%)
  between operations  0.71 us (1%)
    pallas_call x2, Pallas kernels, cross(): pl.pallas_call(functools.partial(cross_kernel, size, first), grid_spec=pl...  34.8 us
    ppermute x8, starting transfers between devices, exchange(): return lax.ppermute(block, axis, [(i, i ^ distance) for i in range(n)])  8.07 us
    ppermute x1, waiting for transfers between devices, per_device(): others.append(lax.ppermute(block, ('row', 'col'), swap))  5.38 us
    pallas_call x1, Pallas kernels, whiten(): pl.pallas_call(functools.partial(whiten_kernel, sizes), in_specs=[pl.Bloc...  3.46 us
    ppermute x1, starting transfers between devices, per_device(): others = [lax.ppermute(blocks[0], ('row', 'col'), swap)]  3.02 us
    ppermute x1, starting transfers between devices, per_device(): others.append(lax.ppermute(block, ('row', 'col'), swap))  1.92 us
    ppermute x8, waiting for transfers between devices, exchange(): return lax.ppermute(block, axis, [(i, i ^ distance) for i in range(n)])  1.57 us
    ppermute x1, waiting for transfers between devices, per_device(): others = [lax.ppermute(blocks[0], ('row', 'col'), swap)]  1.51 us
  transfers between devices with their start and end apart: 10, of which 4 were waited for; matrix products, arithmetic and copies ran while one was open for 0% of the time, Pallas kernels for 15%

profile of v8, /device:TPU:0, one launch (start us, length us, event | category | flops | bytes accessed | tf_op | source)
XLA Modules:
  0.0 60.4 jit_solution(858106136630681442)
XLA Ops:
  0.7 3.5 %whiten.1 = (f32[8,1024]{1,0:T(8,128)S(1)}, f32[24,1024]{1,0:T(8,128)S(1)}) custom-call(s32[1]{0:T(128)S(6)} %copy.7.offset_ref, f32[1832,64]{1,0:T(8,128)} %constant.13.clone.table_hbm, bf16[1024,1664]{1,0:T(8,128)(2,1)} %records_hbm.1, s32[1,1024]{1,0:T(1,128)} %bitcast.14), custom_call_target="tpu_custom_call" | custom-call | flops 218103808 | bytes 3407872 | tf_op jit(solution)/shard_map/whiten/pallas_call | solution.py:69
  4.1 3.0 %collective-permute-start.2 = (f32[8,1024]{1,0:T(8,128)S(1)}, f32[8,1024]{1,0:T(8,128)S(1)}, u32[]{:S(2)}, u32[]{:S(2)}) collective-permute-start(f32[8,1024]{1,0:T(8,128)S(1)} %get-tuple-element.10), channel_id=1, source_target_pairs={{0,16},{2,24},{4,0},{6,8},{8,18},{10,26},{12,2},{14,10},{16,20},{1... | collective-permute-start | bytes 98312 | tf_op jit(solution)/shard_map/ppermute | solution.py:262
  7.1 0.9 %collective-permute-start.6 = (f32[1,8,1024]{2,1,0:T(8,128)S(1)}, f32[1,8,1024]{2,1,0:T(8,128)S(1)}, u32[]{:S(2)}, u32[]{:S(2)}) collective-permute-start(f32[1,8,1024]{2,1,0:T(8,128)S(1)} %bitcast.8), channel_id=1, source_target_pairs={{0,2},{2,0},{4,6},{6,4},{1,3},{3,1},{5,7},{7,5},{8,10},{10,8},{12,... | collective-permute-start | bytes 98312 | tf_op jit(solution)/shard_map/ppermute | solution.py:242
  8.0 1.1 %collective-permute-start = (f32[1,24,1024]{2,1,0:T(8,128)S(1)}, f32[1,24,1024]{2,1,0:T(8,128)S(1)}, u32[]{:S(2)}, u32[]{:S(2)}) collective-permute-start(f32[1,24,1024]{2,1,0:T(8,128)S(1)} %bitcast.6), channel_id=1, source_target_pairs={{0,2},{2,0},{4,6},{6,4},{1,3},{3,1},{5,7},{7,5},{8,10},{10,8},{12,... | collective-permute-start | bytes 294920 | tf_op jit(solution)/shard_map/ppermute | solution.py:242
  9.2 1.5 %collective-permute-done.2 = f32[8,1024]{1,0:T(8,128)S(1)} collective-permute-done((f32[8,1024]{1,0:T(8,128)S(1)}, f32[8,1024]{1,0:T(8,128)S(1)}, u32[]{:S(2)}, u32[]{:S(2)}) %collective-permute-start.2) | collective-permute-done | bytes 32800 | tf_op jit(solution)/shard_map/ppermute | solution.py:262
  10.7 0.6 collective-permute-start.8
  11.3 0.4 collective-permute-done.6
  11.6 1.1 %collective-permute-start.7 = (f32[2,8,1024]{2,1,0:T(8,128)S(1)}, f32[2,8,1024]{2,1,0:T(8,128)S(1)}, u32[]{:S(2)}, u32[]{:S(2)}) collective-permute-start(f32[2,8,1024]{2,1,0:T(8,128)S(1)} %pad_maximum_fusion.2.own_low), channel_id=1, source_target_pairs={{0,4},{2,6},{4,0},{6,2},{1,5},{3,7},{5,1},{7,3},{8,12},{10,14},{12... | collective-permute-start | bytes 196616 | tf_op jit(solution)/shard_map/ppermute | solution.py:242
  12.7 1.9 %collective-permute-start.3 = (f32[24,1024]{1,0:T(8,128)S(1)}, f32[24,1024]{1,0:T(8,128)S(1)}, u32[]{:S(2)}, u32[]{:S(2)}) collective-permute-start(f32[24,1024]{1,0:T(8,128)S(1)} %get-tuple-element.11), channel_id=1, source_target_pairs={{0,16},{2,24},{4,0},{6,8},{8,18},{10,26},{12,2},{14,10},{16,20},{1... | collective-permute-start | bytes 294920 | tf_op jit(solution)/shard_map/ppermute | solution.py:265
  14.6 0.0 collective-permute-done.8
  14.6 2.2 %collective-permute-start.9 = (f32[2,8,1024]{2,1,0:T(8,128)S(1)}, f32[2,8,1024]{2,1,0:T(8,128)S(1)}, u32[]{:S(2)}, u32[]{:S(2)}) collective-permute-start(f32[2,8,1024]{2,1,0:T(8,128)S(1)} %pad_maximum_fusion.3.mirror_low), channel_id=1, source_target_pairs={{0,16},{8,24},{16,0},{24,8},{1,17},{9,25},{17,1},{25,9},{2,18},{10... | collective-permute-start | bytes 196616 | tf_op jit(solution)/shard_map/ppermute | solution.py:242
  16.8 5.4 %collective-permute-done.3 = f32[24,1024]{1,0:T(8,128)S(1)} collective-permute-done((f32[24,1024]{1,0:T(8,128)S(1)}, f32[24,1024]{1,0:T(8,128)S(1)}, u32[]{:S(2)}, u32[]{:S(2)}) %collective-permute-start.3) | collective-permute-done | bytes 98336 | tf_op jit(solution)/shard_map/ppermute | solution.py:265
  22.2 0.0 collective-permute-start.4
  22.2 0.0 collective-permute-done
  22.3 0.1 collective-permute-start.1
  22.3 1.2 %collective-permute-done.4 = f32[1,24,1024]{2,1,0:T(8,128)S(1)} collective-permute-done((f32[1,24,1024]{2,1,0:T(8,128)S(1)}, f32[1,24,1024]{2,1,0:T(8,128)S(1)}, u32[]{:S(2)}, u32[]{:S(2)}) %collective-permute-start.4) | collective-permute-done | bytes 98336 | tf_op jit(solution)/shard_map/ppermute | solution.py:242
  23.6 2.1 %collective-permute-start.5 = (f32[2,24,1024]{2,1,0:T(8,128)S(1)}, f32[2,24,1024]{2,1,0:T(8,128)S(1)}, u32[]{:S(2)}, u32[]{:S(2)}) collective-permute-start(f32[2,24,1024]{2,1,0:T(8,128)S(1)} %pad_maximum_fusion.1.mirror_low), channel_id=1, source_target_pairs={{0,16},{8,24},{16,0},{24,8},{1,17},{9,25},{17,1},{25,9},{2,18},{10... | collective-permute-start | bytes 589832 | tf_op jit(solution)/shard_map/ppermute | solution.py:242
  25.6 0.0 collective-permute-done.7.own_high
  25.6 0.0 collective-permute-done.9.mirror_high
  25.6 9.2 %cross.2.refs_0_ = bf16[16,2,1024,1024]{3,2,1,0:T(8,128)(2,1)} custom-call(s32[1]{0:T(128)} %bitcast.turn_ref, f32[2,8,1024]{2,1,0:T(8,128)S(1)} %pad_maximum_fusion.2.own_low, f32[2,8,1024]{2,1,0:T(8,128)S(1)} %collective-permute-done.7.own_high, f32[2,8,1024]{2,1,0:T(8,128)S(1)} %pad_maximum_fusion.3.mirror_low, ...), custom_call_target="tpu_custom_call" | custom-call | flops 4294967296 | bytes 16777216 | tf_op jit(solution)/shard_map/cross/pallas_call | solution.py:211
  34.9 0.0 collective-permute-done.1.own_high
  34.9 0.0 collective-permute-done.5.mirror_high
  34.9 25.5 %cross.3 = bf16[16,2,1024,1024]{3,2,1,0:T(8,128)(2,1)} custom-call(s32[1]{0:T(128)} %bitcast.turn_ref, f32[2,24,1024]{2,1,0:T(8,128)S(1)} %pad_maximum_fusion.own_low, f32[2,24,1024]{2,1,0:T(8,128)S(1)} %collective-permute-done.1.own_high, f32[2,24,1024]{2,1,0:T(8,128)S(1)} %pad_maximum_fusion.1.mirror_low, ...), custom_call_target="tpu_custom_call", output_to_operand_aliasing={{}: (5, {})} | custom-call | flops 12884901888 | bytes 50331648 | tf_op jit(solution)/shard_map/cross/pallas_call | solution.py:211
  (4 shorter events, 0.0 us)
Async XLA Ops:
  4.1 6.6 %collective-permute-start.2 = (f32[8,1024]{1,0:T(8,128)S(1)}, f32[8,1024]{1,0:T(8,128)S(1)}, u32[]{:S(2)}, u32[]{:S(2)}) collective-permute-start(f32[8,1024]{1,0:T(8,128)S(1)} %get-tuple-element.10), channel_id=1, source_target_pairs={{0,16},{2,24},{4,0},{6,8},{8,18},{10,26},{12,2},{14,10},{16,20},{1... | collective-permute-start | bytes 98312 | tf_op jit(solution)/shard_map/ppermute | solution.py:262
  7.1 4.5 %collective-permute-start.6 = (f32[1,8,1024]{2,1,0:T(8,128)S(1)}, f32[1,8,1024]{2,1,0:T(8,128)S(1)}, u32[]{:S(2)}, u32[]{:S(2)}) collective-permute-start(f32[1,8,1024]{2,1,0:T(8,128)S(1)} %bitcast.8), channel_id=1, source_target_pairs={{0,2},{2,0},{4,6},{6,4},{1,3},{3,1},{5,7},{7,5},{8,10},{10,8},{12,... | collective-permute-start | bytes 98312 | tf_op jit(solution)/shard_map/ppermute | solution.py:242
  8.0 14.2 %collective-permute-start = (f32[1,24,1024]{2,1,0:T(8,128)S(1)}, f32[1,24,1024]{2,1,0:T(8,128)S(1)}, u32[]{:S(2)}, u32[]{:S(2)}) collective-permute-start(f32[1,24,1024]{2,1,0:T(8,128)S(1)} %bitcast.6), channel_id=1, source_target_pairs={{0,2},{2,0},{4,6},{6,4},{1,3},{3,1},{5,7},{7,5},{8,10},{10,8},{12,... | collective-permute-start | bytes 294920 | tf_op jit(solution)/shard_map/ppermute | solution.py:242
  10.7 4.0 %collective-permute-start.8 = (f32[1,8,1024]{2,1,0:T(8,128)S(1)}, f32[1,8,1024]{2,1,0:T(8,128)S(1)}, u32[]{:S(2)}, u32[]{:S(2)}) collective-permute-start(f32[1,8,1024]{2,1,0:T(8,128)S(1)} %bitcast.12), channel_id=1, source_target_pairs={{0,8},{8,0},{16,24},{24,16},{1,9},{9,1},{17,25},{25,17},{2,10},{10... | collective-permute-start | bytes 98312 | tf_op jit(solution)/shard_map/ppermute | solution.py:242
  11.6 14.0 %collective-permute-start.7 = (f32[2,8,1024]{2,1,0:T(8,128)S(1)}, f32[2,8,1024]{2,1,0:T(8,128)S(1)}, u32[]{:S(2)}, u32[]{:S(2)}) collective-permute-start(f32[2,8,1024]{2,1,0:T(8,128)S(1)} %pad_maximum_fusion.2.own_low), channel_id=1, source_target_pairs={{0,4},{2,6},{4,0},{6,2},{1,5},{3,7},{5,1},{7,3},{8,12},{10,14},{12... | collective-permute-start | bytes 196616 | tf_op jit(solution)/shard_map/ppermute | solution.py:242
  12.7 9.5 %collective-permute-start.3 = (f32[24,1024]{1,0:T(8,128)S(1)}, f32[24,1024]{1,0:T(8,128)S(1)}, u32[]{:S(2)}, u32[]{:S(2)}) collective-permute-start(f32[24,1024]{1,0:T(8,128)S(1)} %get-tuple-element.11), channel_id=1, source_target_pairs={{0,16},{2,24},{4,0},{6,8},{8,18},{10,26},{12,2},{14,10},{16,20},{1... | collective-permute-start | bytes 294920 | tf_op jit(solution)/shard_map/ppermute | solution.py:265
  14.6 11.0 %collective-permute-start.9 = (f32[2,8,1024]{2,1,0:T(8,128)S(1)}, f32[2,8,1024]{2,1,0:T(8,128)S(1)}, u32[]{:S(2)}, u32[]{:S(2)}) collective-permute-start(f32[2,8,1024]{2,1,0:T(8,128)S(1)} %pad_maximum_fusion.3.mirror_low), channel_id=1, source_target_pairs={{0,16},{8,24},{16,0},{24,8},{1,17},{9,25},{17,1},{25,9},{2,18},{10... | collective-permute-start | bytes 196616 | tf_op jit(solution)/shard_map/ppermute | solution.py:242
  22.2 1.3 %collective-permute-start.4 = (f32[1,24,1024]{2,1,0:T(8,128)S(1)}, f32[1,24,1024]{2,1,0:T(8,128)S(1)}, u32[]{:S(2)}, u32[]{:S(2)}) collective-permute-start(f32[1,24,1024]{2,1,0:T(8,128)S(1)} %bitcast.10), channel_id=1, source_target_pairs={{0,8},{8,0},{16,24},{24,16},{1,9},{9,1},{17,25},{25,17},{2,10},{10... | collective-permute-start | bytes 294920 | tf_op jit(solution)/shard_map/ppermute | solution.py:242
  22.3 12.6 %collective-permute-start.1 = (f32[2,24,1024]{2,1,0:T(8,128)S(1)}, f32[2,24,1024]{2,1,0:T(8,128)S(1)}, u32[]{:S(2)}, u32[]{:S(2)}) collective-permute-start(f32[2,24,1024]{2,1,0:T(8,128)S(1)} %pad_maximum_fusion.own_low), channel_id=1, source_target_pairs={{0,4},{2,6},{4,0},{6,2},{1,5},{3,7},{5,1},{7,3},{8,12},{10,14},{12... | collective-permute-start | bytes 589832 | tf_op jit(solution)/shard_map/ppermute | solution.py:242
  23.6 11.3 %collective-permute-start.5 = (f32[2,24,1024]{2,1,0:T(8,128)S(1)}, f32[2,24,1024]{2,1,0:T(8,128)S(1)}, u32[]{:S(2)}, u32[]{:S(2)}) collective-permute-start(f32[2,24,1024]{2,1,0:T(8,128)S(1)} %pad_maximum_fusion.1.mirror_low), channel_id=1, source_target_pairs={{0,16},{8,24},{16,0},{24,8},{1,17},{9,25},{17,1},{25,9},{2,18},{10... | collective-permute-start | bytes 589832 | tf_op jit(solution)/shard_map/ppermute | solution.py:242

commit v9 on v8

--- a/solution.py
+++ b/solution.py
@@ -15,8 +15,8 @@
 EPSILON = 1e-05
 PAD = 168
 GROUP = 4
-SPLIT = 4
-BUFFERS = 8
+SPLIT = 2
+BUFFERS = 4
 SLOTS = 8
 
 
@@ -242,8 +242,8 @@
     return lax.ppermute(block, axis, [(i, i ^ distance) for i in range(n)])
 
 
-def double(held, axis):
-    distance = 1
+def double(block, axis):
+    held, distance = block[None], 1
     while distance < lax.axis_size(axis) // 2:
         held = jnp.concatenate([held, exchange(held, axis, distance)])
         distance *= 2
@@ -258,16 +258,15 @@
     across = n // 2
     turn = (row ^ col ^ across).reshape(1)
     swap = [(r * n + w, (w ^ across) * n + r) for r in range(n) for w in range(n)]
-    blocks = whiten(records, offsets, live_flags, sizes)
-    others = [lax.ppermute(blocks[0], ("row", "col"), swap)]
-    for block in blocks[1:]:
-        block, others[-1] = lax.optimization_barrier((block, others[-1]))
-        others.append(lax.ppermute(block, ("row", "col"), swap))
-    own = [double(block[None], "col") for block in blocks]
-    own_far = [exchange(near, "col", n // 2) for near in own]
-    mirror = [double(other[None], "row") for other in others]
-    mirror_far = [exchange(near, "row", n // 2) for near in mirror]
-    parts = zip(zip(own, own_far), zip(mirror, mirror_far))
+    (whitened,) = whiten(records, offsets, live_flags, (bins,))
+    other = lax.ppermute(whitened, ("row", "col"), swap)
+    own, mirror = double(whitened, "col"), double(other, "row")
+    parts, first = [], 0
+    for size in sizes:
+        rows = slice(2 * first, 2 * (first + size))
+        halves = ((own[:, rows], "col"), (mirror[:, rows], "row"))
+        parts.append([(near, exchange(near, axis, n // 2)) for near, axis in halves])
+        first += size
     out, first = None, 0
     for size, pairs in zip(sizes, parts):
         out = cross(turn, *pairs, out, first, size, bins)

time: 60.6 us -> 55.2 us (0.911)
  Pallas kernels: 38.2 us -> 31.8 us
  waiting for transfers between devices: 8.46 us -> 13.5 us
  starting transfers between devices: 13 us -> 9.05 us
    pallas_call x2, Pallas kernels: 34.8 us -> 28.4 us  [cross(): pl.pallas_call(functools.partial(cross_kernel, size, first), grid_spec=pl...]
    ppermute x8 -> x6, waiting for transfers between devices: 1.57 us -> 6.25 us  [exchange(): return lax.ppermute(block, axis, [(i, i ^ distance) for i in range(n)])]
    ppermute x8 -> x6, starting transfers between devices: 8.07 us -> 6.03 us  [exchange(): return lax.ppermute(block, axis, [(i, i ^ distance) for i in range(n)])]
    ppermute x2 -> x1, starting transfers between devices: 4.94 us -> 3.02 us  [per_device(): other = lax.ppermute(whitened, ('row', 'col'), swap)]
    ppermute x2 -> x1, waiting for transfers between devices: 6.89 us -> 7.21 us  [per_device(): other = lax.ppermute(whitened, ('row', 'col'), swap)]
  transfers between devices with their start and end apart: 10 -> 7, of which waited for: 4 -> 3; matrix products, arithmetic and copies ran while one was open for 0% -> 0% of each run, Pallas kernels for 15% -> 14%
where the time goes in v9:
time: 55.2 us; the launch traced here: 55.1 us
  Pallas kernels  31.8 us (58%)
  waiting for transfers between devices  13.5 us (24%)
  starting transfers between devices  9.05 us (16%)
  between operations  0.71 us (1%)
    pallas_call x2, Pallas kernels, cross(): pl.pallas_call(functools.partial(cross_kernel, size, first), grid_spec=pl...  28.4 us
    ppermute x1, waiting for transfers between devices, per_device(): other = lax.ppermute(whitened, ('row', 'col'), swap)  7.21 us
    ppermute x6, waiting for transfers between devices, exchange(): return lax.ppermute(block, axis, [(i, i ^ distance) for i in range(n)])  6.25 us
    ppermute x6, starting transfers between devices, exchange(): return lax.ppermute(block, axis, [(i, i ^ distance) for i in range(n)])  6.03 us
    pallas_call x1, Pallas kernels, whiten(): pl.pallas_call(functools.partial(whiten_kernel, sizes), in_specs=[pl.Bloc...  3.46 us
    ppermute x1, starting transfers between devices, per_device(): other = lax.ppermute(whitened, ('row', 'col'), swap)  3.02 us
  transfers between devices with their start and end apart: 7, of which 3 were waited for; matrix products, arithmetic and copies ran while one was open for 0% of the time, Pallas kernels for 14%

profile of v9, /device:TPU:0, one launch (start us, length us, event | category | flops | bytes accessed | tf_op | source)
XLA Modules:
  0.0 55.1 jit_solution(12586285576844099313)
XLA Ops:
  0.7 3.5 %whiten.1 = f32[32,1024]{1,0:T(8,128)S(1)} custom-call(s32[1]{0:T(128)S(6)} %copy.7.offset_ref, f32[1832,64]{1,0:T(8,128)} %constant.13.clone.table_hbm, bf16[1024,1664]{1,0:T(8,128)(2,1)} %records_hbm.1, s32[1,1024]{1,0:T(1,128)} %bitcast.10), custom_call_target="tpu_custom_call" | custom-call | flops 218103808 | bytes 3407872 | tf_op jit(solution)/shard_map/whiten/pallas_call | solution.py:69
  4.1 3.0 %collective-permute-start.2 = (f32[32,1024]{1,0:T(8,128)S(1)}, f32[32,1024]{1,0:T(8,128)S(1)}, u32[]{:S(2)}, u32[]{:S(2)}) collective-permute-start(f32[32,1024]{1,0:T(8,128)S(1)} %whiten.1), channel_id=1, source_target_pairs={{0,16},{2,24},{4,0},{6,8},{8,18},{10,26},{12,2},{14,10},{16,20},{1... | collective-permute-start | bytes 393224 | tf_op jit(solution)/shard_map/ppermute | solution.py:262
  7.1 0.9 %collective-permute-start = (f32[1,32,1024]{2,1,0:T(8,128)S(1)}, f32[1,32,1024]{2,1,0:T(8,128)S(1)}, u32[]{:S(2)}, u32[]{:S(2)}) collective-permute-start(f32[1,32,1024]{2,1,0:T(8,128)S(1)} %bitcast.4), channel_id=1, source_target_pairs={{0,2},{2,0},{4,6},{6,4},{1,3},{3,1},{5,7},{7,5},{8,10},{10,8},{12,... | collective-permute-start | bytes 393224 | tf_op jit(solution)/shard_map/ppermute | solution.py:242
  8.0 7.2 %collective-permute-done.2 = f32[32,1024]{1,0:T(8,128)S(1)} collective-permute-done((f32[32,1024]{1,0:T(8,128)S(1)}, f32[32,1024]{1,0:T(8,128)S(1)}, u32[]{:S(2)}, u32[]{:S(2)}) %collective-permute-start.2) | collective-permute-done | bytes 131104 | tf_op jit(solution)/shard_map/ppermute | solution.py:262
  15.3 0.0 collective-permute-start.3
  15.3 1.3 %collective-permute-done = f32[1,32,1024]{2,1,0:T(8,128)S(1)} collective-permute-done((f32[1,32,1024]{2,1,0:T(8,128)S(1)}, f32[1,32,1024]{2,1,0:T(8,128)S(1)}, u32[]{:S(2)}, u32[]{:S(2)}) %collective-permute-start) | collective-permute-done | bytes 131104 | tf_op jit(solution)/shard_map/ppermute | solution.py:242
  16.6 0.0 collective-permute-start.5
  16.6 3.0 %collective-permute-start.1 = (f32[2,24,1024]{2,1,0:T(8,128)S(1)}, f32[2,24,1024]{2,1,0:T(8,128)S(1)}, u32[]{:S(2)}, u32[]{:S(2)}) collective-permute-start(f32[2,24,1024]{2,1,0:T(8,128)S(1)} %fusion.1.own_low), channel_id=1, source_target_pairs={{0,4},{2,6},{4,0},{6,2},{1,5},{3,7},{5,1},{7,3},{8,12},{10,14},{12... | collective-permute-start | bytes 589832 | tf_op jit(solution)/shard_map/ppermute | solution.py:242
  19.6 0.0 collective-permute-done.3
  19.6 0.1 collective-permute-start.6
  19.7 2.1 %collective-permute-start.4 = (f32[2,24,1024]{2,1,0:T(8,128)S(1)}, f32[2,24,1024]{2,1,0:T(8,128)S(1)}, u32[]{:S(2)}, u32[]{:S(2)}) collective-permute-start(f32[2,24,1024]{2,1,0:T(8,128)S(1)} %fusion.mirror_low), channel_id=1, source_target_pairs={{0,16},{8,24},{16,0},{24,8},{1,17},{9,25},{17,1},{25,9},{2,18},{10... | collective-permute-start | bytes 589832 | tf_op jit(solution)/shard_map/ppermute | solution.py:242
  21.8 4.9 %collective-permute-done.5.own_high = f32[2,8,1024]{2,1,0:T(8,128)S(1)} collective-permute-done((f32[2,8,1024]{2,1,0:T(8,128)S(1)}, f32[2,8,1024]{2,1,0:T(8,128)S(1)}, u32[]{:S(2)}, u32[]{:S(2)}) %collective-permute-start.5) | collective-permute-done | bytes 65568 | tf_op jit(solution)/shard_map/ppermute | solution.py:242
  26.7 0.0 collective-permute-done.6.mirror_high
  26.7 7.8 %cross.2.refs_0_ = bf16[16,2,1024,1024]{3,2,1,0:T(8,128)(2,1)} custom-call(s32[1]{0:T(128)} %bitcast.turn_ref, f32[2,8,1024]{2,1,0:T(8,128)S(1)} %pad_maximum_fusion.1.own_low, f32[2,8,1024]{2,1,0:T(8,128)S(1)} %collective-permute-done.5.own_high, f32[2,8,1024]{2,1,0:T(8,128)S(1)} %pad_maximum_fusion.mirror_low, ...), custom_call_target="tpu_custom_call" | custom-call | flops 4294967296 | bytes 16777216 | tf_op jit(solution)/shard_map/cross/pallas_call | solution.py:211
  34.5 0.0 collective-permute-done.1.own_high
  34.5 0.0 collective-permute-done.4.mirror_high
  34.5 20.6 %cross.3 = bf16[16,2,1024,1024]{3,2,1,0:T(8,128)(2,1)} custom-call(s32[1]{0:T(128)} %bitcast.turn_ref, f32[2,24,1024]{2,1,0:T(8,128)S(1)} %fusion.1.own_low, f32[2,24,1024]{2,1,0:T(8,128)S(1)} %collective-permute-done.1.own_high, f32[2,24,1024]{2,1,0:T(8,128)S(1)} %fusion.mirror_low, ...), custom_call_target="tpu_custom_call", output_to_operand_aliasing={{}: (5, {})} | custom-call | flops 12884901888 | bytes 50331648 | tf_op jit(solution)/shard_map/cross/pallas_call | solution.py:211
  (4 shorter events, 0.0 us)
Async XLA Ops:
  4.1 11.1 %collective-permute-start.2 = (f32[32,1024]{1,0:T(8,128)S(1)}, f32[32,1024]{1,0:T(8,128)S(1)}, u32[]{:S(2)}, u32[]{:S(2)}) collective-permute-start(f32[32,1024]{1,0:T(8,128)S(1)} %whiten.1), channel_id=1, source_target_pairs={{0,16},{2,24},{4,0},{6,8},{8,18},{10,26},{12,2},{14,10},{16,20},{1... | collective-permute-start | bytes 393224 | tf_op jit(solution)/shard_map/ppermute | solution.py:262
  7.1 9.5 %collective-permute-start = (f32[1,32,1024]{2,1,0:T(8,128)S(1)}, f32[1,32,1024]{2,1,0:T(8,128)S(1)}, u32[]{:S(2)}, u32[]{:S(2)}) collective-permute-start(f32[1,32,1024]{2,1,0:T(8,128)S(1)} %bitcast.4), channel_id=1, source_target_pairs={{0,2},{2,0},{4,6},{6,4},{1,3},{3,1},{5,7},{7,5},{8,10},{10,8},{12,... | collective-permute-start | bytes 393224 | tf_op jit(solution)/shard_map/ppermute | solution.py:242
  15.3 4.4 %collective-permute-start.3 = (f32[1,32,1024]{2,1,0:T(8,128)S(1)}, f32[1,32,1024]{2,1,0:T(8,128)S(1)}, u32[]{:S(2)}, u32[]{:S(2)}) collective-permute-start(f32[1,32,1024]{2,1,0:T(8,128)S(1)} %bitcast.7), channel_id=1, source_target_pairs={{0,8},{8,0},{16,24},{24,16},{1,9},{9,1},{17,25},{25,17},{2,10},{10... | collective-permute-start | bytes 393224 | tf_op jit(solution)/shard_map/ppermute | solution.py:242
  16.6 10.1 %collective-permute-start.5 = (f32[2,8,1024]{2,1,0:T(8,128)S(1)}, f32[2,8,1024]{2,1,0:T(8,128)S(1)}, u32[]{:S(2)}, u32[]{:S(2)}) collective-permute-start(f32[2,8,1024]{2,1,0:T(8,128)S(1)} %pad_maximum_fusion.1.own_low), channel_id=1, source_target_pairs={{0,4},{2,6},{4,0},{6,2},{1,5},{3,7},{5,1},{7,3},{8,12},{10,14},{12... | collective-permute-start | bytes 196616 | tf_op jit(solution)/shard_map/ppermute | solution.py:242
  16.6 17.9 %collective-permute-start.1 = (f32[2,24,1024]{2,1,0:T(8,128)S(1)}, f32[2,24,1024]{2,1,0:T(8,128)S(1)}, u32[]{:S(2)}, u32[]{:S(2)}) collective-permute-start(f32[2,24,1024]{2,1,0:T(8,128)S(1)} %fusion.1.own_low), channel_id=1, source_target_pairs={{0,4},{2,6},{4,0},{6,2},{1,5},{3,7},{5,1},{7,3},{8,12},{10,14},{12... | collective-permute-start | bytes 589832 | tf_op jit(solution)/shard_map/ppermute | solution.py:242
  19.6 7.1 %collective-permute-start.6 = (f32[2,8,1024]{2,1,0:T(8,128)S(1)}, f32[2,8,1024]{2,1,0:T(8,128)S(1)}, u32[]{:S(2)}, u32[]{:S(2)}) collective-permute-start(f32[2,8,1024]{2,1,0:T(8,128)S(1)} %pad_maximum_fusion.mirror_low), channel_id=1, source_target_pairs={{0,16},{8,24},{16,0},{24,8},{1,17},{9,25},{17,1},{25,9},{2,18},{10... | collective-permute-start | bytes 196616 | tf_op jit(solution)/shard_map/ppermute | solution.py:242
  19.7 14.8 %collective-permute-start.4 = (f32[2,24,1024]{2,1,0:T(8,128)S(1)}, f32[2,24,1024]{2,1,0:T(8,128)S(1)}, u32[]{:S(2)}, u32[]{:S(2)}) collective-permute-start(f32[2,24,1024]{2,1,0:T(8,128)S(1)} %fusion.mirror_low), channel_id=1, source_target_pairs={{0,16},{8,24},{16,0},{24,8},{1,17},{9,25},{17,1},{25,9},{2,18},{10... | collective-permute-start | bytes 589832 | tf_op jit(solution)/shard_map/ppermute | solution.py:242

commit v10 on v7

--- a/solution.py
+++ b/solution.py
@@ -97,7 +97,6 @@
 
 def cross_kernel(size, first, turn_ref, own_low, own_high, mirror_low, mirror_high, *refs):
     out_hbm, held, left, right, picked, done, sems = refs[-7:]
-    step = pl.program_id(0)
     half = own_low.shape[0]
     windows = 2 * half
     rows = 2 * GROUP
@@ -107,11 +106,8 @@
     height = done.shape[2]
     tile = min(256, height)
     pieces = [(q, t) for q in range(2) for t in range(height // tile)]
-    slot, inner = step % BUFFERS, step // 2 % GROUP
-    top = pl.multiple_of(step % 2 * height, height)
-
-    def gather(low, high, turn):
-        at = pl.multiple_of(step, rows)
+
+    def gather(low, high, turn, at):
         for w in range(windows):
             part = (low if w < half else high)[w % half, pl.ds(at, rows), :]
             held[pl.ds(pl.multiple_of((w ^ turn) * rows, 8), rows), :] = part
@@ -125,78 +121,83 @@
             sems.at[slot, q * (height // tile) + t],
         )
 
-    @pl.when(step == 0)
-    def _():
-        picked[...] = jnp.zeros_like(picked)
-        right[...] = jnp.zeros_like(right)
-
-    @pl.when(step % (2 * GROUP) == 0)
-    def _():
-        high, low = split(gather(own_low, own_high, 0) * (1.0 / windows))
+    picked[:, width:] = jnp.zeros((height, depth - width), jnp.bfloat16)
+    right[:, 3 * terms :] = jnp.zeros((2, depth - 3 * terms, channels), jnp.bfloat16)
+
+    def prepare(at):
+        high, low = split(gather(own_low, own_high, 0, at) * (1.0 / windows))
         blank = [jnp.zeros((width - 3 * terms, channels), jnp.float32)] if width > 3 * terms else []
         left[...] = jnp.concatenate([high, high, low, *blank], axis=0).T.astype(jnp.bfloat16)
-        values = gather(mirror_low, mirror_high, turn_ref[0])
+        values = gather(mirror_low, mirror_high, turn_ref[0], at)
         part = lax.broadcasted_iota(jnp.int32, values.shape, 0) % 2
         turned = jnp.where(part == 0, -pltpu.roll(values, terms - 1, 0), pltpu.roll(values, 1, 0))
         for q, block in enumerate((values, turned)):
             high, low = split(block)
             right[q, : 3 * terms] = jnp.concatenate([high, low, high], axis=0).astype(jnp.bfloat16)
 
-    @pl.when(step >= BUFFERS)
-    def _():
+    def body(step, carry):
+        slot, inner = step % BUFFERS, step // 2 % GROUP
+        top = pl.multiple_of(step % 2 * height, height)
+
+        @pl.when(step % (2 * GROUP) == 0)
+        def _():
+            prepare(pl.multiple_of(step, rows))
+
+        @pl.when(step >= BUFFERS)
+        def _():
+            for q, t in pieces:
+                copy(step - BUFFERS, slot, q, t).wait()
+
+        lane = lax.broadcasted_iota(jnp.int32, (1, width), 1)
+        mask = jnp.where(lane % rows // 2 == inner, 1.0, 0.0).astype(jnp.bfloat16)
+        picked[:, :width] = left[pl.ds(top, height), :] * mask
+
+        def multiply(*accs):
+            def stage(number):
+                n, k = stages[number]
+                for q in range(2):
+                    held_block = right[q, k * 256 : (k + 1) * 256, n * 256 : (n + 1) * 256]
+                    pltpu.matmul_push_rhs(held_block, number % 2, q)
+
+            def retire(n, j, place):
+                for q in range(2):
+                    done[slot, q, j * CHUNK : (j + 1) * CHUNK, n * 256 : (n + 1) * 256] = pltpu.matmul_pop(
+                        accs[q * SLOTS + place]
+                    ).astype(jnp.bfloat16)
+
+            chunks, deep = height // CHUNK, depth // 256
+            stages = [(n, k) for n in range(channels // 256) for k in range(deep)]
+            waiting = []
+            stage(0)
+            for number, (n, k) in enumerate(stages):
+                for j in range(chunks):
+                    place = (n * chunks + j) % SLOTS
+                    if k == 0 and len(waiting) > SLOTS // 2:
+                        retire(*waiting.pop(0))
+                    for q in range(2):
+                        pltpu.matmul_acc_lhs(
+                            accs[q * SLOTS + place],
+                            picked[j * CHUNK : (j + 1) * CHUNK, k * 256 : (k + 1) * 256],
+                            load_staged_rhs=number % 2 if j == 0 else None,
+                        )
+                    if j == 0 and number + 1 < len(stages):
+                        stage(number + 1)
+                    if k == deep - 1:
+                        waiting.append((n, j, place))
+            for entry in waiting:
+                retire(*entry)
+
+        pl.run_scoped(
+            multiply, *(pltpu.ACC(q)((CHUNK, 256), jnp.float32) for q in range(2) for _ in range(SLOTS))
+        )
         for q, t in pieces:
-            copy(step - BUFFERS, slot, q, t).wait()
-
-    lane = lax.broadcasted_iota(jnp.int32, (1, width), 1)
-    mask = jnp.where(lane % rows // 2 == inner, 1.0, 0.0).astype(jnp.bfloat16)
-    picked[:, :width] = left[pl.ds(top, height), :] * mask
-
-    def multiply(*accs):
-        def stage(number):
-            n, k = stages[number]
-            for q in range(2):
-                held_block = right[q, k * 256 : (k + 1) * 256, n * 256 : (n + 1) * 256]
-                pltpu.matmul_push_rhs(held_block, number % 2, q)
-
-        def retire(n, j, place):
-            for q in range(2):
-                done[slot, q, j * CHUNK : (j + 1) * CHUNK, n * 256 : (n + 1) * 256] = pltpu.matmul_pop(
-                    accs[q * SLOTS + place]
-                ).astype(jnp.bfloat16)
-
-        chunks, deep = height // CHUNK, depth // 256
-        stages = [(n, k) for n in range(channels // 256) for k in range(deep)]
-        waiting = []
-        stage(0)
-        for number, (n, k) in enumerate(stages):
-            for j in range(chunks):
-                place = (n * chunks + j) % SLOTS
-                if k == 0 and len(waiting) > SLOTS // 2:
-                    retire(*waiting.pop(0))
-                for q in range(2):
-                    pltpu.matmul_acc_lhs(
-                        accs[q * SLOTS + place],
-                        picked[j * CHUNK : (j + 1) * CHUNK, k * 256 : (k + 1) * 256],
-                        load_staged_rhs=number % 2 if j == 0 else None,
-                    )
-                if j == 0 and number + 1 < len(stages):
-                    stage(number + 1)
-                if k == deep - 1:
-                    waiting.append((n, j, place))
-        for entry in waiting:
-            retire(*entry)
-
-    pl.run_scoped(
-        multiply, *(pltpu.ACC(q)((CHUNK, 256), jnp.float32) for q in range(2) for _ in range(SLOTS))
-    )
-    for q, t in pieces:
-        copy(step, slot, q, t).start(priority=t % 2)
-
-    @pl.when(step == 2 * size - 1)
-    def _():
-        for last in range(2 * size - BUFFERS, 2 * size):
-            for q, t in pieces:
-                copy(last, last % BUFFERS, q, t).wait()
+            copy(step, slot, q, t).start(priority=t % 2)
+        return carry
+
+    lax.fori_loop(0, 2 * size, body, 0)
+    for last in range(2 * size - BUFFERS, 2 * size):
+        for q, t in pieces:
+            copy(last, last % BUFFERS, q, t).wait()
 
 
 def cross(turn, own, mirror, so_far, first, size, bins):
@@ -209,21 +210,18 @@
     previous = [] if so_far is None else [so_far]
     return pl.pallas_call(
         functools.partial(cross_kernel, size, first),
-        grid_spec=pltpu.PrefetchScalarGridSpec(
-            num_scalar_prefetch=1,
-            grid=(2 * size,),
-            in_specs=[pl.BlockSpec(x.shape, lambda f, s: (0, 0, 0)) for x in (*own, *mirror)]
-            + [pl.BlockSpec(memory_space=pl.ANY)] * len(previous),
-            out_specs=pl.BlockSpec(memory_space=pl.ANY),
-            scratch_shapes=[
-                pltpu.VMEM((terms, channels), jnp.float32),
-                pltpu.VMEM((channels, width), jnp.bfloat16),
-                pltpu.VMEM((2, depth, channels), jnp.bfloat16),
-                pltpu.VMEM((height, depth), jnp.bfloat16),
-                pltpu.VMEM((BUFFERS, 2, height, channels), jnp.bfloat16),
-                pltpu.SemaphoreType.DMA((BUFFERS, 2 * (height // min(256, height)))),
-            ],
-        ),
+        in_specs=[pl.BlockSpec(memory_space=pltpu.SMEM)]
+        + [pl.BlockSpec(memory_space=pltpu.VMEM)] * 4
+        + [pl.BlockSpec(memory_space=pl.ANY)] * len(previous),
+        out_specs=pl.BlockSpec(memory_space=pl.ANY),
+        scratch_shapes=[
+            pltpu.VMEM((terms, channels), jnp.float32),
+            pltpu.VMEM((channels, width), jnp.bfloat16),
+            pltpu.VMEM((2, depth, channels), jnp.bfloat16),
+            pltpu.VMEM((height, depth), jnp.bfloat16),
+            pltpu.VMEM((BUFFERS, 2, height, channels), jnp.bfloat16),
+            pltpu.SemaphoreType.DMA((BUFFERS, 2 * (height // min(256, height)))),
+        ],
         out_shape=jax.ShapeDtypeStruct((bins, 2, channels, channels), jnp.bfloat16),
         input_output_aliases={5: 0} if previous else {},
         compiler_params=pltpu.CompilerParams(vmem_limit_bytes=48 * 2**20),

time: 50.5 us -> 49.9 us (0.988)
  Pallas kernels: 31.8 us -> 31 us
    pallas_call x2, Pallas kernels: 28.4 us -> 27.5 us  [cross(): pl.pallas_call(functools.partial(cross_kernel, size, first), in_specs=[pl...]
where the time goes in v10:
time: 49.9 us; the launch traced here: 49.7 us
  Pallas kernels  31 us (62%)
  starting transfers between devices  11.1 us (22%)
  waiting for transfers between devices  6.88 us (14%)
  between operations  0.7 us (1%)
    pallas_call x2, Pallas kernels, cross(): pl.pallas_call(functools.partial(cross_kernel, size, first), in_specs=[pl...  27.5 us
    ppermute x8, starting transfers between devices, exchange(): return lax.ppermute(block, axis, [(i, i ^ distance) for i in range(n)])  6.41 us
    ppermute x8, waiting for transfers between devices, exchange(): return lax.ppermute(block, axis, [(i, i ^ distance) for i in range(n)])  5.68 us
    ppermute x2, starting transfers between devices, per_device(): other = lax.ppermute(block, ('row', 'col'), swap)  4.71 us
    pallas_call x1, Pallas kernels, whiten(): pl.pallas_call(functools.partial(whiten_kernel, sizes), in_specs=[pl.Bloc...  3.46 us
    ppermute x2, waiting for transfers between devices, per_device(): other = lax.ppermute(block, ('row', 'col'), swap)  1.2 us
  transfers between devices with their start and end apart: 10, of which 4 were waited for; matrix products, arithmetic and copies ran while one was open for 0% of the time, Pallas kernels for 15%

profile of v10, /device:TPU:0, one launch (start us, length us, event | category | flops | bytes accessed | tf_op | source)
XLA Modules:
  0.0 49.7 jit_solution(7057844528541235840)
XLA Ops:
  0.7 3.5 %whiten.1 = (f32[8,1024]{1,0:T(8,128)S(1)}, f32[24,1024]{1,0:T(8,128)S(1)}) custom-call(s32[1]{0:T(128)S(6)} %copy.7.offset_ref, f32[1832,64]{1,0:T(8,128)} %constant.13.clone.table_hbm, bf16[1024,1664]{1,0:T(8,128)(2,1)} %records_hbm.1, s32[1,1024]{1,0:T(1,128)} %bitcast.14), custom_call_target="tpu_custom_call" | custom-call | flops 218103808 | bytes 3407872 | tf_op jit(solution)/shard_map/whiten/pallas_call | solution.py:69
  4.1 3.0 %collective-permute-start.7 = (f32[8,1024]{1,0:T(8,128)S(1)}, f32[8,1024]{1,0:T(8,128)S(1)}, u32[]{:S(2)}, u32[]{:S(2)}) collective-permute-start(f32[8,1024]{1,0:T(8,128)S(1)} %get-tuple-element.8), channel_id=1, source_target_pairs={{0,16},{2,24},{4,0},{6,8},{8,18},{10,26},{12,2},{14,10},{16,20},{1... | collective-permute-start | bytes 98312 | tf_op jit(solution)/shard_map/ppermute | solution.py:260
  7.1 0.9 %collective-permute-start.5 = (f32[1,8,1024]{2,1,0:T(8,128)S(1)}, f32[1,8,1024]{2,1,0:T(8,128)S(1)}, u32[]{:S(2)}, u32[]{:S(2)}) collective-permute-start(f32[1,8,1024]{2,1,0:T(8,128)S(1)} %bitcast.8), channel_id=1, source_target_pairs={{0,2},{2,0},{4,6},{6,4},{1,3},{3,1},{5,7},{7,5},{8,10},{10,8},{12,... | collective-permute-start | bytes 98312 | tf_op jit(solution)/shard_map/ppermute | solution.py:239
  8.0 1.7 %collective-permute-start.2 = (f32[24,1024]{1,0:T(8,128)S(1)}, f32[24,1024]{1,0:T(8,128)S(1)}, u32[]{:S(2)}, u32[]{:S(2)}) collective-permute-start(f32[24,1024]{1,0:T(8,128)S(1)} %get-tuple-element.7), channel_id=1, source_target_pairs={{0,16},{2,24},{4,0},{6,8},{8,18},{10,26},{12,2},{14,10},{16,20},{1... | collective-permute-start | bytes 294920 | tf_op jit(solution)/shard_map/ppermute | solution.py:260
  9.7 2.2 %collective-permute-start = (f32[1,24,1024]{2,1,0:T(8,128)S(1)}, f32[1,24,1024]{2,1,0:T(8,128)S(1)}, u32[]{:S(2)}, u32[]{:S(2)}) collective-permute-start(f32[1,24,1024]{2,1,0:T(8,128)S(1)} %bitcast.6), channel_id=1, source_target_pairs={{0,2},{2,0},{4,6},{6,4},{1,3},{3,1},{5,7},{7,5},{8,10},{10,8},{12,... | collective-permute-start | bytes 294920 | tf_op jit(solution)/shard_map/ppermute | solution.py:239
  11.9 0.0 collective-permute-done.7
  11.9 0.1 collective-permute-start.8
  12.1 0.0 collective-permute-done.5
  12.1 0.4 collective-permute-start.6
  12.5 0.6 %collective-permute-done.8 = f32[1,8,1024]{2,1,0:T(8,128)S(1)} collective-permute-done((f32[1,8,1024]{2,1,0:T(8,128)S(1)}, f32[1,8,1024]{2,1,0:T(8,128)S(1)}, u32[]{:S(2)}, u32[]{:S(2)}) %collective-permute-start.8) | collective-permute-done | bytes 32800 | tf_op jit(solution)/shard_map/ppermute | solution.py:239
  13.2 1.6 %collective-permute-start.9 = (f32[2,8,1024]{2,1,0:T(8,128)S(1)}, f32[2,8,1024]{2,1,0:T(8,128)S(1)}, u32[]{:S(2)}, u32[]{:S(2)}) collective-permute-start(f32[2,8,1024]{2,1,0:T(8,128)S(1)} %pad_maximum_fusion.3.mirror_low), channel_id=1, source_target_pairs={{0,16},{8,24},{16,0},{24,8},{1,17},{9,25},{17,1},{25,9},{2,18},{10... | collective-permute-start | bytes 196616 | tf_op jit(solution)/shard_map/ppermute | solution.py:239
  14.7 1.2 %collective-permute-done.2 = f32[24,1024]{1,0:T(8,128)S(1)} collective-permute-done((f32[24,1024]{1,0:T(8,128)S(1)}, f32[24,1024]{1,0:T(8,128)S(1)}, u32[]{:S(2)}, u32[]{:S(2)}) %collective-permute-start.2) | collective-permute-done | bytes 98336 | tf_op jit(solution)/shard_map/ppermute | solution.py:260
  15.9 0.0 collective-permute-start.3
  15.9 3.8 %collective-permute-done = f32[1,24,1024]{2,1,0:T(8,128)S(1)} collective-permute-done((f32[1,24,1024]{2,1,0:T(8,128)S(1)}, f32[1,24,1024]{2,1,0:T(8,128)S(1)}, u32[]{:S(2)}, u32[]{:S(2)}) %collective-permute-start) | collective-permute-done | bytes 98336 | tf_op jit(solution)/shard_map/ppermute | solution.py:239
  19.7 0.1 collective-permute-start.1
  19.8 0.0 collective-permute-done.3
  19.8 1.1 %collective-permute-start.4 = (f32[2,24,1024]{2,1,0:T(8,128)S(1)}, f32[2,24,1024]{2,1,0:T(8,128)S(1)}, u32[]{:S(2)}, u32[]{:S(2)}) collective-permute-start(f32[2,24,1024]{2,1,0:T(8,128)S(1)} %pad_maximum_fusion.1.mirror_low), channel_id=1, source_target_pairs={{0,16},{8,24},{16,0},{24,8},{1,17},{9,25},{17,1},{25,9},{2,18},{10... | collective-permute-start | bytes 589832 | tf_op jit(solution)/shard_map/ppermute | solution.py:239
  20.9 0.0 collective-permute-done.6.own_high
  20.9 0.0 collective-permute-done.9.mirror_high
  20.9 7.6 %cross.2.refs_0_ = bf16[16,2,1024,1024]{3,2,1,0:T(8,128)(2,1)} custom-call(s32[1]{0:T(128)} %bitcast.turn_ref, f32[2,8,1024]{2,1,0:T(8,128)S(1)} %pad_maximum_fusion.2.own_low, f32[2,8,1024]{2,1,0:T(8,128)S(1)} %collective-permute-done.6.own_high, f32[2,8,1024]{2,1,0:T(8,128)S(1)} %pad_maximum_fusion.3.mirror_low, ...), custom_call_target="tpu_custom_call" | custom-call | flops 4294967296 | bytes 16777216 | tf_op jit(solution)/shard_map/cross/pallas_call | solution.py:211
  28.5 1.3 %collective-permute-done.1.own_high = f32[2,24,1024]{2,1,0:T(8,128)S(1)} collective-permute-done((f32[2,24,1024]{2,1,0:T(8,128)S(1)}, f32[2,24,1024]{2,1,0:T(8,128)S(1)}, u32[]{:S(2)}, u32[]{:S(2)}) %collective-permute-start.1) | collective-permute-done | bytes 196640 | tf_op jit(solution)/shard_map/ppermute | solution.py:239
  29.8 0.0 collective-permute-done.4.mirror_high
  29.8 19.9 %cross.3 = bf16[16,2,1024,1024]{3,2,1,0:T(8,128)(2,1)} custom-call(s32[1]{0:T(128)} %bitcast.turn_ref, f32[2,24,1024]{2,1,0:T(8,128)S(1)} %pad_maximum_fusion.own_low, f32[2,24,1024]{2,1,0:T(8,128)S(1)} %collective-permute-done.1.own_high, f32[2,24,1024]{2,1,0:T(8,128)S(1)} %pad_maximum_fusion.1.mirror_low, ...), custom_call_target="tpu_custom_call", output_to_operand_aliasing={{}: (5, {})} | custom-call | flops 12884901888 | bytes 50331648 | tf_op jit(solution)/shard_map/cross/pallas_call | solution.py:211
  (4 shorter events, 0.0 us)
Async XLA Ops:
  4.1 7.8 %collective-permute-start.7 = (f32[8,1024]{1,0:T(8,128)S(1)}, f32[8,1024]{1,0:T(8,128)S(1)}, u32[]{:S(2)}, u32[]{:S(2)}) collective-permute-start(f32[8,1024]{1,0:T(8,128)S(1)} %get-tuple-element.8), channel_id=1, source_target_pairs={{0,16},{2,24},{4,0},{6,8},{8,18},{10,26},{12,2},{14,10},{16,20},{1... | collective-permute-start | bytes 98312 | tf_op jit(solution)/shard_map/ppermute | solution.py:260
  7.1 4.9 %collective-permute-start.5 = (f32[1,8,1024]{2,1,0:T(8,128)S(1)}, f32[1,8,1024]{2,1,0:T(8,128)S(1)}, u32[]{:S(2)}, u32[]{:S(2)}) collective-permute-start(f32[1,8,1024]{2,1,0:T(8,128)S(1)} %bitcast.8), channel_id=1, source_target_pairs={{0,2},{2,0},{4,6},{6,4},{1,3},{3,1},{5,7},{7,5},{8,10},{10,8},{12,... | collective-permute-start | bytes 98312 | tf_op jit(solution)/shard_map/ppermute | solution.py:239
  8.0 7.9 %collective-permute-start.2 = (f32[24,1024]{1,0:T(8,128)S(1)}, f32[24,1024]{1,0:T(8,128)S(1)}, u32[]{:S(2)}, u32[]{:S(2)}) collective-permute-start(f32[24,1024]{1,0:T(8,128)S(1)} %get-tuple-element.7), channel_id=1, source_target_pairs={{0,16},{2,24},{4,0},{6,8},{8,18},{10,26},{12,2},{14,10},{16,20},{1... | collective-permute-start | bytes 294920 | tf_op jit(solution)/shard_map/ppermute | solution.py:260
  9.7 9.9 %collective-permute-start = (f32[1,24,1024]{2,1,0:T(8,128)S(1)}, f32[1,24,1024]{2,1,0:T(8,128)S(1)}, u32[]{:S(2)}, u32[]{:S(2)}) collective-permute-start(f32[1,24,1024]{2,1,0:T(8,128)S(1)} %bitcast.6), channel_id=1, source_target_pairs={{0,2},{2,0},{4,6},{6,4},{1,3},{3,1},{5,7},{7,5},{8,10},{10,8},{12,... | collective-permute-start | bytes 294920 | tf_op jit(solution)/shard_map/ppermute | solution.py:239
  11.9 1.2 %collective-permute-start.8 = (f32[1,8,1024]{2,1,0:T(8,128)S(1)}, f32[1,8,1024]{2,1,0:T(8,128)S(1)}, u32[]{:S(2)}, u32[]{:S(2)}) collective-permute-start(f32[1,8,1024]{2,1,0:T(8,128)S(1)} %bitcast.12), channel_id=1, source_target_pairs={{0,8},{8,0},{16,24},{24,16},{1,9},{9,1},{17,25},{25,17},{2,10},{10... | collective-permute-start | bytes 98312 | tf_op jit(solution)/shard_map/ppermute | solution.py:239
  12.1 8.8 %collective-permute-start.6 = (f32[2,8,1024]{2,1,0:T(8,128)S(1)}, f32[2,8,1024]{2,1,0:T(8,128)S(1)}, u32[]{:S(2)}, u32[]{:S(2)}) collective-permute-start(f32[2,8,1024]{2,1,0:T(8,128)S(1)} %pad_maximum_fusion.2.own_low), channel_id=1, source_target_pairs={{0,4},{2,6},{4,0},{6,2},{1,5},{3,7},{5,1},{7,3},{8,12},{10,14},{12... | collective-permute-start | bytes 196616 | tf_op jit(solution)/shard_map/ppermute | solution.py:239
  13.2 7.8 %collective-permute-start.9 = (f32[2,8,1024]{2,1,0:T(8,128)S(1)}, f32[2,8,1024]{2,1,0:T(8,128)S(1)}, u32[]{:S(2)}, u32[]{:S(2)}) collective-permute-start(f32[2,8,1024]{2,1,0:T(8,128)S(1)} %pad_maximum_fusion.3.mirror_low), channel_id=1, source_target_pairs={{0,16},{8,24},{16,0},{24,8},{1,17},{9,25},{17,1},{25,9},{2,18},{10... | collective-permute-start | bytes 196616 | tf_op jit(solution)/shard_map/ppermute | solution.py:239
  15.9 3.9 %collective-permute-start.3 = (f32[1,24,1024]{2,1,0:T(8,128)S(1)}, f32[1,24,1024]{2,1,0:T(8,128)S(1)}, u32[]{:S(2)}, u32[]{:S(2)}) collective-permute-start(f32[1,24,1024]{2,1,0:T(8,128)S(1)} %bitcast.10), channel_id=1, source_target_pairs={{0,8},{8,0},{16,24},{24,16},{1,9},{9,1},{17,25},{25,17},{2,10},{10... | collective-permute-start | bytes 294920 | tf_op jit(solution)/shard_map/ppermute | solution.py:239
  19.7 10.1 %collective-permute-start.1 = (f32[2,24,1024]{2,1,0:T(8,128)S(1)}, f32[2,24,1024]{2,1,0:T(8,128)S(1)}, u32[]{:S(2)}, u32[]{:S(2)}) collective-permute-start(f32[2,24,1024]{2,1,0:T(8,128)S(1)} %pad_maximum_fusion.own_low), channel_id=1, source_target_pairs={{0,4},{2,6},{4,0},{6,2},{1,5},{3,7},{5,1},{7,3},{8,12},{10,14},{12... | collective-permute-start | bytes 589832 | tf_op jit(solution)/shard_map/ppermute | solution.py:239
  19.8 10.0 %collective-permute-start.4 = (f32[2,24,1024]{2,1,0:T(8,128)S(1)}, f32[2,24,1024]{2,1,0:T(8,128)S(1)}, u32[]{:S(2)}, u32[]{:S(2)}) collective-permute-start(f32[2,24,1024]{2,1,0:T(8,128)S(1)} %pad_maximum_fusion.1.mirror_low), channel_id=1, source_target_pairs={{0,16},{8,24},{16,0},{24,8},{1,17},{9,25},{17,1},{25,9},{2,18},{10... | collective-permute-start | bytes 589832 | tf_op jit(solution)/shard_map/ppermute | solution.py:239

commit v11 on v10

--- a/solution.py
+++ b/solution.py
@@ -252,9 +252,9 @@
     n = lax.axis_size("col")
     bins = NB // lax.axis_size("bin")
     sizes = (GROUP, bins - GROUP)
-    across = n // 2
-    turn = (row ^ col ^ across).reshape(1)
-    swap = [(r * n + w, (w ^ across) * n + r) for r in range(n) for w in range(n)]
+    across = [n // 4 if (c ^ c >> 1) & 1 else n // 2 for c in range(n)]
+    turn = (row ^ col ^ jnp.where((col ^ col >> 1) & 1 == 1, n // 4, n // 2)).reshape(1)
+    swap = [(r * n + w, (w ^ across[r]) * n + r) for r in range(n) for w in range(n)]
     parts = []
     for block in whiten(records, offsets, live_flags, sizes):
         other = lax.ppermute(block, ("row", "col"), swap)

time: 49.9 us -> 48.6 us (0.974)
  waiting for transfers between devices: 6.88 us -> 4.65 us
  starting transfers between devices: 11.1 us -> 12.1 us
    ppermute x8, waiting for transfers between devices: 5.68 us -> 2.75 us  [exchange(): return lax.ppermute(block, axis, [(i, i ^ distance) for i in range(n)])]
    ppermute x2, waiting for transfers between devices: 1.2 us -> 1.89 us  [per_device(): other = lax.ppermute(block, ('row', 'col'), swap)]
    ppermute x2, starting transfers between devices: 4.71 us -> 5.22 us  [per_device(): other = lax.ppermute(block, ('row', 'col'), swap)]
  transfers between devices with their start and end apart: 10 -> 10, of which waited for: 4 -> 4; matrix products, arithmetic and copies ran while one was open for 0% -> 0% of each run, Pallas kernels for 15% -> 16%
where the time goes in v11:
time: 48.6 us; the launch traced here: 48.5 us
  Pallas kernels  31 us (64%)
  starting transfers between devices  12.1 us (25%)
  waiting for transfers between devices  4.65 us (10%)
  between operations  0.7 us (1%)
    pallas_call x2, Pallas kernels, cross(): pl.pallas_call(functools.partial(cross_kernel, size, first), in_specs=[pl...  27.5 us
    ppermute x8, starting transfers between devices, exchange(): return lax.ppermute(block, axis, [(i, i ^ distance) for i in range(n)])  6.9 us
    ppermute x2, starting transfers between devices, per_device(): other = lax.ppermute(block, ('row', 'col'), swap)  5.22 us
    pallas_call x1, Pallas kernels, whiten(): pl.pallas_call(functools.partial(whiten_kernel, sizes), in_specs=[pl.Bloc...  3.46 us
    ppermute x8, waiting for transfers between devices, exchange(): return lax.ppermute(block, axis, [(i, i ^ distance) for i in range(n)])  2.75 us
    ppermute x2, waiting for transfers between devices, per_device(): other = lax.ppermute(block, ('row', 'col'), swap)  1.89 us
  transfers between devices with their start and end apart: 10, of which 4 were waited for; matrix products, arithmetic and copies ran while one was open for 0% of the time, Pallas kernels for 16%

profile of v11, /device:TPU:0, one launch (start us, length us, event | category | flops | bytes accessed | tf_op | source)
XLA Modules:
  0.0 48.5 jit_solution(11338017238456611483)
XLA Ops:
  0.7 3.5 %whiten.1 = (f32[8,1024]{1,0:T(8,128)S(1)}, f32[24,1024]{1,0:T(8,128)S(1)}) custom-call(s32[1]{0:T(128)S(6)} %copy.7.offset_ref, f32[1832,64]{1,0:T(8,128)} %constant.15.clone.table_hbm, bf16[1024,1664]{1,0:T(8,128)(2,1)} %records_hbm.1, s32[1,1024]{1,0:T(1,128)} %bitcast.14), custom_call_target="tpu_custom_call" | custom-call | flops 218103808 | bytes 3407872 | tf_op jit(solution)/shard_map/whiten/pallas_call | solution.py:69
  4.1 3.0 %collective-permute-start.7 = (f32[8,1024]{1,0:T(8,128)S(1)}, f32[8,1024]{1,0:T(8,128)S(1)}, u32[]{:S(2)}, u32[]{:S(2)}) collective-permute-start(f32[8,1024]{1,0:T(8,128)S(1)} %get-tuple-element.8), channel_id=1, source_target_pairs={{0,16},{2,24},{4,0},{6,8},{8,10},{10,2},{12,26},{14,18},{16,12},{1... | collective-permute-start | bytes 98312 | tf_op jit(solution)/shard_map/ppermute | solution.py:260
  7.2 0.9 %collective-permute-start.5 = (f32[1,8,1024]{2,1,0:T(8,128)S(1)}, f32[1,8,1024]{2,1,0:T(8,128)S(1)}, u32[]{:S(2)}, u32[]{:S(2)}) collective-permute-start(f32[1,8,1024]{2,1,0:T(8,128)S(1)} %bitcast.8), channel_id=1, source_target_pairs={{0,2},{2,0},{4,6},{6,4},{1,3},{3,1},{5,7},{7,5},{8,10},{10,8},{12,... | collective-permute-start | bytes 98312 | tf_op jit(solution)/shard_map/ppermute | solution.py:239
  8.1 2.2 %collective-permute-start.2 = (f32[24,1024]{1,0:T(8,128)S(1)}, f32[24,1024]{1,0:T(8,128)S(1)}, u32[]{:S(2)}, u32[]{:S(2)}) collective-permute-start(f32[24,1024]{1,0:T(8,128)S(1)} %get-tuple-element.7), channel_id=1, source_target_pairs={{0,16},{2,24},{4,0},{6,8},{8,10},{10,2},{12,26},{14,18},{16,12},{1... | collective-permute-start | bytes 294920 | tf_op jit(solution)/shard_map/ppermute | solution.py:260
  10.2 1.7 %collective-permute-start = (f32[1,24,1024]{2,1,0:T(8,128)S(1)}, f32[1,24,1024]{2,1,0:T(8,128)S(1)}, u32[]{:S(2)}, u32[]{:S(2)}) collective-permute-start(f32[1,24,1024]{2,1,0:T(8,128)S(1)} %bitcast.6), channel_id=1, source_target_pairs={{0,2},{2,0},{4,6},{6,4},{1,3},{3,1},{5,7},{7,5},{8,10},{10,8},{12,... | collective-permute-start | bytes 294920 | tf_op jit(solution)/shard_map/ppermute | solution.py:239
  11.9 0.0 collective-permute-done.7
  11.9 0.0 collective-permute-start.8
  11.9 0.0 collective-permute-done.5
  12.0 1.8 %collective-permute-start.6 = (f32[2,8,1024]{2,1,0:T(8,128)S(1)}, f32[2,8,1024]{2,1,0:T(8,128)S(1)}, u32[]{:S(2)}, u32[]{:S(2)}) collective-permute-start(f32[2,8,1024]{2,1,0:T(8,128)S(1)} %pad_maximum_fusion.2.own_low), channel_id=1, source_target_pairs={{0,4},{2,6},{4,0},{6,2},{1,5},{3,7},{5,1},{7,3},{8,12},{10,14},{12... | collective-permute-start | bytes 196616 | tf_op jit(solution)/shard_map/ppermute | solution.py:239
  13.7 0.0 collective-permute-done.8
  13.8 0.4 collective-permute-start.9
  14.2 1.9 %collective-permute-done.2 = f32[24,1024]{1,0:T(8,128)S(1)} collective-permute-done((f32[24,1024]{1,0:T(8,128)S(1)}, f32[24,1024]{1,0:T(8,128)S(1)}, u32[]{:S(2)}, u32[]{:S(2)}) %collective-permute-start.2) | collective-permute-done | bytes 98336 | tf_op jit(solution)/shard_map/ppermute | solution.py:260
  16.1 0.0 collective-permute-start.3
  16.1 0.6 %collective-permute-done = f32[1,24,1024]{2,1,0:T(8,128)S(1)} collective-permute-done((f32[1,24,1024]{2,1,0:T(8,128)S(1)}, f32[1,24,1024]{2,1,0:T(8,128)S(1)}, u32[]{:S(2)}, u32[]{:S(2)}) %collective-permute-start) | collective-permute-done | bytes 98336 | tf_op jit(solution)/shard_map/ppermute | solution.py:239
  16.7 2.0 %collective-permute-start.1 = (f32[2,24,1024]{2,1,0:T(8,128)S(1)}, f32[2,24,1024]{2,1,0:T(8,128)S(1)}, u32[]{:S(2)}, u32[]{:S(2)}) collective-permute-start(f32[2,24,1024]{2,1,0:T(8,128)S(1)} %pad_maximum_fusion.own_low), channel_id=1, source_target_pairs={{0,4},{2,6},{4,0},{6,2},{1,5},{3,7},{5,1},{7,3},{8,12},{10,14},{12... | collective-permute-start | bytes 589832 | tf_op jit(solution)/shard_map/ppermute | solution.py:239
  18.8 0.0 collective-permute-done.3
  18.8 0.1 collective-permute-start.4
  18.9 0.4 collective-permute-done.6.own_high
  19.3 0.0 collective-permute-done.9.mirror_high
  19.3 7.6 %cross.2.refs_0_ = bf16[16,2,1024,1024]{3,2,1,0:T(8,128)(2,1)} custom-call(s32[1]{0:T(128)} %bitcast.turn_ref, f32[2,8,1024]{2,1,0:T(8,128)S(1)} %pad_maximum_fusion.2.own_low, f32[2,8,1024]{2,1,0:T(8,128)S(1)} %collective-permute-done.6.own_high, f32[2,8,1024]{2,1,0:T(8,128)S(1)} %pad_maximum_fusion.3.mirror_low, ...), custom_call_target="tpu_custom_call" | custom-call | flops 4294967296 | bytes 16777216 | tf_op jit(solution)/shard_map/cross/pallas_call | solution.py:211
  26.9 1.7 %collective-permute-done.1.own_high = f32[2,24,1024]{2,1,0:T(8,128)S(1)} collective-permute-done((f32[2,24,1024]{2,1,0:T(8,128)S(1)}, f32[2,24,1024]{2,1,0:T(8,128)S(1)}, u32[]{:S(2)}, u32[]{:S(2)}) %collective-permute-start.1) | collective-permute-done | bytes 196640 | tf_op jit(solution)/shard_map/ppermute | solution.py:239
  28.6 0.0 collective-permute-done.4.mirror_high
  28.6 19.9 %cross.3 = bf16[16,2,1024,1024]{3,2,1,0:T(8,128)(2,1)} custom-call(s32[1]{0:T(128)} %bitcast.turn_ref, f32[2,24,1024]{2,1,0:T(8,128)S(1)} %pad_maximum_fusion.own_low, f32[2,24,1024]{2,1,0:T(8,128)S(1)} %collective-permute-done.1.own_high, f32[2,24,1024]{2,1,0:T(8,128)S(1)} %pad_maximum_fusion.1.mirror_low, ...), custom_call_target="tpu_custom_call", output_to_operand_aliasing={{}: (5, {})} | custom-call | flops 12884901888 | bytes 50331648 | tf_op jit(solution)/shard_map/cross/pallas_call | solution.py:211
  (4 shorter events, 0.0 us)
Async XLA Ops:
  4.1 7.8 %collective-permute-start.7 = (f32[8,1024]{1,0:T(8,128)S(1)}, f32[8,1024]{1,0:T(8,128)S(1)}, u32[]{:S(2)}, u32[]{:S(2)}) collective-permute-start(f32[8,1024]{1,0:T(8,128)S(1)} %get-tuple-element.8), channel_id=1, source_target_pairs={{0,16},{2,24},{4,0},{6,8},{8,10},{10,2},{12,26},{14,18},{16,12},{1... | collective-permute-start | bytes 98312 | tf_op jit(solution)/shard_map/ppermute | solution.py:260
  7.2 4.8 %collective-permute-start.5 = (f32[1,8,1024]{2,1,0:T(8,128)S(1)}, f32[1,8,1024]{2,1,0:T(8,128)S(1)}, u32[]{:S(2)}, u32[]{:S(2)}) collective-permute-start(f32[1,8,1024]{2,1,0:T(8,128)S(1)} %bitcast.8), channel_id=1, source_target_pairs={{0,2},{2,0},{4,6},{6,4},{1,3},{3,1},{5,7},{7,5},{8,10},{10,8},{12,... | collective-permute-start | bytes 98312 | tf_op jit(solution)/shard_map/ppermute | solution.py:239
  8.1 8.0 %collective-permute-start.2 = (f32[24,1024]{1,0:T(8,128)S(1)}, f32[24,1024]{1,0:T(8,128)S(1)}, u32[]{:S(2)}, u32[]{:S(2)}) collective-permute-start(f32[24,1024]{1,0:T(8,128)S(1)} %get-tuple-element.7), channel_id=1, source_target_pairs={{0,16},{2,24},{4,0},{6,8},{8,10},{10,2},{12,26},{14,18},{16,12},{1... | collective-permute-start | bytes 294920 | tf_op jit(solution)/shard_map/ppermute | solution.py:260
  10.2 6.4 %collective-permute-start = (f32[1,24,1024]{2,1,0:T(8,128)S(1)}, f32[1,24,1024]{2,1,0:T(8,128)S(1)}, u32[]{:S(2)}, u32[]{:S(2)}) collective-permute-start(f32[1,24,1024]{2,1,0:T(8,128)S(1)} %bitcast.6), channel_id=1, source_target_pairs={{0,2},{2,0},{4,6},{6,4},{1,3},{3,1},{5,7},{7,5},{8,10},{10,8},{12,... | collective-permute-start | bytes 294920 | tf_op jit(solution)/shard_map/ppermute | solution.py:239
  11.9 1.8 %collective-permute-start.8 = (f32[1,8,1024]{2,1,0:T(8,128)S(1)}, f32[1,8,1024]{2,1,0:T(8,128)S(1)}, u32[]{:S(2)}, u32[]{:S(2)}) collective-permute-start(f32[1,8,1024]{2,1,0:T(8,128)S(1)} %bitcast.12), channel_id=1, source_target_pairs={{0,8},{8,0},{16,24},{24,16},{1,9},{9,1},{17,25},{25,17},{2,10},{10... | collective-permute-start | bytes 98312 | tf_op jit(solution)/shard_map/ppermute | solution.py:239
  12.0 7.3 %collective-permute-start.6 = (f32[2,8,1024]{2,1,0:T(8,128)S(1)}, f32[2,8,1024]{2,1,0:T(8,128)S(1)}, u32[]{:S(2)}, u32[]{:S(2)}) collective-permute-start(f32[2,8,1024]{2,1,0:T(8,128)S(1)} %pad_maximum_fusion.2.own_low), channel_id=1, source_target_pairs={{0,4},{2,6},{4,0},{6,2},{1,5},{3,7},{5,1},{7,3},{8,12},{10,14},{12... | collective-permute-start | bytes 196616 | tf_op jit(solution)/shard_map/ppermute | solution.py:239
  13.8 5.5 %collective-permute-start.9 = (f32[2,8,1024]{2,1,0:T(8,128)S(1)}, f32[2,8,1024]{2,1,0:T(8,128)S(1)}, u32[]{:S(2)}, u32[]{:S(2)}) collective-permute-start(f32[2,8,1024]{2,1,0:T(8,128)S(1)} %pad_maximum_fusion.3.mirror_low), channel_id=1, source_target_pairs={{0,16},{8,24},{16,0},{24,8},{1,17},{9,25},{17,1},{25,9},{2,18},{10... | collective-permute-start | bytes 196616 | tf_op jit(solution)/shard_map/ppermute | solution.py:239
  16.1 2.7 %collective-permute-start.3 = (f32[1,24,1024]{2,1,0:T(8,128)S(1)}, f32[1,24,1024]{2,1,0:T(8,128)S(1)}, u32[]{:S(2)}, u32[]{:S(2)}) collective-permute-start(f32[1,24,1024]{2,1,0:T(8,128)S(1)} %bitcast.10), channel_id=1, source_target_pairs={{0,8},{8,0},{16,24},{24,16},{1,9},{9,1},{17,25},{25,17},{2,10},{10... | collective-permute-start | bytes 294920 | tf_op jit(solution)/shard_map/ppermute | solution.py:239
  16.7 11.9 %collective-permute-start.1 = (f32[2,24,1024]{2,1,0:T(8,128)S(1)}, f32[2,24,1024]{2,1,0:T(8,128)S(1)}, u32[]{:S(2)}, u32[]{:S(2)}) collective-permute-start(f32[2,24,1024]{2,1,0:T(8,128)S(1)} %pad_maximum_fusion.own_low), channel_id=1, source_target_pairs={{0,4},{2,6},{4,0},{6,2},{1,5},{3,7},{5,1},{7,3},{8,12},{10,14},{12... | collective-permute-start | bytes 589832 | tf_op jit(solution)/shard_map/ppermute | solution.py:239
  18.8 9.8 %collective-permute-start.4 = (f32[2,24,1024]{2,1,0:T(8,128)S(1)}, f32[2,24,1024]{2,1,0:T(8,128)S(1)}, u32[]{:S(2)}, u32[]{:S(2)}) collective-permute-start(f32[2,24,1024]{2,1,0:T(8,128)S(1)} %pad_maximum_fusion.1.mirror_low), channel_id=1, source_target_pairs={{0,16},{8,24},{16,0},{24,8},{1,17},{9,25},{17,1},{25,9},{2,18},{10... | collective-permute-start | bytes 589832 | tf_op jit(solution)/shard_map/ppermute | solution.py:239

commit v12 on v11

--- a/solution.py
+++ b/solution.py
@@ -255,14 +255,18 @@
     across = [n // 4 if (c ^ c >> 1) & 1 else n // 2 for c in range(n)]
     turn = (row ^ col ^ jnp.where((col ^ col >> 1) & 1 == 1, n // 4, n // 2)).reshape(1)
     swap = [(r * n + w, (w ^ across[r]) * n + r) for r in range(n) for w in range(n)]
-    parts = []
-    for block in whiten(records, offsets, live_flags, sizes):
-        other = lax.ppermute(block, ("row", "col"), swap)
-        pairs = []
-        for x, axis in ((block, "col"), (other, "row")):
-            near = double(x[None], axis)
-            pairs.append((near, exchange(near, axis, n // 2)))
-        parts.append(pairs)
+    (whitened,) = whiten(records, offsets, live_flags, (bins,))
+    other = lax.ppermute(whitened, ("row", "col"), swap)
+    own, mirror = double(whitened[None], "col"), double(other[None], "row")
+    parts, first = [], 0
+    for size in sizes:
+        rows = slice(2 * first, 2 * (first + size))
+        near = own[:, rows]
+        if parts:
+            near, parts[-1] = lax.optimization_barrier((near, parts[-1]))
+        right = mirror[:, rows]
+        parts.append(([near, exchange(near, "col", n // 2)], [right, exchange(right, "row", n // 2)]))
+        first += size
     out, first = None, 0
     for size, (own, mirror) in zip(sizes, parts):
         out = cross(turn, own, mirror, out, first, size, bins)

time: 48.6 us -> 53.9 us (1.11)
  waiting for transfers between devices: 4.65 us -> 12.8 us
  starting transfers between devices: 12.1 us -> 9.18 us
    ppermute x2 -> x1, waiting for transfers between devices: 1.89 us -> 7.07 us  [per_device(): other = lax.ppermute(whitened, ('row', 'col'), swap)]
    ppermute x8 -> x6, waiting for transfers between devices: 2.75 us -> 5.75 us  [exchange(): return lax.ppermute(block, axis, [(i, i ^ distance) for i in range(n)])]
    ppermute x2 -> x1, starting transfers between devices: 5.22 us -> 3.03 us  [per_device(): other = lax.ppermute(whitened, ('row', 'col'), swap)]
    ppermute x8 -> x6, starting transfers between devices: 6.9 us -> 6.15 us  [exchange(): return lax.ppermute(block, axis, [(i, i ^ distance) for i in range(n)])]
  transfers between devices with their start and end apart: 10 -> 7, of which waited for: 4 -> 5; matrix products, arithmetic and copies ran while one was open for 0% -> 0% of each run, Pallas kernels for 16% -> 14%
where the time goes in v12:
time: 53.9 us; the launch traced here: 53.7 us
  Pallas kernels  31 us (58%)
  waiting for transfers between devices  12.8 us (24%)
  starting transfers between devices  9.18 us (17%)
  between operations  0.71 us (1%)
    pallas_call x2, Pallas kernels, cross(): pl.pallas_call(functools.partial(cross_kernel, size, first), in_specs=[pl...  27.5 us
    ppermute x1, waiting for transfers between devices, per_device(): other = lax.ppermute(whitened, ('row', 'col'), swap)  7.07 us
    ppermute x6, starting transfers between devices, exchange(): return lax.ppermute(block, axis, [(i, i ^ distance) for i in range(n)])  6.15 us
    ppermute x6, waiting for transfers between devices, exchange(): return lax.ppermute(block, axis, [(i, i ^ distance) for i in range(n)])  5.75 us
    pallas_call x1, Pallas kernels, whiten(): pl.pallas_call(functools.partial(whiten_kernel, sizes), in_specs=[pl.Bloc...  3.46 us
    ppermute x1, starting transfers between devices, per_device(): other = lax.ppermute(whitened, ('row', 'col'), swap)  3.03 us
  transfers between devices with their start and end apart: 7, of which 5 were waited for; matrix products, arithmetic and copies ran while one was open for 0% of the time, Pallas kernels for 14%

profile of v12, /device:TPU:0, one launch (start us, length us, event | category | flops | bytes accessed | tf_op | source)
XLA Modules:
  0.0 53.7 jit_solution(15798366920821360062)
XLA Ops:
  0.7 3.5 %whiten.1 = f32[32,1024]{1,0:T(8,128)S(1)} custom-call(s32[1]{0:T(128)S(6)} %copy.7.offset_ref, f32[1832,64]{1,0:T(8,128)} %constant.15.clone.table_hbm, bf16[1024,1664]{1,0:T(8,128)(2,1)} %records_hbm.1, s32[1,1024]{1,0:T(1,128)} %bitcast.10), custom_call_target="tpu_custom_call" | custom-call | flops 218103808 | bytes 3407872 | tf_op jit(solution)/shard_map/whiten/pallas_call | solution.py:69
  4.1 3.0 %collective-permute-start.2 = (f32[32,1024]{1,0:T(8,128)S(1)}, f32[32,1024]{1,0:T(8,128)S(1)}, u32[]{:S(2)}, u32[]{:S(2)}) collective-permute-start(f32[32,1024]{1,0:T(8,128)S(1)} %whiten.1), channel_id=1, source_target_pairs={{0,16},{2,24},{4,0},{6,8},{8,10},{10,2},{12,26},{14,18},{16,12},{1... | collective-permute-start | bytes 393224 | tf_op jit(solution)/shard_map/ppermute | solution.py:259
  7.1 0.9 %collective-permute-start = (f32[1,32,1024]{2,1,0:T(8,128)S(1)}, f32[1,32,1024]{2,1,0:T(8,128)S(1)}, u32[]{:S(2)}, u32[]{:S(2)}) collective-permute-start(f32[1,32,1024]{2,1,0:T(8,128)S(1)} %bitcast.4), channel_id=1, source_target_pairs={{0,2},{2,0},{4,6},{6,4},{1,3},{3,1},{5,7},{7,5},{8,10},{10,8},{12,... | collective-permute-start | bytes 393224 | tf_op jit(solution)/shard_map/ppermute | solution.py:239
  8.1 7.1 %collective-permute-done.2 = f32[32,1024]{1,0:T(8,128)S(1)} collective-permute-done((f32[32,1024]{1,0:T(8,128)S(1)}, f32[32,1024]{1,0:T(8,128)S(1)}, u32[]{:S(2)}, u32[]{:S(2)}) %collective-permute-start.2) | collective-permute-done | bytes 131104 | tf_op jit(solution)/shard_map/ppermute | solution.py:259
  15.1 0.0 collective-permute-start.3
  15.1 1.3 %collective-permute-done = f32[1,32,1024]{2,1,0:T(8,128)S(1)} collective-permute-done((f32[1,32,1024]{2,1,0:T(8,128)S(1)}, f32[1,32,1024]{2,1,0:T(8,128)S(1)}, u32[]{:S(2)}, u32[]{:S(2)}) %collective-permute-start) | collective-permute-done | bytes 131104 | tf_op jit(solution)/shard_map/ppermute | solution.py:239
  16.4 1.9 %collective-permute-start.1 = (f32[2,8,1024]{2,1,0:T(8,128)S(1)}, f32[2,8,1024]{2,1,0:T(8,128)S(1)}, u32[]{:S(2)}, u32[]{:S(2)}) collective-permute-start(f32[2,8,1024]{2,1,0:T(8,128)S(1)} %pad_maximum_fusion.2.own_low), channel_id=1, source_target_pairs={{0,4},{2,6},{4,0},{6,2},{1,5},{3,7},{5,1},{7,3},{8,12},{10,14},{12... | collective-permute-start | bytes 196616 | tf_op jit(solution)/shard_map/ppermute | solution.py:239
  18.3 0.0 collective-permute-done.3
  18.4 0.1 collective-permute-start.4
  18.5 2.1 %collective-permute-start.6 = (f32[2,24,1024]{2,1,0:T(8,128)S(1)}, f32[2,24,1024]{2,1,0:T(8,128)S(1)}, u32[]{:S(2)}, u32[]{:S(2)}) collective-permute-start(f32[2,24,1024]{2,1,0:T(8,128)S(1)} %pad_maximum_fusion.mirror_low), channel_id=1, source_target_pairs={{0,16},{8,24},{16,0},{24,8},{1,17},{9,25},{17,1},{25,9},{2,18},{10... | collective-permute-start | bytes 589832 | tf_op jit(solution)/shard_map/ppermute | solution.py:239
  20.5 1.2 %collective-permute-done.1.own_high = f32[2,8,1024]{2,1,0:T(8,128)S(1)} collective-permute-done((f32[2,8,1024]{2,1,0:T(8,128)S(1)}, f32[2,8,1024]{2,1,0:T(8,128)S(1)}, u32[]{:S(2)}, u32[]{:S(2)}) %collective-permute-start.1) | collective-permute-done | bytes 65568 | tf_op jit(solution)/shard_map/ppermute | solution.py:239
  21.8 1.6 %collective-permute-done.4.mirror_high = f32[2,8,1024]{2,1,0:T(8,128)S(1)} collective-permute-done((f32[2,8,1024]{2,1,0:T(8,128)S(1)}, f32[2,8,1024]{2,1,0:T(8,128)S(1)}, u32[]{:S(2)}, u32[]{:S(2)}) %collective-permute-start.4) | collective-permute-done | bytes 65568 | tf_op jit(solution)/shard_map/ppermute | solution.py:239
  23.3 1.2 %collective-permute-start.5 = (f32[2,24,1024]{2,1,0:T(8,128)S(1)}, f32[2,24,1024]{2,1,0:T(8,128)S(1)}, u32[]{:S(2)}, u32[]{:S(2)}) collective-permute-start(f32[2,24,1024]{2,1,0:T(8,128)S(1)} %fusion.own_low), channel_id=1, source_target_pairs={{0,4},{2,6},{4,0},{6,2},{1,5},{3,7},{5,1},{7,3},{8,12},{10,14},{12... | collective-permute-start | bytes 589832 | tf_op jit(solution)/shard_map/ppermute | solution.py:239
  24.5 7.6 %cross.2.refs_0_ = bf16[16,2,1024,1024]{3,2,1,0:T(8,128)(2,1)} custom-call(s32[1]{0:T(128)} %bitcast.turn_ref, f32[2,8,1024]{2,1,0:T(8,128)S(1)} %pad_maximum_fusion.2.own_low, f32[2,8,1024]{2,1,0:T(8,128)S(1)} %collective-permute-done.1.own_high, f32[2,8,1024]{2,1,0:T(8,128)S(1)} %pad_maximum_fusion.1.mirror_low, ...), custom_call_target="tpu_custom_call" | custom-call | flops 4294967296 | bytes 16777216 | tf_op jit(solution)/shard_map/cross/pallas_call | solution.py:211
  32.1 0.0 collective-permute-done.6.mirror_high
  32.1 1.7 %collective-permute-done.5.own_high = f32[2,24,1024]{2,1,0:T(8,128)S(1)} collective-permute-done((f32[2,24,1024]{2,1,0:T(8,128)S(1)}, f32[2,24,1024]{2,1,0:T(8,128)S(1)}, u32[]{:S(2)}, u32[]{:S(2)}) %collective-permute-start.5) | collective-permute-done | bytes 196640 | tf_op jit(solution)/shard_map/ppermute | solution.py:239
  33.8 19.9 %cross.3 = bf16[16,2,1024,1024]{3,2,1,0:T(8,128)(2,1)} custom-call(s32[1]{0:T(128)} %bitcast.turn_ref, f32[2,24,1024]{2,1,0:T(8,128)S(1)} %fusion.own_low, f32[2,24,1024]{2,1,0:T(8,128)S(1)} %collective-permute-done.5.own_high, f32[2,24,1024]{2,1,0:T(8,128)S(1)} %pad_maximum_fusion.mirror_low, ...), custom_call_target="tpu_custom_call", output_to_operand_aliasing={{}: (5, {})} | custom-call | flops 12884901888 | bytes 50331648 | tf_op jit(solution)/shard_map/cross/pallas_call | solution.py:211
  (4 shorter events, 0.0 us)
Async XLA Ops:
  4.1 11.0 %collective-permute-start.2 = (f32[32,1024]{1,0:T(8,128)S(1)}, f32[32,1024]{1,0:T(8,128)S(1)}, u32[]{:S(2)}, u32[]{:S(2)}) collective-permute-start(f32[32,1024]{1,0:T(8,128)S(1)} %whiten.1), channel_id=1, source_target_pairs={{0,16},{2,24},{4,0},{6,8},{8,10},{10,2},{12,26},{14,18},{16,12},{1... | collective-permute-start | bytes 393224 | tf_op jit(solution)/shard_map/ppermute | solution.py:259
  7.1 9.2 %collective-permute-start = (f32[1,32,1024]{2,1,0:T(8,128)S(1)}, f32[1,32,1024]{2,1,0:T(8,128)S(1)}, u32[]{:S(2)}, u32[]{:S(2)}) collective-permute-start(f32[1,32,1024]{2,1,0:T(8,128)S(1)} %bitcast.4), channel_id=1, source_target_pairs={{0,2},{2,0},{4,6},{6,4},{1,3},{3,1},{5,7},{7,5},{8,10},{10,8},{12,... | collective-permute-start | bytes 393224 | tf_op jit(solution)/shard_map/ppermute | solution.py:239
  15.1 3.2 %collective-permute-start.3 = (f32[1,32,1024]{2,1,0:T(8,128)S(1)}, f32[1,32,1024]{2,1,0:T(8,128)S(1)}, u32[]{:S(2)}, u32[]{:S(2)}) collective-permute-start(f32[1,32,1024]{2,1,0:T(8,128)S(1)} %bitcast.7), channel_id=1, source_target_pairs={{0,8},{8,0},{16,24},{24,16},{1,9},{9,1},{17,25},{25,17},{2,10},{10... | collective-permute-start | bytes 393224 | tf_op jit(solution)/shard_map/ppermute | solution.py:239
  16.4 5.4 %collective-permute-start.1 = (f32[2,8,1024]{2,1,0:T(8,128)S(1)}, f32[2,8,1024]{2,1,0:T(8,128)S(1)}, u32[]{:S(2)}, u32[]{:S(2)}) collective-permute-start(f32[2,8,1024]{2,1,0:T(8,128)S(1)} %pad_maximum_fusion.2.own_low), channel_id=1, source_target_pairs={{0,4},{2,6},{4,0},{6,2},{1,5},{3,7},{5,1},{7,3},{8,12},{10,14},{12... | collective-permute-start | bytes 196616 | tf_op jit(solution)/shard_map/ppermute | solution.py:239
  18.4 5.0 %collective-permute-start.4 = (f32[2,8,1024]{2,1,0:T(8,128)S(1)}, f32[2,8,1024]{2,1,0:T(8,128)S(1)}, u32[]{:S(2)}, u32[]{:S(2)}) collective-permute-start(f32[2,8,1024]{2,1,0:T(8,128)S(1)} %pad_maximum_fusion.1.mirror_low), channel_id=1, source_target_pairs={{0,16},{8,24},{16,0},{24,8},{1,17},{9,25},{17,1},{25,9},{2,18},{10... | collective-permute-start | bytes 196616 | tf_op jit(solution)/shard_map/ppermute | solution.py:239
  18.5 13.7 %collective-permute-start.6 = (f32[2,24,1024]{2,1,0:T(8,128)S(1)}, f32[2,24,1024]{2,1,0:T(8,128)S(1)}, u32[]{:S(2)}, u32[]{:S(2)}) collective-permute-start(f32[2,24,1024]{2,1,0:T(8,128)S(1)} %pad_maximum_fusion.mirror_low), channel_id=1, source_target_pairs={{0,16},{8,24},{16,0},{24,8},{1,17},{9,25},{17,1},{25,9},{2,18},{10... | collective-permute-start | bytes 589832 | tf_op jit(solution)/shard_map/ppermute | solution.py:239
  23.3 10.5 %collective-permute-start.5 = (f32[2,24,1024]{2,1,0:T(8,128)S(1)}, f32[2,24,1024]{2,1,0:T(8,128)S(1)}, u32[]{:S(2)}, u32[]{:S(2)}) collective-permute-start(f32[2,24,1024]{2,1,0:T(8,128)S(1)} %fusion.own_low), channel_id=1, source_target_pairs={{0,4},{2,6},{4,0},{6,2},{1,5},{3,7},{5,1},{7,3},{8,12},{10,14},{12... | collective-permute-start | bytes 589832 | tf_op jit(solution)/shard_map/ppermute | solution.py:239

commit v13 on v11

--- a/solution.py
+++ b/solution.py
@@ -240,10 +240,10 @@
 
 
 def double(held, axis):
-    distance = 1
-    while distance < lax.axis_size(axis) // 2:
+    distance = lax.axis_size(axis) // 2
+    while distance > 1:
         held = jnp.concatenate([held, exchange(held, axis, distance)])
-        distance *= 2
+        distance //= 2
     return held
 
 
@@ -253,7 +253,9 @@
     bins = NB // lax.axis_size("bin")
     sizes = (GROUP, bins - GROUP)
     across = [n // 4 if (c ^ c >> 1) & 1 else n // 2 for c in range(n)]
-    turn = (row ^ col ^ jnp.where((col ^ col >> 1) & 1 == 1, n // 4, n // 2)).reshape(1)
+    away = row ^ col ^ jnp.where((col ^ col >> 1) & 1 == 1, n // 4, n // 2)
+    bits = n.bit_length() - 1
+    turn = sum((away >> i & 1) << (bits - 1 - i) for i in range(bits)).reshape(1)
     swap = [(r * n + w, (w ^ across[r]) * n + r) for r in range(n) for w in range(n)]
     parts = []
     for block in whiten(records, offsets, live_flags, sizes):
@@ -261,7 +263,7 @@
         pairs = []
         for x, axis in ((block, "col"), (other, "row")):
             near = double(x[None], axis)
-            pairs.append((near, exchange(near, axis, n // 2)))
+            pairs.append((near, exchange(near, axis, 1)))
         parts.append(pairs)
     out, first = None, 0
     for size, (own, mirror) in zip(sizes, parts):

time: 48.6 us -> 51.9 us (1.068)
  waiting for transfers between devices: 4.65 us -> 9.86 us
  starting transfers between devices: 12.1 us -> 10.2 us
    ppermute x8, waiting for transfers between devices: 2.75 us -> 5.79 us  [exchange(): return lax.ppermute(block, axis, [(i, i ^ distance) for i in range(n)])]
    ppermute x2, waiting for transfers between devices: 1.89 us -> 4.08 us  [per_device(): other = lax.ppermute(block, ('row', 'col'), swap)]
    ppermute x8, starting transfers between devices: 6.9 us -> 5.61 us  [exchange(): return lax.ppermute(block, axis, [(i, i ^ distance) for i in range(n)])]
    ppermute x2, starting transfers between devices: 5.22 us -> 4.55 us  [per_device(): other = lax.ppermute(block, ('row', 'col'), swap)]
  transfers between devices with their start and end apart: 10 -> 10, of which waited for: 4 -> 4; matrix products, arithmetic and copies ran while one was open for 0% -> 0% of each run, Pallas kernels for 16% -> 15%
where the time goes in v13:
time: 51.9 us; the launch traced here: 51.8 us
  Pallas kernels  31 us (60%)
  starting transfers between devices  10.2 us (20%)
  waiting for transfers between devices  9.86 us (19%)
  between operations  0.73 us (1%)
    pallas_call x2, Pallas kernels, cross(): pl.pallas_call(functools.partial(cross_kernel, size, first), in_specs=[pl...  27.5 us
    ppermute x8, waiting for transfers between devices, exchange(): return lax.ppermute(block, axis, [(i, i ^ distance) for i in range(n)])  5.79 us
    ppermute x8, starting transfers between devices, exchange(): return lax.ppermute(block, axis, [(i, i ^ distance) for i in range(n)])  5.61 us
    ppermute x2, starting transfers between devices, per_device(): other = lax.ppermute(block, ('row', 'col'), swap)  4.55 us
    ppermute x2, waiting for transfers between devices, per_device(): other = lax.ppermute(block, ('row', 'col'), swap)  4.08 us
    pallas_call x1, Pallas kernels, whiten(): pl.pallas_call(functools.partial(whiten_kernel, sizes), in_specs=[pl.Bloc...  3.46 us
  transfers between devices with their start and end apart: 10, of which 4 were waited for; matrix products, arithmetic and copies ran while one was open for 0% of the time, Pallas kernels for 15%

profile of v13, /device:TPU:0, one launch (start us, length us, event | category | flops | bytes accessed | tf_op | source)
XLA Modules:
  0.0 51.8 jit_solution(6782872354501560993)
XLA Ops:
  0.7 3.5 %whiten.1 = (f32[8,1024]{1,0:T(8,128)S(1)}, f32[24,1024]{1,0:T(8,128)S(1)}) custom-call(s32[1]{0:T(128)S(6)} %copy.7.offset_ref, f32[1832,64]{1,0:T(8,128)} %constant.17.clone.table_hbm, bf16[1024,1664]{1,0:T(8,128)(2,1)} %records_hbm.1, s32[1,1024]{1,0:T(1,128)} %bitcast.14), custom_call_target="tpu_custom_call" | custom-call | flops 218103808 | bytes 3407872 | tf_op jit(solution)/shard_map/whiten/pallas_call | solution.py:69
  4.1 3.0 %collective-permute-start.7 = (f32[8,1024]{1,0:T(8,128)S(1)}, f32[8,1024]{1,0:T(8,128)S(1)}, u32[]{:S(2)}, u32[]{:S(2)}) collective-permute-start(f32[8,1024]{1,0:T(8,128)S(1)} %get-tuple-element.8), channel_id=1, source_target_pairs={{0,16},{2,24},{4,0},{6,8},{8,10},{10,2},{12,26},{14,18},{16,12},{1... | collective-permute-start | bytes 98312 | tf_op jit(solution)/shard_map/ppermute | solution.py:262
  7.2 1.1 %collective-permute-start.5 = (f32[1,8,1024]{2,1,0:T(8,128)S(1)}, f32[1,8,1024]{2,1,0:T(8,128)S(1)}, u32[]{:S(2)}, u32[]{:S(2)}) collective-permute-start(f32[1,8,1024]{2,1,0:T(8,128)S(1)} %bitcast.8), channel_id=1, source_target_pairs={{0,4},{2,6},{4,0},{6,2},{1,5},{3,7},{5,1},{7,3},{8,12},{10,14},{12... | collective-permute-start | bytes 98312 | tf_op jit(solution)/shard_map/ppermute | solution.py:239
  8.3 1.5 %collective-permute-start.2 = (f32[24,1024]{1,0:T(8,128)S(1)}, f32[24,1024]{1,0:T(8,128)S(1)}, u32[]{:S(2)}, u32[]{:S(2)}) collective-permute-start(f32[24,1024]{1,0:T(8,128)S(1)} %get-tuple-element.7), channel_id=1, source_target_pairs={{0,16},{2,24},{4,0},{6,8},{8,10},{10,2},{12,26},{14,18},{16,12},{1... | collective-permute-start | bytes 294920 | tf_op jit(solution)/shard_map/ppermute | solution.py:262
  9.8 1.4 %collective-permute-start = (f32[1,24,1024]{2,1,0:T(8,128)S(1)}, f32[1,24,1024]{2,1,0:T(8,128)S(1)}, u32[]{:S(2)}, u32[]{:S(2)}) collective-permute-start(f32[1,24,1024]{2,1,0:T(8,128)S(1)} %bitcast.6), channel_id=1, source_target_pairs={{0,4},{2,6},{4,0},{6,2},{1,5},{3,7},{5,1},{7,3},{8,12},{10,14},{12... | collective-permute-start | bytes 294920 | tf_op jit(solution)/shard_map/ppermute | solution.py:239
  11.2 0.0 collective-permute-done.7
  11.2 2.3 %collective-permute-start.8 = (f32[1,8,1024]{2,1,0:T(8,128)S(1)}, f32[1,8,1024]{2,1,0:T(8,128)S(1)}, u32[]{:S(2)}, u32[]{:S(2)}) collective-permute-start(f32[1,8,1024]{2,1,0:T(8,128)S(1)} %bitcast.12), channel_id=1, source_target_pairs={{0,16},{8,24},{16,0},{24,8},{1,17},{9,25},{17,1},{25,9},{2,18},{10... | collective-permute-start | bytes 98312 | tf_op jit(solution)/shard_map/ppermute | solution.py:239
  13.5 0.0 collective-permute-done.5
  13.5 0.6 %collective-permute-start.6 = (f32[2,8,1024]{2,1,0:T(8,128)S(1)}, f32[2,8,1024]{2,1,0:T(8,128)S(1)}, u32[]{:S(2)}, u32[]{:S(2)}) collective-permute-start(f32[2,8,1024]{2,1,0:T(8,128)S(1)} %pad_maximum_fusion.2.own_low), channel_id=1, source_target_pairs={{0,2},{2,0},{4,6},{6,4},{1,3},{3,1},{5,7},{7,5},{8,10},{10,8},{12,... | collective-permute-start | bytes 196616 | tf_op jit(solution)/shard_map/ppermute | solution.py:239
  14.2 1.3 %collective-permute-done.8 = f32[1,8,1024]{2,1,0:T(8,128)S(1)} collective-permute-done((f32[1,8,1024]{2,1,0:T(8,128)S(1)}, f32[1,8,1024]{2,1,0:T(8,128)S(1)}, u32[]{:S(2)}, u32[]{:S(2)}) %collective-permute-start.8) | collective-permute-done | bytes 32800 | tf_op jit(solution)/shard_map/ppermute | solution.py:239
  15.4 0.0 collective-permute-start.9
  15.4 4.1 %collective-permute-done.2 = f32[24,1024]{1,0:T(8,128)S(1)} collective-permute-done((f32[24,1024]{1,0:T(8,128)S(1)}, f32[24,1024]{1,0:T(8,128)S(1)}, u32[]{:S(2)}, u32[]{:S(2)}) %collective-permute-start.2) | collective-permute-done | bytes 98336 | tf_op jit(solution)/shard_map/ppermute | solution.py:262
  19.5 0.0 collective-permute-start.3
  19.5 1.8 %collective-permute-done = f32[1,24,1024]{2,1,0:T(8,128)S(1)} collective-permute-done((f32[1,24,1024]{2,1,0:T(8,128)S(1)}, f32[1,24,1024]{2,1,0:T(8,128)S(1)}, u32[]{:S(2)}, u32[]{:S(2)}) %collective-permute-start) | collective-permute-done | bytes 98336 | tf_op jit(solution)/shard_map/ppermute | solution.py:239
  21.3 0.1 collective-permute-start.1
  21.4 2.7 %collective-permute-done.3 = f32[1,24,1024]{2,1,0:T(8,128)S(1)} collective-permute-done((f32[1,24,1024]{2,1,0:T(8,128)S(1)}, f32[1,24,1024]{2,1,0:T(8,128)S(1)}, u32[]{:S(2)}, u32[]{:S(2)}) %collective-permute-start.3) | collective-permute-done | bytes 98336 | tf_op jit(solution)/shard_map/ppermute | solution.py:239
  24.1 0.1 collective-permute-start.4
  24.2 0.0 collective-permute-done.6.own_high
  24.2 0.0 collective-permute-done.9.mirror_high
  24.2 7.6 %cross.2.refs_0_ = bf16[16,2,1024,1024]{3,2,1,0:T(8,128)(2,1)} custom-call(s32[1]{0:T(128)} %bitcast.turn_ref, f32[2,8,1024]{2,1,0:T(8,128)S(1)} %pad_maximum_fusion.2.own_low, f32[2,8,1024]{2,1,0:T(8,128)S(1)} %collective-permute-done.6.own_high, f32[2,8,1024]{2,1,0:T(8,128)S(1)} %pad_maximum_fusion.3.mirror_low, ...), custom_call_target="tpu_custom_call" | custom-call | flops 4294967296 | bytes 16777216 | tf_op jit(solution)/shard_map/cross/pallas_call | solution.py:211
  31.9 0.0 collective-permute-done.1.own_high
  31.9 0.0 collective-permute-done.4.mirror_high
  31.9 19.9 %cross.3 = bf16[16,2,1024,1024]{3,2,1,0:T(8,128)(2,1)} custom-call(s32[1]{0:T(128)} %bitcast.turn_ref, f32[2,24,1024]{2,1,0:T(8,128)S(1)} %pad_maximum_fusion.own_low, f32[2,24,1024]{2,1,0:T(8,128)S(1)} %collective-permute-done.1.own_high, f32[2,24,1024]{2,1,0:T(8,128)S(1)} %pad_maximum_fusion.1.mirror_low, ...), custom_call_target="tpu_custom_call", output_to_operand_aliasing={{}: (5, {})} | custom-call | flops 12884901888 | bytes 50331648 | tf_op jit(solution)/shard_map/cross/pallas_call | solution.py:211
  (4 shorter events, 0.0 us)
Async XLA Ops:
  4.1 7.1 %collective-permute-start.7 = (f32[8,1024]{1,0:T(8,128)S(1)}, f32[8,1024]{1,0:T(8,128)S(1)}, u32[]{:S(2)}, u32[]{:S(2)}) collective-permute-start(f32[8,1024]{1,0:T(8,128)S(1)} %get-tuple-element.8), channel_id=1, source_target_pairs={{0,16},{2,24},{4,0},{6,8},{8,10},{10,2},{12,26},{14,18},{16,12},{1... | collective-permute-start | bytes 98312 | tf_op jit(solution)/shard_map/ppermute | solution.py:262
  7.2 6.4 %collective-permute-start.5 = (f32[1,8,1024]{2,1,0:T(8,128)S(1)}, f32[1,8,1024]{2,1,0:T(8,128)S(1)}, u32[]{:S(2)}, u32[]{:S(2)}) collective-permute-start(f32[1,8,1024]{2,1,0:T(8,128)S(1)} %bitcast.8), channel_id=1, source_target_pairs={{0,4},{2,6},{4,0},{6,2},{1,5},{3,7},{5,1},{7,3},{8,12},{10,14},{12... | collective-permute-start | bytes 98312 | tf_op jit(solution)/shard_map/ppermute | solution.py:239
  8.3 11.2 %collective-permute-start.2 = (f32[24,1024]{1,0:T(8,128)S(1)}, f32[24,1024]{1,0:T(8,128)S(1)}, u32[]{:S(2)}, u32[]{:S(2)}) collective-permute-start(f32[24,1024]{1,0:T(8,128)S(1)} %get-tuple-element.7), channel_id=1, source_target_pairs={{0,16},{2,24},{4,0},{6,8},{8,10},{10,2},{12,26},{14,18},{16,12},{1... | collective-permute-start | bytes 294920 | tf_op jit(solution)/shard_map/ppermute | solution.py:262
  9.8 11.5 %collective-permute-start = (f32[1,24,1024]{2,1,0:T(8,128)S(1)}, f32[1,24,1024]{2,1,0:T(8,128)S(1)}, u32[]{:S(2)}, u32[]{:S(2)}) collective-permute-start(f32[1,24,1024]{2,1,0:T(8,128)S(1)} %bitcast.6), channel_id=1, source_target_pairs={{0,4},{2,6},{4,0},{6,2},{1,5},{3,7},{5,1},{7,3},{8,12},{10,14},{12... | collective-permute-start | bytes 294920 | tf_op jit(solution)/shard_map/ppermute | solution.py:239
  11.2 4.2 %collective-permute-start.8 = (f32[1,8,1024]{2,1,0:T(8,128)S(1)}, f32[1,8,1024]{2,1,0:T(8,128)S(1)}, u32[]{:S(2)}, u32[]{:S(2)}) collective-permute-start(f32[1,8,1024]{2,1,0:T(8,128)S(1)} %bitcast.12), channel_id=1, source_target_pairs={{0,16},{8,24},{16,0},{24,8},{1,17},{9,25},{17,1},{25,9},{2,18},{10... | collective-permute-start | bytes 98312 | tf_op jit(solution)/shard_map/ppermute | solution.py:239
  13.5 10.7 %collective-permute-start.6 = (f32[2,8,1024]{2,1,0:T(8,128)S(1)}, f32[2,8,1024]{2,1,0:T(8,128)S(1)}, u32[]{:S(2)}, u32[]{:S(2)}) collective-permute-start(f32[2,8,1024]{2,1,0:T(8,128)S(1)} %pad_maximum_fusion.2.own_low), channel_id=1, source_target_pairs={{0,2},{2,0},{4,6},{6,4},{1,3},{3,1},{5,7},{7,5},{8,10},{10,8},{12,... | collective-permute-start | bytes 196616 | tf_op jit(solution)/shard_map/ppermute | solution.py:239
  15.4 8.8 %collective-permute-start.9 = (f32[2,8,1024]{2,1,0:T(8,128)S(1)}, f32[2,8,1024]{2,1,0:T(8,128)S(1)}, u32[]{:S(2)}, u32[]{:S(2)}) collective-permute-start(f32[2,8,1024]{2,1,0:T(8,128)S(1)} %pad_maximum_fusion.3.mirror_low), channel_id=1, source_target_pairs={{0,8},{8,0},{16,24},{24,16},{1,9},{9,1},{17,25},{25,17},{2,10},{10... | collective-permute-start | bytes 196616 | tf_op jit(solution)/shard_map/ppermute | solution.py:239
  19.5 4.6 %collective-permute-start.3 = (f32[1,24,1024]{2,1,0:T(8,128)S(1)}, f32[1,24,1024]{2,1,0:T(8,128)S(1)}, u32[]{:S(2)}, u32[]{:S(2)}) collective-permute-start(f32[1,24,1024]{2,1,0:T(8,128)S(1)} %bitcast.10), channel_id=1, source_target_pairs={{0,16},{8,24},{16,0},{24,8},{1,17},{9,25},{17,1},{25,9},{2,18},{10... | collective-permute-start | bytes 294920 | tf_op jit(solution)/shard_map/ppermute | solution.py:239
  21.3 10.5 %collective-permute-start.1 = (f32[2,24,1024]{2,1,0:T(8,128)S(1)}, f32[2,24,1024]{2,1,0:T(8,128)S(1)}, u32[]{:S(2)}, u32[]{:S(2)}) collective-permute-start(f32[2,24,1024]{2,1,0:T(8,128)S(1)} %pad_maximum_fusion.own_low), channel_id=1, source_target_pairs={{0,2},{2,0},{4,6},{6,4},{1,3},{3,1},{5,7},{7,5},{8,10},{10,8},{12,... | collective-permute-start | bytes 589832 | tf_op jit(solution)/shard_map/ppermute | solution.py:239
  24.1 7.7 %collective-permute-start.4 = (f32[2,24,1024]{2,1,0:T(8,128)S(1)}, f32[2,24,1024]{2,1,0:T(8,128)S(1)}, u32[]{:S(2)}, u32[]{:S(2)}) collective-permute-start(f32[2,24,1024]{2,1,0:T(8,128)S(1)} %pad_maximum_fusion.1.mirror_low), channel_id=1, source_target_pairs={{0,8},{8,0},{16,24},{24,16},{1,9},{9,1},{17,25},{25,17},{2,10},{10... | collective-permute-start | bytes 589832 | tf_op jit(solution)/shard_map/ppermute | solution.py:239

commit v14 on v11

--- a/solution.py
+++ b/solution.py
@@ -95,7 +95,7 @@
     return high, values - high
 
 
-def cross_kernel(size, first, turn_ref, own_low, own_high, mirror_low, mirror_high, *refs):
+def cross_kernel(size, first, orders, turn_ref, own_low, own_high, mirror_low, mirror_high, *refs):
     out_hbm, held, left, right, picked, done, sems = refs[-7:]
     half = own_low.shape[0]
     windows = 2 * half
@@ -107,10 +107,10 @@
     tile = min(256, height)
     pieces = [(q, t) for q in range(2) for t in range(height // tile)]
 
-    def gather(low, high, turn, at):
-        for w in range(windows):
+    def gather(low, high, order, turn, at):
+        for w, distance in enumerate(order):
             part = (low if w < half else high)[w % half, pl.ds(at, rows), :]
-            held[pl.ds(pl.multiple_of((w ^ turn) * rows, 8), rows), :] = part
+            held[pl.ds(pl.multiple_of((distance ^ turn) * rows, 8), rows), :] = part
         return held[...]
 
     def copy(at_step, slot, q, t):
@@ -125,10 +125,10 @@
     right[:, 3 * terms :] = jnp.zeros((2, depth - 3 * terms, channels), jnp.bfloat16)
 
     def prepare(at):
-        high, low = split(gather(own_low, own_high, 0, at) * (1.0 / windows))
+        high, low = split(gather(own_low, own_high, orders[0], 0, at) * (1.0 / windows))
         blank = [jnp.zeros((width - 3 * terms, channels), jnp.float32)] if width > 3 * terms else []
         left[...] = jnp.concatenate([high, high, low, *blank], axis=0).T.astype(jnp.bfloat16)
-        values = gather(mirror_low, mirror_high, turn_ref[0], at)
+        values = gather(mirror_low, mirror_high, orders[1], turn_ref[0], at)
         part = lax.broadcasted_iota(jnp.int32, values.shape, 0) % 2
         turned = jnp.where(part == 0, -pltpu.roll(values, terms - 1, 0), pltpu.roll(values, 1, 0))
         for q, block in enumerate((values, turned)):
@@ -201,6 +201,7 @@
 
 
 def cross(turn, own, mirror, so_far, first, size, bins):
+    (own, own_order), (mirror, mirror_order) = own, mirror
     windows = 2 * own[0].shape[0]
     channels = own[0].shape[2]
     terms = windows * 2 * GROUP
@@ -209,7 +210,7 @@
     height = channels // 2
     previous = [] if so_far is None else [so_far]
     return pl.pallas_call(
-        functools.partial(cross_kernel, size, first),
+        functools.partial(cross_kernel, size, first, (own_order, mirror_order)),
         in_specs=[pl.BlockSpec(memory_space=pltpu.SMEM)]
         + [pl.BlockSpec(memory_space=pltpu.VMEM)] * 4
         + [pl.BlockSpec(memory_space=pl.ANY)] * len(previous),
@@ -239,12 +240,13 @@
     return lax.ppermute(block, axis, [(i, i ^ distance) for i in range(n)])
 
 
-def double(held, axis):
-    distance = 1
-    while distance < lax.axis_size(axis) // 2:
+def gathered(block, axis, distances):
+    held, order = block[None], [0]
+    for distance in distances[:-1]:
         held = jnp.concatenate([held, exchange(held, axis, distance)])
-        distance *= 2
-    return held
+        order += [d ^ distance for d in order]
+    order += [d ^ distances[-1] for d in order]
+    return (held, exchange(held, axis, distances[-1])), tuple(order)
 
 
 def per_device(records, offsets, live_flags):
@@ -255,14 +257,12 @@
     across = [n // 4 if (c ^ c >> 1) & 1 else n // 2 for c in range(n)]
     turn = (row ^ col ^ jnp.where((col ^ col >> 1) & 1 == 1, n // 4, n // 2)).reshape(1)
     swap = [(r * n + w, (w ^ across[r]) * n + r) for r in range(n) for w in range(n)]
+    rising = [1 << i for i in range(n.bit_length() - 1)]
     parts = []
     for block in whiten(records, offsets, live_flags, sizes):
         other = lax.ppermute(block, ("row", "col"), swap)
-        pairs = []
-        for x, axis in ((block, "col"), (other, "row")):
-            near = double(x[None], axis)
-            pairs.append((near, exchange(near, axis, n // 2)))
-        parts.append(pairs)
+        own = gathered(block, "col", rising if parts else rising[::-1])
+        parts.append((own, gathered(other, "row", rising)))
     out, first = None, 0
     for size, (own, mirror) in zip(sizes, parts):
         out = cross(turn, own, mirror, out, first, size, bins)

time: 48.6 us -> 49.1 us (1.010)
  waiting for transfers between devices: 4.65 us -> 5.9 us
  starting transfers between devices: 12.1 us -> 11.3 us
    ppermute x8, waiting for transfers between devices: 2.75 us -> 4.46 us  [exchange(): return lax.ppermute(block, axis, [(i, i ^ distance) for i in range(n)])]
    ppermute x2, starting transfers between devices: 5.22 us -> 4.55 us  [per_device(): other = lax.ppermute(block, ('row', 'col'), swap)]
  transfers between devices with their start and end apart: 10 -> 10, of which waited for: 4 -> 5; matrix products, arithmetic and copies ran while one was open for 0% -> 0% of each run, Pallas kernels for 16% -> 16%
where the time goes in v14:
time: 49.1 us; the launch traced here: 48.9 us
  Pallas kernels  31 us (63%)
  starting transfers between devices  11.3 us (23%)
  waiting for transfers between devices  5.9 us (12%)
  between operations  0.69 us (1%)
    pallas_call x2, Pallas kernels, cross(): pl.pallas_call(functools.partial(cross_kernel, size, first, (own_order, m...  27.5 us
    ppermute x8, starting transfers between devices, exchange(): return lax.ppermute(block, axis, [(i, i ^ distance) for i in range(n)])  6.77 us
    ppermute x2, starting transfers between devices, per_device(): other = lax.ppermute(block, ('row', 'col'), swap)  4.55 us
    ppermute x8, waiting for transfers between devices, exchange(): return lax.ppermute(block, axis, [(i, i ^ distance) for i in range(n)])  4.46 us
    pallas_call x1, Pallas kernels, whiten(): pl.pallas_call(functools.partial(whiten_kernel, sizes), in_specs=[pl.Bloc...  3.46 us
    ppermute x2, waiting for transfers between devices, per_device(): other = lax.ppermute(block, ('row', 'col'), swap)  1.44 us
  transfers between devices with their start and end apart: 10, of which 5 were waited for; matrix products, arithmetic and copies ran while one was open for 0% of the time, Pallas kernels for 16%

profile of v14, /device:TPU:0, one launch (start us, length us, event | category | flops | bytes accessed | tf_op | source)
XLA Modules:
  0.0 48.9 jit_solution(14860235399485781766)
XLA Ops:
  0.7 3.5 %whiten.1 = (f32[8,1024]{1,0:T(8,128)S(1)}, f32[24,1024]{1,0:T(8,128)S(1)}) custom-call(s32[1]{0:T(128)S(6)} %copy.7.offset_ref, f32[1832,64]{1,0:T(8,128)} %constant.15.clone.table_hbm, bf16[1024,1664]{1,0:T(8,128)(2,1)} %records_hbm.1, s32[1,1024]{1,0:T(1,128)} %bitcast.14), custom_call_target="tpu_custom_call" | custom-call | flops 218103808 | bytes 3407872 | tf_op jit(solution)/shard_map/whiten/pallas_call | solution.py:69
  4.1 3.0 %collective-permute-start.7 = (f32[8,1024]{1,0:T(8,128)S(1)}, f32[8,1024]{1,0:T(8,128)S(1)}, u32[]{:S(2)}, u32[]{:S(2)}) collective-permute-start(f32[8,1024]{1,0:T(8,128)S(1)} %get-tuple-element.8), channel_id=1, source_target_pairs={{0,16},{2,24},{4,0},{6,8},{8,10},{10,2},{12,26},{14,18},{16,12},{1... | collective-permute-start | bytes 98312 | tf_op jit(solution)/shard_map/ppermute | solution.py:263
  7.2 1.1 %collective-permute-start.5 = (f32[1,8,1024]{2,1,0:T(8,128)S(1)}, f32[1,8,1024]{2,1,0:T(8,128)S(1)}, u32[]{:S(2)}, u32[]{:S(2)}) collective-permute-start(f32[1,8,1024]{2,1,0:T(8,128)S(1)} %bitcast.8), channel_id=1, source_target_pairs={{0,4},{2,6},{4,0},{6,2},{1,5},{3,7},{5,1},{7,3},{8,12},{10,14},{12... | collective-permute-start | bytes 98312 | tf_op jit(solution)/shard_map/ppermute | solution.py:240
  8.3 1.5 %collective-permute-start.2 = (f32[24,1024]{1,0:T(8,128)S(1)}, f32[24,1024]{1,0:T(8,128)S(1)}, u32[]{:S(2)}, u32[]{:S(2)}) collective-permute-start(f32[24,1024]{1,0:T(8,128)S(1)} %get-tuple-element.7), channel_id=1, source_target_pairs={{0,16},{2,24},{4,0},{6,8},{8,10},{10,2},{12,26},{14,18},{16,12},{1... | collective-permute-start | bytes 294920 | tf_op jit(solution)/shard_map/ppermute | solution.py:263
  9.8 2.3 %collective-permute-start = (f32[1,24,1024]{2,1,0:T(8,128)S(1)}, f32[1,24,1024]{2,1,0:T(8,128)S(1)}, u32[]{:S(2)}, u32[]{:S(2)}) collective-permute-start(f32[1,24,1024]{2,1,0:T(8,128)S(1)} %bitcast.6), channel_id=1, source_target_pairs={{0,2},{2,0},{4,6},{6,4},{1,3},{3,1},{5,7},{7,5},{8,10},{10,8},{12,... | collective-permute-start | bytes 294920 | tf_op jit(solution)/shard_map/ppermute | solution.py:240
  12.2 0.0 collective-permute-done.7
  12.2 0.0 collective-permute-start.8
  12.2 1.0 %collective-permute-done.5 = f32[1,8,1024]{2,1,0:T(8,128)S(1)} collective-permute-done((f32[1,8,1024]{2,1,0:T(8,128)S(1)}, f32[1,8,1024]{2,1,0:T(8,128)S(1)}, u32[]{:S(2)}, u32[]{:S(2)}) %collective-permute-start.5) | collective-permute-done | bytes 32800 | tf_op jit(solution)/shard_map/ppermute | solution.py:240
  13.2 0.0 collective-permute-start.6
  13.2 0.2 collective-permute-done.8
  13.4 2.3 %collective-permute-start.9 = (f32[2,8,1024]{2,1,0:T(8,128)S(1)}, f32[2,8,1024]{2,1,0:T(8,128)S(1)}, u32[]{:S(2)}, u32[]{:S(2)}) collective-permute-start(f32[2,8,1024]{2,1,0:T(8,128)S(1)} %pad_maximum_fusion.3.mirror_low), channel_id=1, source_target_pairs={{0,16},{8,24},{16,0},{24,8},{1,17},{9,25},{17,1},{25,9},{2,18},{10... | collective-permute-start | bytes 196616 | tf_op jit(solution)/shard_map/ppermute | solution.py:240
  15.7 1.4 %collective-permute-done.2 = f32[24,1024]{1,0:T(8,128)S(1)} collective-permute-done((f32[24,1024]{1,0:T(8,128)S(1)}, f32[24,1024]{1,0:T(8,128)S(1)}, u32[]{:S(2)}, u32[]{:S(2)}) %collective-permute-start.2) | collective-permute-done | bytes 98336 | tf_op jit(solution)/shard_map/ppermute | solution.py:263
  17.1 0.0 collective-permute-start.3
  17.1 2.1 %collective-permute-done = f32[1,24,1024]{2,1,0:T(8,128)S(1)} collective-permute-done((f32[1,24,1024]{2,1,0:T(8,128)S(1)}, f32[1,24,1024]{2,1,0:T(8,128)S(1)}, u32[]{:S(2)}, u32[]{:S(2)}) %collective-permute-start) | collective-permute-done | bytes 98336 | tf_op jit(solution)/shard_map/ppermute | solution.py:240
  19.2 0.6 %collective-permute-start.1 = (f32[2,24,1024]{2,1,0:T(8,128)S(1)}, f32[2,24,1024]{2,1,0:T(8,128)S(1)}, u32[]{:S(2)}, u32[]{:S(2)}) collective-permute-start(f32[2,24,1024]{2,1,0:T(8,128)S(1)} %pad_maximum_fusion.own_low), channel_id=1, source_target_pairs={{0,4},{2,6},{4,0},{6,2},{1,5},{3,7},{5,1},{7,3},{8,12},{10,14},{12... | collective-permute-start | bytes 589832 | tf_op jit(solution)/shard_map/ppermute | solution.py:240
  19.8 0.0 collective-permute-done.3
  19.8 0.4 collective-permute-start.4
  20.2 0.0 collective-permute-done.6.own_high
  20.2 0.0 collective-permute-done.9.mirror_high
  20.2 7.6 %cross.2.refs_0_ = bf16[16,2,1024,1024]{3,2,1,0:T(8,128)(2,1)} custom-call(s32[1]{0:T(128)} %bitcast.turn_ref, f32[2,8,1024]{2,1,0:T(8,128)S(1)} %pad_maximum_fusion.2.own_low, f32[2,8,1024]{2,1,0:T(8,128)S(1)} %collective-permute-done.6.own_high, f32[2,8,1024]{2,1,0:T(8,128)S(1)} %pad_maximum_fusion.3.mirror_low, ...), custom_call_target="tpu_custom_call" | custom-call | flops 4294967296 | bytes 16777216 | tf_op jit(solution)/shard_map/cross/pallas_call | solution.py:212
  27.8 1.2 %collective-permute-done.1.own_high = f32[2,24,1024]{2,1,0:T(8,128)S(1)} collective-permute-done((f32[2,24,1024]{2,1,0:T(8,128)S(1)}, f32[2,24,1024]{2,1,0:T(8,128)S(1)}, u32[]{:S(2)}, u32[]{:S(2)}) %collective-permute-start.1) | collective-permute-done | bytes 196640 | tf_op jit(solution)/shard_map/ppermute | solution.py:240
  29.0 0.0 collective-permute-done.4.mirror_high
  29.0 19.9 %cross.3 = bf16[16,2,1024,1024]{3,2,1,0:T(8,128)(2,1)} custom-call(s32[1]{0:T(128)} %bitcast.turn_ref, f32[2,24,1024]{2,1,0:T(8,128)S(1)} %pad_maximum_fusion.own_low, f32[2,24,1024]{2,1,0:T(8,128)S(1)} %collective-permute-done.1.own_high, f32[2,24,1024]{2,1,0:T(8,128)S(1)} %pad_maximum_fusion.1.mirror_low, ...), custom_call_target="tpu_custom_call", output_to_operand_aliasing={{}: (5, {})} | custom-call | flops 12884901888 | bytes 50331648 | tf_op jit(solution)/shard_map/cross/pallas_call | solution.py:212
  (4 shorter events, 0.0 us)
Async XLA Ops:
  4.1 8.0 %collective-permute-start.7 = (f32[8,1024]{1,0:T(8,128)S(1)}, f32[8,1024]{1,0:T(8,128)S(1)}, u32[]{:S(2)}, u32[]{:S(2)}) collective-permute-start(f32[8,1024]{1,0:T(8,128)S(1)} %get-tuple-element.8), channel_id=1, source_target_pairs={{0,16},{2,24},{4,0},{6,8},{8,10},{10,2},{12,26},{14,18},{16,12},{1... | collective-permute-start | bytes 98312 | tf_op jit(solution)/shard_map/ppermute | solution.py:263
  7.2 6.0 %collective-permute-start.5 = (f32[1,8,1024]{2,1,0:T(8,128)S(1)}, f32[1,8,1024]{2,1,0:T(8,128)S(1)}, u32[]{:S(2)}, u32[]{:S(2)}) collective-permute-start(f32[1,8,1024]{2,1,0:T(8,128)S(1)} %bitcast.8), channel_id=1, source_target_pairs={{0,4},{2,6},{4,0},{6,2},{1,5},{3,7},{5,1},{7,3},{8,12},{10,14},{12... | collective-permute-start | bytes 98312 | tf_op jit(solution)/shard_map/ppermute | solution.py:240
  8.3 8.8 %collective-permute-start.2 = (f32[24,1024]{1,0:T(8,128)S(1)}, f32[24,1024]{1,0:T(8,128)S(1)}, u32[]{:S(2)}, u32[]{:S(2)}) collective-permute-start(f32[24,1024]{1,0:T(8,128)S(1)} %get-tuple-element.7), channel_id=1, source_target_pairs={{0,16},{2,24},{4,0},{6,8},{8,10},{10,2},{12,26},{14,18},{16,12},{1... | collective-permute-start | bytes 294920 | tf_op jit(solution)/shard_map/ppermute | solution.py:263
  9.8 9.4 %collective-permute-start = (f32[1,24,1024]{2,1,0:T(8,128)S(1)}, f32[1,24,1024]{2,1,0:T(8,128)S(1)}, u32[]{:S(2)}, u32[]{:S(2)}) collective-permute-start(f32[1,24,1024]{2,1,0:T(8,128)S(1)} %bitcast.6), channel_id=1, source_target_pairs={{0,2},{2,0},{4,6},{6,4},{1,3},{3,1},{5,7},{7,5},{8,10},{10,8},{12,... | collective-permute-start | bytes 294920 | tf_op jit(solution)/shard_map/ppermute | solution.py:240
  12.2 1.2 %collective-permute-start.8 = (f32[1,8,1024]{2,1,0:T(8,128)S(1)}, f32[1,8,1024]{2,1,0:T(8,128)S(1)}, u32[]{:S(2)}, u32[]{:S(2)}) collective-permute-start(f32[1,8,1024]{2,1,0:T(8,128)S(1)} %bitcast.12), channel_id=1, source_target_pairs={{0,8},{8,0},{16,24},{24,16},{1,9},{9,1},{17,25},{25,17},{2,10},{10... | collective-permute-start | bytes 98312 | tf_op jit(solution)/shard_map/ppermute | solution.py:240
  13.2 7.0 %collective-permute-start.6 = (f32[2,8,1024]{2,1,0:T(8,128)S(1)}, f32[2,8,1024]{2,1,0:T(8,128)S(1)}, u32[]{:S(2)}, u32[]{:S(2)}) collective-permute-start(f32[2,8,1024]{2,1,0:T(8,128)S(1)} %pad_maximum_fusion.2.own_low), channel_id=1, source_target_pairs={{0,2},{2,0},{4,6},{6,4},{1,3},{3,1},{5,7},{7,5},{8,10},{10,8},{12,... | collective-permute-start | bytes 196616 | tf_op jit(solution)/shard_map/ppermute | solution.py:240
  13.4 6.8 %collective-permute-start.9 = (f32[2,8,1024]{2,1,0:T(8,128)S(1)}, f32[2,8,1024]{2,1,0:T(8,128)S(1)}, u32[]{:S(2)}, u32[]{:S(2)}) collective-permute-start(f32[2,8,1024]{2,1,0:T(8,128)S(1)} %pad_maximum_fusion.3.mirror_low), channel_id=1, source_target_pairs={{0,16},{8,24},{16,0},{24,8},{1,17},{9,25},{17,1},{25,9},{2,18},{10... | collective-permute-start | bytes 196616 | tf_op jit(solution)/shard_map/ppermute | solution.py:240
  17.1 2.7 %collective-permute-start.3 = (f32[1,24,1024]{2,1,0:T(8,128)S(1)}, f32[1,24,1024]{2,1,0:T(8,128)S(1)}, u32[]{:S(2)}, u32[]{:S(2)}) collective-permute-start(f32[1,24,1024]{2,1,0:T(8,128)S(1)} %bitcast.10), channel_id=1, source_target_pairs={{0,8},{8,0},{16,24},{24,16},{1,9},{9,1},{17,25},{25,17},{2,10},{10... | collective-permute-start | bytes 294920 | tf_op jit(solution)/shard_map/ppermute | solution.py:240
  19.2 9.8 %collective-permute-start.1 = (f32[2,24,1024]{2,1,0:T(8,128)S(1)}, f32[2,24,1024]{2,1,0:T(8,128)S(1)}, u32[]{:S(2)}, u32[]{:S(2)}) collective-permute-start(f32[2,24,1024]{2,1,0:T(8,128)S(1)} %pad_maximum_fusion.own_low), channel_id=1, source_target_pairs={{0,4},{2,6},{4,0},{6,2},{1,5},{3,7},{5,1},{7,3},{8,12},{10,14},{12... | collective-permute-start | bytes 589832 | tf_op jit(solution)/shard_map/ppermute | solution.py:240
  19.8 9.2 %collective-permute-start.4 = (f32[2,24,1024]{2,1,0:T(8,128)S(1)}, f32[2,24,1024]{2,1,0:T(8,128)S(1)}, u32[]{:S(2)}, u32[]{:S(2)}) collective-permute-start(f32[2,24,1024]{2,1,0:T(8,128)S(1)} %pad_maximum_fusion.1.mirror_low), channel_id=1, source_target_pairs={{0,16},{8,24},{16,0},{24,8},{1,17},{9,25},{17,1},{25,9},{2,18},{10... | collective-permute-start | bytes 589832 | tf_op jit(solution)/shard_map/ppermute | solution.py:240

commit v15 on v11

--- a/solution.py
+++ b/solution.py
@@ -28,6 +28,7 @@
     parts = np.stack([np.cos(angle) * taper, -np.sin(angle) * taper], axis=1)
     table = np.zeros((PAD + samples, 2 * NB), np.float32)
     table[PAD : PAD + L] = parts.reshape(2 * NB, L).T
+    table = np.concatenate([table[: PAD + samples // 2], table[samples // 2 :]], axis=1)
     return jnp.asarray(table.astype(jnp.bfloat16).astype(np.float32))
 
 
@@ -44,7 +45,9 @@
     for copy in copies:
         copy.start()
     copies[0].wait()
-    shifted[...] = table[pl.ds(PAD - offset_ref[0], samples), :].astype(jnp.bfloat16)
+    turned = table[pl.ds(PAD - offset_ref[0], samples // 2), :].astype(jnp.bfloat16)
+    shifted[: samples // 2] = turned[:, : 2 * NB]
+    shifted[samples // 2 :] = turned[:, 2 * NB :]
     copies[1].wait()
     start = pl.multiple_of(lax.axis_index("bin") * (2 * sum(sizes)), 8)
     for i in range(pieces):
@@ -71,7 +74,7 @@
         in_specs=[pl.BlockSpec(memory_space=pltpu.SMEM)] + [pl.BlockSpec(memory_space=pl.ANY)] * 3,
         out_specs=[pl.BlockSpec(memory_space=pltpu.VMEM)] * len(rows),
         scratch_shapes=[
-            pltpu.VMEM((PAD + samples, 2 * NB), jnp.float32),
+            pltpu.VMEM((PAD + samples // 2, 4 * NB), jnp.float32),
             pltpu.VMEM((pieces, block, samples), jnp.bfloat16),
             pltpu.VMEM((1, channels), jnp.int32),
             pltpu.VMEM((samples, 2 * NB), jnp.bfloat16),
@@ -135,7 +138,7 @@
             high, low = split(block)
             right[q, : 3 * terms] = jnp.concatenate([high, low, high], axis=0).astype(jnp.bfloat16)
 
-    def body(step, carry):
+    def body(step, carry, cuts=1):
         slot, inner = step % BUFFERS, step // 2 % GROUP
         top = pl.multiple_of(step % 2 * height, height)
 
@@ -152,7 +155,7 @@
         mask = jnp.where(lane % rows // 2 == inner, 1.0, 0.0).astype(jnp.bfloat16)
         picked[:, :width] = left[pl.ds(top, height), :] * mask
 
-        def multiply(*accs):
+        def multiply(cut, *accs):
             def stage(number):
                 n, k = stages[number]
                 for q in range(2):
@@ -165,12 +168,12 @@
                         accs[q * SLOTS + place]
                     ).astype(jnp.bfloat16)
 
-            chunks, deep = height // CHUNK, depth // 256
+            chunks, deep = height // CHUNK // cuts, depth // 256
             stages = [(n, k) for n in range(channels // 256) for k in range(deep)]
             waiting = []
             stage(0)
             for number, (n, k) in enumerate(stages):
-                for j in range(chunks):
+                for j in range(cut * chunks, (cut + 1) * chunks):
                     place = (n * chunks + j) % SLOTS
                     if k == 0 and len(waiting) > SLOTS // 2:
                         retire(*waiting.pop(0))
@@ -178,23 +181,26 @@
                         pltpu.matmul_acc_lhs(
                             accs[q * SLOTS + place],
                             picked[j * CHUNK : (j + 1) * CHUNK, k * 256 : (k + 1) * 256],
-                            load_staged_rhs=number % 2 if j == 0 else None,
+                            load_staged_rhs=number % 2 if j == cut * chunks else None,
                         )
-                    if j == 0 and number + 1 < len(stages):
+                    if j == cut * chunks and number + 1 < len(stages):
                         stage(number + 1)
                     if k == deep - 1:
                         waiting.append((n, j, place))
             for entry in waiting:
                 retire(*entry)
 
-        pl.run_scoped(
-            multiply, *(pltpu.ACC(q)((CHUNK, 256), jnp.float32) for q in range(2) for _ in range(SLOTS))
-        )
-        for q, t in pieces:
-            copy(step, slot, q, t).start(priority=t % 2)
+        accs = [pltpu.ACC(q)((CHUNK, 256), jnp.float32) for q in range(2) for _ in range(SLOTS)]
+        share = len(pieces) // 2 // cuts
+        for cut in range(cuts):
+            pl.run_scoped(functools.partial(multiply, cut), *accs)
+            for q, t in pieces:
+                if t // share == cut:
+                    copy(step, slot, q, t).start(priority=t % 2)
         return carry
 
-    lax.fori_loop(0, 2 * size, body, 0)
+    body(jnp.int32(0), 0, height // tile)
+    lax.fori_loop(1, 2 * size, body, 0)
     for last in range(2 * size - BUFFERS, 2 * size):
         for q, t in pieces:
             copy(last, last % BUFFERS, q, t).wait()

time: 48.6 us -> 48.3 us (level)
  Pallas kernels: 31 us -> 30.5 us
  transfers between devices with their start and end apart: 10 -> 10, of which waited for: 4 -> 4; matrix products, arithmetic and copies ran while one was open for 0% -> 0% of each run, Pallas kernels for 16% -> 15%
where the time goes in v15:
time: 48.3 us; the launch traced here: 48.2 us
  Pallas kernels  30.5 us (63%)
  starting transfers between devices  12.1 us (25%)
  waiting for transfers between devices  4.8 us (10%)
  between operations  0.7 us (1%)
    pallas_call x2, Pallas kernels, cross(): pl.pallas_call(functools.partial(cross_kernel, size, first), in_specs=[pl...  27.2 us
    ppermute x8, starting transfers between devices, exchange(): return lax.ppermute(block, axis, [(i, i ^ distance) for i in range(n)])  6.89 us
    ppermute x2, starting transfers between devices, per_device(): other = lax.ppermute(block, ('row', 'col'), swap)  5.22 us
    pallas_call x1, Pallas kernels, whiten(): pl.pallas_call(functools.partial(whiten_kernel, sizes), in_specs=[pl.Bloc...  3.34 us
    ppermute x8, waiting for transfers between devices, exchange(): return lax.ppermute(block, axis, [(i, i ^ distance) for i in range(n)])  2.9 us
    ppermute x2, waiting for transfers between devices, per_device(): other = lax.ppermute(block, ('row', 'col'), swap)  1.9 us
  transfers between devices with their start and end apart: 10, of which 4 were waited for; matrix products, arithmetic and copies ran while one was open for 0% of the time, Pallas kernels for 15%

profile of v15, /device:TPU:0, one launch (start us, length us, event | category | flops | bytes accessed | tf_op | source)
XLA Modules:
  0.0 48.2 jit_solution(16888592678239189792)
XLA Ops:
  0.7 3.3 %whiten.1 = (f32[8,1024]{1,0:T(8,128)S(1)}, f32[24,1024]{1,0:T(8,128)S(1)}) custom-call(s32[1]{0:T(128)S(6)} %copy.7.offset_ref, f32[1000,128]{1,0:T(8,128)} %constant.15.clone.table_hbm, bf16[1024,1664]{1,0:T(8,128)(2,1)} %records_hbm.1, s32[1,1024]{1,0:T(1,128)} %bitcast.14), custom_call_target="tpu_custom_call" | custom-call | flops 218103808 | bytes 3407872 | tf_op jit(solution)/shard_map/whiten/pallas_call | solution.py:72
  4.0 3.0 %collective-permute-start.7 = (f32[8,1024]{1,0:T(8,128)S(1)}, f32[8,1024]{1,0:T(8,128)S(1)}, u32[]{:S(2)}, u32[]{:S(2)}) collective-permute-start(f32[8,1024]{1,0:T(8,128)S(1)} %get-tuple-element.8), channel_id=1, source_target_pairs={{0,16},{2,24},{4,0},{6,8},{8,10},{10,2},{12,26},{14,18},{16,12},{1... | collective-permute-start | bytes 98312 | tf_op jit(solution)/shard_map/ppermute | solution.py:266
  7.0 0.9 %collective-permute-start.5 = (f32[1,8,1024]{2,1,0:T(8,128)S(1)}, f32[1,8,1024]{2,1,0:T(8,128)S(1)}, u32[]{:S(2)}, u32[]{:S(2)}) collective-permute-start(f32[1,8,1024]{2,1,0:T(8,128)S(1)} %bitcast.8), channel_id=1, source_target_pairs={{0,2},{2,0},{4,6},{6,4},{1,3},{3,1},{5,7},{7,5},{8,10},{10,8},{12,... | collective-permute-start | bytes 98312 | tf_op jit(solution)/shard_map/ppermute | solution.py:245
  7.9 2.2 %collective-permute-start.2 = (f32[24,1024]{1,0:T(8,128)S(1)}, f32[24,1024]{1,0:T(8,128)S(1)}, u32[]{:S(2)}, u32[]{:S(2)}) collective-permute-start(f32[24,1024]{1,0:T(8,128)S(1)} %get-tuple-element.7), channel_id=1, source_target_pairs={{0,16},{2,24},{4,0},{6,8},{8,10},{10,2},{12,26},{14,18},{16,12},{1... | collective-permute-start | bytes 294920 | tf_op jit(solution)/shard_map/ppermute | solution.py:266
  10.1 1.7 %collective-permute-start = (f32[1,24,1024]{2,1,0:T(8,128)S(1)}, f32[1,24,1024]{2,1,0:T(8,128)S(1)}, u32[]{:S(2)}, u32[]{:S(2)}) collective-permute-start(f32[1,24,1024]{2,1,0:T(8,128)S(1)} %bitcast.6), channel_id=1, source_target_pairs={{0,2},{2,0},{4,6},{6,4},{1,3},{3,1},{5,7},{7,5},{8,10},{10,8},{12,... | collective-permute-start | bytes 294920 | tf_op jit(solution)/shard_map/ppermute | solution.py:245
  11.8 0.0 collective-permute-done.7
  11.8 0.0 collective-permute-start.8
  11.8 0.0 collective-permute-done.5
  11.8 1.8 %collective-permute-start.6 = (f32[2,8,1024]{2,1,0:T(8,128)S(1)}, f32[2,8,1024]{2,1,0:T(8,128)S(1)}, u32[]{:S(2)}, u32[]{:S(2)}) collective-permute-start(f32[2,8,1024]{2,1,0:T(8,128)S(1)} %pad_maximum_fusion.2.own_low), channel_id=1, source_target_pairs={{0,4},{2,6},{4,0},{6,2},{1,5},{3,7},{5,1},{7,3},{8,12},{10,14},{12... | collective-permute-start | bytes 196616 | tf_op jit(solution)/shard_map/ppermute | solution.py:245
  13.6 0.0 collective-permute-done.8
  13.6 0.4 collective-permute-start.9
  14.0 1.9 %collective-permute-done.2 = f32[24,1024]{1,0:T(8,128)S(1)} collective-permute-done((f32[24,1024]{1,0:T(8,128)S(1)}, f32[24,1024]{1,0:T(8,128)S(1)}, u32[]{:S(2)}, u32[]{:S(2)}) %collective-permute-start.2) | collective-permute-done | bytes 98336 | tf_op jit(solution)/shard_map/ppermute | solution.py:266
  15.9 0.0 collective-permute-start.3
  15.9 0.6 %collective-permute-done = f32[1,24,1024]{2,1,0:T(8,128)S(1)} collective-permute-done((f32[1,24,1024]{2,1,0:T(8,128)S(1)}, f32[1,24,1024]{2,1,0:T(8,128)S(1)}, u32[]{:S(2)}, u32[]{:S(2)}) %collective-permute-start) | collective-permute-done | bytes 98336 | tf_op jit(solution)/shard_map/ppermute | solution.py:245
  16.6 2.0 %collective-permute-start.1 = (f32[2,24,1024]{2,1,0:T(8,128)S(1)}, f32[2,24,1024]{2,1,0:T(8,128)S(1)}, u32[]{:S(2)}, u32[]{:S(2)}) collective-permute-start(f32[2,24,1024]{2,1,0:T(8,128)S(1)} %pad_maximum_fusion.own_low), channel_id=1, source_target_pairs={{0,4},{2,6},{4,0},{6,2},{1,5},{3,7},{5,1},{7,3},{8,12},{10,14},{12... | collective-permute-start | bytes 589832 | tf_op jit(solution)/shard_map/ppermute | solution.py:245
  18.6 0.0 collective-permute-done.3
  18.6 0.1 collective-permute-start.4
  18.7 0.4 collective-permute-done.6.own_high
  19.2 0.0 collective-permute-done.9.mirror_high
  19.2 7.5 %cross.2.refs_0_ = bf16[16,2,1024,1024]{3,2,1,0:T(8,128)(2,1)} custom-call(s32[1]{0:T(128)} %bitcast.turn_ref, f32[2,8,1024]{2,1,0:T(8,128)S(1)} %pad_maximum_fusion.2.own_low, f32[2,8,1024]{2,1,0:T(8,128)S(1)} %collective-permute-done.6.own_high, f32[2,8,1024]{2,1,0:T(8,128)S(1)} %pad_maximum_fusion.3.mirror_low, ...), custom_call_target="tpu_custom_call" | custom-call | flops 4294967296 | bytes 16777216 | tf_op jit(solution)/shard_map/cross/pallas_call | solution.py:217
  26.6 1.8 %collective-permute-done.1.own_high = f32[2,24,1024]{2,1,0:T(8,128)S(1)} collective-permute-done((f32[2,24,1024]{2,1,0:T(8,128)S(1)}, f32[2,24,1024]{2,1,0:T(8,128)S(1)}, u32[]{:S(2)}, u32[]{:S(2)}) %collective-permute-start.1) | collective-permute-done | bytes 196640 | tf_op jit(solution)/shard_map/ppermute | solution.py:245
  28.5 0.0 collective-permute-done.4.mirror_high
  28.5 19.7 %cross.3 = bf16[16,2,1024,1024]{3,2,1,0:T(8,128)(2,1)} custom-call(s32[1]{0:T(128)} %bitcast.turn_ref, f32[2,24,1024]{2,1,0:T(8,128)S(1)} %pad_maximum_fusion.own_low, f32[2,24,1024]{2,1,0:T(8,128)S(1)} %collective-permute-done.1.own_high, f32[2,24,1024]{2,1,0:T(8,128)S(1)} %pad_maximum_fusion.1.mirror_low, ...), custom_call_target="tpu_custom_call", output_to_operand_aliasing={{}: (5, {})} | custom-call | flops 12884901888 | bytes 50331648 | tf_op jit(solution)/shard_map/cross/pallas_call | solution.py:217
  (4 shorter events, 0.0 us)
Async XLA Ops:
  4.0 7.8 %collective-permute-start.7 = (f32[8,1024]{1,0:T(8,128)S(1)}, f32[8,1024]{1,0:T(8,128)S(1)}, u32[]{:S(2)}, u32[]{:S(2)}) collective-permute-start(f32[8,1024]{1,0:T(8,128)S(1)} %get-tuple-element.8), channel_id=1, source_target_pairs={{0,16},{2,24},{4,0},{6,8},{8,10},{10,2},{12,26},{14,18},{16,12},{1... | collective-permute-start | bytes 98312 | tf_op jit(solution)/shard_map/ppermute | solution.py:266
  7.0 4.8 %collective-permute-start.5 = (f32[1,8,1024]{2,1,0:T(8,128)S(1)}, f32[1,8,1024]{2,1,0:T(8,128)S(1)}, u32[]{:S(2)}, u32[]{:S(2)}) collective-permute-start(f32[1,8,1024]{2,1,0:T(8,128)S(1)} %bitcast.8), channel_id=1, source_target_pairs={{0,2},{2,0},{4,6},{6,4},{1,3},{3,1},{5,7},{7,5},{8,10},{10,8},{12,... | collective-permute-start | bytes 98312 | tf_op jit(solution)/shard_map/ppermute | solution.py:245
  7.9 8.0 %collective-permute-start.2 = (f32[24,1024]{1,0:T(8,128)S(1)}, f32[24,1024]{1,0:T(8,128)S(1)}, u32[]{:S(2)}, u32[]{:S(2)}) collective-permute-start(f32[24,1024]{1,0:T(8,128)S(1)} %get-tuple-element.7), channel_id=1, source_target_pairs={{0,16},{2,24},{4,0},{6,8},{8,10},{10,2},{12,26},{14,18},{16,12},{1... | collective-permute-start | bytes 294920 | tf_op jit(solution)/shard_map/ppermute | solution.py:266
  10.1 6.5 %collective-permute-start = (f32[1,24,1024]{2,1,0:T(8,128)S(1)}, f32[1,24,1024]{2,1,0:T(8,128)S(1)}, u32[]{:S(2)}, u32[]{:S(2)}) collective-permute-start(f32[1,24,1024]{2,1,0:T(8,128)S(1)} %bitcast.6), channel_id=1, source_target_pairs={{0,2},{2,0},{4,6},{6,4},{1,3},{3,1},{5,7},{7,5},{8,10},{10,8},{12,... | collective-permute-start | bytes 294920 | tf_op jit(solution)/shard_map/ppermute | solution.py:245
  11.8 1.8 %collective-permute-start.8 = (f32[1,8,1024]{2,1,0:T(8,128)S(1)}, f32[1,8,1024]{2,1,0:T(8,128)S(1)}, u32[]{:S(2)}, u32[]{:S(2)}) collective-permute-start(f32[1,8,1024]{2,1,0:T(8,128)S(1)} %bitcast.12), channel_id=1, source_target_pairs={{0,8},{8,0},{16,24},{24,16},{1,9},{9,1},{17,25},{25,17},{2,10},{10... | collective-permute-start | bytes 98312 | tf_op jit(solution)/shard_map/ppermute | solution.py:245
  11.8 7.3 %collective-permute-start.6 = (f32[2,8,1024]{2,1,0:T(8,128)S(1)}, f32[2,8,1024]{2,1,0:T(8,128)S(1)}, u32[]{:S(2)}, u32[]{:S(2)}) collective-permute-start(f32[2,8,1024]{2,1,0:T(8,128)S(1)} %pad_maximum_fusion.2.own_low), channel_id=1, source_target_pairs={{0,4},{2,6},{4,0},{6,2},{1,5},{3,7},{5,1},{7,3},{8,12},{10,14},{12... | collective-permute-start | bytes 196616 | tf_op jit(solution)/shard_map/ppermute | solution.py:245
  13.6 5.5 %collective-permute-start.9 = (f32[2,8,1024]{2,1,0:T(8,128)S(1)}, f32[2,8,1024]{2,1,0:T(8,128)S(1)}, u32[]{:S(2)}, u32[]{:S(2)}) collective-permute-start(f32[2,8,1024]{2,1,0:T(8,128)S(1)} %pad_maximum_fusion.3.mirror_low), channel_id=1, source_target_pairs={{0,16},{8,24},{16,0},{24,8},{1,17},{9,25},{17,1},{25,9},{2,18},{10... | collective-permute-start | bytes 196616 | tf_op jit(solution)/shard_map/ppermute | solution.py:245
  15.9 2.7 %collective-permute-start.3 = (f32[1,24,1024]{2,1,0:T(8,128)S(1)}, f32[1,24,1024]{2,1,0:T(8,128)S(1)}, u32[]{:S(2)}, u32[]{:S(2)}) collective-permute-start(f32[1,24,1024]{2,1,0:T(8,128)S(1)} %bitcast.10), channel_id=1, source_target_pairs={{0,8},{8,0},{16,24},{24,16},{1,9},{9,1},{17,25},{25,17},{2,10},{10... | collective-permute-start | bytes 294920 | tf_op jit(solution)/shard_map/ppermute | solution.py:245
  16.6 11.9 %collective-permute-start.1 = (f32[2,24,1024]{2,1,0:T(8,128)S(1)}, f32[2,24,1024]{2,1,0:T(8,128)S(1)}, u32[]{:S(2)}, u32[]{:S(2)}) collective-permute-start(f32[2,24,1024]{2,1,0:T(8,128)S(1)} %pad_maximum_fusion.own_low), channel_id=1, source_target_pairs={{0,4},{2,6},{4,0},{6,2},{1,5},{3,7},{5,1},{7,3},{8,12},{10,14},{12... | collective-permute-start | bytes 589832 | tf_op jit(solution)/shard_map/ppermute | solution.py:245
  18.6 9.8 %collective-permute-start.4 = (f32[2,24,1024]{2,1,0:T(8,128)S(1)}, f32[2,24,1024]{2,1,0:T(8,128)S(1)}, u32[]{:S(2)}, u32[]{:S(2)}) collective-permute-start(f32[2,24,1024]{2,1,0:T(8,128)S(1)} %pad_maximum_fusion.1.mirror_low), channel_id=1, source_target_pairs={{0,16},{8,24},{16,0},{24,8},{1,17},{9,25},{17,1},{25,9},{2,18},{10... | collective-permute-start | bytes 589832 | tf_op jit(solution)/shard_map/ppermute | solution.py:245

commit v16 on v15

--- a/solution.py
+++ b/solution.py
@@ -258,8 +258,8 @@
     n = lax.axis_size("col")
     bins = NB // lax.axis_size("bin")
     sizes = (GROUP, bins - GROUP)
-    across = [n // 4 if (c ^ c >> 1) & 1 else n // 2 for c in range(n)]
-    turn = (row ^ col ^ jnp.where((col ^ col >> 1) & 1 == 1, n // 4, n // 2)).reshape(1)
+    across = [n // 2 if (c ^ c >> 1) & 1 else n // 4 for c in range(n)]
+    turn = (row ^ col ^ jnp.where((col ^ col >> 1) & 1 == 1, n // 2, n // 4)).reshape(1)
     swap = [(r * n + w, (w ^ across[r]) * n + r) for r in range(n) for w in range(n)]
     parts = []
     for block in whiten(records, offsets, live_flags, sizes):

time: 48.3 us -> 48.4 us (level)
  starting transfers between devices: 12.1 us -> 17 us
  waiting for transfers between devices: 4.8 us -> 0.03 us
    ppermute x8, starting transfers between devices: 6.89 us -> 15.5 us  [exchange(): return lax.ppermute(block, axis, [(i, i ^ distance) for i in range(n)])]
    ppermute x2, starting transfers between devices: 5.22 us -> 1.51 us  [per_device(): other = lax.ppermute(block, ('row', 'col'), swap)]
    ppermute x8, waiting for transfers between devices: 2.9 us -> 0.02 us  [exchange(): return lax.ppermute(block, axis, [(i, i ^ distance) for i in range(n)])]
    ppermute x2, waiting for transfers between devices: 1.9 us -> 0.01 us  [per_device(): other = lax.ppermute(block, ('row', 'col'), swap)]
  transfers between devices with their start and end apart: 10 -> 10, of which waited for: 4 -> 0; matrix products, arithmetic and copies ran while one was open for 0% -> 0% of each run, Pallas kernels for 15% -> 15%
where the time goes in v16:
time: 48.4 us; the launch traced here: 48.3 us
  Pallas kernels  30.5 us (63%)
  starting transfers between devices  17 us (35%)
  between operations  0.71 us (1%)
    pallas_call x2, Pallas kernels, cross(): pl.pallas_call(functools.partial(cross_kernel, size, first), in_specs=[pl...  27.2 us
    ppermute x8, starting transfers between devices, exchange(): return lax.ppermute(block, axis, [(i, i ^ distance) for i in range(n)])  15.5 us
    pallas_call x1, Pallas kernels, whiten(): pl.pallas_call(functools.partial(whiten_kernel, sizes), in_specs=[pl.Bloc...  3.34 us
    ppermute x2, starting transfers between devices, per_device(): other = lax.ppermute(block, ('row', 'col'), swap)  1.51 us
  transfers between devices with their start and end apart: 10, of which 0 were waited for; matrix products, arithmetic and copies ran while one was open for 0% of the time, Pallas kernels for 15%

profile of v16, /device:TPU:0, one launch (start us, length us, event | category | flops | bytes accessed | tf_op | source)
XLA Modules:
  0.0 48.3 jit_solution(16589196489808948093)
XLA Ops:
  0.7 3.3 %whiten.1 = (f32[8,1024]{1,0:T(8,128)S(1)}, f32[24,1024]{1,0:T(8,128)S(1)}) custom-call(s32[1]{0:T(128)S(6)} %copy.7.offset_ref, f32[1000,128]{1,0:T(8,128)} %constant.15.clone.table_hbm, bf16[1024,1664]{1,0:T(8,128)(2,1)} %records_hbm.1, s32[1,1024]{1,0:T(1,128)} %bitcast.14), custom_call_target="tpu_custom_call" | custom-call | flops 218103808 | bytes 3407872 | tf_op jit(solution)/shard_map/whiten/pallas_call | solution.py:72
  4.0 0.5 %collective-permute-start.7 = (f32[8,1024]{1,0:T(8,128)S(1)}, f32[8,1024]{1,0:T(8,128)S(1)}, u32[]{:S(2)}, u32[]{:S(2)}) collective-permute-start(f32[8,1024]{1,0:T(8,128)S(1)} %get-tuple-element.8), channel_id=1, source_target_pairs={{0,8},{2,0},{4,24},{6,16},{8,18},{10,26},{12,2},{14,10},{16,20},{1... | collective-permute-start | bytes 98312 | tf_op jit(solution)/shard_map/ppermute | solution.py:266
  4.5 2.6 %collective-permute-start.5 = (f32[1,8,1024]{2,1,0:T(8,128)S(1)}, f32[1,8,1024]{2,1,0:T(8,128)S(1)}, u32[]{:S(2)}, u32[]{:S(2)}) collective-permute-start(f32[1,8,1024]{2,1,0:T(8,128)S(1)} %bitcast.8), channel_id=1, source_target_pairs={{0,2},{2,0},{4,6},{6,4},{1,3},{3,1},{5,7},{7,5},{8,10},{10,8},{12,... | collective-permute-start | bytes 98312 | tf_op jit(solution)/shard_map/ppermute | solution.py:245
  7.2 1.0 %collective-permute-start.2 = (f32[24,1024]{1,0:T(8,128)S(1)}, f32[24,1024]{1,0:T(8,128)S(1)}, u32[]{:S(2)}, u32[]{:S(2)}) collective-permute-start(f32[24,1024]{1,0:T(8,128)S(1)} %get-tuple-element.7), channel_id=1, source_target_pairs={{0,8},{2,0},{4,24},{6,16},{8,18},{10,26},{12,2},{14,10},{16,20},{1... | collective-permute-start | bytes 294920 | tf_op jit(solution)/shard_map/ppermute | solution.py:266
  8.2 1.0 %collective-permute-start = (f32[1,24,1024]{2,1,0:T(8,128)S(1)}, f32[1,24,1024]{2,1,0:T(8,128)S(1)}, u32[]{:S(2)}, u32[]{:S(2)}) collective-permute-start(f32[1,24,1024]{2,1,0:T(8,128)S(1)} %bitcast.6), channel_id=1, source_target_pairs={{0,2},{2,0},{4,6},{6,4},{1,3},{3,1},{5,7},{7,5},{8,10},{10,8},{12,... | collective-permute-start | bytes 294920 | tf_op jit(solution)/shard_map/ppermute | solution.py:245
  9.2 0.0 collective-permute-done.7
  9.2 2.1 %collective-permute-start.8 = (f32[1,8,1024]{2,1,0:T(8,128)S(1)}, f32[1,8,1024]{2,1,0:T(8,128)S(1)}, u32[]{:S(2)}, u32[]{:S(2)}) collective-permute-start(f32[1,8,1024]{2,1,0:T(8,128)S(1)} %bitcast.12), channel_id=1, source_target_pairs={{0,8},{8,0},{16,24},{24,16},{1,9},{9,1},{17,25},{25,17},{2,10},{10... | collective-permute-start | bytes 98312 | tf_op jit(solution)/shard_map/ppermute | solution.py:245
  11.3 0.0 collective-permute-done.5
  11.3 2.2 %collective-permute-start.6 = (f32[2,8,1024]{2,1,0:T(8,128)S(1)}, f32[2,8,1024]{2,1,0:T(8,128)S(1)}, u32[]{:S(2)}, u32[]{:S(2)}) collective-permute-start(f32[2,8,1024]{2,1,0:T(8,128)S(1)} %pad_maximum_fusion.2.own_low), channel_id=1, source_target_pairs={{0,4},{2,6},{4,0},{6,2},{1,5},{3,7},{5,1},{7,3},{8,12},{10,14},{12... | collective-permute-start | bytes 196616 | tf_op jit(solution)/shard_map/ppermute | solution.py:245
  13.5 0.0 collective-permute-done.8
  13.6 1.4 %collective-permute-start.9 = (f32[2,8,1024]{2,1,0:T(8,128)S(1)}, f32[2,8,1024]{2,1,0:T(8,128)S(1)}, u32[]{:S(2)}, u32[]{:S(2)}) collective-permute-start(f32[2,8,1024]{2,1,0:T(8,128)S(1)} %pad_maximum_fusion.3.mirror_low), channel_id=1, source_target_pairs={{0,16},{8,24},{16,0},{24,8},{1,17},{9,25},{17,1},{25,9},{2,18},{10... | collective-permute-start | bytes 196616 | tf_op jit(solution)/shard_map/ppermute | solution.py:245
  15.0 0.0 collective-permute-done.2
  15.0 0.0 collective-permute-start.3
  15.0 0.0 collective-permute-done
  15.0 3.4 %collective-permute-start.1 = (f32[2,24,1024]{2,1,0:T(8,128)S(1)}, f32[2,24,1024]{2,1,0:T(8,128)S(1)}, u32[]{:S(2)}, u32[]{:S(2)}) collective-permute-start(f32[2,24,1024]{2,1,0:T(8,128)S(1)} %pad_maximum_fusion.own_low), channel_id=1, source_target_pairs={{0,4},{2,6},{4,0},{6,2},{1,5},{3,7},{5,1},{7,3},{8,12},{10,14},{12... | collective-permute-start | bytes 589832 | tf_op jit(solution)/shard_map/ppermute | solution.py:245
  18.4 0.0 collective-permute-done.3
  18.4 2.6 %collective-permute-start.4 = (f32[2,24,1024]{2,1,0:T(8,128)S(1)}, f32[2,24,1024]{2,1,0:T(8,128)S(1)}, u32[]{:S(2)}, u32[]{:S(2)}) collective-permute-start(f32[2,24,1024]{2,1,0:T(8,128)S(1)} %pad_maximum_fusion.1.mirror_low), channel_id=1, source_target_pairs={{0,16},{8,24},{16,0},{24,8},{1,17},{9,25},{17,1},{25,9},{2,18},{10... | collective-permute-start | bytes 589832 | tf_op jit(solution)/shard_map/ppermute | solution.py:245
  21.1 0.0 collective-permute-done.6.own_high
  21.1 0.0 collective-permute-done.9.mirror_high
  21.1 7.5 %cross.2.refs_0_ = bf16[16,2,1024,1024]{3,2,1,0:T(8,128)(2,1)} custom-call(s32[1]{0:T(128)} %bitcast.turn_ref, f32[2,8,1024]{2,1,0:T(8,128)S(1)} %pad_maximum_fusion.2.own_low, f32[2,8,1024]{2,1,0:T(8,128)S(1)} %collective-permute-done.6.own_high, f32[2,8,1024]{2,1,0:T(8,128)S(1)} %pad_maximum_fusion.3.mirror_low, ...), custom_call_target="tpu_custom_call" | custom-call | flops 4294967296 | bytes 16777216 | tf_op jit(solution)/shard_map/cross/pallas_call | solution.py:217
  28.5 0.0 collective-permute-done.1.own_high
  28.5 0.0 collective-permute-done.4.mirror_high
  28.6 19.7 %cross.3 = bf16[16,2,1024,1024]{3,2,1,0:T(8,128)(2,1)} custom-call(s32[1]{0:T(128)} %bitcast.turn_ref, f32[2,24,1024]{2,1,0:T(8,128)S(1)} %pad_maximum_fusion.own_low, f32[2,24,1024]{2,1,0:T(8,128)S(1)} %collective-permute-done.1.own_high, f32[2,24,1024]{2,1,0:T(8,128)S(1)} %pad_maximum_fusion.1.mirror_low, ...), custom_call_target="tpu_custom_call", output_to_operand_aliasing={{}: (5, {})} | custom-call | flops 12884901888 | bytes 50331648 | tf_op jit(solution)/shard_map/cross/pallas_call | solution.py:217
  (4 shorter events, 0.0 us)
Async XLA Ops:
  4.0 5.2 %collective-permute-start.7 = (f32[8,1024]{1,0:T(8,128)S(1)}, f32[8,1024]{1,0:T(8,128)S(1)}, u32[]{:S(2)}, u32[]{:S(2)}) collective-permute-start(f32[8,1024]{1,0:T(8,128)S(1)} %get-tuple-element.8), channel_id=1, source_target_pairs={{0,8},{2,0},{4,24},{6,16},{8,18},{10,26},{12,2},{14,10},{16,20},{1... | collective-permute-start | bytes 98312 | tf_op jit(solution)/shard_map/ppermute | solution.py:266
  4.5 6.8 %collective-permute-start.5 = (f32[1,8,1024]{2,1,0:T(8,128)S(1)}, f32[1,8,1024]{2,1,0:T(8,128)S(1)}, u32[]{:S(2)}, u32[]{:S(2)}) collective-permute-start(f32[1,8,1024]{2,1,0:T(8,128)S(1)} %bitcast.8), channel_id=1, source_target_pairs={{0,2},{2,0},{4,6},{6,4},{1,3},{3,1},{5,7},{7,5},{8,10},{10,8},{12,... | collective-permute-start | bytes 98312 | tf_op jit(solution)/shard_map/ppermute | solution.py:245
  7.2 7.8 %collective-permute-start.2 = (f32[24,1024]{1,0:T(8,128)S(1)}, f32[24,1024]{1,0:T(8,128)S(1)}, u32[]{:S(2)}, u32[]{:S(2)}) collective-permute-start(f32[24,1024]{1,0:T(8,128)S(1)} %get-tuple-element.7), channel_id=1, source_target_pairs={{0,8},{2,0},{4,24},{6,16},{8,18},{10,26},{12,2},{14,10},{16,20},{1... | collective-permute-start | bytes 294920 | tf_op jit(solution)/shard_map/ppermute | solution.py:266
  8.2 6.8 %collective-permute-start = (f32[1,24,1024]{2,1,0:T(8,128)S(1)}, f32[1,24,1024]{2,1,0:T(8,128)S(1)}, u32[]{:S(2)}, u32[]{:S(2)}) collective-permute-start(f32[1,24,1024]{2,1,0:T(8,128)S(1)} %bitcast.6), channel_id=1, source_target_pairs={{0,2},{2,0},{4,6},{6,4},{1,3},{3,1},{5,7},{7,5},{8,10},{10,8},{12,... | collective-permute-start | bytes 294920 | tf_op jit(solution)/shard_map/ppermute | solution.py:245
  9.2 4.3 %collective-permute-start.8 = (f32[1,8,1024]{2,1,0:T(8,128)S(1)}, f32[1,8,1024]{2,1,0:T(8,128)S(1)}, u32[]{:S(2)}, u32[]{:S(2)}) collective-permute-start(f32[1,8,1024]{2,1,0:T(8,128)S(1)} %bitcast.12), channel_id=1, source_target_pairs={{0,8},{8,0},{16,24},{24,16},{1,9},{9,1},{17,25},{25,17},{2,10},{10... | collective-permute-start | bytes 98312 | tf_op jit(solution)/shard_map/ppermute | solution.py:245
  11.3 9.7 %collective-permute-start.6 = (f32[2,8,1024]{2,1,0:T(8,128)S(1)}, f32[2,8,1024]{2,1,0:T(8,128)S(1)}, u32[]{:S(2)}, u32[]{:S(2)}) collective-permute-start(f32[2,8,1024]{2,1,0:T(8,128)S(1)} %pad_maximum_fusion.2.own_low), channel_id=1, source_target_pairs={{0,4},{2,6},{4,0},{6,2},{1,5},{3,7},{5,1},{7,3},{8,12},{10,14},{12... | collective-permute-start | bytes 196616 | tf_op jit(solution)/shard_map/ppermute | solution.py:245
  13.6 7.5 %collective-permute-start.9 = (f32[2,8,1024]{2,1,0:T(8,128)S(1)}, f32[2,8,1024]{2,1,0:T(8,128)S(1)}, u32[]{:S(2)}, u32[]{:S(2)}) collective-permute-start(f32[2,8,1024]{2,1,0:T(8,128)S(1)} %pad_maximum_fusion.3.mirror_low), channel_id=1, source_target_pairs={{0,16},{8,24},{16,0},{24,8},{1,17},{9,25},{17,1},{25,9},{2,18},{10... | collective-permute-start | bytes 196616 | tf_op jit(solution)/shard_map/ppermute | solution.py:245
  15.0 3.4 %collective-permute-start.3 = (f32[1,24,1024]{2,1,0:T(8,128)S(1)}, f32[1,24,1024]{2,1,0:T(8,128)S(1)}, u32[]{:S(2)}, u32[]{:S(2)}) collective-permute-start(f32[1,24,1024]{2,1,0:T(8,128)S(1)} %bitcast.10), channel_id=1, source_target_pairs={{0,8},{8,0},{16,24},{24,16},{1,9},{9,1},{17,25},{25,17},{2,10},{10... | collective-permute-start | bytes 294920 | tf_op jit(solution)/shard_map/ppermute | solution.py:245
  15.0 13.5 %collective-permute-start.1 = (f32[2,24,1024]{2,1,0:T(8,128)S(1)}, f32[2,24,1024]{2,1,0:T(8,128)S(1)}, u32[]{:S(2)}, u32[]{:S(2)}) collective-permute-start(f32[2,24,1024]{2,1,0:T(8,128)S(1)} %pad_maximum_fusion.own_low), channel_id=1, source_target_pairs={{0,4},{2,6},{4,0},{6,2},{1,5},{3,7},{5,1},{7,3},{8,12},{10,14},{12... | collective-permute-start | bytes 589832 | tf_op jit(solution)/shard_map/ppermute | solution.py:245
  18.4 10.1 %collective-permute-start.4 = (f32[2,24,1024]{2,1,0:T(8,128)S(1)}, f32[2,24,1024]{2,1,0:T(8,128)S(1)}, u32[]{:S(2)}, u32[]{:S(2)}) collective-permute-start(f32[2,24,1024]{2,1,0:T(8,128)S(1)} %pad_maximum_fusion.1.mirror_low), channel_id=1, source_target_pairs={{0,16},{8,24},{16,0},{24,8},{1,17},{9,25},{17,1},{25,9},{2,18},{10... | collective-permute-start | bytes 589832 | tf_op jit(solution)/shard_map/ppermute | solution.py:245

commit v17 on v15

--- a/solution.py
+++ b/solution.py
@@ -16,7 +16,7 @@
 PAD = 168
 GROUP = 4
 CHUNK = 128
-BUFFERS = 4
+BUFFERS = 3
 SLOTS = 8
 
 
@@ -117,10 +117,10 @@
         return held[...]
 
     def copy(at_step, slot, q, t):
-        target = pl.ds(pl.multiple_of(at_step % 2 * height + t * tile, tile), tile)
+        piece = pl.ds(t * tile, tile)
         return pltpu.make_async_copy(
-            done.at[slot, q, pl.ds(t * tile, tile)],
-            out_hbm.at[first + at_step // 2, q, target],
+            done.at[slot, q, piece],
+            out_hbm.at[first + at_step, q, piece],
             sems.at[slot, q * (height // tile) + t],
         )
 
@@ -139,12 +139,11 @@
             right[q, : 3 * terms] = jnp.concatenate([high, low, high], axis=0).astype(jnp.bfloat16)
 
     def body(step, carry, cuts=1):
-        slot, inner = step % BUFFERS, step // 2 % GROUP
-        top = pl.multiple_of(step % 2 * height, height)
-
-        @pl.when(step % (2 * GROUP) == 0)
+        slot, inner = step % BUFFERS, step % GROUP
+
+        @pl.when(inner == 0)
         def _():
-            prepare(pl.multiple_of(step, rows))
+            prepare(pl.multiple_of(step * 2, rows))
 
         @pl.when(step >= BUFFERS)
         def _():
@@ -153,7 +152,7 @@
 
         lane = lax.broadcasted_iota(jnp.int32, (1, width), 1)
         mask = jnp.where(lane % rows // 2 == inner, 1.0, 0.0).astype(jnp.bfloat16)
-        picked[:, :width] = left[pl.ds(top, height), :] * mask
+        picked[:, :width] = left[...] * mask
 
         def multiply(cut, *accs):
             def stage(number):
@@ -200,8 +199,8 @@
         return carry
 
     body(jnp.int32(0), 0, height // tile)
-    lax.fori_loop(1, 2 * size, body, 0)
-    for last in range(2 * size - BUFFERS, 2 * size):
+    lax.fori_loop(1, size, body, 0)
+    for last in range(size - BUFFERS, size):
         for q, t in pieces:
             copy(last, last % BUFFERS, q, t).wait()
 
@@ -212,7 +211,7 @@
     terms = windows * 2 * GROUP
     width = -(-3 * terms // 128) * 128
     depth = -(-3 * terms // 256) * 256
-    height = channels // 2
+    height = channels
     previous = [] if so_far is None else [so_far]
     return pl.pallas_call(
         functools.partial(cross_kernel, size, first),

time: 48.3 us -> 46.8 us (0.969)
  Pallas kernels: 30.5 us -> 29 us
    pallas_call x2, Pallas kernels: 27.2 us -> 25.6 us  [cross(): pl.pallas_call(functools.partial(cross_kernel, size, first), in_specs=[pl...]
  transfers between devices with their start and end apart: 10 -> 10, of which waited for: 4 -> 4; matrix products, arithmetic and copies ran while one was open for 0% -> 0% of each run, Pallas kernels for 15% -> 16%
where the time goes in v17:
time: 46.8 us; the launch traced here: 46.6 us
  Pallas kernels  29 us (62%)
  starting transfers between devices  12.1 us (26%)
  waiting for transfers between devices  4.79 us (10%)
  between operations  0.7 us (1%)
    pallas_call x2, Pallas kernels, cross(): pl.pallas_call(functools.partial(cross_kernel, size, first), in_specs=[pl...  25.6 us
    ppermute x8, starting transfers between devices, exchange(): return lax.ppermute(block, axis, [(i, i ^ distance) for i in range(n)])  6.89 us
    ppermute x2, starting transfers between devices, per_device(): other = lax.ppermute(block, ('row', 'col'), swap)  5.22 us
    pallas_call x1, Pallas kernels, whiten(): pl.pallas_call(functools.partial(whiten_kernel, sizes), in_specs=[pl.Bloc...  3.34 us
    ppermute x8, waiting for transfers between devices, exchange(): return lax.ppermute(block, axis, [(i, i ^ distance) for i in range(n)])  2.89 us
    ppermute x2, waiting for transfers between devices, per_device(): other = lax.ppermute(block, ('row', 'col'), swap)  1.9 us
  transfers between devices with their start and end apart: 10, of which 4 were waited for; matrix products, arithmetic and copies ran while one was open for 0% of the time, Pallas kernels for 16%

profile of v17, /device:TPU:0, one launch (start us, length us, event | category | flops | bytes accessed | tf_op | source)
XLA Modules:
  0.0 46.6 jit_solution(5262908149549761842)
XLA Ops:
  0.7 3.3 %whiten.1 = (f32[8,1024]{1,0:T(8,128)S(1)}, f32[24,1024]{1,0:T(8,128)S(1)}) custom-call(s32[1]{0:T(128)S(6)} %copy.7.offset_ref, f32[1000,128]{1,0:T(8,128)} %constant.15.clone.table_hbm, bf16[1024,1664]{1,0:T(8,128)(2,1)} %records_hbm.1, s32[1,1024]{1,0:T(1,128)} %bitcast.14), custom_call_target="tpu_custom_call" | custom-call | flops 218103808 | bytes 3407872 | tf_op jit(solution)/shard_map/whiten/pallas_call | solution.py:72
  4.0 3.0 %collective-permute-start.7 = (f32[8,1024]{1,0:T(8,128)S(1)}, f32[8,1024]{1,0:T(8,128)S(1)}, u32[]{:S(2)}, u32[]{:S(2)}) collective-permute-start(f32[8,1024]{1,0:T(8,128)S(1)} %get-tuple-element.8), channel_id=1, source_target_pairs={{0,16},{2,24},{4,0},{6,8},{8,10},{10,2},{12,26},{14,18},{16,12},{1... | collective-permute-start | bytes 98312 | tf_op jit(solution)/shard_map/ppermute | solution.py:265
  7.0 0.9 %collective-permute-start.5 = (f32[1,8,1024]{2,1,0:T(8,128)S(1)}, f32[1,8,1024]{2,1,0:T(8,128)S(1)}, u32[]{:S(2)}, u32[]{:S(2)}) collective-permute-start(f32[1,8,1024]{2,1,0:T(8,128)S(1)} %bitcast.8), channel_id=1, source_target_pairs={{0,2},{2,0},{4,6},{6,4},{1,3},{3,1},{5,7},{7,5},{8,10},{10,8},{12,... | collective-permute-start | bytes 98312 | tf_op jit(solution)/shard_map/ppermute | solution.py:244
  7.9 2.2 %collective-permute-start.2 = (f32[24,1024]{1,0:T(8,128)S(1)}, f32[24,1024]{1,0:T(8,128)S(1)}, u32[]{:S(2)}, u32[]{:S(2)}) collective-permute-start(f32[24,1024]{1,0:T(8,128)S(1)} %get-tuple-element.7), channel_id=1, source_target_pairs={{0,16},{2,24},{4,0},{6,8},{8,10},{10,2},{12,26},{14,18},{16,12},{1... | collective-permute-start | bytes 294920 | tf_op jit(solution)/shard_map/ppermute | solution.py:265
  10.1 1.7 %collective-permute-start = (f32[1,24,1024]{2,1,0:T(8,128)S(1)}, f32[1,24,1024]{2,1,0:T(8,128)S(1)}, u32[]{:S(2)}, u32[]{:S(2)}) collective-permute-start(f32[1,24,1024]{2,1,0:T(8,128)S(1)} %bitcast.6), channel_id=1, source_target_pairs={{0,2},{2,0},{4,6},{6,4},{1,3},{3,1},{5,7},{7,5},{8,10},{10,8},{12,... | collective-permute-start | bytes 294920 | tf_op jit(solution)/shard_map/ppermute | solution.py:244
  11.8 0.0 collective-permute-done.7
  11.8 0.0 collective-permute-start.8
  11.8 0.0 collective-permute-done.5
  11.8 1.8 %collective-permute-start.6 = (f32[2,8,1024]{2,1,0:T(8,128)S(1)}, f32[2,8,1024]{2,1,0:T(8,128)S(1)}, u32[]{:S(2)}, u32[]{:S(2)}) collective-permute-start(f32[2,8,1024]{2,1,0:T(8,128)S(1)} %pad_maximum_fusion.2.own_low), channel_id=1, source_target_pairs={{0,4},{2,6},{4,0},{6,2},{1,5},{3,7},{5,1},{7,3},{8,12},{10,14},{12... | collective-permute-start | bytes 196616 | tf_op jit(solution)/shard_map/ppermute | solution.py:244
  13.6 0.0 collective-permute-done.8
  13.6 0.4 collective-permute-start.9
  14.0 1.9 %collective-permute-done.2 = f32[24,1024]{1,0:T(8,128)S(1)} collective-permute-done((f32[24,1024]{1,0:T(8,128)S(1)}, f32[24,1024]{1,0:T(8,128)S(1)}, u32[]{:S(2)}, u32[]{:S(2)}) %collective-permute-start.2) | collective-permute-done | bytes 98336 | tf_op jit(solution)/shard_map/ppermute | solution.py:265
  15.9 0.0 collective-permute-start.3
  15.9 0.6 %collective-permute-done = f32[1,24,1024]{2,1,0:T(8,128)S(1)} collective-permute-done((f32[1,24,1024]{2,1,0:T(8,128)S(1)}, f32[1,24,1024]{2,1,0:T(8,128)S(1)}, u32[]{:S(2)}, u32[]{:S(2)}) %collective-permute-start) | collective-permute-done | bytes 98336 | tf_op jit(solution)/shard_map/ppermute | solution.py:244
  16.6 2.0 %collective-permute-start.1 = (f32[2,24,1024]{2,1,0:T(8,128)S(1)}, f32[2,24,1024]{2,1,0:T(8,128)S(1)}, u32[]{:S(2)}, u32[]{:S(2)}) collective-permute-start(f32[2,24,1024]{2,1,0:T(8,128)S(1)} %pad_maximum_fusion.own_low), channel_id=1, source_target_pairs={{0,4},{2,6},{4,0},{6,2},{1,5},{3,7},{5,1},{7,3},{8,12},{10,14},{12... | collective-permute-start | bytes 589832 | tf_op jit(solution)/shard_map/ppermute | solution.py:244
  18.6 0.0 collective-permute-done.3
  18.6 0.1 collective-permute-start.4
  18.7 0.4 collective-permute-done.6.own_high
  19.2 0.0 collective-permute-done.9.mirror_high
  19.2 7.5 %cross.2.refs_0_ = bf16[16,2,1024,1024]{3,2,1,0:T(8,128)(2,1)} custom-call(s32[1]{0:T(128)} %bitcast.turn_ref, f32[2,8,1024]{2,1,0:T(8,128)S(1)} %pad_maximum_fusion.2.own_low, f32[2,8,1024]{2,1,0:T(8,128)S(1)} %collective-permute-done.6.own_high, f32[2,8,1024]{2,1,0:T(8,128)S(1)} %pad_maximum_fusion.3.mirror_low, ...), custom_call_target="tpu_custom_call" | custom-call | flops 4294967296 | bytes 16777216 | tf_op jit(solution)/shard_map/cross/pallas_call | solution.py:216
  26.7 1.8 %collective-permute-done.1.own_high = f32[2,24,1024]{2,1,0:T(8,128)S(1)} collective-permute-done((f32[2,24,1024]{2,1,0:T(8,128)S(1)}, f32[2,24,1024]{2,1,0:T(8,128)S(1)}, u32[]{:S(2)}, u32[]{:S(2)}) %collective-permute-start.1) | collective-permute-done | bytes 196640 | tf_op jit(solution)/shard_map/ppermute | solution.py:244
  28.5 0.0 collective-permute-done.4.mirror_high
  28.5 18.1 %cross.3 = bf16[16,2,1024,1024]{3,2,1,0:T(8,128)(2,1)} custom-call(s32[1]{0:T(128)} %bitcast.turn_ref, f32[2,24,1024]{2,1,0:T(8,128)S(1)} %pad_maximum_fusion.own_low, f32[2,24,1024]{2,1,0:T(8,128)S(1)} %collective-permute-done.1.own_high, f32[2,24,1024]{2,1,0:T(8,128)S(1)} %pad_maximum_fusion.1.mirror_low, ...), custom_call_target="tpu_custom_call", output_to_operand_aliasing={{}: (5, {})} | custom-call | flops 12884901888 | bytes 50331648 | tf_op jit(solution)/shard_map/cross/pallas_call | solution.py:216
  (4 shorter events, 0.0 us)
Async XLA Ops:
  4.0 7.8 %collective-permute-start.7 = (f32[8,1024]{1,0:T(8,128)S(1)}, f32[8,1024]{1,0:T(8,128)S(1)}, u32[]{:S(2)}, u32[]{:S(2)}) collective-permute-start(f32[8,1024]{1,0:T(8,128)S(1)} %get-tuple-element.8), channel_id=1, source_target_pairs={{0,16},{2,24},{4,0},{6,8},{8,10},{10,2},{12,26},{14,18},{16,12},{1... | collective-permute-start | bytes 98312 | tf_op jit(solution)/shard_map/ppermute | solution.py:265
  7.0 4.8 %collective-permute-start.5 = (f32[1,8,1024]{2,1,0:T(8,128)S(1)}, f32[1,8,1024]{2,1,0:T(8,128)S(1)}, u32[]{:S(2)}, u32[]{:S(2)}) collective-permute-start(f32[1,8,1024]{2,1,0:T(8,128)S(1)} %bitcast.8), channel_id=1, source_target_pairs={{0,2},{2,0},{4,6},{6,4},{1,3},{3,1},{5,7},{7,5},{8,10},{10,8},{12,... | collective-permute-start | bytes 98312 | tf_op jit(solution)/shard_map/ppermute | solution.py:244
  7.9 8.0 %collective-permute-start.2 = (f32[24,1024]{1,0:T(8,128)S(1)}, f32[24,1024]{1,0:T(8,128)S(1)}, u32[]{:S(2)}, u32[]{:S(2)}) collective-permute-start(f32[24,1024]{1,0:T(8,128)S(1)} %get-tuple-element.7), channel_id=1, source_target_pairs={{0,16},{2,24},{4,0},{6,8},{8,10},{10,2},{12,26},{14,18},{16,12},{1... | collective-permute-start | bytes 294920 | tf_op jit(solution)/shard_map/ppermute | solution.py:265
  10.1 6.5 %collective-permute-start = (f32[1,24,1024]{2,1,0:T(8,128)S(1)}, f32[1,24,1024]{2,1,0:T(8,128)S(1)}, u32[]{:S(2)}, u32[]{:S(2)}) collective-permute-start(f32[1,24,1024]{2,1,0:T(8,128)S(1)} %bitcast.6), channel_id=1, source_target_pairs={{0,2},{2,0},{4,6},{6,4},{1,3},{3,1},{5,7},{7,5},{8,10},{10,8},{12,... | collective-permute-start | bytes 294920 | tf_op jit(solution)/shard_map/ppermute | solution.py:244
  11.8 1.8 %collective-permute-start.8 = (f32[1,8,1024]{2,1,0:T(8,128)S(1)}, f32[1,8,1024]{2,1,0:T(8,128)S(1)}, u32[]{:S(2)}, u32[]{:S(2)}) collective-permute-start(f32[1,8,1024]{2,1,0:T(8,128)S(1)} %bitcast.12), channel_id=1, source_target_pairs={{0,8},{8,0},{16,24},{24,16},{1,9},{9,1},{17,25},{25,17},{2,10},{10... | collective-permute-start | bytes 98312 | tf_op jit(solution)/shard_map/ppermute | solution.py:244
  11.8 7.3 %collective-permute-start.6 = (f32[2,8,1024]{2,1,0:T(8,128)S(1)}, f32[2,8,1024]{2,1,0:T(8,128)S(1)}, u32[]{:S(2)}, u32[]{:S(2)}) collective-permute-start(f32[2,8,1024]{2,1,0:T(8,128)S(1)} %pad_maximum_fusion.2.own_low), channel_id=1, source_target_pairs={{0,4},{2,6},{4,0},{6,2},{1,5},{3,7},{5,1},{7,3},{8,12},{10,14},{12... | collective-permute-start | bytes 196616 | tf_op jit(solution)/shard_map/ppermute | solution.py:244
  13.6 5.5 %collective-permute-start.9 = (f32[2,8,1024]{2,1,0:T(8,128)S(1)}, f32[2,8,1024]{2,1,0:T(8,128)S(1)}, u32[]{:S(2)}, u32[]{:S(2)}) collective-permute-start(f32[2,8,1024]{2,1,0:T(8,128)S(1)} %pad_maximum_fusion.3.mirror_low), channel_id=1, source_target_pairs={{0,16},{8,24},{16,0},{24,8},{1,17},{9,25},{17,1},{25,9},{2,18},{10... | collective-permute-start | bytes 196616 | tf_op jit(solution)/shard_map/ppermute | solution.py:244
  15.9 2.7 %collective-permute-start.3 = (f32[1,24,1024]{2,1,0:T(8,128)S(1)}, f32[1,24,1024]{2,1,0:T(8,128)S(1)}, u32[]{:S(2)}, u32[]{:S(2)}) collective-permute-start(f32[1,24,1024]{2,1,0:T(8,128)S(1)} %bitcast.10), channel_id=1, source_target_pairs={{0,8},{8,0},{16,24},{24,16},{1,9},{9,1},{17,25},{25,17},{2,10},{10... | collective-permute-start | bytes 294920 | tf_op jit(solution)/shard_map/ppermute | solution.py:244
  16.6 11.9 %collective-permute-start.1 = (f32[2,24,1024]{2,1,0:T(8,128)S(1)}, f32[2,24,1024]{2,1,0:T(8,128)S(1)}, u32[]{:S(2)}, u32[]{:S(2)}) collective-permute-start(f32[2,24,1024]{2,1,0:T(8,128)S(1)} %pad_maximum_fusion.own_low), channel_id=1, source_target_pairs={{0,4},{2,6},{4,0},{6,2},{1,5},{3,7},{5,1},{7,3},{8,12},{10,14},{12... | collective-permute-start | bytes 589832 | tf_op jit(solution)/shard_map/ppermute | solution.py:244
  18.6 9.8 %collective-permute-start.4 = (f32[2,24,1024]{2,1,0:T(8,128)S(1)}, f32[2,24,1024]{2,1,0:T(8,128)S(1)}, u32[]{:S(2)}, u32[]{:S(2)}) collective-permute-start(f32[2,24,1024]{2,1,0:T(8,128)S(1)} %pad_maximum_fusion.1.mirror_low), channel_id=1, source_target_pairs={{0,16},{8,24},{16,0},{24,8},{1,17},{9,25},{17,1},{25,9},{2,18},{10... | collective-permute-start | bytes 589832 | tf_op jit(solution)/shard_map/ppermute | solution.py:244

commit v18 on v17

--- a/solution.py
+++ b/solution.py
@@ -198,8 +198,8 @@
                     copy(step, slot, q, t).start(priority=t % 2)
         return carry
 
-    body(jnp.int32(0), 0, height // tile)
-    lax.fori_loop(1, size, body, 0)
+    lax.fori_loop(0, size - 1, body, 0)
+    body(jnp.int32(size - 1), 0, min(2, height // tile))
     for last in range(size - BUFFERS, size):
         for q, t in pieces:
             copy(last, last % BUFFERS, q, t).wait()
@@ -257,8 +257,8 @@
     n = lax.axis_size("col")
     bins = NB // lax.axis_size("bin")
     sizes = (GROUP, bins - GROUP)
-    across = [n // 4 if (c ^ c >> 1) & 1 else n // 2 for c in range(n)]
-    turn = (row ^ col ^ jnp.where((col ^ col >> 1) & 1 == 1, n // 4, n // 2)).reshape(1)
+    across = [n // 2 if (c ^ c >> 1) & 1 else n // 4 for c in range(n)]
+    turn = (row ^ col ^ jnp.where((col ^ col >> 1) & 1 == 1, n // 2, n // 4)).reshape(1)
     swap = [(r * n + w, (w ^ across[r]) * n + r) for r in range(n) for w in range(n)]
     parts = []
     for block in whiten(records, offsets, live_flags, sizes):

time: 46.8 us -> 47.1 us (level)
  starting transfers between devices: 12.1 us -> 17 us
  waiting for transfers between devices: 4.79 us -> 0.03 us
    ppermute x8, starting transfers between devices: 6.89 us -> 15.5 us  [exchange(): return lax.ppermute(block, axis, [(i, i ^ distance) for i in range(n)])]
    ppermute x2, starting transfers between devices: 5.22 us -> 1.51 us  [per_device(): other = lax.ppermute(block, ('row', 'col'), swap)]
    ppermute x8, waiting for transfers between devices: 2.89 us -> 0.02 us  [exchange(): return lax.ppermute(block, axis, [(i, i ^ distance) for i in range(n)])]
    ppermute x2, waiting for transfers between devices: 1.9 us -> 0.01 us  [per_device(): other = lax.ppermute(block, ('row', 'col'), swap)]
  transfers between devices with their start and end apart: 10 -> 10, of which waited for: 4 -> 0; matrix products, arithmetic and copies ran while one was open for 0% -> 0% of each run, Pallas kernels for 16% -> 16%
where the time goes in v18:
time: 47.1 us; the launch traced here: 46.9 us
  Pallas kernels  29.2 us (62%)
  starting transfers between devices  17 us (36%)
  between operations  0.71 us (2%)
    pallas_call x2, Pallas kernels, cross(): pl.pallas_call(functools.partial(cross_kernel, size, first), in_specs=[pl...  25.8 us
    ppermute x8, starting transfers between devices, exchange(): return lax.ppermute(block, axis, [(i, i ^ distance) for i in range(n)])  15.5 us
    pallas_call x1, Pallas kernels, whiten(): pl.pallas_call(functools.partial(whiten_kernel, sizes), in_specs=[pl.Bloc...  3.34 us
    ppermute x2, starting transfers between devices, per_device(): other = lax.ppermute(block, ('row', 'col'), swap)  1.51 us
  transfers between devices with their start and end apart: 10, of which 0 were waited for; matrix products, arithmetic and copies ran while one was open for 0% of the time, Pallas kernels for 16%

profile of v18, /device:TPU:0, one launch (start us, length us, event | category | flops | bytes accessed | tf_op | source)
XLA Modules:
  0.0 46.9 jit_solution(4566277777646743690)
XLA Ops:
  0.7 3.3 %whiten.1 = (f32[8,1024]{1,0:T(8,128)S(1)}, f32[24,1024]{1,0:T(8,128)S(1)}) custom-call(s32[1]{0:T(128)S(6)} %copy.7.offset_ref, f32[1000,128]{1,0:T(8,128)} %constant.15.clone.table_hbm, bf16[1024,1664]{1,0:T(8,128)(2,1)} %records_hbm.1, s32[1,1024]{1,0:T(1,128)} %bitcast.14), custom_call_target="tpu_custom_call" | custom-call | flops 218103808 | bytes 3407872 | tf_op jit(solution)/shard_map/whiten/pallas_call | solution.py:72
  4.0 0.5 %collective-permute-start.7 = (f32[8,1024]{1,0:T(8,128)S(1)}, f32[8,1024]{1,0:T(8,128)S(1)}, u32[]{:S(2)}, u32[]{:S(2)}) collective-permute-start(f32[8,1024]{1,0:T(8,128)S(1)} %get-tuple-element.8), channel_id=1, source_target_pairs={{0,8},{2,0},{4,24},{6,16},{8,18},{10,26},{12,2},{14,10},{16,20},{1... | collective-permute-start | bytes 98312 | tf_op jit(solution)/shard_map/ppermute | solution.py:265
  4.5 2.6 %collective-permute-start.5 = (f32[1,8,1024]{2,1,0:T(8,128)S(1)}, f32[1,8,1024]{2,1,0:T(8,128)S(1)}, u32[]{:S(2)}, u32[]{:S(2)}) collective-permute-start(f32[1,8,1024]{2,1,0:T(8,128)S(1)} %bitcast.8), channel_id=1, source_target_pairs={{0,2},{2,0},{4,6},{6,4},{1,3},{3,1},{5,7},{7,5},{8,10},{10,8},{12,... | collective-permute-start | bytes 98312 | tf_op jit(solution)/shard_map/ppermute | solution.py:244
  7.2 1.0 %collective-permute-start.2 = (f32[24,1024]{1,0:T(8,128)S(1)}, f32[24,1024]{1,0:T(8,128)S(1)}, u32[]{:S(2)}, u32[]{:S(2)}) collective-permute-start(f32[24,1024]{1,0:T(8,128)S(1)} %get-tuple-element.7), channel_id=1, source_target_pairs={{0,8},{2,0},{4,24},{6,16},{8,18},{10,26},{12,2},{14,10},{16,20},{1... | collective-permute-start | bytes 294920 | tf_op jit(solution)/shard_map/ppermute | solution.py:265
  8.2 1.0 %collective-permute-start = (f32[1,24,1024]{2,1,0:T(8,128)S(1)}, f32[1,24,1024]{2,1,0:T(8,128)S(1)}, u32[]{:S(2)}, u32[]{:S(2)}) collective-permute-start(f32[1,24,1024]{2,1,0:T(8,128)S(1)} %bitcast.6), channel_id=1, source_target_pairs={{0,2},{2,0},{4,6},{6,4},{1,3},{3,1},{5,7},{7,5},{8,10},{10,8},{12,... | collective-permute-start | bytes 294920 | tf_op jit(solution)/shard_map/ppermute | solution.py:244
  9.2 0.0 collective-permute-done.7
  9.2 2.1 %collective-permute-start.8 = (f32[1,8,1024]{2,1,0:T(8,128)S(1)}, f32[1,8,1024]{2,1,0:T(8,128)S(1)}, u32[]{:S(2)}, u32[]{:S(2)}) collective-permute-start(f32[1,8,1024]{2,1,0:T(8,128)S(1)} %bitcast.12), channel_id=1, source_target_pairs={{0,8},{8,0},{16,24},{24,16},{1,9},{9,1},{17,25},{25,17},{2,10},{10... | collective-permute-start | bytes 98312 | tf_op jit(solution)/shard_map/ppermute | solution.py:244
  11.3 0.0 collective-permute-done.5
  11.3 2.2 %collective-permute-start.6 = (f32[2,8,1024]{2,1,0:T(8,128)S(1)}, f32[2,8,1024]{2,1,0:T(8,128)S(1)}, u32[]{:S(2)}, u32[]{:S(2)}) collective-permute-start(f32[2,8,1024]{2,1,0:T(8,128)S(1)} %pad_maximum_fusion.2.own_low), channel_id=1, source_target_pairs={{0,4},{2,6},{4,0},{6,2},{1,5},{3,7},{5,1},{7,3},{8,12},{10,14},{12... | collective-permute-start | bytes 196616 | tf_op jit(solution)/shard_map/ppermute | solution.py:244
  13.5 0.0 collective-permute-done.8
  13.6 1.4 %collective-permute-start.9 = (f32[2,8,1024]{2,1,0:T(8,128)S(1)}, f32[2,8,1024]{2,1,0:T(8,128)S(1)}, u32[]{:S(2)}, u32[]{:S(2)}) collective-permute-start(f32[2,8,1024]{2,1,0:T(8,128)S(1)} %pad_maximum_fusion.3.mirror_low), channel_id=1, source_target_pairs={{0,16},{8,24},{16,0},{24,8},{1,17},{9,25},{17,1},{25,9},{2,18},{10... | collective-permute-start | bytes 196616 | tf_op jit(solution)/shard_map/ppermute | solution.py:244
  15.0 0.0 collective-permute-done.2
  15.0 0.0 collective-permute-start.3
  15.0 0.0 collective-permute-done
  15.0 3.4 %collective-permute-start.1 = (f32[2,24,1024]{2,1,0:T(8,128)S(1)}, f32[2,24,1024]{2,1,0:T(8,128)S(1)}, u32[]{:S(2)}, u32[]{:S(2)}) collective-permute-start(f32[2,24,1024]{2,1,0:T(8,128)S(1)} %pad_maximum_fusion.own_low), channel_id=1, source_target_pairs={{0,4},{2,6},{4,0},{6,2},{1,5},{3,7},{5,1},{7,3},{8,12},{10,14},{12... | collective-permute-start | bytes 589832 | tf_op jit(solution)/shard_map/ppermute | solution.py:244
  18.4 0.0 collective-permute-done.3
  18.4 2.6 %collective-permute-start.4 = (f32[2,24,1024]{2,1,0:T(8,128)S(1)}, f32[2,24,1024]{2,1,0:T(8,128)S(1)}, u32[]{:S(2)}, u32[]{:S(2)}) collective-permute-start(f32[2,24,1024]{2,1,0:T(8,128)S(1)} %pad_maximum_fusion.1.mirror_low), channel_id=1, source_target_pairs={{0,16},{8,24},{16,0},{24,8},{1,17},{9,25},{17,1},{25,9},{2,18},{10... | collective-permute-start | bytes 589832 | tf_op jit(solution)/shard_map/ppermute | solution.py:244
  21.1 0.0 collective-permute-done.6.own_high
  21.1 0.0 collective-permute-done.9.mirror_high
  21.1 7.6 %cross.2.refs_0_ = bf16[16,2,1024,1024]{3,2,1,0:T(8,128)(2,1)} custom-call(s32[1]{0:T(128)} %bitcast.turn_ref, f32[2,8,1024]{2,1,0:T(8,128)S(1)} %pad_maximum_fusion.2.own_low, f32[2,8,1024]{2,1,0:T(8,128)S(1)} %collective-permute-done.6.own_high, f32[2,8,1024]{2,1,0:T(8,128)S(1)} %pad_maximum_fusion.3.mirror_low, ...), custom_call_target="tpu_custom_call" | custom-call | flops 4294967296 | bytes 16777216 | tf_op jit(solution)/shard_map/cross/pallas_call | solution.py:216
  28.6 0.0 collective-permute-done.1.own_high
  28.6 0.0 collective-permute-done.4.mirror_high
  28.7 18.3 %cross.3 = bf16[16,2,1024,1024]{3,2,1,0:T(8,128)(2,1)} custom-call(s32[1]{0:T(128)} %bitcast.turn_ref, f32[2,24,1024]{2,1,0:T(8,128)S(1)} %pad_maximum_fusion.own_low, f32[2,24,1024]{2,1,0:T(8,128)S(1)} %collective-permute-done.1.own_high, f32[2,24,1024]{2,1,0:T(8,128)S(1)} %pad_maximum_fusion.1.mirror_low, ...), custom_call_target="tpu_custom_call", output_to_operand_aliasing={{}: (5, {})} | custom-call | flops 12884901888 | bytes 50331648 | tf_op jit(solution)/shard_map/cross/pallas_call | solution.py:216
  (4 shorter events, 0.0 us)
Async XLA Ops:
  4.0 5.2 %collective-permute-start.7 = (f32[8,1024]{1,0:T(8,128)S(1)}, f32[8,1024]{1,0:T(8,128)S(1)}, u32[]{:S(2)}, u32[]{:S(2)}) collective-permute-start(f32[8,1024]{1,0:T(8,128)S(1)} %get-tuple-element.8), channel_id=1, source_target_pairs={{0,8},{2,0},{4,24},{6,16},{8,18},{10,26},{12,2},{14,10},{16,20},{1... | collective-permute-start | bytes 98312 | tf_op jit(solution)/shard_map/ppermute | solution.py:265
  4.5 6.8 %collective-permute-start.5 = (f32[1,8,1024]{2,1,0:T(8,128)S(1)}, f32[1,8,1024]{2,1,0:T(8,128)S(1)}, u32[]{:S(2)}, u32[]{:S(2)}) collective-permute-start(f32[1,8,1024]{2,1,0:T(8,128)S(1)} %bitcast.8), channel_id=1, source_target_pairs={{0,2},{2,0},{4,6},{6,4},{1,3},{3,1},{5,7},{7,5},{8,10},{10,8},{12,... | collective-permute-start | bytes 98312 | tf_op jit(solution)/shard_map/ppermute | solution.py:244
  7.2 7.8 %collective-permute-start.2 = (f32[24,1024]{1,0:T(8,128)S(1)}, f32[24,1024]{1,0:T(8,128)S(1)}, u32[]{:S(2)}, u32[]{:S(2)}) collective-permute-start(f32[24,1024]{1,0:T(8,128)S(1)} %get-tuple-element.7), channel_id=1, source_target_pairs={{0,8},{2,0},{4,24},{6,16},{8,18},{10,26},{12,2},{14,10},{16,20},{1... | collective-permute-start | bytes 294920 | tf_op jit(solution)/shard_map/ppermute | solution.py:265
  8.2 6.8 %collective-permute-start = (f32[1,24,1024]{2,1,0:T(8,128)S(1)}, f32[1,24,1024]{2,1,0:T(8,128)S(1)}, u32[]{:S(2)}, u32[]{:S(2)}) collective-permute-start(f32[1,24,1024]{2,1,0:T(8,128)S(1)} %bitcast.6), channel_id=1, source_target_pairs={{0,2},{2,0},{4,6},{6,4},{1,3},{3,1},{5,7},{7,5},{8,10},{10,8},{12,... | collective-permute-start | bytes 294920 | tf_op jit(solution)/shard_map/ppermute | solution.py:244
  9.2 4.3 %collective-permute-start.8 = (f32[1,8,1024]{2,1,0:T(8,128)S(1)}, f32[1,8,1024]{2,1,0:T(8,128)S(1)}, u32[]{:S(2)}, u32[]{:S(2)}) collective-permute-start(f32[1,8,1024]{2,1,0:T(8,128)S(1)} %bitcast.12), channel_id=1, source_target_pairs={{0,8},{8,0},{16,24},{24,16},{1,9},{9,1},{17,25},{25,17},{2,10},{10... | collective-permute-start | bytes 98312 | tf_op jit(solution)/shard_map/ppermute | solution.py:244
  11.3 9.7 %collective-permute-start.6 = (f32[2,8,1024]{2,1,0:T(8,128)S(1)}, f32[2,8,1024]{2,1,0:T(8,128)S(1)}, u32[]{:S(2)}, u32[]{:S(2)}) collective-permute-start(f32[2,8,1024]{2,1,0:T(8,128)S(1)} %pad_maximum_fusion.2.own_low), channel_id=1, source_target_pairs={{0,4},{2,6},{4,0},{6,2},{1,5},{3,7},{5,1},{7,3},{8,12},{10,14},{12... | collective-permute-start | bytes 196616 | tf_op jit(solution)/shard_map/ppermute | solution.py:244
  13.6 7.5 %collective-permute-start.9 = (f32[2,8,1024]{2,1,0:T(8,128)S(1)}, f32[2,8,1024]{2,1,0:T(8,128)S(1)}, u32[]{:S(2)}, u32[]{:S(2)}) collective-permute-start(f32[2,8,1024]{2,1,0:T(8,128)S(1)} %pad_maximum_fusion.3.mirror_low), channel_id=1, source_target_pairs={{0,16},{8,24},{16,0},{24,8},{1,17},{9,25},{17,1},{25,9},{2,18},{10... | collective-permute-start | bytes 196616 | tf_op jit(solution)/shard_map/ppermute | solution.py:244
  15.0 3.4 %collective-permute-start.3 = (f32[1,24,1024]{2,1,0:T(8,128)S(1)}, f32[1,24,1024]{2,1,0:T(8,128)S(1)}, u32[]{:S(2)}, u32[]{:S(2)}) collective-permute-start(f32[1,24,1024]{2,1,0:T(8,128)S(1)} %bitcast.10), channel_id=1, source_target_pairs={{0,8},{8,0},{16,24},{24,16},{1,9},{9,1},{17,25},{25,17},{2,10},{10... | collective-permute-start | bytes 294920 | tf_op jit(solution)/shard_map/ppermute | solution.py:244
  15.0 13.6 %collective-permute-start.1 = (f32[2,24,1024]{2,1,0:T(8,128)S(1)}, f32[2,24,1024]{2,1,0:T(8,128)S(1)}, u32[]{:S(2)}, u32[]{:S(2)}) collective-permute-start(f32[2,24,1024]{2,1,0:T(8,128)S(1)} %pad_maximum_fusion.own_low), channel_id=1, source_target_pairs={{0,4},{2,6},{4,0},{6,2},{1,5},{3,7},{5,1},{7,3},{8,12},{10,14},{12... | collective-permute-start | bytes 589832 | tf_op jit(solution)/shard_map/ppermute | solution.py:244
  18.4 10.2 %collective-permute-start.4 = (f32[2,24,1024]{2,1,0:T(8,128)S(1)}, f32[2,24,1024]{2,1,0:T(8,128)S(1)}, u32[]{:S(2)}, u32[]{:S(2)}) collective-permute-start(f32[2,24,1024]{2,1,0:T(8,128)S(1)} %pad_maximum_fusion.1.mirror_low), channel_id=1, source_target_pairs={{0,16},{8,24},{16,0},{24,8},{1,17},{9,25},{17,1},{25,9},{2,18},{10... | collective-permute-start | bytes 589832 | tf_op jit(solution)/shard_map/ppermute | solution.py:244

commit v19 on v17

--- a/solution.py
+++ b/solution.py
@@ -124,7 +124,7 @@
             sems.at[slot, q * (height // tile) + t],
         )
 
-    picked[:, width:] = jnp.zeros((height, depth - width), jnp.bfloat16)
+    picked[:, :, width:] = jnp.zeros((2, height, depth - width), jnp.bfloat16)
     right[:, 3 * terms :] = jnp.zeros((2, depth - 3 * terms, channels), jnp.bfloat16)
 
     def prepare(at):
@@ -138,21 +138,23 @@
             high, low = split(block)
             right[q, : 3 * terms] = jnp.concatenate([high, low, high], axis=0).astype(jnp.bfloat16)
 
+    def pick(at_step, inner):
+        lane = lax.broadcasted_iota(jnp.int32, (1, width), 1)
+        mask = jnp.where(lane % rows // 2 == inner, 1.0, 0.0).astype(jnp.bfloat16)
+        picked[at_step % 2, :, :width] = left[...] * mask
+
     def body(step, carry, cuts=1):
         slot, inner = step % BUFFERS, step % GROUP
 
         @pl.when(inner == 0)
         def _():
             prepare(pl.multiple_of(step * 2, rows))
+            pick(step, 0)
 
         @pl.when(step >= BUFFERS)
         def _():
             for q, t in pieces:
                 copy(step - BUFFERS, slot, q, t).wait()
-
-        lane = lax.broadcasted_iota(jnp.int32, (1, width), 1)
-        mask = jnp.where(lane % rows // 2 == inner, 1.0, 0.0).astype(jnp.bfloat16)
-        picked[:, :width] = left[...] * mask
 
         def multiply(cut, *accs):
             def stage(number):
@@ -179,13 +181,15 @@
                     for q in range(2):
                         pltpu.matmul_acc_lhs(
                             accs[q * SLOTS + place],
-                            picked[j * CHUNK : (j + 1) * CHUNK, k * 256 : (k + 1) * 256],
+                            picked[step % 2, j * CHUNK : (j + 1) * CHUNK, k * 256 : (k + 1) * 256],
                             load_staged_rhs=number % 2 if j == cut * chunks else None,
                         )
                     if j == cut * chunks and number + 1 < len(stages):
                         stage(number + 1)
                     if k == deep - 1:
                         waiting.append((n, j, place))
+            if cut == cuts - 1:
+                pick(step + 1, inner + 1)
             for entry in waiting:
                 retire(*entry)
 
@@ -223,7 +227,7 @@
             pltpu.VMEM((terms, channels), jnp.float32),
             pltpu.VMEM((channels, width), jnp.bfloat16),
             pltpu.VMEM((2, depth, channels), jnp.bfloat16),
-            pltpu.VMEM((height, depth), jnp.bfloat16),
+            pltpu.VMEM((2, height, depth), jnp.bfloat16),
             pltpu.VMEM((BUFFERS, 2, height, channels), jnp.bfloat16),
             pltpu.SemaphoreType.DMA((BUFFERS, 2 * (height // min(256, height)))),
         ],

time: 46.8 us -> 46.8 us (level)
  no operation moved by 1% of the time
where the time goes in v19:
time: 46.8 us; the launch traced here: 46.7 us
  Pallas kernels  29.1 us (62%)
  starting transfers between devices  12.1 us (26%)
  waiting for transfers between devices  4.75 us (10%)
  between operations  0.7 us (1%)
    pallas_call x2, Pallas kernels, cross(): pl.pallas_call(functools.partial(cross_kernel, size, first), in_specs=[pl...  25.7 us
    ppermute x8, starting transfers between devices, exchange(): return lax.ppermute(block, axis, [(i, i ^ distance) for i in range(n)])  6.89 us
    ppermute x2, starting transfers between devices, per_device(): other = lax.ppermute(block, ('row', 'col'), swap)  5.22 us
    pallas_call x1, Pallas kernels, whiten(): pl.pallas_call(functools.partial(whiten_kernel, sizes), in_specs=[pl.Bloc...  3.34 us
    ppermute x8, waiting for transfers between devices, exchange(): return lax.ppermute(block, axis, [(i, i ^ distance) for i in range(n)])  2.85 us
    ppermute x2, waiting for transfers between devices, per_device(): other = lax.ppermute(block, ('row', 'col'), swap)  1.9 us
  transfers between devices with their start and end apart: 10, of which 4 were waited for; matrix products, arithmetic and copies ran while one was open for 0% of the time, Pallas kernels for 16%

profile of v19, /device:TPU:0, one launch (start us, length us, event | category | flops | bytes accessed | tf_op | source)
XLA Modules:
  0.0 46.7 jit_solution(15705278908696367176)
XLA Ops:
  0.7 3.3 %whiten.1 = (f32[8,1024]{1,0:T(8,128)S(1)}, f32[24,1024]{1,0:T(8,128)S(1)}) custom-call(s32[1]{0:T(128)S(6)} %copy.7.offset_ref, f32[1000,128]{1,0:T(8,128)} %constant.15.clone.table_hbm, bf16[1024,1664]{1,0:T(8,128)(2,1)} %records_hbm.1, s32[1,1024]{1,0:T(1,128)} %bitcast.14), custom_call_target="tpu_custom_call" | custom-call | flops 218103808 | bytes 3407872 | tf_op jit(solution)/shard_map/whiten/pallas_call | solution.py:72
  4.0 3.0 %collective-permute-start.7 = (f32[8,1024]{1,0:T(8,128)S(1)}, f32[8,1024]{1,0:T(8,128)S(1)}, u32[]{:S(2)}, u32[]{:S(2)}) collective-permute-start(f32[8,1024]{1,0:T(8,128)S(1)} %get-tuple-element.8), channel_id=1, source_target_pairs={{0,16},{2,24},{4,0},{6,8},{8,10},{10,2},{12,26},{14,18},{16,12},{1... | collective-permute-start | bytes 98312 | tf_op jit(solution)/shard_map/ppermute | solution.py:269
  7.0 0.9 %collective-permute-start.5 = (f32[1,8,1024]{2,1,0:T(8,128)S(1)}, f32[1,8,1024]{2,1,0:T(8,128)S(1)}, u32[]{:S(2)}, u32[]{:S(2)}) collective-permute-start(f32[1,8,1024]{2,1,0:T(8,128)S(1)} %bitcast.8), channel_id=1, source_target_pairs={{0,2},{2,0},{4,6},{6,4},{1,3},{3,1},{5,7},{7,5},{8,10},{10,8},{12,... | collective-permute-start | bytes 98312 | tf_op jit(solution)/shard_map/ppermute | solution.py:248
  7.9 2.2 %collective-permute-start.2 = (f32[24,1024]{1,0:T(8,128)S(1)}, f32[24,1024]{1,0:T(8,128)S(1)}, u32[]{:S(2)}, u32[]{:S(2)}) collective-permute-start(f32[24,1024]{1,0:T(8,128)S(1)} %get-tuple-element.7), channel_id=1, source_target_pairs={{0,16},{2,24},{4,0},{6,8},{8,10},{10,2},{12,26},{14,18},{16,12},{1... | collective-permute-start | bytes 294920 | tf_op jit(solution)/shard_map/ppermute | solution.py:269
  10.1 1.7 %collective-permute-start = (f32[1,24,1024]{2,1,0:T(8,128)S(1)}, f32[1,24,1024]{2,1,0:T(8,128)S(1)}, u32[]{:S(2)}, u32[]{:S(2)}) collective-permute-start(f32[1,24,1024]{2,1,0:T(8,128)S(1)} %bitcast.6), channel_id=1, source_target_pairs={{0,2},{2,0},{4,6},{6,4},{1,3},{3,1},{5,7},{7,5},{8,10},{10,8},{12,... | collective-permute-start | bytes 294920 | tf_op jit(solution)/shard_map/ppermute | solution.py:248
  11.8 0.0 collective-permute-done.7
  11.8 0.0 collective-permute-start.8
  11.8 0.0 collective-permute-done.5
  11.8 1.8 %collective-permute-start.6 = (f32[2,8,1024]{2,1,0:T(8,128)S(1)}, f32[2,8,1024]{2,1,0:T(8,128)S(1)}, u32[]{:S(2)}, u32[]{:S(2)}) collective-permute-start(f32[2,8,1024]{2,1,0:T(8,128)S(1)} %pad_maximum_fusion.2.own_low), channel_id=1, source_target_pairs={{0,4},{2,6},{4,0},{6,2},{1,5},{3,7},{5,1},{7,3},{8,12},{10,14},{12... | collective-permute-start | bytes 196616 | tf_op jit(solution)/shard_map/ppermute | solution.py:248
  13.6 0.0 collective-permute-done.8
  13.6 0.4 collective-permute-start.9
  14.0 1.9 %collective-permute-done.2 = f32[24,1024]{1,0:T(8,128)S(1)} collective-permute-done((f32[24,1024]{1,0:T(8,128)S(1)}, f32[24,1024]{1,0:T(8,128)S(1)}, u32[]{:S(2)}, u32[]{:S(2)}) %collective-permute-start.2) | collective-permute-done | bytes 98336 | tf_op jit(solution)/shard_map/ppermute | solution.py:269
  15.9 0.0 collective-permute-start.3
  15.9 0.6 %collective-permute-done = f32[1,24,1024]{2,1,0:T(8,128)S(1)} collective-permute-done((f32[1,24,1024]{2,1,0:T(8,128)S(1)}, f32[1,24,1024]{2,1,0:T(8,128)S(1)}, u32[]{:S(2)}, u32[]{:S(2)}) %collective-permute-start) | collective-permute-done | bytes 98336 | tf_op jit(solution)/shard_map/ppermute | solution.py:248
  16.6 2.0 %collective-permute-start.1 = (f32[2,24,1024]{2,1,0:T(8,128)S(1)}, f32[2,24,1024]{2,1,0:T(8,128)S(1)}, u32[]{:S(2)}, u32[]{:S(2)}) collective-permute-start(f32[2,24,1024]{2,1,0:T(8,128)S(1)} %pad_maximum_fusion.own_low), channel_id=1, source_target_pairs={{0,4},{2,6},{4,0},{6,2},{1,5},{3,7},{5,1},{7,3},{8,12},{10,14},{12... | collective-permute-start | bytes 589832 | tf_op jit(solution)/shard_map/ppermute | solution.py:248
  18.6 0.0 collective-permute-done.3
  18.6 0.1 collective-permute-start.4
  18.7 0.4 collective-permute-done.6.own_high
  19.2 0.0 collective-permute-done.9.mirror_high
  19.2 7.5 %cross.2.refs_0_ = bf16[16,2,1024,1024]{3,2,1,0:T(8,128)(2,1)} custom-call(s32[1]{0:T(128)} %bitcast.turn_ref, f32[2,8,1024]{2,1,0:T(8,128)S(1)} %pad_maximum_fusion.2.own_low, f32[2,8,1024]{2,1,0:T(8,128)S(1)} %collective-permute-done.6.own_high, f32[2,8,1024]{2,1,0:T(8,128)S(1)} %pad_maximum_fusion.3.mirror_low, ...), custom_call_target="tpu_custom_call" | custom-call | flops 4294967296 | bytes 16777216 | tf_op jit(solution)/shard_map/cross/pallas_call | solution.py:220
  26.7 1.8 %collective-permute-done.1.own_high = f32[2,24,1024]{2,1,0:T(8,128)S(1)} collective-permute-done((f32[2,24,1024]{2,1,0:T(8,128)S(1)}, f32[2,24,1024]{2,1,0:T(8,128)S(1)}, u32[]{:S(2)}, u32[]{:S(2)}) %collective-permute-start.1) | collective-permute-done | bytes 196640 | tf_op jit(solution)/shard_map/ppermute | solution.py:248
  28.5 0.0 collective-permute-done.4.mirror_high
  28.5 18.2 %cross.3 = bf16[16,2,1024,1024]{3,2,1,0:T(8,128)(2,1)} custom-call(s32[1]{0:T(128)} %bitcast.turn_ref, f32[2,24,1024]{2,1,0:T(8,128)S(1)} %pad_maximum_fusion.own_low, f32[2,24,1024]{2,1,0:T(8,128)S(1)} %collective-permute-done.1.own_high, f32[2,24,1024]{2,1,0:T(8,128)S(1)} %pad_maximum_fusion.1.mirror_low, ...), custom_call_target="tpu_custom_call", output_to_operand_aliasing={{}: (5, {})} | custom-call | flops 12884901888 | bytes 50331648 | tf_op jit(solution)/shard_map/cross/pallas_call | solution.py:220
  (4 shorter events, 0.0 us)
Async XLA Ops:
  4.0 7.8 %collective-permute-start.7 = (f32[8,1024]{1,0:T(8,128)S(1)}, f32[8,1024]{1,0:T(8,128)S(1)}, u32[]{:S(2)}, u32[]{:S(2)}) collective-permute-start(f32[8,1024]{1,0:T(8,128)S(1)} %get-tuple-element.8), channel_id=1, source_target_pairs={{0,16},{2,24},{4,0},{6,8},{8,10},{10,2},{12,26},{14,18},{16,12},{1... | collective-permute-start | bytes 98312 | tf_op jit(solution)/shard_map/ppermute | solution.py:269
  7.0 4.8 %collective-permute-start.5 = (f32[1,8,1024]{2,1,0:T(8,128)S(1)}, f32[1,8,1024]{2,1,0:T(8,128)S(1)}, u32[]{:S(2)}, u32[]{:S(2)}) collective-permute-start(f32[1,8,1024]{2,1,0:T(8,128)S(1)} %bitcast.8), channel_id=1, source_target_pairs={{0,2},{2,0},{4,6},{6,4},{1,3},{3,1},{5,7},{7,5},{8,10},{10,8},{12,... | collective-permute-start | bytes 98312 | tf_op jit(solution)/shard_map/ppermute | solution.py:248
  7.9 8.0 %collective-permute-start.2 = (f32[24,1024]{1,0:T(8,128)S(1)}, f32[24,1024]{1,0:T(8,128)S(1)}, u32[]{:S(2)}, u32[]{:S(2)}) collective-permute-start(f32[24,1024]{1,0:T(8,128)S(1)} %get-tuple-element.7), channel_id=1, source_target_pairs={{0,16},{2,24},{4,0},{6,8},{8,10},{10,2},{12,26},{14,18},{16,12},{1... | collective-permute-start | bytes 294920 | tf_op jit(solution)/shard_map/ppermute | solution.py:269
  10.1 6.5 %collective-permute-start = (f32[1,24,1024]{2,1,0:T(8,128)S(1)}, f32[1,24,1024]{2,1,0:T(8,128)S(1)}, u32[]{:S(2)}, u32[]{:S(2)}) collective-permute-start(f32[1,24,1024]{2,1,0:T(8,128)S(1)} %bitcast.6), channel_id=1, source_target_pairs={{0,2},{2,0},{4,6},{6,4},{1,3},{3,1},{5,7},{7,5},{8,10},{10,8},{12,... | collective-permute-start | bytes 294920 | tf_op jit(solution)/shard_map/ppermute | solution.py:248
  11.8 1.8 %collective-permute-start.8 = (f32[1,8,1024]{2,1,0:T(8,128)S(1)}, f32[1,8,1024]{2,1,0:T(8,128)S(1)}, u32[]{:S(2)}, u32[]{:S(2)}) collective-permute-start(f32[1,8,1024]{2,1,0:T(8,128)S(1)} %bitcast.12), channel_id=1, source_target_pairs={{0,8},{8,0},{16,24},{24,16},{1,9},{9,1},{17,25},{25,17},{2,10},{10... | collective-permute-start | bytes 98312 | tf_op jit(solution)/shard_map/ppermute | solution.py:248
  11.8 7.3 %collective-permute-start.6 = (f32[2,8,1024]{2,1,0:T(8,128)S(1)}, f32[2,8,1024]{2,1,0:T(8,128)S(1)}, u32[]{:S(2)}, u32[]{:S(2)}) collective-permute-start(f32[2,8,1024]{2,1,0:T(8,128)S(1)} %pad_maximum_fusion.2.own_low), channel_id=1, source_target_pairs={{0,4},{2,6},{4,0},{6,2},{1,5},{3,7},{5,1},{7,3},{8,12},{10,14},{12... | collective-permute-start | bytes 196616 | tf_op jit(solution)/shard_map/ppermute | solution.py:248
  13.6 5.5 %collective-permute-start.9 = (f32[2,8,1024]{2,1,0:T(8,128)S(1)}, f32[2,8,1024]{2,1,0:T(8,128)S(1)}, u32[]{:S(2)}, u32[]{:S(2)}) collective-permute-start(f32[2,8,1024]{2,1,0:T(8,128)S(1)} %pad_maximum_fusion.3.mirror_low), channel_id=1, source_target_pairs={{0,16},{8,24},{16,0},{24,8},{1,17},{9,25},{17,1},{25,9},{2,18},{10... | collective-permute-start | bytes 196616 | tf_op jit(solution)/shard_map/ppermute | solution.py:248
  15.9 2.7 %collective-permute-start.3 = (f32[1,24,1024]{2,1,0:T(8,128)S(1)}, f32[1,24,1024]{2,1,0:T(8,128)S(1)}, u32[]{:S(2)}, u32[]{:S(2)}) collective-permute-start(f32[1,24,1024]{2,1,0:T(8,128)S(1)} %bitcast.10), channel_id=1, source_target_pairs={{0,8},{8,0},{16,24},{24,16},{1,9},{9,1},{17,25},{25,17},{2,10},{10... | collective-permute-start | bytes 294920 | tf_op jit(solution)/shard_map/ppermute | solution.py:248
  16.6 11.9 %collective-permute-start.1 = (f32[2,24,1024]{2,1,0:T(8,128)S(1)}, f32[2,24,1024]{2,1,0:T(8,128)S(1)}, u32[]{:S(2)}, u32[]{:S(2)}) collective-permute-start(f32[2,24,1024]{2,1,0:T(8,128)S(1)} %pad_maximum_fusion.own_low), channel_id=1, source_target_pairs={{0,4},{2,6},{4,0},{6,2},{1,5},{3,7},{5,1},{7,3},{8,12},{10,14},{12... | collective-permute-start | bytes 589832 | tf_op jit(solution)/shard_map/ppermute | solution.py:248
  18.6 9.8 %collective-permute-start.4 = (f32[2,24,1024]{2,1,0:T(8,128)S(1)}, f32[2,24,1024]{2,1,0:T(8,128)S(1)}, u32[]{:S(2)}, u32[]{:S(2)}) collective-permute-start(f32[2,24,1024]{2,1,0:T(8,128)S(1)} %pad_maximum_fusion.1.mirror_low), channel_id=1, source_target_pairs={{0,16},{8,24},{16,0},{24,8},{1,17},{9,25},{17,1},{25,9},{2,18},{10... | collective-permute-start | bytes 589832 | tf_op jit(solution)/shard_map/ppermute | solution.py:248
